TPU v7x, 32 devices: a whole 2x2x4 slice. The times are simulated.
32 devices in a mesh: leaf: 4 (over y, x), front: 8 (over z, core).
Axes of the slice: x: 2, y: 2, z: 4, core: 2. Of those that a mesh axis runs over, the one named last changes fastest.
Arguments:
- front: float32 [2048, 2048], P('leaf', 'front'), as said below
- updates: float32 [128, 128, 128], P(('leaf', 'front')), may hold values from -4 to 4
- target_owner: int32 [128], P(('leaf', 'front')), may hold values from 0 to 7, as said below
- target_slot: int32 [128], P(('leaf', 'front')), may hold values from 0 to 7
Outputs:
- factored: float32 [2048, 2048], P('leaf', 'front')
Inputs may be any that keep to these rules, and one draw needn't show every extreme that they name: `target_owner`: among the 4 blocks of one device every owner index appears at most once; in every group of devices sharing an index of leaf, some owner index is named by every device of the group. The front is symmetric.
All inputs are finite; a program needn't handle non-finite values.
Results may differ from a plain program's by a relative error of at most 0.00015.
Values sent between devices are 32-bit elements; how exact they have to be, the bound alone decides.
No kernel may reach another device: no remote copies, remote signals or barrier semaphores. Data moves between devices by JAX's collectives and lax.ppermute only.
A program may use at most 128 MiB of HBM per device.

v0:
```python
import jax
import jax.numpy as jnp
from jax import lax
from jax.sharding import PartitionSpec as P


def spread(value, axis, source):
    kept = jnp.where(lax.axis_index(axis) == source, value, 0).astype(value.dtype)
    return lax.psum(kept, axis)


def assemble(front, updates, target_owner, target_slot):
    nrows, width = front.shape
    tile = updates.shape[1]
    nfront = lax.axis_size("front")
    buffer = jnp.zeros((nfront, tile, tile), jnp.float32).at[target_owner].set(updates)
    labels = jnp.zeros((nfront,), jnp.float32).at[target_owner].set(target_slot.astype(jnp.float32))
    arrived, places = (
        lax.all_to_all(buffer, "front", split_axis=0, concat_axis=0, tiled=True),
        lax.all_to_all(labels, "front", split_axis=0, concat_axis=0, tiled=True),
    )
    places = places.astype(jnp.int32)
    col_tiles = width // tile
    grid = front.reshape(nrows // tile, tile, col_tiles, tile)
    grid = grid.at[places // col_tiles, :, places % col_tiles, :].add(arrived)
    return grid.reshape(nrows, width)


def eliminate(shard, panel, start, row_ids, col_ids, column):
    nrows, width = panel.shape
    diag = spread(panel[start : start + width], "leaf", 0)
    chol = jnp.linalg.cholesky(diag)
    eye = jnp.eye(width, dtype=jnp.float32)
    inverse = lax.linalg.triangular_solve(chol, eye, left_side=True, lower=True)
    prod = jnp.dot(panel, inverse.T, precision=lax.Precision.HIGHEST)
    lower = jnp.where(row_ids[:, None] >= start, prod, panel)
    owner_row = column * width // nrows
    offset = column * width - owner_row * nrows
    mine = lax.dynamic_slice_in_dim(lower, offset, width, 0)
    across = spread(mine, "leaf", owner_row)
    trail = jnp.where(row_ids[:, None] >= start + width, lower, 0.0)
    updated = shard - jnp.dot(trail, across.T, precision=lax.Precision.HIGHEST)
    updated = jnp.where(col_ids[None, :] >= start + width, updated, shard)
    return (jnp.where(column == start // width, lower, updated), lower)


def shards(front, updates, target_owner, target_slot):
    nrows, width = front.shape
    column = lax.axis_index("front")
    row_ids = lax.axis_index("leaf") * nrows + jnp.arange(nrows, dtype=jnp.int32)
    col_ids = column * width + jnp.arange(width, dtype=jnp.int32)
    shard = assemble(front, updates, target_owner, target_slot)
    first = spread(shard, "front", 0)
    shard, lower = eliminate(shard, first, 0, row_ids, col_ids, column)
    second = spread(shard, "front", 1)
    shard, lower = eliminate(shard, second, width, row_ids, col_ids, column)
    return shard


def solution(mesh):
    return jax.shard_map(
        shards,
        mesh=mesh,
        in_specs=(
            P("leaf", "front"),
            P(("leaf", "front"), None, None),
            P(("leaf", "front")),
            P(("leaf", "front")),
        ),
        out_specs=P("leaf", "front"),
        check_vma=False,
    )
```

profile of v0, /device:TPU:11, one launch (start us, length us, event | category | flops | bytes accessed | tf_op | source)
XLA Modules:
  0.0 466.8 jit_solution(13415349420826600793)
XLA Ops:
  8.5 5.6 %all-to-all-start = ((f32[8,1,1]{2,1,0:T(1,128)}), f32[8,1,1]{2,1,0:T(1,128)S(1)}, u32[]{:S(2)}, u32[]{:S(2)}) async-start(f32[8,1,1]{2,1,0:T(1,128)} %copy.32), calls=%async_computation | async-start | bytes 8192 | tf_op jit(solution)/shard_map/all_to_all | solution.py:20
  15.1 2.2 scatter_fusion
  17.9 5.2 %all-to-all-start.1 = ((f32[8,128,128]{2,1,0:T(8,128)}), f32[8,128,128]{2,1,0:T(8,128)S(1)}, u32[]{:S(2)}, u32[]{:S(2)}) async-start(f32[8,128,128]{2,1,0:T(8,128)} %scatter_fusion), calls=%async_computation.1 | async-start | bytes 1048576 | tf_op jit(solution)/shard_map/all_to_all | solution.py:19
  23.7 11.2 %all-to-all-done.1 = f32[8,128,128]{2,1,0:T(8,128)S(1)} async-done(((f32[8,128,128]{2,1,0:T(8,128)}), f32[8,128,128]{2,1,0:T(8,128)S(1)}, u32[]{:S(2)}, u32[]{:S(2)}) %all-to-all-start.1) | async-done | bytes 524320 | tf_op jit(solution)/shard_map/all_to_all | solution.py:19
  34.9 1.1 scatter_fusion.1
  37.1 55.5 %all-reduce.8.cloned.1.call-done = f32[512,256]{0,1:T(8,128)} async-done(((f32[512,256]{0,1:T(8,128)}), f32[512,256]{0,1:T(8,128)}) %all-reduce.8.cloned.1.call-update) | async-done | bytes 524304 | tf_op jit(solution)/shard_map/psum | solution.py:9
  92.7 1.7 slice_select_fusion.1
  94.5 45.1 %all-reduce.10.cloned.1.call-done = f32[256,256]{0,1:T(8,128)} async-done(((f32[256,256]{0,1:T(8,128)}), f32[256,256]{0,1:T(8,128)}) %all-reduce.10.cloned.1.call-update) | async-done | bytes 262160 | tf_op jit(solution)/shard_map/psum | solution.py:9
  139.6 1.1 copy.35
  140.8 11.7 %cholesky.130 = f32[128,128]{1,0:T(8,128)S(1)} custom-call(f32[128,128]{1,0:T(8,128)S(1)} %cholesky.194), custom_call_target="Cholesky" | custom-call | tf_op jit(solution)/shard_map/jit(cholesky)/cholesky | solution.py:32
  152.6 9.8 %custom-call.15 = f32[1,128,128]{1,2,0:T(8,128)S(1)} custom-call(f32[1,128,128]{2,1,0:T(8,128)S(1)} %get-tuple-element.50), custom_call_target="InvertDiagBlocksLowerTriangular" | custom-call | tf_op jit(solution)/shard_map/jit(cholesky)/cholesky | solution.py:32
  162.9 11.7 %cholesky.147 = f32[128,128]{1,0:T(8,128)S(1)} custom-call(f32[128,128]{1,0:T(8,128)S(1)} %convolution_subtract_fusion.5), custom_call_target="Cholesky" | custom-call | tf_op jit(solution)/shard_map/jit(cholesky)/cholesky | solution.py:32
  176.9 4.3 while.4
  177.7 1.4 bitcast_dynamic-update-slice_fusion.4
  179.7 1.4 bitcast_dynamic-update-slice_fusion.4
  181.2 19.7 %custom-call.16 = f32[2,128,128]{1,2,0:T(8,128)S(1)} custom-call(f32[2,128,128]{2,1,0:T(8,128)S(1)} %get-tuple-element.21), custom_call_target="InvertDiagBlocksLowerTriangular" | custom-call | tf_op jit(solution)/shard_map/triangular_solve/custom-call.0 | solution.py:34
  203.4 43.0 %all-reduce.12.cloned.1.call-done = f32[256,256]{0,1:T(8,128)} async-done(((f32[256,256]{0,1:T(8,128)}), f32[256,256]{0,1:T(8,128)}) %all-reduce.12.cloned.1.call-update) | async-done | bytes 262160 | tf_op jit(solution)/shard_map/psum | solution.py:9
  246.4 2.5 broadcast_select_fusion
  248.9 54.4 %all-reduce.14.cloned.1.call-done = f32[512,256]{0,1:T(8,128)} async-done(((f32[512,256]{0,1:T(8,128)}), f32[512,256]{0,1:T(8,128)}) %all-reduce.14.cloned.1.call-update) | async-done | bytes 524304 | tf_op jit(solution)/shard_map/psum | solution.py:9
  303.4 1.7 slice_select_fusion
  305.1 44.8 %all-reduce.16.cloned.1.call-done = f32[256,256]{0,1:T(8,128)} async-done(((f32[256,256]{0,1:T(8,128)}), f32[256,256]{0,1:T(8,128)}) %all-reduce.16.cloned.1.call-update) | async-done | bytes 262160 | tf_op jit(solution)/shard_map/psum | solution.py:9
  349.9 1.1 copy.38
  351.1 11.7 %cholesky.164 = f32[128,128]{1,0:T(8,128)S(1)} custom-call(f32[128,128]{1,0:T(8,128)S(1)} %cholesky.197), custom_call_target="Cholesky" | custom-call | tf_op jit(solution)/shard_map/jit(cholesky)/cholesky | solution.py:32
  362.9 9.8 %custom-call.17 = f32[1,128,128]{1,2,0:T(8,128)S(1)} custom-call(f32[1,128,128]{2,1,0:T(8,128)S(1)} %get-tuple-element.46), custom_call_target="InvertDiagBlocksLowerTriangular" | custom-call | tf_op jit(solution)/shard_map/jit(cholesky)/cholesky | solution.py:32
  373.2 11.7 %cholesky.181 = f32[128,128]{1,0:T(8,128)S(1)} custom-call(f32[128,128]{1,0:T(8,128)S(1)} %convolution_subtract_fusion.4), custom_call_target="Cholesky" | custom-call | tf_op jit(solution)/shard_map/jit(cholesky)/cholesky | solution.py:32
  387.7 4.3 while.5
  388.6 1.4 bitcast_dynamic-update-slice_fusion.5
  390.6 1.4 bitcast_dynamic-update-slice_fusion.5
  392.1 19.7 %custom-call.18 = f32[2,128,128]{1,2,0:T(8,128)S(1)} custom-call(f32[2,128,128]{2,1,0:T(8,128)S(1)} %get-tuple-element.22), custom_call_target="InvertDiagBlocksLowerTriangular" | custom-call | tf_op jit(solution)/shard_map/triangular_solve/custom-call.0 | solution.py:34
  414.2 43.0 %all-reduce.18.cloned.1.call-done = f32[256,256]{0,1:T(8,128)} async-done(((f32[256,256]{0,1:T(8,128)}), f32[256,256]{0,1:T(8,128)}) %all-reduce.18.cloned.1.call-update) | async-done | bytes 262160 | tf_op jit(solution)/shard_map/psum | solution.py:9
  457.3 1.7 fusion.1
  458.9 1.0 copy.41
  (85 shorter events, 16.1 us)
Async XLA Ops:
  6.5 0.7 copy-start.6
  8.5 9.4 %all-to-all-start = ((f32[8,1,1]{2,1,0:T(1,128)}), f32[8,1,1]{2,1,0:T(1,128)S(1)}, u32[]{:S(2)}, u32[]{:S(2)}) async-start(f32[8,1,1]{2,1,0:T(1,128)} %copy.32), calls=%async_computation | async-start | bytes 8192 | tf_op jit(solution)/shard_map/all_to_all | solution.py:20
  14.1 1.0 copy-start.5
  17.3 5.8 %copy-start.4 = (f32[512,256]{1,0:T(8,128)S(1)}, f32[512,256]{1,0:T(8,128)}, u32[]{:S(2)}) copy-start(f32[512,256]{1,0:T(8,128)} %param.7) | copy-start | bytes 1572868
  17.9 17.0 %all-to-all-start.1 = ((f32[8,128,128]{2,1,0:T(8,128)}), f32[8,128,128]{2,1,0:T(8,128)S(1)}, u32[]{:S(2)}, u32[]{:S(2)}) async-start(f32[8,128,128]{2,1,0:T(8,128)} %scatter_fusion), calls=%async_computation.1 | async-start | bytes 1048576 | tf_op jit(solution)/shard_map/all_to_all | solution.py:19
  23.1 69.6 %all-reduce.8.cloned.1.call-start = ((), (), s32[]{:S(2)}) async-start(), calls=%async_computation.2 | async-start | bytes 1048576 | tf_op jit(solution)/shard_map/psum | solution.py:9
  37.1 102.5 %all-reduce.10.cloned.1.call-start = ((), (), s32[]{:S(2)}) async-start(), calls=%async_computation.3 | async-start | bytes 524288 | tf_op jit(solution)/shard_map/psum | solution.py:9
  94.4 152.0 %all-reduce.12.cloned.1.call-start = ((), (), s32[]{:S(2)}) async-start(), calls=%async_computation.4 | async-start | bytes 524288 | tf_op jit(solution)/shard_map/psum | solution.py:9
  139.6 1.2 copy-start.2
  200.8 1.0 copy-start
  203.3 100.1 %all-reduce.14.cloned.1.call-start = ((), (), s32[]{:S(2)}) async-start(), calls=%async_computation.5 | async-start | bytes 1048576 | tf_op jit(solution)/shard_map/psum | solution.py:9
  248.9 101.0 %all-reduce.16.cloned.1.call-start = ((), (), s32[]{:S(2)}) async-start(), calls=%async_computation.6 | async-start | bytes 524288 | tf_op jit(solution)/shard_map/psum | solution.py:9
  305.0 152.2 %all-reduce.18.cloned.1.call-start = ((), (), s32[]{:S(2)}) async-start(), calls=%async_computation.7 | async-start | bytes 524288 | tf_op jit(solution)/shard_map/psum | solution.py:9
  349.9 1.2 copy-start.3
  411.7 1.0 copy-start.1
Sparse Core Ops, SparseCore 0:
  37.2 55.4 all-reduce.7
  95.8 43.7 all-reduce.9
  203.4 42.9 all-reduce.11
  249.0 54.3 all-reduce.13
  306.1 43.7 all-reduce.15
  414.3 42.9 all-reduce.17
where the time goes:
time: 469 us; the launch traced here: 467 us
  waiting for transfers between devices  298 us (64%)
  other arithmetic  116 us (25%)
  local copies, waits for them, and re-layouts  16.8 us (4%)
  between operations  16.6 us (4%)
  starting transfers between devices  11 us (2%)
  matrix products  8.1 us (2%)
    psum x6, waiting for transfers between devices, spread(): return lax.psum(kept, axis)  286 us
    another operation x13, other arithmetic, eliminate(): chol = jnp.linalg.cholesky(diag)  68.7 us
    another operation x5, other arithmetic, eliminate(): inverse = lax.linalg.triangular_solve(chol, eye, left_side=True, lower=True)  39.4 us
    all_to_all x1, waiting for transfers between devices, assemble(): lax.all_to_all(buffer, 'front', split_axis=0, concat_axis=0, tiled=True)  11.2 us
  transfers between devices with their start and end apart: 8, of which 8 were waited for; matrix products, arithmetic and copies ran while one was open for 1% of the time, Pallas kernels for 0%

commit v1 on v0

--- a/solution.py
+++ b/solution.py
@@ -1,7 +1,17 @@
+import functools
+
 import jax
 import jax.numpy as jnp
 from jax import lax
+from jax.experimental import pallas as pl
+from jax.experimental.pallas import tpu as pltpu
 from jax.sharding import PartitionSpec as P
+
+F32 = jnp.float32
+BF16 = jnp.bfloat16
+AXES = ("leaf", "front")
+EXACT = lax.Precision.HIGHEST
+VMEM_LIMIT = 40 * 1024 * 1024
 
 
 def spread(value, axis, source):
@@ -13,8 +23,8 @@
     nrows, width = front.shape
     tile = updates.shape[1]
     nfront = lax.axis_size("front")
-    buffer = jnp.zeros((nfront, tile, tile), jnp.float32).at[target_owner].set(updates)
-    labels = jnp.zeros((nfront,), jnp.float32).at[target_owner].set(target_slot.astype(jnp.float32))
+    buffer = jnp.zeros((nfront, tile, tile), F32).at[target_owner].set(updates)
+    labels = jnp.zeros((nfront,), F32).at[target_owner].set(target_slot.astype(F32))
     arrived, places = (
         lax.all_to_all(buffer, "front", split_axis=0, concat_axis=0, tiled=True),
         lax.all_to_all(labels, "front", split_axis=0, concat_axis=0, tiled=True),
@@ -30,21 +40,21 @@
     nrows, width = panel.shape
     diag = spread(panel[start : start + width], "leaf", 0)
     chol = jnp.linalg.cholesky(diag)
-    eye = jnp.eye(width, dtype=jnp.float32)
+    eye = jnp.eye(width, dtype=F32)
     inverse = lax.linalg.triangular_solve(chol, eye, left_side=True, lower=True)
-    prod = jnp.dot(panel, inverse.T, precision=lax.Precision.HIGHEST)
+    prod = jnp.dot(panel, inverse.T, precision=EXACT)
     lower = jnp.where(row_ids[:, None] >= start, prod, panel)
     owner_row = column * width // nrows
     offset = column * width - owner_row * nrows
     mine = lax.dynamic_slice_in_dim(lower, offset, width, 0)
     across = spread(mine, "leaf", owner_row)
     trail = jnp.where(row_ids[:, None] >= start + width, lower, 0.0)
-    updated = shard - jnp.dot(trail, across.T, precision=lax.Precision.HIGHEST)
+    updated = shard - jnp.dot(trail, across.T, precision=EXACT)
     updated = jnp.where(col_ids[None, :] >= start + width, updated, shard)
     return (jnp.where(column == start // width, lower, updated), lower)
 
 
-def shards(front, updates, target_owner, target_slot):
+def general(front, updates, target_owner, target_slot):
     nrows, width = front.shape
     column = lax.axis_index("front")
     row_ids = lax.axis_index("leaf") * nrows + jnp.arange(nrows, dtype=jnp.int32)
@@ -57,7 +67,339 @@
     return shard
 
 
+def lane_of(x, c):
+    return jnp.take_along_axis(x, jnp.full(x.shape, c, jnp.int32), axis=1)
+
+
+def row_of(x, i):
+    return jnp.broadcast_to(x[i : i + 1, :], x.shape)
+
+
+def parts(x):
+    high = x.astype(BF16).astype(F32)
+    rest = x - high
+    mid = rest.astype(BF16).astype(F32)
+    return high, mid, (rest - mid).astype(BF16).astype(F32)
+
+
+def factor_inverse(a):
+    n = a.shape[0]
+    panels, per = n // 8, 2
+    sub = lax.broadcasted_iota(jnp.int32, (8, n), 0)
+    lane = lax.broadcasted_iota(jnp.int32, (8, n), 1)
+    work = [
+        [a[8 * k : 8 * k + 8, :], jnp.where(lane == sub + 8 * k, 1.0, 0.0).astype(F32)]
+        for k in range(panels)
+    ]
+    out, held = [], []
+    for k in range(panels):
+        rows, ident = work[k]
+        cols = [lane_of(rows, 8 * k + j) for j in range(8)]
+        d = {(i, j): row_of(cols[j], i) for j in range(8) for i in range(j, 8)}
+        up = [row_of(rows, j) for j in range(8)]
+        inv = [row_of(ident, j) for j in range(8)]
+        last = min(panels - 1, (k // per + 1) * per - 1)
+        below = {
+            b: [lane_of(work[b][0], 8 * k + j) for j in range(8)]
+            for b in range(k + 1, last + 1)
+        }
+        for j in range(8):
+            r = lax.rsqrt(d[j, j])
+            for i in range(j + 1, 8):
+                d[i, j] = d[i, j] * r
+            for i in range(j + 1, 8):
+                for m in range(j + 1, i + 1):
+                    d[i, m] = d[i, m] - d[i, j] * d[m, j]
+            up[j] = up[j] * r
+            inv[j] = inv[j] * r
+            for i in range(j + 1, 8):
+                up[i] = up[i] - d[i, j] * up[j]
+                inv[i] = inv[i] - d[i, j] * inv[j]
+            for b, c in below.items():
+                c[j] = c[j] * r
+                for i in range(j + 1, 8):
+                    c[i] = c[i] - d[i, j] * c[j]
+                work[b] = [work[b][0] - c[j] * up[j], work[b][1] - c[j] * inv[j]]
+        u, w = up[0], inv[0]
+        for j in range(1, 8):
+            u = jnp.where(sub == j, up[j], u)
+            w = jnp.where(sub == j, inv[j], w)
+        out.append(w)
+        held.append((u, w))
+        if k % per == per - 1 and k + 1 < panels:
+            us = jnp.concatenate([p[0] for p in held], 0)
+            ws = jnp.concatenate([p[1] for p in held], 0)
+            uh, um, ul = parts(us)
+            wh, wm, wl = parts(ws)
+            right = jnp.concatenate(
+                [
+                    jnp.concatenate([uh, um, ul, uh, um, uh], 0),
+                    jnp.concatenate([wh, wm, wl, wh, wm, wh], 0),
+                ],
+                1,
+            ).astype(BF16)
+            left = jnp.concatenate([uh, uh, uh, um, um, ul], 0).T
+            left = left[8 * (k + 1) :, :].astype(BF16)
+            change = jnp.dot(left, right, preferred_element_type=F32)
+            for b in range(k + 1, panels):
+                part = change[8 * (b - k - 1) : 8 * (b - k), :]
+                work[b] = [work[b][0] - part[:, :n], work[b][1] - part[:, n:]]
+            held = []
+    return jnp.concatenate(out, 0)
+
+
+def dot(a, b):
+    return jnp.dot(a, b, precision=EXACT, preferred_element_type=F32)
+
+
+def dot_t(a, b):
+    return lax.dot_general(
+        a, b, (((1,), (1,)), ((), ())), precision=EXACT, preferred_element_type=F32
+    )
+
+
+def factor_pair(a):
+    h = a.shape[0] // 2
+    w11 = factor_inverse(a[:h, :h])
+    l21 = dot_t(a[h:, :h], w11)
+    w22 = factor_inverse(a[h:, h:] - dot_t(l21, l21))
+    w21 = -dot(w22, dot(l21, w11))
+    return w11, w21, w22
+
+
+def store_inverse(ref, blocks):
+    w11, w21, w22 = blocks
+    h = w11.shape[0]
+    ref[:h, :h] = w11
+    ref[:h, h:] = jnp.zeros_like(w11)
+    ref[h:, :h] = w21
+    ref[h:, h:] = w22
+
+
+def symmetric(a):
+    return (a + a.T) * 0.5
+
+
+def add_blocks(ref, labels, blocks, owner, tile, rows):
+    for i in range(blocks.shape[0]):
+        place = labels[2 * i + owner]
+        down = pl.multiple_of(place // 2 * tile, tile)
+        right = pl.multiple_of(place % 2 * tile, tile)
+        ref[pl.ds(down, tile), pl.ds(right, tile)] += blocks[
+            i, owner * tile : (owner + 1) * tile, :
+        ]
+
+
+def first_kernel(labels, front, blocks, w_ref, l_ref, work):
+    tile = blocks.shape[2]
+    width = front.shape[1]
+    work[...] = front[...]
+    add_blocks(work, labels, blocks, 0, tile, None)
+    store_inverse(w_ref, factor_pair(symmetric(work[:width, :])))
+    l_ref[...] = dot_t(work[width:, :], w_ref[...])
+
+
+def second_kernel(labels, front, blocks, lower, w_ref, work):
+    tile = blocks.shape[2]
+    width = front.shape[1]
+    work[...] = jnp.concatenate([jnp.zeros_like(front), front[...]], 0)
+    add_blocks(work, labels, blocks, 1, tile, None)
+    diag = work[width:, :] - dot_t(lower[...], lower[...])
+    store_inverse(w_ref, factor_pair(symmetric(diag)))
+
+
+def matched_kernel(labels, half, front, blocks, out_ref, work):
+    tile = blocks.shape[2]
+    width = front.shape[1]
+    work[...] = jnp.zeros_like(work)
+    for owner in range(2):
+        for i in range(blocks.shape[0]):
+            place = labels[2 * i + owner]
+            down = pl.multiple_of(place // 2 * tile, tile)
+            right = pl.multiple_of(owner * width + place % 2 * tile, tile)
+            work[pl.ds(down, tile), pl.ds(right, tile)] += blocks[
+                i, owner * tile : (owner + 1) * tile, :
+            ]
+    start = pl.multiple_of(half[0] * width, width)
+    out_ref[...] = front[...].T + work[pl.ds(start, width), :]
+
+
+def last_kernel(
+    labels, info, places, shard, arrived, pieces, blocks, matched, w1, l21, w2, out_ref, band
+):
+    tile = blocks.shape[2]
+    nrows, width = shard.shape
+    group, column = info[0], info[1]
+    out_ref[...] = shard[...]
+    for i in range(arrived.shape[0]):
+        place = places[i]
+        down = pl.multiple_of(place // 2 * tile, tile)
+        right = pl.multiple_of(place % 2 * tile, tile)
+        out_ref[pl.ds(down, tile), pl.ds(right, tile)] += arrived[i, :tile, :]
+    for i in range(pieces.shape[0]):
+        r, c = i // 2 * tile, i % 2 * width
+        band[r : r + tile, c : c + width] = pieces[i]
+    for owner in range(2):
+        for i in range(blocks.shape[0]):
+            place = labels[2 * i + owner]
+            down = pl.multiple_of(place // 2 * tile, tile)
+            right = pl.multiple_of(owner * width + place % 2 * tile, tile)
+            band[pl.ds(down, tile), pl.ds(right, tile)] += blocks[
+                i, owner * tile : (owner + 1) * tile, :
+            ]
+    rows = group * nrows + lax.broadcasted_iota(jnp.int32, (nrows, width), 0)
+    first = dot_t(band[:, :width], w1[...])
+    raw = band[:, width:]
+    second = dot_t(raw - dot_t(first, l21[...]), w2[...])
+
+    @pl.when(column == 0)
+    def _():
+        out_ref[...] = first
+
+    @pl.when(column == 1)
+    def _():
+        out_ref[...] = jnp.where(rows >= width, second, raw)
+
+    @pl.when(column >= 2)
+    def _():
+        m1 = dot_t(matched[:, :width], w1[...])
+        m2 = dot_t(matched[:, width:] - dot_t(m1, l21[...]), w2[...])
+        t1 = jnp.where(rows >= width, first, 0.0)
+        t2 = jnp.where(rows >= 2 * width, second, 0.0)
+        out_ref[...] = out_ref[...] - (dot_t(t1, m1) + dot_t(t2, m2))
+
+
+def kernel(body, outs, scratch, smem, n_vmem, flops):
+    spec = [pl.BlockSpec(memory_space=pltpu.SMEM)] * smem
+    spec += [pl.BlockSpec(memory_space=pltpu.VMEM)] * n_vmem
+    return pl.pallas_call(
+        body,
+        out_shape=outs,
+        in_specs=spec,
+        scratch_shapes=[pltpu.VMEM(s, F32) for s in scratch],
+        compiler_params=pltpu.CompilerParams(vmem_limit_bytes=VMEM_LIMIT),
+        cost_estimate=pl.CostEstimate(
+            flops=flops, bytes_accessed=1 << 20, transcendentals=0
+        ),
+    )
+
+
+def aligned(front, updates, target_owner, target_slot):
+    nrows, width = front.shape
+    sends, tile = updates.shape[:2]
+    nleaf, nfront = lax.axis_size("leaf"), lax.axis_size("front")
+    nz = nfront // 2
+    group, column = lax.axis_index("leaf"), lax.axis_index("front")
+    layer, core = column // 2, column % 2
+
+    def dev(g, z, c):
+        return g * nfront + 2 * z + c
+
+    def send(x, pairs):
+        return lax.ppermute(x, AXES, pairs)
+
+    cores = [
+        (dev(g, z, c), dev(g, z, 1 - c))
+        for g in range(nleaf)
+        for z in range(nz)
+        for c in range(2)
+    ]
+    slots = target_slot.astype(F32)
+    hit = target_owner[None, :] == jnp.arange(nfront, dtype=jnp.int32)[:, None]
+    buffer = jnp.zeros((nfront, tile, tile), F32)
+    place = jnp.zeros((nfront,), F32)
+    for j in range(sends):
+        buffer = buffer + jnp.where(hit[:, j, None, None], updates[j][None], 0.0)
+        place = place + jnp.where(hit[:, j], slots[j], 0.0)
+    tags = jnp.broadcast_to(place[:, None, None], (nfront, 8, tile))
+    payload = jnp.concatenate([buffer[0], buffer[1], tags[0], tags[1]], 0)
+
+    got = [payload]
+    for s in range(1, nz):
+        pairs = [
+            (dev(g, z, c), dev(g, z ^ s, c))
+            for g in range(nleaf)
+            for z in range(nz)
+            for c in range(2)
+        ]
+        got.append(send(payload, pairs))
+    mine = jnp.stack(got)
+    blocks = jnp.concatenate([mine, send(mine, cores)], 0)
+    labels = blocks[:, 2 * tile :: 8, 0].reshape(-1).astype(jnp.int32)
+
+    diag_front = send(front[width:], [(dev(0, 0, 1), dev(0, 0, 0))])
+    piece = jnp.where(layer == 0, front[:tile], 0.0)
+    for s in range(1, nz):
+        pairs = [(dev(g, 0, c), dev(g, s, c)) for g in range(nleaf) for c in range(2)]
+        piece = piece + send(front[s * tile : (s + 1) * tile], pairs)
+    pieces = lax.all_gather(piece, "front", axis=0, tiled=False)
+    turned = send(front, [(dev(0, z, c), dev(z, z, c)) for z in range(1, nz) for c in range(2)])
+
+    half = core.reshape(1)
+    matched = kernel(
+        matched_kernel,
+        jax.ShapeDtypeStruct((width, 2 * width), F32),
+        [(nrows, 2 * width)],
+        2,
+        2,
+        1 << 20,
+    )(labels, half, turned, blocks)
+    away = jnp.where(layer == group, matched, 0.0)
+    for s in range(1, nleaf):
+        pairs = [(dev(z, z, c), dev(z ^ s, z, c)) for z in range(1, nz) for c in range(2)]
+        away = away + send(matched, pairs)
+
+    def share(x):
+        for_group = jnp.where(group == 0, x, 0.0)
+        for s in range(1, nleaf):
+            for_group = for_group + send(x, [(dev(0, 0, 0), dev(s, 0, 0))])
+        for_layer = jnp.where(layer == 0, for_group, 0.0)
+        for s in range(1, nz):
+            for_layer = for_layer + send(
+                for_group, [(dev(g, 0, 0), dev(g, s, 0)) for g in range(nleaf)]
+            )
+        other = send(for_layer, [(dev(g, z, 0), dev(g, z, 1)) for g in range(nleaf) for z in range(nz)])
+        return jnp.where(core == 0, for_layer, other)
+
+    square = jax.ShapeDtypeStruct((width, width), F32)
+    w1, l21 = kernel(first_kernel, (square, square), [(nrows, width)], 1, 2, 1 << 31)(
+        labels, front, blocks
+    )
+    w2 = kernel(second_kernel, square, [(nrows, width)], 1, 3, 1 << 31)(
+        labels, diag_front, blocks, l21
+    )
+    early = share(jnp.concatenate([w1, l21], 0))
+    w2 = share(w2)
+
+    outgoing = jnp.concatenate([buffer, tags], 1)
+    arrived = lax.all_to_all(outgoing, "front", split_axis=0, concat_axis=0, tiled=True)
+    places = arrived[:, tile, 0].astype(jnp.int32)
+    info = jnp.stack([group, column]).astype(jnp.int32)
+    return kernel(
+        last_kernel,
+        jax.ShapeDtypeStruct((nrows, width), F32),
+        [(nrows, 2 * width)],
+        3,
+        8,
+        1 << 31,
+    )(labels, info, places, front, arrived, pieces, blocks, away, early[:width], early[width:], w2)
+
+
 def solution(mesh):
+    nleaf, nfront = mesh.shape["leaf"], mesh.shape["front"]
+
+    def shards(front, updates, target_owner, target_slot):
+        nrows, width = front.shape
+        tile = updates.shape[1]
+        lines_up = (
+            nrows == 2 * width
+            and width == 2 * tile
+            and nfront == 2 * nleaf
+            and nleaf == nrows // tile
+        )
+        plan = aligned if lines_up else general
+        return plan(front, updates, target_owner, target_slot)
+
     return jax.shard_map(
         shards,
         mesh=mesh,

time: 469 us -> 146 us (0.31)
  the two profiles are of different devices: /device:TPU:11 before, /device:TPU:25 now
where the time goes in v1:
time: 146 us; the launch traced here: 145 us
  starting transfers between devices  43.5 us (30%)
  waiting for transfers between devices  38.1 us (26%)
  Pallas kernels  26.1 us (18%)
  other arithmetic  16 us (11%)
  between operations  13.8 us (9%)
  local copies, waits for them, and re-layouts  7.22 us (5%)
    ppermute x26, waiting for transfers between devices, send(): return lax.ppermute(x, AXES, pairs)  38 us
    ppermute x26, starting transfers between devices, send(): return lax.ppermute(x, AXES, pairs)  32.6 us
    all_to_all x1, starting transfers between devices, aligned(): lax.all_to_all(outgoing, 'front', split_axis=0, concat_axis=0, tiled=True)  10.9 us
    pallas_call x1, Pallas kernels, aligned(): kernel(second_kernel, square, [(nrows, width)], 1, 3, 1 << 31)  9.32 us
    pallas_call x1, Pallas kernels, aligned(): kernel(first_kernel, (square, square), [(nrows, width)], 1, 2, 1 << 31)  9.27 us
    pallas_call x1, Pallas kernels, aligned(): kernel(last_kernel, jax.ShapeDtypeStruct((nrows, width), F32), [(nrows, 2...  6.58 us
    add x2, other arithmetic, aligned(): place = place + jnp.where(hit[:, j], slots[j], 0.0)  5.06 us
    add x2, other arithmetic, share(): for_group = for_group + send(x, [(dev(0, 0, 0), dev(s, 0, 0))])  3.63 us
  transfers between devices with their start and end apart: 28, of which 6 were waited for; matrix products, arithmetic and copies ran while one was open for 10% of the time, Pallas kernels for 7%

profile of v1, /device:TPU:25, one launch (start us, length us, event | category | flops | bytes accessed | tf_op | source)
XLA Modules:
  0.0 144.8 jit_solution(8344665616238642579)
XLA Ops:
  9.2 2.5 %fusion.3 = f32[8,1]{0,1:T(1,128)S(1)} fusion(pred[8,4]{0,1:T(4,128)(4,1)S(1)} %iota_compare_fusion, f32[]{:T(128)} %bitcast.13, f32[]{:T(128)} %bitcast.12, f32[]{:T(128)} %bitcast.11, f32[]{:T(128)} %bitcast.10), kind=kLoop, calls=%fused_computation.39 | loop fusion | flops 56 | bytes 80 | tf_op jit(solution)/shard_map/add | solution.py:313
  14.1 3.4 %collective-permute-start.2 = (f32[272,128]{1,0:T(8,128)S(1)}, f32[272,128]{1,0:T(8,128)S(1)}, u32[]{:S(2)}, u32[]{:S(2)}) collective-permute-start(f32[272,128]{1,0:T(8,128)S(1)} %get-tuple-element.21), channel_id=1, source_target_pairs={{0,6},{1,7},{2,4},{3,5},{4,2},{5,3},{6,0},{7,1},{8,14},{9,15},{10,... | collective-permute-start | bytes 417800 | tf_op jit(solution)/shard_map/ppermute | solution.py:299
  18.3 1.9 %collective-permute-done = f32[272,128]{1,0:T(8,128)S(1)} collective-permute-done((f32[272,128]{1,0:T(8,128)S(1)}, f32[272,128]{1,0:T(8,128)S(1)}, u32[]{:S(2)}, u32[]{:S(2)}) %collective-permute-start) | collective-permute-done | bytes 139296 | tf_op jit(solution)/shard_map/ppermute | solution.py:299
  20.2 5.2 %collective-permute-done.1 = f32[272,128]{1,0:T(8,128)S(1)} collective-permute-done((f32[272,128]{1,0:T(8,128)S(1)}, f32[272,128]{1,0:T(8,128)S(1)}, u32[]{:S(2)}, u32[]{:S(2)}) %collective-permute-start.1) | collective-permute-done | bytes 139296 | tf_op jit(solution)/shard_map/ppermute | solution.py:299
  25.5 2.9 %collective-permute-start.3 = (f32[4,272,128]{2,1,0:T(8,128)S(1)}, f32[4,272,128]{2,1,0:T(8,128)S(1)}, u32[]{:S(2)}, u32[]{:S(2)}) collective-permute-start(f32[4,272,128]{2,1,0:T(8,128)S(1)} %pad_maximum_fusion), channel_id=1, source_target_pairs={{0,1},{1,0},{2,3},{3,2},{4,5},{5,4},{6,7},{7,6},{8,9},{9,8},{10,11... | collective-permute-start | bytes 1671176 | tf_op jit(solution)/shard_map/ppermute | solution.py:299
  28.5 1.5 %collective-permute-done.3 = f32[4,272,128]{2,1,0:T(8,128)S(1)} collective-permute-done((f32[4,272,128]{2,1,0:T(8,128)S(1)}, f32[4,272,128]{2,1,0:T(8,128)S(1)}, u32[]{:S(2)}, u32[]{:S(2)}) %collective-permute-start.3) | collective-permute-done | bytes 557088 | tf_op jit(solution)/shard_map/ppermute | solution.py:299
  30.4 9.3 %shard_map.47 = (f32[256,256]{1,0:T(8,128)S(1)}, f32[256,256]{1,0:T(8,128)S(1)}) custom-call(s32[16]{0:T(128)S(1)} %convert_element_type.15.labels, f32[512,256]{1,0:T(8,128)S(1)} %copy-done, f32[8,272,128]{2,1,0:T(8,128)S(1)} %constant_dynamic-update-slice_fusion.blocks), custom_call_target="tpu_custom_call" | custom-call | flops 2147483648 | bytes 1048576 | tf_op jit(solution)/shard_map/pallas_call | solution.py:365
  39.6 9.3 %shard_map.48 = f32[256,256]{1,0:T(8,128)S(1)} custom-call(s32[16]{0:T(128)S(1)} %convert_element_type.15.labels, f32[256,256]{1,0:T(8,128)S(1)} %collective-permute-done.18.front, f32[8,272,128]{2,1,0:T(8,128)S(1)} %constant_dynamic-update-slice_fusion.blocks, f32[256,256]{1,0:T(8,128)S(1)} %get-tuple-element.8.lower), custom_call_target="tpu_custom_call" | custom-call | flops 2147483648 | bytes 1048576 | tf_op jit(solution)/shard_map/pallas_call | solution.py:368
  49.7 2.5 %select_add_fusion.1 = f32[8]{0:T(128)S(1)} fusion(f32[]{:T(128)} %bitcast.13, f32[]{:T(128)} %bitcast.12, f32[]{:T(128)} %bitcast.11, f32[]{:T(128)} %bitcast.10, pred[8,4]{0,1:T(4,128)(4,1)S(1)} %iota_compare_fusion), kind=kLoop, calls=%fused_computation.41 | loop fusion | flops 56 | bytes 80 | tf_op jit(solution)/shard_map/add | solution.py:313
  52.2 1.4 collective-permute-start.20
  53.6 1.4 collective-permute-start.21
  56.4 1.5 %collective-permute-start.11 = (f32[512,256]{1,0:T(8,128)}, f32[512,256]{1,0:T(8,128)}, u32[]{:S(2)}, u32[]{:S(2)}) collective-permute-start(f32[512,256]{1,0:T(8,128)} %constant_dynamic-update-slice_fusion.5), channel_id=1, source_target_pairs={{0,8}} | collective-permute-start | bytes 1572872 | tf_op jit(solution)/shard_map/ppermute | solution.py:299
  57.9 1.4 %collective-permute-start.12 = (f32[512,256]{1,0:T(8,128)}, f32[512,256]{1,0:T(8,128)}, u32[]{:S(2)}, u32[]{:S(2)}) collective-permute-start(f32[512,256]{1,0:T(8,128)} %constant_dynamic-update-slice_fusion.5), channel_id=1, source_target_pairs={{0,16}} | collective-permute-start | bytes 1572872 | tf_op jit(solution)/shard_map/ppermute | solution.py:299
  59.3 1.5 %collective-permute-start.13 = (f32[512,256]{1,0:T(8,128)}, f32[512,256]{1,0:T(8,128)}, u32[]{:S(2)}, u32[]{:S(2)}) collective-permute-start(f32[512,256]{1,0:T(8,128)} %constant_dynamic-update-slice_fusion.5), channel_id=1, source_target_pairs={{0,24}} | collective-permute-start | bytes 1572872 | tf_op jit(solution)/shard_map/ppermute | solution.py:299
  61.7 10.9 %all-to-all-start = ((f32[8,136,128]{2,1,0:T(8,128)}), f32[8,136,128]{2,1,0:T(8,128)S(1)}, u32[]{:S(2)}, u32[]{:S(2)}) async-start(f32[8,136,128]{2,1,0:T(8,128)} %pad_maximum_fusion.1), calls=%async_computation | async-start | bytes 1114112 | tf_op jit(solution)/shard_map/all_to_all | solution.py:375
  73.3 1.3 collective-permute-start.7
  76.5 1.3 collective-permute-start.5
  79.8 2.5 %add_add_fusion.1 = f32[512,256]{1,0:T(8,128)} fusion(f32[512,256]{1,0:T(8,128)} %collective-permute-done.13, f32[512,256]{1,0:T(8,128)} %collective-permute-done.12, f32[512,256]{1,0:T(8,128)} %collective-permute-done.11, f32[512,256]{1,0:T(8,128)} %constant_dynamic-update-slice_fusion.5, pred[]{:T(512)S(6)} %eq.37), kind=kLoop, calls=%fused_computation.3 | loop fusion | flops 524288 | bytes 2621441 | tf_op jit(solution)/shard_map/add | solution.py:355
  82.3 1.5 %collective-permute-start.14 = (f32[512,256]{1,0:T(8,128)}, f32[512,256]{1,0:T(8,128)}, u32[]{:S(2)}, u32[]{:S(2)}) collective-permute-start(f32[512,256]{1,0:T(8,128)} %add_add_fusion.1), channel_id=1, source_target_pairs={{0,2},{8,10},{16,18},{24,26}} | collective-permute-start | bytes 1572872 | tf_op jit(solution)/shard_map/ppermute | solution.py:299
  83.8 1.3 collective-permute-start.23
  85.1 6.3 %collective-permute-done.6 = f32[128,256]{1,0:T(8,128)} collective-permute-done((f32[128,256]{1,0:T(8,128)S(1)}, f32[128,256]{1,0:T(8,128)}, u32[]{:S(2)}, u32[]{:S(2)}) %collective-permute-start.6) | collective-permute-done | bytes 131104 | tf_op jit(solution)/shard_map/ppermute | solution.py:299
  91.4 1.4 collective-permute-start.24
  92.8 1.5 %collective-permute-start.15 = (f32[512,256]{1,0:T(8,128)}, f32[512,256]{1,0:T(8,128)}, u32[]{:S(2)}, u32[]{:S(2)}) collective-permute-start(f32[512,256]{1,0:T(8,128)} %add_add_fusion.1), channel_id=1, source_target_pairs={{0,4},{8,12},{16,20},{24,28}} | collective-permute-start | bytes 1572872 | tf_op jit(solution)/shard_map/ppermute | solution.py:299
  94.3 1.5 %collective-permute-start.16 = (f32[512,256]{1,0:T(8,128)}, f32[512,256]{1,0:T(8,128)}, u32[]{:S(2)}, u32[]{:S(2)}) collective-permute-start(f32[512,256]{1,0:T(8,128)} %add_add_fusion.1), channel_id=1, source_target_pairs={{0,6},{8,14},{16,22},{24,30}} | collective-permute-start | bytes 1572872 | tf_op jit(solution)/shard_map/ppermute | solution.py:299
  95.7 1.7 %add_add_fusion.5 = f32[128,256]{1,0:T(8,128)} fusion(f32[128,256]{1,0:T(8,128)} %collective-permute-done.6, f32[128,256]{1,0:T(8,128)} %collective-permute-done.5, f32[128,256]{1,0:T(8,128)S(1)} %collective-permute-done.4, f32[512,256]{1,0:T(8,128)S(1)} %copy-done, pred[]{:T(512)S(6)} %eq.34), kind=kLoop, calls=%fused_computation.10 | loop fusion | flops 131072 | bytes 655361 | tf_op jit(solution)/shard_map/add | solution.py:334
  98.7 1.3 collective-permute-start.10
  102.6 1.3 collective-permute-start.25
  103.9 1.5 %add_add_fusion = f32[512,256]{1,0:T(8,128)S(1)} fusion(f32[512,256]{1,0:T(8,128)} %collective-permute-done.16, f32[512,256]{1,0:T(8,128)} %collective-permute-done.15, f32[512,256]{1,0:T(8,128)} %collective-permute-done.14, f32[512,256]{1,0:T(8,128)} %add_add_fusion.1, pred[]{:T(512)S(6)} %eq.34), kind=kLoop, calls=%fused_computation.2 | loop fusion | flops 524288 | bytes 2621441 | tf_op jit(solution)/shard_map/add | solution.py:358
  105.4 1.3 collective-permute-start.17
  106.7 7.7 %collective-permute-done.10 = f32[256,512]{1,0:T(8,128)S(1)} collective-permute-done((f32[256,512]{1,0:T(8,128)S(1)}, f32[256,512]{1,0:T(8,128)S(1)}, u32[]{:S(2)}, u32[]{:S(2)}) %collective-permute-start.10) | collective-permute-done | bytes 524320 | tf_op jit(solution)/shard_map/ppermute | solution.py:299
  114.7 15.3 %collective-permute-done.17 = f32[512,256]{1,0:T(8,128)S(1)} collective-permute-done((f32[512,256]{1,0:T(8,128)S(1)}, f32[512,256]{1,0:T(8,128)S(1)}, u32[]{:S(2)}, u32[]{:S(2)}) %collective-permute-start.17) | collective-permute-done | bytes 524320 | tf_op jit(solution)/shard_map/ppermute | solution.py:299
  131.3 6.6 %shard_map.49 = f32[512,256]{1,0:T(8,128)} custom-call(s32[16]{0:T(128)S(1)} %convert_element_type.15.labels, s32[2]{0:T(128)S(1)} %pad_add_fusion.info, s32[8]{0:T(128)S(1)} %fusion.places, f32[512,256]{1,0:T(8,128)S(1)} %copy-done, f32[8,136,128]{2,1,0:T(8,128)S(1)} %all-to-all-done.arrived, f32[8,128,256]{2,1,0:T(8,128)S(1)} %bitcast.47, ...), custom_call_target="tpu_custom_call" | custom-call | flops 2147483648 | bytes 1048576 | tf_op jit(solution)/shard_map/pallas_call | solution.py:378
  (80 shorter events, 19.2 us)
Async XLA Ops:
  6.5 2.0 %copy-start.4 = (s32[4]{0:T(128)S(1)}, s32[4]{0:T(128)}, u32[]{:S(2)}) copy-start(s32[4]{0:T(128)} %param.7) | copy-start | bytes 52
  6.5 10.9 %copy-start = (f32[512,256]{1,0:T(8,128)S(1)}, f32[512,256]{1,0:T(8,128)}, u32[]{:S(2)}) copy-start(f32[512,256]{1,0:T(8,128)} %shard.1) | copy-start | bytes 1572868
  13.8 6.4 %collective-permute-start = (f32[272,128]{1,0:T(8,128)S(1)}, f32[272,128]{1,0:T(8,128)S(1)}, u32[]{:S(2)}, u32[]{:S(2)}) collective-permute-start(f32[272,128]{1,0:T(8,128)S(1)} %get-tuple-element.21), channel_id=1, source_target_pairs={{0,2},{1,3},{2,0},{3,1},{4,6},{5,7},{6,4},{7,5},{8,10},{9,11},{10,... | collective-permute-start | bytes 417800 | tf_op jit(solution)/shard_map/ppermute | solution.py:299
  14.1 11.4 %collective-permute-start.1 = (f32[272,128]{1,0:T(8,128)S(1)}, f32[272,128]{1,0:T(8,128)S(1)}, u32[]{:S(2)}, u32[]{:S(2)}) collective-permute-start(f32[272,128]{1,0:T(8,128)S(1)} %get-tuple-element.21), channel_id=1, source_target_pairs={{0,4},{1,5},{2,6},{3,7},{4,0},{5,1},{6,2},{7,3},{8,12},{9,13},{10,... | collective-permute-start | bytes 417800 | tf_op jit(solution)/shard_map/ppermute | solution.py:299
  14.1 11.4 %collective-permute-start.2 = (f32[272,128]{1,0:T(8,128)S(1)}, f32[272,128]{1,0:T(8,128)S(1)}, u32[]{:S(2)}, u32[]{:S(2)}) collective-permute-start(f32[272,128]{1,0:T(8,128)S(1)} %get-tuple-element.21), channel_id=1, source_target_pairs={{0,6},{1,7},{2,4},{3,5},{4,2},{5,3},{6,0},{7,1},{8,14},{9,15},{10,... | collective-permute-start | bytes 417800 | tf_op jit(solution)/shard_map/ppermute | solution.py:299
  17.5 22.2 %collective-permute-start.18 = (f32[256,256]{1,0:T(8,128)S(1)}, f32[256,256]{1,0:T(8,128)S(1)}, u32[]{:S(2)}, u32[]{:S(2)}) collective-permute-start(f32[256,256]{1,0:T(8,128)S(1)} %slice.109), channel_id=1, source_target_pairs={{1,0}} | collective-permute-start | bytes 786440 | tf_op jit(solution)/shard_map/ppermute | solution.py:299
  25.5 4.5 %collective-permute-start.3 = (f32[4,272,128]{2,1,0:T(8,128)S(1)}, f32[4,272,128]{2,1,0:T(8,128)S(1)}, u32[]{:S(2)}, u32[]{:S(2)}) collective-permute-start(f32[4,272,128]{2,1,0:T(8,128)S(1)} %pad_maximum_fusion), channel_id=1, source_target_pairs={{0,1},{1,0},{2,3},{3,2},{4,5},{5,4},{6,7},{7,6},{8,9},{9,8},{10,11... | collective-permute-start | bytes 1671176 | tf_op jit(solution)/shard_map/ppermute | solution.py:299
  49.0 10.3 %collective-permute-start.19 = (f32[256,256]{1,0:T(8,128)S(1)}, f32[256,256]{1,0:T(8,128)S(1)}, u32[]{:S(2)}, u32[]{:S(2)}) collective-permute-start(f32[256,256]{1,0:T(8,128)S(1)} %shard_map.48), channel_id=1, source_target_pairs={{0,8}} | collective-permute-start | bytes 786440 | tf_op jit(solution)/shard_map/ppermute | solution.py:299
  52.2 21.1 %collective-permute-start.20 = (f32[256,256]{1,0:T(8,128)S(1)}, f32[256,256]{1,0:T(8,128)}, u32[]{:S(2)}, u32[]{:S(2)}) collective-permute-start(f32[256,256]{1,0:T(8,128)S(1)} %shard_map.48), channel_id=1, source_target_pairs={{0,16}} | collective-permute-start | bytes 786440 | tf_op jit(solution)/shard_map/ppermute | solution.py:299
  53.6 21.1 %collective-permute-start.21 = (f32[256,256]{1,0:T(8,128)S(1)}, f32[256,256]{1,0:T(8,128)}, u32[]{:S(2)}, u32[]{:S(2)}) collective-permute-start(f32[256,256]{1,0:T(8,128)S(1)} %shard_map.48), channel_id=1, source_target_pairs={{0,24}} | collective-permute-start | bytes 786440 | tf_op jit(solution)/shard_map/ppermute | solution.py:299
  56.4 20.1 %collective-permute-start.11 = (f32[512,256]{1,0:T(8,128)}, f32[512,256]{1,0:T(8,128)}, u32[]{:S(2)}, u32[]{:S(2)}) collective-permute-start(f32[512,256]{1,0:T(8,128)} %constant_dynamic-update-slice_fusion.5), channel_id=1, source_target_pairs={{0,8}} | collective-permute-start | bytes 1572872 | tf_op jit(solution)/shard_map/ppermute | solution.py:299
  57.9 20.0 %collective-permute-start.12 = (f32[512,256]{1,0:T(8,128)}, f32[512,256]{1,0:T(8,128)}, u32[]{:S(2)}, u32[]{:S(2)}) collective-permute-start(f32[512,256]{1,0:T(8,128)} %constant_dynamic-update-slice_fusion.5), channel_id=1, source_target_pairs={{0,16}} | collective-permute-start | bytes 1572872 | tf_op jit(solution)/shard_map/ppermute | solution.py:299
  59.3 2.4 %copy-start.3 = (f32[256,256]{1,0:T(8,128)}, f32[256,256]{1,0:T(8,128)S(1)}, u32[]{:S(2)}) copy-start(f32[256,256]{1,0:T(8,128)S(1)} %collective-permute-done.19) | copy-start | bytes 786436
  59.3 19.8 %collective-permute-start.13 = (f32[512,256]{1,0:T(8,128)}, f32[512,256]{1,0:T(8,128)}, u32[]{:S(2)}, u32[]{:S(2)}) collective-permute-start(f32[512,256]{1,0:T(8,128)} %constant_dynamic-update-slice_fusion.5), channel_id=1, source_target_pairs={{0,24}} | collective-permute-start | bytes 1572872 | tf_op jit(solution)/shard_map/ppermute | solution.py:299
  61.7 36.7 %all-to-all-start = ((f32[8,136,128]{2,1,0:T(8,128)}), f32[8,136,128]{2,1,0:T(8,128)S(1)}, u32[]{:S(2)}, u32[]{:S(2)}) async-start(f32[8,136,128]{2,1,0:T(8,128)} %pad_maximum_fusion.1), calls=%async_computation | async-start | bytes 1114112 | tf_op jit(solution)/shard_map/all_to_all | solution.py:375
  72.6 57.5 %all-gather.3.cloned.1.call-start = ((), (), s32[]{:S(2)}) async-start(), calls=%async_computation.1 | async-start | bytes 1179648 | tf_op jit(solution)/shard_map/all_gather | solution.py:335
  73.3 19.5 %collective-permute-start.7 = (f32[512,256]{1,0:T(8,128)S(1)}, f32[512,256]{1,0:T(8,128)S(1)}, u32[]{:S(2)}, u32[]{:S(2)}) collective-permute-start(f32[512,256]{1,0:T(8,128)S(1)} %copy-done), channel_id=1, source_target_pairs={{2,10},{3,11},{4,20},{5,21},{6,30},{7,31}} | collective-permute-start | bytes 1572872 | tf_op jit(solution)/shard_map/ppermute | solution.py:299
  74.7 7.6 %collective-permute-start.4 = (f32[128,256]{1,0:T(8,128)}, f32[128,256]{1,0:T(8,128)S(1)}, u32[]{:S(2)}, u32[]{:S(2)}) collective-permute-start(f32[128,256]{1,0:T(8,128)} %get-tuple-element.11), channel_id=1, source_target_pairs={{0,2},{1,3},{8,10},{9,11},{16,18},{17,19},{24,26},{25,27}} | collective-permute-start | bytes 393224 | tf_op jit(solution)/shard_map/ppermute | solution.py:299
  76.5 7.2 %collective-permute-start.5 = (f32[128,256]{1,0:T(8,128)}, f32[128,256]{1,0:T(8,128)}, u32[]{:S(2)}, u32[]{:S(2)}) collective-permute-start(f32[128,256]{1,0:T(8,128)} %get-tuple-element.13), channel_id=1, source_target_pairs={{0,4},{1,5},{8,12},{9,13},{16,20},{17,21},{24,28},{25,29}} | collective-permute-start | bytes 393224 | tf_op jit(solution)/shard_map/ppermute | solution.py:299
  77.9 13.6 %collective-permute-start.6 = (f32[128,256]{1,0:T(8,128)S(1)}, f32[128,256]{1,0:T(8,128)}, u32[]{:S(2)}, u32[]{:S(2)}) collective-permute-start(f32[128,256]{1,0:T(8,128)S(1)} %get-tuple-element.12), channel_id=1, source_target_pairs={{0,6},{1,7},{8,14},{9,15},{16,22},{17,23},{24,30},{25,31}} | collective-permute-start | bytes 393224 | tf_op jit(solution)/shard_map/ppermute | solution.py:299
  79.2 15.1 %collective-permute-start.22 = (f32[256,256]{1,0:T(8,128)S(1)}, f32[256,256]{1,0:T(8,128)S(1)}, u32[]{:S(2)}, u32[]{:S(2)}) collective-permute-start(f32[256,256]{1,0:T(8,128)S(1)} %add_add_fusion.4), channel_id=1, source_target_pairs={{0,2},{8,10},{16,18},{24,26}} | collective-permute-start | bytes 786440 | tf_op jit(solution)/shard_map/ppermute | solution.py:299
  82.3 18.4 %collective-permute-start.14 = (f32[512,256]{1,0:T(8,128)}, f32[512,256]{1,0:T(8,128)}, u32[]{:S(2)}, u32[]{:S(2)}) collective-permute-start(f32[512,256]{1,0:T(8,128)} %add_add_fusion.1), channel_id=1, source_target_pairs={{0,2},{8,10},{16,18},{24,26}} | collective-permute-start | bytes 1572872 | tf_op jit(solution)/shard_map/ppermute | solution.py:299
  83.8 14.9 %collective-permute-start.23 = (f32[256,256]{1,0:T(8,128)S(1)}, f32[256,256]{1,0:T(8,128)}, u32[]{:S(2)}, u32[]{:S(2)}) collective-permute-start(f32[256,256]{1,0:T(8,128)S(1)} %add_add_fusion.4), channel_id=1, source_target_pairs={{0,4},{8,12},{16,20},{24,28}} | collective-permute-start | bytes 786440 | tf_op jit(solution)/shard_map/ppermute | solution.py:299
  91.4 8.5 %collective-permute-start.24 = (f32[256,256]{1,0:T(8,128)S(1)}, f32[256,256]{1,0:T(8,128)}, u32[]{:S(2)}, u32[]{:S(2)}) collective-permute-start(f32[256,256]{1,0:T(8,128)S(1)} %add_add_fusion.4), channel_id=1, source_target_pairs={{0,6},{8,14},{16,22},{24,30}} | collective-permute-start | bytes 786440 | tf_op jit(solution)/shard_map/ppermute | solution.py:299
  92.8 9.8 %collective-permute-start.15 = (f32[512,256]{1,0:T(8,128)}, f32[512,256]{1,0:T(8,128)}, u32[]{:S(2)}, u32[]{:S(2)}) collective-permute-start(f32[512,256]{1,0:T(8,128)} %add_add_fusion.1), channel_id=1, source_target_pairs={{0,4},{8,12},{16,20},{24,28}} | collective-permute-start | bytes 1572872 | tf_op jit(solution)/shard_map/ppermute | solution.py:299
  94.3 3.2 %copy-start.2 = (f32[256,256]{1,0:T(8,128)}, f32[256,256]{1,0:T(8,128)S(1)}, u32[]{:S(2)}) copy-start(f32[256,256]{1,0:T(8,128)S(1)} %collective-permute-done.22) | copy-start | bytes 786436
  94.3 9.6 %collective-permute-start.16 = (f32[512,256]{1,0:T(8,128)}, f32[512,256]{1,0:T(8,128)}, u32[]{:S(2)}, u32[]{:S(2)}) collective-permute-start(f32[512,256]{1,0:T(8,128)} %add_add_fusion.1), channel_id=1, source_target_pairs={{0,6},{8,14},{16,22},{24,30}} | collective-permute-start | bytes 1572872 | tf_op jit(solution)/shard_map/ppermute | solution.py:299
  98.7 15.7 %collective-permute-start.10 = (f32[256,512]{1,0:T(8,128)S(1)}, f32[256,512]{1,0:T(8,128)S(1)}, u32[]{:S(2)}, u32[]{:S(2)}) collective-permute-start(f32[256,512]{1,0:T(8,128)S(1)} %shard_map.46), channel_id=1, source_target_pairs={{10,18},{11,19},{20,12},{21,13},{30,6},{31,7}} | collective-permute-start | bytes 1572872 | tf_op jit(solution)/shard_map/ppermute | solution.py:299
  100.0 14.4 %collective-permute-start.8 = (f32[256,512]{1,0:T(8,128)S(1)}, f32[256,512]{1,0:T(8,128)S(1)}, u32[]{:S(2)}, u32[]{:S(2)}) collective-permute-start(f32[256,512]{1,0:T(8,128)S(1)} %shard_map.46), channel_id=1, source_target_pairs={{10,2},{11,3},{20,28},{21,29},{30,22},{31,23}} | collective-permute-start | bytes 1572872 | tf_op jit(solution)/shard_map/ppermute | solution.py:299
  100.7 13.7 %collective-permute-start.9 = (f32[256,512]{1,0:T(8,128)S(1)}, f32[256,512]{1,0:T(8,128)S(1)}, u32[]{:S(2)}, u32[]{:S(2)}) collective-permute-start(f32[256,512]{1,0:T(8,128)S(1)} %shard_map.46), channel_id=1, source_target_pairs={{10,26},{11,27},{20,4},{21,5},{30,14},{31,15}} | collective-permute-start | bytes 1572872 | tf_op jit(solution)/shard_map/ppermute | solution.py:299
  102.6 12.0 %collective-permute-start.25 = (f32[256,256]{1,0:T(8,128)S(1)}, f32[256,256]{1,0:T(8,128)S(1)}, u32[]{:S(2)}, u32[]{:S(2)}) collective-permute-start(f32[256,256]{1,0:T(8,128)S(1)} %add_add_fusion.3), channel_id=1, source_target_pairs={{0,1},{2,3},{4,5},{6,7},{8,9},{10,11},{12,13},{14,15},{16,17},{18,... | collective-permute-start | bytes 786440 | tf_op jit(solution)/shard_map/ppermute | solution.py:299
  105.4 24.5 %collective-permute-start.17 = (f32[512,256]{1,0:T(8,128)S(1)}, f32[512,256]{1,0:T(8,128)S(1)}, u32[]{:S(2)}, u32[]{:S(2)}) collective-permute-start(f32[512,256]{1,0:T(8,128)S(1)} %add_add_fusion), channel_id=1, source_target_pairs={{0,1},{2,3},{4,5},{6,7},{8,9},{10,11},{12,13},{14,15},{16,17},{18,... | collective-permute-start | bytes 1572872 | tf_op jit(solution)/shard_map/ppermute | solution.py:299
  (1 other events, 1.2 us)
Sparse Core Ops, SparseCore 0:
  97.5 25.3 all-gather.2

commit v2 on v0

--- a/solution.py
+++ b/solution.py
@@ -1,7 +1,17 @@
+import functools
+
 import jax
 import jax.numpy as jnp
 from jax import lax
+from jax.experimental import pallas as pl
+from jax.experimental.pallas import tpu as pltpu
 from jax.sharding import PartitionSpec as P
+
+F32 = jnp.float32
+BF16 = jnp.bfloat16
+AXES = ("leaf", "front")
+EXACT = lax.Precision.HIGHEST
+VMEM_LIMIT = 40 * 1024 * 1024
 
 
 def spread(value, axis, source):
@@ -13,8 +23,8 @@
     nrows, width = front.shape
     tile = updates.shape[1]
     nfront = lax.axis_size("front")
-    buffer = jnp.zeros((nfront, tile, tile), jnp.float32).at[target_owner].set(updates)
-    labels = jnp.zeros((nfront,), jnp.float32).at[target_owner].set(target_slot.astype(jnp.float32))
+    buffer = jnp.zeros((nfront, tile, tile), F32).at[target_owner].set(updates)
+    labels = jnp.zeros((nfront,), F32).at[target_owner].set(target_slot.astype(F32))
     arrived, places = (
         lax.all_to_all(buffer, "front", split_axis=0, concat_axis=0, tiled=True),
         lax.all_to_all(labels, "front", split_axis=0, concat_axis=0, tiled=True),
@@ -30,21 +40,21 @@
     nrows, width = panel.shape
     diag = spread(panel[start : start + width], "leaf", 0)
     chol = jnp.linalg.cholesky(diag)
-    eye = jnp.eye(width, dtype=jnp.float32)
+    eye = jnp.eye(width, dtype=F32)
     inverse = lax.linalg.triangular_solve(chol, eye, left_side=True, lower=True)
-    prod = jnp.dot(panel, inverse.T, precision=lax.Precision.HIGHEST)
+    prod = jnp.dot(panel, inverse.T, precision=EXACT)
     lower = jnp.where(row_ids[:, None] >= start, prod, panel)
     owner_row = column * width // nrows
     offset = column * width - owner_row * nrows
     mine = lax.dynamic_slice_in_dim(lower, offset, width, 0)
     across = spread(mine, "leaf", owner_row)
     trail = jnp.where(row_ids[:, None] >= start + width, lower, 0.0)
-    updated = shard - jnp.dot(trail, across.T, precision=lax.Precision.HIGHEST)
+    updated = shard - jnp.dot(trail, across.T, precision=EXACT)
     updated = jnp.where(col_ids[None, :] >= start + width, updated, shard)
     return (jnp.where(column == start // width, lower, updated), lower)
 
 
-def shards(front, updates, target_owner, target_slot):
+def general(front, updates, target_owner, target_slot):
     nrows, width = front.shape
     column = lax.axis_index("front")
     row_ids = lax.axis_index("leaf") * nrows + jnp.arange(nrows, dtype=jnp.int32)
@@ -57,7 +67,428 @@
     return shard
 
 
+def lane_of(x, c):
+    return jnp.take_along_axis(x, jnp.full(x.shape, c, jnp.int32), axis=1)
+
+
+def row_of(x, i):
+    return jnp.broadcast_to(x[i : i + 1, :], x.shape)
+
+
+def parts(x):
+    high = x.astype(BF16).astype(F32)
+    rest = x - high
+    mid = rest.astype(BF16).astype(F32)
+    return high, mid, (rest - mid).astype(BF16).astype(F32)
+
+
+def factor_inverse(a):
+    n = a.shape[0]
+    panels, per = n // 8, 2
+    sub = lax.broadcasted_iota(jnp.int32, (8, n), 0)
+    lane = lax.broadcasted_iota(jnp.int32, (8, n), 1)
+    work = [
+        [a[8 * k : 8 * k + 8, :], jnp.where(lane == sub + 8 * k, 1.0, 0.0).astype(F32)]
+        for k in range(panels)
+    ]
+    out, held = [], []
+    for k in range(panels):
+        rows, ident = work[k]
+        cols = [lane_of(rows, 8 * k + j) for j in range(8)]
+        d = {(i, j): row_of(cols[j], i) for j in range(8) for i in range(j, 8)}
+        up = [row_of(rows, j) for j in range(8)]
+        inv = [row_of(ident, j) for j in range(8)]
+        last = min(panels - 1, (k // per + 1) * per - 1)
+        below = {
+            b: [lane_of(work[b][0], 8 * k + j) for j in range(8)]
+            for b in range(k + 1, last + 1)
+        }
+        for j in range(8):
+            r = lax.rsqrt(d[j, j])
+            for i in range(j + 1, 8):
+                d[i, j] = d[i, j] * r
+            for i in range(j + 1, 8):
+                for m in range(j + 1, i + 1):
+                    d[i, m] = d[i, m] - d[i, j] * d[m, j]
+            up[j] = up[j] * r
+            inv[j] = inv[j] * r
+            for i in range(j + 1, 8):
+                up[i] = up[i] - d[i, j] * up[j]
+                inv[i] = inv[i] - d[i, j] * inv[j]
+            for b, c in below.items():
+                c[j] = c[j] * r
+                for i in range(j + 1, 8):
+                    c[i] = c[i] - d[i, j] * c[j]
+                work[b] = [work[b][0] - c[j] * up[j], work[b][1] - c[j] * inv[j]]
+        u, w = up[0], inv[0]
+        for j in range(1, 8):
+            u = jnp.where(sub == j, up[j], u)
+            w = jnp.where(sub == j, inv[j], w)
+        out.append(w)
+        held.append((u, w))
+        if k % per == per - 1 and k + 1 < panels:
+            us = jnp.concatenate([p[0] for p in held], 0)
+            ws = jnp.concatenate([p[1] for p in held], 0)
+            uh, um, ul = parts(us)
+            wh, wm, wl = parts(ws)
+            right = jnp.concatenate(
+                [
+                    jnp.concatenate([uh, um, ul, uh, um, uh], 0),
+                    jnp.concatenate([wh, wm, wl, wh, wm, wh], 0),
+                ],
+                1,
+            ).astype(BF16)
+            left = jnp.concatenate([uh, uh, uh, um, um, ul], 0).T
+            left = left[8 * (k + 1) :, :].astype(BF16)
+            change = jnp.dot(left, right, preferred_element_type=F32)
+            for b in range(k + 1, panels):
+                part = change[8 * (b - k - 1) : 8 * (b - k), :]
+                work[b] = [work[b][0] - part[:, :n], work[b][1] - part[:, n:]]
+            held = []
+    return jnp.concatenate(out, 0)
+
+
+def dot(a, b):
+    return jnp.dot(a, b, precision=EXACT, preferred_element_type=F32)
+
+
+def dot_t(a, b):
+    return lax.dot_general(
+        a, b, (((1,), (1,)), ((), ())), precision=EXACT, preferred_element_type=F32
+    )
+
+
+def factor_pair(a):
+    h = a.shape[0] // 2
+    w11 = factor_inverse(a[:h, :h])
+    l21 = dot_t(a[h:, :h], w11)
+    w22 = factor_inverse(a[h:, h:] - dot_t(l21, l21))
+    w21 = -dot(w22, dot(l21, w11))
+    return w11, w21, w22
+
+
+def store_inverse(ref, blocks):
+    w11, w21, w22 = blocks
+    h = w11.shape[0]
+    ref[:h, :h] = w11
+    ref[:h, h:] = jnp.zeros_like(w11)
+    ref[h:, :h] = w21
+    ref[h:, h:] = w22
+
+
+def symmetric(a):
+    return (a + a.T) * 0.5
+
+
+def place_of(tags):
+    return tags[0, 0].astype(jnp.int32)
+
+
+def add_block(ref, block, place, tile, start=0):
+    down = pl.multiple_of(place // 2 * tile, tile)
+    right = pl.multiple_of(start + place % 2 * tile, tile)
+    ref[pl.ds(down, tile), pl.ds(right, tile)] += block
+
+
+def add_band_blocks(ref, blocks, width):
+    tile = blocks[0].shape[1]
+    for owner in range(2):
+        for b in blocks:
+            tag = b[2 * tile + 8 * owner : 2 * tile + 8 * owner + 8, :]
+            add_block(ref, b[owner * tile : (owner + 1) * tile, :], place_of(tag), tile, owner * width)
+
+
+def sort_kernel(owner, slot, updates, out_ref, pay_ref):
+    sends, tile = updates.shape[:2]
+    out_ref[...] = jnp.zeros_like(out_ref)
+    for j in range(sends):
+        out_ref[owner[j], :tile, :] = updates[j]
+        out_ref[owner[j], tile:, :] = jnp.full((8, tile), slot[j].astype(F32))
+    for o in range(2):
+        pay_ref[o * tile : (o + 1) * tile, :] = out_ref[o, :tile, :]
+        pay_ref[2 * tile + 8 * o : 2 * tile + 8 * o + 8, :] = out_ref[o, tile:, :]
+
+
+def matched_kernel(info, front, turned, *refs):
+    blocks, out_ref, band = refs[:-2], refs[-2], refs[-1]
+    width = front.shape[1]
+
+    @pl.when(info[0] == info[1])
+    def _():
+        band[...] = jnp.zeros_like(band)
+        add_band_blocks(band, blocks, width)
+        start = pl.multiple_of(info[2] * width, width)
+        own = jnp.where(info[0] == 0, front[...], turned[...])
+        out_ref[...] = own.T + band[pl.ds(start, width), :]
+
+
+def pack(ref, blocks):
+    w11, w21, w22 = blocks
+    n = w11.shape[0]
+    row = lax.broadcasted_iota(jnp.int32, (n, n), 0)
+    col = lax.broadcasted_iota(jnp.int32, (n, n), 1)
+    ref[:n, :] = jnp.where(row >= col, w11, w22.T)
+    ref[n : 2 * n, :] = w21
+    diag = jnp.sum(jnp.where(row == col, w22, 0.0), 0, keepdims=True)
+    ref[2 * n :, :] = jnp.broadcast_to(diag, (8, n))
+
+
+def unpack(ref):
+    n = ref.shape[1]
+    row = lax.broadcasted_iota(jnp.int32, (n, n), 0)
+    col = lax.broadcasted_iota(jnp.int32, (n, n), 1)
+    both, zero = ref[:n, :], jnp.zeros((n, n), F32)
+    w11 = jnp.where(row >= col, both, 0.0)
+    w22 = jnp.where(row > col, both.T, jnp.where(row == col, ref[2 * n : 2 * n + 1, :], 0.0))
+    return jnp.concatenate(
+        [jnp.concatenate([w11, zero], 1), jnp.concatenate([ref[n : 2 * n, :], w22], 1)], 0
+    )
+
+
+def first_kernel(info, matched, w_ref):
+    width = matched.shape[0]
+
+    @pl.when(info[3] == 0)
+    def _():
+        pack(w_ref, factor_pair(symmetric(matched[:, :width])))
+
+
+def second_kernel(info, below, w1, w_ref):
+    width = below.shape[0]
+
+    @pl.when(info[3] == 0)
+    def _():
+        lower = dot_t(below[:, :width], unpack(w1))
+        pack(w_ref, factor_pair(symmetric(below[:, width:] - dot_t(lower, lower))))
+
+
+def middle_kernel(info, shard, arrived, piece, piece2, matched, m1, m2, m3, diag, diag2, w, w2, *refs):
+    blocks = refs[:8]
+    out_ref, q_ref, n_ref, band, line, square, tri = refs[8:]
+    tile = arrived.shape[2]
+    nrows, width = shard.shape
+    group, layer, core, column = info[0], info[1], info[2], info[4]
+    out_ref[...] = shard[...]
+    for i in range(arrived.shape[0]):
+        add_block(out_ref, arrived[i, :tile, :], place_of(arrived[i, tile:, :]), tile)
+    @pl.when(core == 1)
+    def _():
+        square[...] = diag[...]
+        tri[...] = w[...]
+
+    @pl.when(core == 0)
+    def _():
+        square[...] = diag2[...]
+        tri[...] = w2[...]
+
+    for k, m in enumerate((matched, m1, m2, m3)):
+
+        @pl.when((group ^ layer) == k)
+        def _(m=m):
+            line[...] = m[...]
+
+    w1 = unpack(tri)
+    l21 = dot_t(square[...], w1)
+    by_rows = ((group >= 2) & (layer >= 2)) | (group == layer)
+    for c, (same, swapped) in enumerate(((piece, piece2), (piece2, piece))):
+
+        @pl.when(by_rows & (core == 0))
+        def _(c=c, p=same):
+            band[c * width : (c + 1) * width, :] = p[...].T
+
+        @pl.when(by_rows & (core == 1))
+        def _(c=c, p=swapped):
+            band[c * width : (c + 1) * width, :] = p[...].T
+
+        @pl.when(~by_rows & (core == 0))
+        def _(c=c, p=same):
+            band[:, c * width : (c + 1) * width] = p[...]
+
+        @pl.when(~by_rows & (core == 1))
+        def _(c=c, p=swapped):
+            band[:, c * width : (c + 1) * width] = p[...]
+
+    add_band_blocks(band, blocks, width)
+
+    @pl.when(column == 0)
+    def _():
+        out_ref[...] = dot_t(out_ref[...], w1)
+        q_ref[...] = jnp.zeros_like(q_ref)
+        n_ref[...] = jnp.zeros_like(n_ref)
+
+    @pl.when(column > 0)
+    def _():
+        @pl.when(group == 0)
+        def _():
+            q_ref[:width, :] = jnp.zeros((width, width), F32)
+            q_ref[width:, :] = l21
+
+        @pl.when(group > 0)
+        def _():
+            q_ref[...] = dot_t(band[:, :width], w1)
+
+        @pl.when(column == 1)
+        def _():
+            q_ref[...] = out_ref[...] - dot_t(q_ref[...], l21)
+            n_ref[...] = jnp.zeros_like(n_ref)
+
+        @pl.when(column > 1)
+        def _():
+            mine = dot_t(line[:, :width], w1)
+            n_ref[...] = line[:, width:] - dot_t(mine, l21)
+            out_ref[...] = out_ref[...] - dot_t(q_ref[...], mine)
+            q_ref[...] = band[:, width:] - dot_t(q_ref[...], l21)
+
+
+def last_kernel(info, out1, q, n, w, w2, out_ref, tri):
+    nrows, width = out1.shape
+    group, core, column = info[0], info[2], info[4]
+
+    @pl.when(core == 0)
+    def _():
+        tri[...] = w[...]
+
+    @pl.when(core == 1)
+    def _():
+        tri[...] = w2[...]
+
+    @pl.when(column == 0)
+    def _():
+        out_ref[...] = out1[...]
+
+    @pl.when(column > 0)
+    def _():
+        inverse = unpack(tri)
+        second = dot_t(q[...], inverse)
+
+        @pl.when(column == 1)
+        def _():
+            rows = group * nrows + lax.broadcasted_iota(jnp.int32, (nrows, width), 0)
+            out_ref[...] = jnp.where(rows >= width, second, out1[...])
+
+        @pl.when((column > 1) & (group == 0))
+        def _():
+            out_ref[...] = out1[...]
+
+        @pl.when((column > 1) & (group > 0))
+        def _():
+            out_ref[...] = out1[...] - dot_t(second, dot_t(n[...], inverse))
+
+
+def kernel(body, outs, args, smem=1, scratch=(), flops=1 << 20):
+    spec = [pl.BlockSpec(memory_space=pltpu.SMEM)] * smem
+    spec += [pl.BlockSpec(memory_space=pltpu.VMEM)] * (len(args) - smem)
+    return pl.pallas_call(
+        body,
+        out_shape=outs,
+        in_specs=spec,
+        scratch_shapes=[pltpu.VMEM(s, F32) for s in scratch],
+        compiler_params=pltpu.CompilerParams(vmem_limit_bytes=VMEM_LIMIT),
+        cost_estimate=pl.CostEstimate(flops=flops, bytes_accessed=1 << 20, transcendentals=0),
+    )(*args)
+
+
+def aligned(front, updates, target_owner, target_slot):
+    nrows, width = front.shape
+    tile = updates.shape[1]
+    nleaf, nfront = lax.axis_size("leaf"), lax.axis_size("front")
+    groups, layers = range(nleaf), range(nfront // 2)
+    group, column = lax.axis_index("leaf"), lax.axis_index("front")
+    layer, core = column // 2, column % 2
+    info = jnp.stack([group, layer, core, group * nfront + column, column]).astype(jnp.int32)
+
+    def dev(g, z, c):
+        return g * nfront + 2 * z + c
+
+    def send(x, pairs):
+        return lax.ppermute(x, AXES, pairs)
+
+    def out(*shape):
+        return jax.ShapeDtypeStruct(shape, F32)
+
+    both = range(2)
+    swap = [(dev(g, z, c), dev(g, z, 1 - c)) for g in groups for z in layers for c in both]
+
+    outgoing, payload = kernel(
+        sort_kernel,
+        (out(nfront, tile + 8, tile), out(2 * tile + 16, tile)),
+        (target_owner, target_slot, updates),
+        smem=2,
+    )
+    blocks = [payload]
+    for s in layers[1:]:
+        pairs = [(dev(g, z, c), dev(g, z ^ s, c)) for g in groups for z in layers for c in both]
+        blocks.append(send(payload, pairs))
+    blocks += [send(b, swap) for b in blocks]
+
+    turned = send(front, [(dev(0, z, c), dev(z, z, c)) for z in layers[1:] for c in both])
+    matched = kernel(
+        matched_kernel, out(width, 2 * width), (info, front, turned, *blocks), scratch=[(nrows, 2 * width)]
+    )
+    below = send(matched, [(dev(0, 0, 1), dev(0, 0, 0))])
+    away = [
+        send(
+            matched,
+            [(dev(z, z, c), dev(z ^ s, z, c)) for z in layers for c in both if (z, c) != (0, 0)],
+        )
+        for s in groups[1:]
+    ]
+    diag = jnp.where(group == 0, matched, away[0] + away[1] + away[2])[:, :width]
+    moved = [send(diag, [(dev(g, 0, 1), dev(g, s, 1)) for g in groups]) for s in layers[1:]]
+    diag = jnp.where(layer == 0, diag, moved[0] + moved[1] + moved[2])
+    diag2 = send(diag, [(dev(g, z, 1), dev(g, z, 0)) for g in groups for z in layers])
+
+    near = send(
+        front, [(dev(g, 0, c), dev(g, z, c)) for g, z in ((1, 2), (2, 1), (3, 1)) for c in both]
+    )
+    far = send(
+        jnp.where(group == layer, turned, near),
+        [(dev(g, z, c), dev(g, 5 - z, c)) for g, z in ((1, 2), (2, 2), (3, 3)) for c in both],
+    )
+    piece = jnp.where(layer == 0, front, jnp.where(group == layer, turned, near + far))
+    piece2 = send(piece, swap)
+
+    def share(x, c):
+        got = [send(x, [(dev(0, 0, c), dev(0, s, c))]) for s in layers[1:]]
+        x = jnp.where(layer == 0, x, got[0] + got[1] + got[2])
+        got = [send(x, [(dev(0, z, c), dev(s, z, c)) for z in layers]) for s in groups[1:]]
+        x = jnp.where(group == 0, x, got[0] + got[1] + got[2])
+        return x, send(x, [(dev(g, z, c), dev(g, z, 1 - c)) for g in groups for z in layers])
+
+    packed = out(2 * tile + 8, tile)
+    w1 = kernel(first_kernel, packed, (info, matched), flops=1 << 32)
+    w2 = kernel(second_kernel, packed, (info, below, w1), flops=1 << 32)
+    w1, w1x = share(send(w1, [(dev(0, 0, 0), dev(0, 0, 1))]), 1)
+    w2, w2x = share(w2, 0)
+
+    arrived = lax.all_to_all(outgoing, "front", split_axis=0, concat_axis=0, tiled=True)
+    out1, q, n = kernel(
+        middle_kernel,
+        (out(nrows, width), out(nrows, width), out(width, width)),
+        (info, front, arrived, piece, piece2, matched, *away, diag, diag2, w1, w1x, *blocks),
+        scratch=[(nrows, 2 * width), (width, 2 * width), (width, width), (2 * tile + 8, tile)],
+        flops=1 << 31,
+    )
+    return kernel(
+        last_kernel, out(nrows, width), (info, out1, q, n, w2, w2x), scratch=[(2 * tile + 8, tile)], flops=1 << 30
+    )
+
+
 def solution(mesh):
+    nleaf, nfront = mesh.shape["leaf"], mesh.shape["front"]
+
+    def shards(front, updates, target_owner, target_slot):
+        nrows, width = front.shape
+        tile = updates.shape[1]
+        lines_up = (
+            nrows == 2 * width
+            and width == 2 * tile
+            and nleaf == 4
+            and nfront == 8
+        )
+        plan = aligned if lines_up else general
+        return plan(front, updates, target_owner, target_slot)
+
     return jax.shard_map(
         shards,
         mesh=mesh,

time: 469 us -> 108 us (0.23)
  the two profiles are of different devices: /device:TPU:11 before, /device:TPU:0 now
where the time goes in v2:
time: 108 us; the launch traced here: 107 us
  starting transfers between devices  54.5 us (50%)
  Pallas kernels  27.1 us (25%)
  waiting for transfers between devices  12.2 us (11%)
  local copies, waits for them, and re-layouts  9.12 us (8%)
  other arithmetic  3.86 us (4%)
    ppermute x34, starting transfers between devices, send(): return lax.ppermute(x, AXES, pairs)  50.9 us
    pallas_call x6, Pallas kernels, kernel(): pl.pallas_call(body, out_shape=outs, in_specs=spec, scratch_shapes=[pltpu...  27.1 us
    ppermute x34, waiting for transfers between devices, send(): return lax.ppermute(x, AXES, pairs)  12.2 us
    unnamed x30, local copies, waits for them, and re-layouts  9.04 us
    all_to_all x1, starting transfers between devices, aligned(): lax.all_to_all(outgoing, 'front', split_axis=0, concat_axis=0, tiled=True)  3.55 us
  transfers between devices with their start and end apart: 35, of which 2 were waited for; matrix products, arithmetic and copies ran while one was open for 4% of the time, Pallas kernels for 24%

profile of v2, /device:TPU:0, one launch (start us, length us, event | category | flops | bytes accessed | tf_op | source)
XLA Modules:
  0.0 107.3 jit_solution(15859284491374299818)
XLA Ops:
  0.7 0.9 copy-done.2
  3.0 1.4 %shard_map.46 = (f32[8,136,128]{2,1,0:T(8,128)}, f32[272,128]{1,0:T(8,128)S(1)}) custom-call(s32[4]{0:T(128)S(1)} %copy-done.13, s32[4]{0:T(128)S(1)} %copy-done.14, f32[4,128,128]{2,1,0:T(8,128)S(1)} %copy-done.2), custom_call_target="tpu_custom_call" | custom-call | flops 1048576 | bytes 1048576 | tf_op jit(solution)/shard_map/pallas_call | solution.py:381
  4.4 5.8 %collective-permute-start.4 = (f32[272,128]{1,0:T(8,128)S(1)}, f32[272,128]{1,0:T(8,128)S(1)}, u32[]{:S(2)}, u32[]{:S(2)}) collective-permute-start(f32[272,128]{1,0:T(8,128)S(1)} %get-tuple-element.11.refs_0_), channel_id=1, source_target_pairs={{0,2},{1,3},{2,0},{3,1},{4,6},{5,7},{6,4},{7,5},{8,10},{9,11},{10,... | collective-permute-start | bytes 417800 | tf_op jit(solution)/shard_map/ppermute | solution.py:404
  10.1 3.5 %collective-permute-start.5 = (f32[272,128]{1,0:T(8,128)S(1)}, f32[272,128]{1,0:T(8,128)S(1)}, u32[]{:S(2)}, u32[]{:S(2)}) collective-permute-start(f32[272,128]{1,0:T(8,128)S(1)} %get-tuple-element.11.refs_0_), channel_id=1, source_target_pairs={{0,4},{1,5},{2,6},{3,7},{4,0},{5,1},{6,2},{7,3},{8,12},{9,13},{10,... | collective-permute-start | bytes 417800 | tf_op jit(solution)/shard_map/ppermute | solution.py:404
  14.2 10.0 %collective-permute-done.5.refs_2_ = f32[272,128]{1,0:T(8,128)S(1)} collective-permute-done((f32[272,128]{1,0:T(8,128)S(1)}, f32[272,128]{1,0:T(8,128)S(1)}, u32[]{:S(2)}, u32[]{:S(2)}) %collective-permute-start.5) | collective-permute-done | bytes 139296 | tf_op jit(solution)/shard_map/ppermute | solution.py:404
  24.8 1.4 %collective-permute-start.1 = (f32[512,256]{1,0:T(8,128)}, f32[512,256]{1,0:T(8,128)}, u32[]{:S(2)}, u32[]{:S(2)}) collective-permute-start(f32[512,256]{1,0:T(8,128)} %shard.1), channel_id=1, source_target_pairs={{8,12},{9,13},{16,18},{17,19},{24,26},{25,27}} | collective-permute-start | bytes 1572872 | tf_op jit(solution)/shard_map/ppermute | solution.py:404
  26.3 1.1 %copy-done = f32[512,256]{1,0:T(8,128)S(1)} copy-done((f32[512,256]{1,0:T(8,128)S(1)}, f32[512,256]{1,0:T(8,128)}, u32[]{:S(2)}) %copy-start) | copy-done | bytes 524312
  27.4 1.0 shard_map.47.matched
  28.4 9.5 %shard_map.48.w1 = f32[264,128]{1,0:T(8,128)} custom-call(s32[5]{0:T(128)S(1)} %stack.23.info, f32[256,512]{1,0:T(8,128)S(1)} %shard_map.47.matched), custom_call_target="tpu_custom_call" | custom-call | flops 4294967296 | bytes 1048576 | tf_op jit(solution)/shard_map/pallas_call | solution.py:381
  37.9 1.9 %collective-permute-start.18 = (f32[264,128]{1,0:T(8,128)}, f32[264,128]{1,0:T(8,128)}, u32[]{:S(2)}, u32[]{:S(2)}) collective-permute-start(f32[264,128]{1,0:T(8,128)} %shard_map.48.w1), channel_id=1, source_target_pairs={{0,1}} | collective-permute-start | bytes 405512 | tf_op jit(solution)/shard_map/ppermute | solution.py:404
  39.8 1.3 %collective-permute-start.26 = (f32[256,512]{1,0:T(8,128)S(1)}, f32[256,512]{1,0:T(8,128)S(1)}, u32[]{:S(2)}, u32[]{:S(2)}) collective-permute-start(f32[256,512]{1,0:T(8,128)S(1)} %shard_map.47.matched), channel_id=1, source_target_pairs={{1,0}} | collective-permute-start | bytes 1572872 | tf_op jit(solution)/shard_map/ppermute | solution.py:404
  41.1 3.5 %all-to-all-start = ((f32[8,136,128]{2,1,0:T(8,128)}), f32[8,136,128]{2,1,0:T(8,128)S(1)}, u32[]{:S(2)}, u32[]{:S(2)}) async-start(f32[8,136,128]{2,1,0:T(8,128)} %get-tuple-element.10), calls=%async_computation | async-start | bytes 1114112 | tf_op jit(solution)/shard_map/all_to_all | solution.py:464
  49.6 1.0 add_select_fusion.4
  50.6 10.3 %shard_map.50 = f32[264,128]{1,0:T(8,128)S(1)} custom-call(s32[5]{0:T(128)S(1)} %stack.23.info, f32[256,512]{1,0:T(8,128)S(1)} %collective-permute-done.26.below, f32[264,128]{1,0:T(8,128)} %shard_map.48.w1), custom_call_target="tpu_custom_call" | custom-call | flops 4294967296 | bytes 1048576 | tf_op jit(solution)/shard_map/pallas_call | solution.py:381
  60.9 1.4 %collective-permute-start.29 = (f32[264,128]{1,0:T(8,128)S(1)}, f32[264,128]{1,0:T(8,128)S(1)}, u32[]{:S(2)}, u32[]{:S(2)}) collective-permute-start(f32[264,128]{1,0:T(8,128)S(1)} %shard_map.50), channel_id=1, source_target_pairs={{0,6}} | collective-permute-start | bytes 405512 | tf_op jit(solution)/shard_map/ppermute | solution.py:404
  66.2 2.8 %collective-permute-start.27 = (f32[264,128]{1,0:T(8,128)S(1)}, f32[264,128]{1,0:T(8,128)S(1)}, u32[]{:S(2)}, u32[]{:S(2)}) collective-permute-start(f32[264,128]{1,0:T(8,128)S(1)} %shard_map.50), channel_id=1, source_target_pairs={{0,2}} | collective-permute-start | bytes 405512 | tf_op jit(solution)/shard_map/ppermute | solution.py:404
  69.0 5.1 %collective-permute-start.28 = (f32[264,128]{1,0:T(8,128)S(1)}, f32[264,128]{1,0:T(8,128)S(1)}, u32[]{:S(2)}, u32[]{:S(2)}) collective-permute-start(f32[264,128]{1,0:T(8,128)S(1)} %shard_map.50), channel_id=1, source_target_pairs={{0,4}} | collective-permute-start | bytes 405512 | tf_op jit(solution)/shard_map/ppermute | solution.py:404
  74.1 1.2 %select_select_fusion.piece = f32[512,256]{1,0:T(8,128)S(1)} fusion(f32[512,256]{1,0:T(8,128)S(1)} %copy-done.1, f32[512,256]{1,0:T(8,128)S(1)} %collective-permute-done.turned, f32[512,256]{1,0:T(8,128)} %collective-permute-done.1, f32[512,256]{1,0:T(8,128)S(1)} %collective-permute-done.2, pred[]{:T(512)S(6)} %eq.9, pred[]{:T(512)S(6)} %eq.8), kind=kLoop, calls=%fused_computation | loop fusion | flops 393216 | bytes 2621442 | tf_op jit(solution)/shard_map/jit(_where)/select_n | solution.py:448
  76.0 2.1 %collective-permute-done.28 = f32[264,128]{1,0:T(8,128)S(1)} collective-permute-done((f32[264,128]{1,0:T(8,128)S(1)}, f32[264,128]{1,0:T(8,128)S(1)}, u32[]{:S(2)}, u32[]{:S(2)}) %collective-permute-start.28) | collective-permute-done | bytes 135200 | tf_op jit(solution)/shard_map/ppermute | solution.py:404
  79.7 5.3 %collective-permute-start.3 = (f32[512,256]{1,0:T(8,128)S(1)}, f32[512,256]{1,0:T(8,128)}, u32[]{:S(2)}, u32[]{:S(2)}) collective-permute-start(f32[512,256]{1,0:T(8,128)S(1)} %select_select_fusion.piece), channel_id=1, source_target_pairs={{0,1},{1,0},{2,3},{3,2},{4,5},{5,4},{6,7},{7,6},{8,9},{9,8},{10,11... | collective-permute-start | bytes 1572872 | tf_op jit(solution)/shard_map/ppermute | solution.py:404
  85.0 1.3 %collective-permute-start.32 = (f32[264,128]{1,0:T(8,128)S(1)}, f32[264,128]{1,0:T(8,128)S(1)}, u32[]{:S(2)}, u32[]{:S(2)}) collective-permute-start(f32[264,128]{1,0:T(8,128)S(1)} %add_select_fusion.2), channel_id=1, source_target_pairs={{0,24},{2,26},{4,28},{6,30}} | collective-permute-start | bytes 405512 | tf_op jit(solution)/shard_map/ppermute | solution.py:404
  86.3 1.3 %collective-permute-start.30 = (f32[264,128]{1,0:T(8,128)S(1)}, f32[264,128]{1,0:T(8,128)S(1)}, u32[]{:S(2)}, u32[]{:S(2)}) collective-permute-start(f32[264,128]{1,0:T(8,128)S(1)} %add_select_fusion.2), channel_id=1, source_target_pairs={{0,8},{2,10},{4,12},{6,14}} | collective-permute-start | bytes 405512 | tf_op jit(solution)/shard_map/ppermute | solution.py:404
  87.6 1.3 %collective-permute-start.31 = (f32[264,128]{1,0:T(8,128)S(1)}, f32[264,128]{1,0:T(8,128)S(1)}, u32[]{:S(2)}, u32[]{:S(2)}) collective-permute-start(f32[264,128]{1,0:T(8,128)S(1)} %add_select_fusion.2), channel_id=1, source_target_pairs={{0,16},{2,18},{4,20},{6,22}} | collective-permute-start | bytes 405512 | tf_op jit(solution)/shard_map/ppermute | solution.py:404
  89.0 1.3 %collective-permute-start.17 = (f32[256,256]{1,0:T(8,128)S(1)}, f32[256,256]{1,0:T(8,128)}, u32[]{:S(2)}, u32[]{:S(2)}) collective-permute-start(f32[256,256]{1,0:T(8,128)S(1)} %add_select_fusion.diag), channel_id=1, source_target_pairs={{1,0},{3,2},{5,4},{7,6},{9,8},{11,10},{13,12},{15,14},{17,16},{19,... | collective-permute-start | bytes 786440 | tf_op jit(solution)/shard_map/ppermute | solution.py:404
  91.0 1.4 %collective-permute-start.25 = (f32[264,128]{1,0:T(8,128)}, f32[264,128]{1,0:T(8,128)}, u32[]{:S(2)}, u32[]{:S(2)}) collective-permute-start(f32[264,128]{1,0:T(8,128)} %add_select_fusion.3.w), channel_id=1, source_target_pairs={{1,0},{3,2},{5,4},{7,6},{9,8},{11,10},{13,12},{15,14},{17,16},{19,... | collective-permute-start | bytes 405512 | tf_op jit(solution)/shard_map/ppermute | solution.py:404
  93.1 5.1 %collective-permute-start.33 = (f32[264,128]{1,0:T(8,128)}, f32[264,128]{1,0:T(8,128)}, u32[]{:S(2)}, u32[]{:S(2)}) collective-permute-start(f32[264,128]{1,0:T(8,128)} %add_select_fusion.1.w), channel_id=1, source_target_pairs={{0,1},{2,3},{4,5},{6,7},{8,9},{10,11},{12,13},{14,15},{16,17},{18,... | collective-permute-start | bytes 405512 | tf_op jit(solution)/shard_map/ppermute | solution.py:404
  98.2 0.9 copy-done.6
  99.1 1.0 copy-done.8
  100.1 1.0 copy-done.10
  101.2 1.0 copy-done.12
  102.2 3.2 %shard_map.49 = (f32[512,256]{1,0:T(8,128)S(1)}, f32[512,256]{1,0:T(8,128)S(1)}, f32[256,256]{1,0:T(8,128)S(1)}) custom-call(s32[5]{0:T(128)S(1)} %stack.23.info, f32[512,256]{1,0:T(8,128)S(1)} %copy-done.1, f32[8,136,128]{2,1,0:T(8,128)S(1)} %all-to-all-done.arrived, f32[512,256]{1,0:T(8,128)S(1)} %select_select_fusion.piece, ...), custom_call_target="tpu_custom_call" | custom-call | flops 2147483648 | bytes 1048576 | tf_op jit(solution)/shard_map/pallas_call | solution.py:381
  105.4 1.8 %shard_map.51 = f32[512,256]{1,0:T(8,128)} custom-call(s32[5]{0:T(128)S(1)} %stack.23.info, f32[512,256]{1,0:T(8,128)S(1)} %get-tuple-element.12.out1, f32[512,256]{1,0:T(8,128)S(1)} %get-tuple-element.13.q, f32[256,256]{1,0:T(8,128)S(1)} %get-tuple-element.14.n, f32[264,128]{1,0:T(8,128)} %add_select_fusion.1.w, f32[264,128]{1,0:T(8,128)} %collective-permute-done.33.w2), custom_call_target="tpu_custom_call" | custom-call | flops 1073741824 | bytes 1048576 | tf_op jit(solution)/shard_map/pallas_call | solution.py:381
  (83 shorter events, 15.5 us)
Async XLA Ops:
  0.0 26.3 %collective-permute-start = (f32[512,256]{1,0:T(8,128)}, f32[512,256]{1,0:T(8,128)S(1)}, u32[]{:S(2)}, u32[]{:S(2)}) collective-permute-start(f32[512,256]{1,0:T(8,128)} %shard.1), channel_id=1, source_target_pairs={{2,10},{3,11},{4,20},{5,21},{6,30},{7,31}} | collective-permute-start | bytes 1572872 | tf_op jit(solution)/shard_map/ppermute | solution.py:404
  4.4 9.3 %collective-permute-start.4 = (f32[272,128]{1,0:T(8,128)S(1)}, f32[272,128]{1,0:T(8,128)S(1)}, u32[]{:S(2)}, u32[]{:S(2)}) collective-permute-start(f32[272,128]{1,0:T(8,128)S(1)} %get-tuple-element.11.refs_0_), channel_id=1, source_target_pairs={{0,2},{1,3},{2,0},{3,1},{4,6},{5,7},{6,4},{7,5},{8,10},{9,11},{10,... | collective-permute-start | bytes 417800 | tf_op jit(solution)/shard_map/ppermute | solution.py:404
  10.1 14.1 %collective-permute-start.5 = (f32[272,128]{1,0:T(8,128)S(1)}, f32[272,128]{1,0:T(8,128)S(1)}, u32[]{:S(2)}, u32[]{:S(2)}) collective-permute-start(f32[272,128]{1,0:T(8,128)S(1)} %get-tuple-element.11.refs_0_), channel_id=1, source_target_pairs={{0,4},{1,5},{2,6},{3,7},{4,0},{5,1},{6,2},{7,3},{8,12},{9,13},{10,... | collective-permute-start | bytes 417800 | tf_op jit(solution)/shard_map/ppermute | solution.py:404
  13.7 10.5 %collective-permute-start.6 = (f32[272,128]{1,0:T(8,128)S(1)}, f32[272,128]{1,0:T(8,128)S(1)}, u32[]{:S(2)}, u32[]{:S(2)}) collective-permute-start(f32[272,128]{1,0:T(8,128)S(1)} %get-tuple-element.11.refs_0_), channel_id=1, source_target_pairs={{0,6},{1,7},{2,4},{3,5},{4,2},{5,3},{6,0},{7,1},{8,14},{9,15},{10,... | collective-permute-start | bytes 417800 | tf_op jit(solution)/shard_map/ppermute | solution.py:404
  13.7 11.1 %collective-permute-start.7 = (f32[272,128]{1,0:T(8,128)S(1)}, f32[272,128]{1,0:T(8,128)S(1)}, u32[]{:S(2)}, u32[]{:S(2)}) collective-permute-start(f32[272,128]{1,0:T(8,128)S(1)} %get-tuple-element.11.refs_0_), channel_id=1, source_target_pairs={{0,1},{1,0},{2,3},{3,2},{4,5},{5,4},{6,7},{7,6},{8,9},{9,8},{10,11... | collective-permute-start | bytes 417800 | tf_op jit(solution)/shard_map/ppermute | solution.py:404
  13.7 12.6 %collective-permute-start.8 = (f32[272,128]{1,0:T(8,128)S(1)}, f32[272,128]{1,0:T(8,128)S(1)}, u32[]{:S(2)}, u32[]{:S(2)}) collective-permute-start(f32[272,128]{1,0:T(8,128)S(1)} %collective-permute-done.4.refs_1_), channel_id=1, source_target_pairs={{0,1},{1,0},{2,3},{3,2},{4,5},{5,4},{6,7},{7,6},{8,9},{9,8},{10,11... | collective-permute-start | bytes 417800 | tf_op jit(solution)/shard_map/ppermute | solution.py:404
  24.8 21.9 %collective-permute-start.1 = (f32[512,256]{1,0:T(8,128)}, f32[512,256]{1,0:T(8,128)}, u32[]{:S(2)}, u32[]{:S(2)}) collective-permute-start(f32[512,256]{1,0:T(8,128)} %shard.1), channel_id=1, source_target_pairs={{8,12},{9,13},{16,18},{17,19},{24,26},{25,27}} | collective-permute-start | bytes 1572872 | tf_op jit(solution)/shard_map/ppermute | solution.py:404
  37.9 7.5 %collective-permute-start.18 = (f32[264,128]{1,0:T(8,128)}, f32[264,128]{1,0:T(8,128)}, u32[]{:S(2)}, u32[]{:S(2)}) collective-permute-start(f32[264,128]{1,0:T(8,128)} %shard_map.48.w1), channel_id=1, source_target_pairs={{0,1}} | collective-permute-start | bytes 405512 | tf_op jit(solution)/shard_map/ppermute | solution.py:404
  39.8 10.8 %collective-permute-start.26 = (f32[256,512]{1,0:T(8,128)S(1)}, f32[256,512]{1,0:T(8,128)S(1)}, u32[]{:S(2)}, u32[]{:S(2)}) collective-permute-start(f32[256,512]{1,0:T(8,128)S(1)} %shard_map.47.matched), channel_id=1, source_target_pairs={{1,0}} | collective-permute-start | bytes 1572872 | tf_op jit(solution)/shard_map/ppermute | solution.py:404
  41.1 57.1 %all-to-all-start = ((f32[8,136,128]{2,1,0:T(8,128)}), f32[8,136,128]{2,1,0:T(8,128)S(1)}, u32[]{:S(2)}, u32[]{:S(2)}) async-start(f32[8,136,128]{2,1,0:T(8,128)} %get-tuple-element.10), calls=%async_computation | async-start | bytes 1114112 | tf_op jit(solution)/shard_map/all_to_all | solution.py:464
  44.7 17.7 %collective-permute-start.11 = (f32[256,512]{1,0:T(8,128)S(1)}, f32[256,512]{1,0:T(8,128)S(1)}, u32[]{:S(2)}, u32[]{:S(2)}) collective-permute-start(f32[256,512]{1,0:T(8,128)S(1)} %shard_map.47.matched), channel_id=1, source_target_pairs={{1,9},{10,2},{11,3},{20,28},{21,29},{30,22},{31,23}} | collective-permute-start | bytes 1572872 | tf_op jit(solution)/shard_map/ppermute | solution.py:404
  46.1 2.2 %collective-permute-start.19 = (f32[264,128]{1,0:T(8,128)}, f32[264,128]{1,0:T(8,128)S(1)}, u32[]{:S(2)}, u32[]{:S(2)}) collective-permute-start(f32[264,128]{1,0:T(8,128)} %collective-permute-done.18), channel_id=1, source_target_pairs={{1,3}} | collective-permute-start | bytes 405512 | tf_op jit(solution)/shard_map/ppermute | solution.py:404
  46.7 2.2 %collective-permute-start.20 = (f32[264,128]{1,0:T(8,128)}, f32[264,128]{1,0:T(8,128)S(1)}, u32[]{:S(2)}, u32[]{:S(2)}) collective-permute-start(f32[264,128]{1,0:T(8,128)} %collective-permute-done.18), channel_id=1, source_target_pairs={{1,5}} | collective-permute-start | bytes 405512 | tf_op jit(solution)/shard_map/ppermute | solution.py:404
  47.5 14.8 %collective-permute-start.12 = (f32[256,512]{1,0:T(8,128)S(1)}, f32[256,512]{1,0:T(8,128)S(1)}, u32[]{:S(2)}, u32[]{:S(2)}) collective-permute-start(f32[256,512]{1,0:T(8,128)S(1)} %shard_map.47.matched), channel_id=1, source_target_pairs={{1,17},{10,26},{11,27},{20,4},{21,5},{30,14},{31,15}} | collective-permute-start | bytes 1572872 | tf_op jit(solution)/shard_map/ppermute | solution.py:404
  48.2 14.1 %collective-permute-start.13 = (f32[256,512]{1,0:T(8,128)S(1)}, f32[256,512]{1,0:T(8,128)S(1)}, u32[]{:S(2)}, u32[]{:S(2)}) collective-permute-start(f32[256,512]{1,0:T(8,128)S(1)} %shard_map.47.matched), channel_id=1, source_target_pairs={{1,25},{10,18},{11,19},{20,12},{21,13},{30,6},{31,7}} | collective-permute-start | bytes 1572872 | tf_op jit(solution)/shard_map/ppermute | solution.py:404
  48.9 17.2 %collective-permute-start.2 = (f32[512,256]{1,0:T(8,128)S(1)}, f32[512,256]{1,0:T(8,128)S(1)}, u32[]{:S(2)}, u32[]{:S(2)}) collective-permute-start(f32[512,256]{1,0:T(8,128)S(1)} %broadcast_select_fusion), channel_id=1, source_target_pairs={{12,14},{13,15},{20,22},{21,23},{30,28},{31,29}} | collective-permute-start | bytes 1572872 | tf_op jit(solution)/shard_map/ppermute | solution.py:404
  60.9 8.1 %collective-permute-start.29 = (f32[264,128]{1,0:T(8,128)S(1)}, f32[264,128]{1,0:T(8,128)S(1)}, u32[]{:S(2)}, u32[]{:S(2)}) collective-permute-start(f32[264,128]{1,0:T(8,128)S(1)} %shard_map.50), channel_id=1, source_target_pairs={{0,6}} | collective-permute-start | bytes 405512 | tf_op jit(solution)/shard_map/ppermute | solution.py:404
  64.1 14.7 %collective-permute-start.16 = (f32[256,256]{1,0:T(8,128)S(1)}, f32[256,256]{1,0:T(8,128)S(1)}, u32[]{:S(2)}, u32[]{:S(2)}) collective-permute-start(f32[256,256]{1,0:T(8,128)S(1)} %slice_select_fusion), channel_id=1, source_target_pairs={{1,7},{9,15},{17,23},{25,31}} | collective-permute-start | bytes 786440 | tf_op jit(solution)/shard_map/ppermute | solution.py:404
  64.8 14.9 %collective-permute-start.14 = (f32[256,256]{1,0:T(8,128)S(1)}, f32[256,256]{1,0:T(8,128)S(1)}, u32[]{:S(2)}, u32[]{:S(2)}) collective-permute-start(f32[256,256]{1,0:T(8,128)S(1)} %slice_select_fusion), channel_id=1, source_target_pairs={{1,3},{9,11},{17,19},{25,27}} | collective-permute-start | bytes 786440 | tf_op jit(solution)/shard_map/ppermute | solution.py:404
  65.5 19.5 %collective-permute-start.15 = (f32[256,256]{1,0:T(8,128)S(1)}, f32[256,256]{1,0:T(8,128)S(1)}, u32[]{:S(2)}, u32[]{:S(2)}) collective-permute-start(f32[256,256]{1,0:T(8,128)S(1)} %slice_select_fusion), channel_id=1, source_target_pairs={{1,5},{9,13},{17,21},{25,29}} | collective-permute-start | bytes 786440 | tf_op jit(solution)/shard_map/ppermute | solution.py:404
  66.2 9.2 %collective-permute-start.27 = (f32[264,128]{1,0:T(8,128)S(1)}, f32[264,128]{1,0:T(8,128)S(1)}, u32[]{:S(2)}, u32[]{:S(2)}) collective-permute-start(f32[264,128]{1,0:T(8,128)S(1)} %shard_map.50), channel_id=1, source_target_pairs={{0,2}} | collective-permute-start | bytes 405512 | tf_op jit(solution)/shard_map/ppermute | solution.py:404
  69.0 9.1 %collective-permute-start.28 = (f32[264,128]{1,0:T(8,128)S(1)}, f32[264,128]{1,0:T(8,128)S(1)}, u32[]{:S(2)}, u32[]{:S(2)}) collective-permute-start(f32[264,128]{1,0:T(8,128)S(1)} %shard_map.50), channel_id=1, source_target_pairs={{0,4}} | collective-permute-start | bytes 405512 | tf_op jit(solution)/shard_map/ppermute | solution.py:404
  75.3 11.0 %collective-permute-start.24 = (f32[264,128]{1,0:T(8,128)S(1)}, f32[264,128]{1,0:T(8,128)S(1)}, u32[]{:S(2)}, u32[]{:S(2)}) collective-permute-start(f32[264,128]{1,0:T(8,128)S(1)} %add_select_fusion.4), channel_id=1, source_target_pairs={{1,25},{3,27},{5,29},{7,31}} | collective-permute-start | bytes 405512 | tf_op jit(solution)/shard_map/ppermute | solution.py:404
  78.1 9.6 %collective-permute-start.22 = (f32[264,128]{1,0:T(8,128)S(1)}, f32[264,128]{1,0:T(8,128)S(1)}, u32[]{:S(2)}, u32[]{:S(2)}) collective-permute-start(f32[264,128]{1,0:T(8,128)S(1)} %add_select_fusion.4), channel_id=1, source_target_pairs={{1,9},{3,11},{5,13},{7,15}} | collective-permute-start | bytes 405512 | tf_op jit(solution)/shard_map/ppermute | solution.py:404
  78.8 10.2 %collective-permute-start.23 = (f32[264,128]{1,0:T(8,128)S(1)}, f32[264,128]{1,0:T(8,128)S(1)}, u32[]{:S(2)}, u32[]{:S(2)}) collective-permute-start(f32[264,128]{1,0:T(8,128)S(1)} %add_select_fusion.4), channel_id=1, source_target_pairs={{1,17},{3,19},{5,21},{7,23}} | collective-permute-start | bytes 405512 | tf_op jit(solution)/shard_map/ppermute | solution.py:404
  79.7 18.5 %collective-permute-start.3 = (f32[512,256]{1,0:T(8,128)S(1)}, f32[512,256]{1,0:T(8,128)}, u32[]{:S(2)}, u32[]{:S(2)}) collective-permute-start(f32[512,256]{1,0:T(8,128)S(1)} %select_select_fusion.piece), channel_id=1, source_target_pairs={{0,1},{1,0},{2,3},{3,2},{4,5},{5,4},{6,7},{7,6},{8,9},{9,8},{10,11... | collective-permute-start | bytes 1572872 | tf_op jit(solution)/shard_map/ppermute | solution.py:404
  85.0 6.0 %collective-permute-start.32 = (f32[264,128]{1,0:T(8,128)S(1)}, f32[264,128]{1,0:T(8,128)S(1)}, u32[]{:S(2)}, u32[]{:S(2)}) collective-permute-start(f32[264,128]{1,0:T(8,128)S(1)} %add_select_fusion.2), channel_id=1, source_target_pairs={{0,24},{2,26},{4,28},{6,30}} | collective-permute-start | bytes 405512 | tf_op jit(solution)/shard_map/ppermute | solution.py:404
  86.3 6.1 %collective-permute-start.30 = (f32[264,128]{1,0:T(8,128)S(1)}, f32[264,128]{1,0:T(8,128)S(1)}, u32[]{:S(2)}, u32[]{:S(2)}) collective-permute-start(f32[264,128]{1,0:T(8,128)S(1)} %add_select_fusion.2), channel_id=1, source_target_pairs={{0,8},{2,10},{4,12},{6,14}} | collective-permute-start | bytes 405512 | tf_op jit(solution)/shard_map/ppermute | solution.py:404
  87.6 4.8 %collective-permute-start.31 = (f32[264,128]{1,0:T(8,128)S(1)}, f32[264,128]{1,0:T(8,128)S(1)}, u32[]{:S(2)}, u32[]{:S(2)}) collective-permute-start(f32[264,128]{1,0:T(8,128)S(1)} %add_select_fusion.2), channel_id=1, source_target_pairs={{0,16},{2,18},{4,20},{6,22}} | collective-permute-start | bytes 405512 | tf_op jit(solution)/shard_map/ppermute | solution.py:404
  89.0 9.2 %collective-permute-start.17 = (f32[256,256]{1,0:T(8,128)S(1)}, f32[256,256]{1,0:T(8,128)}, u32[]{:S(2)}, u32[]{:S(2)}) collective-permute-start(f32[256,256]{1,0:T(8,128)S(1)} %add_select_fusion.diag), channel_id=1, source_target_pairs={{1,0},{3,2},{5,4},{7,6},{9,8},{11,10},{13,12},{15,14},{17,16},{19,... | collective-permute-start | bytes 786440 | tf_op jit(solution)/shard_map/ppermute | solution.py:404
  91.0 7.2 %collective-permute-start.25 = (f32[264,128]{1,0:T(8,128)}, f32[264,128]{1,0:T(8,128)}, u32[]{:S(2)}, u32[]{:S(2)}) collective-permute-start(f32[264,128]{1,0:T(8,128)} %add_select_fusion.3.w), channel_id=1, source_target_pairs={{1,0},{3,2},{5,4},{7,6},{9,8},{11,10},{13,12},{15,14},{17,16},{19,... | collective-permute-start | bytes 405512 | tf_op jit(solution)/shard_map/ppermute | solution.py:404
  93.1 12.3 %collective-permute-start.33 = (f32[264,128]{1,0:T(8,128)}, f32[264,128]{1,0:T(8,128)}, u32[]{:S(2)}, u32[]{:S(2)}) collective-permute-start(f32[264,128]{1,0:T(8,128)} %add_select_fusion.1.w), channel_id=1, source_target_pairs={{0,1},{2,3},{4,5},{6,7},{8,9},{10,11},{12,13},{14,15},{16,17},{18,... | collective-permute-start | bytes 405512 | tf_op jit(solution)/shard_map/ppermute | solution.py:404
  (18 other events, 41.0 us)

commit v3 on v2

--- a/solution.py
+++ b/solution.py
@@ -84,7 +84,7 @@
 
 def factor_inverse(a):
     n = a.shape[0]
-    panels, per = n // 8, 2
+    panels, per, ahead = n // 8, 2, 2
     sub = lax.broadcasted_iota(jnp.int32, (8, n), 0)
     lane = lax.broadcasted_iota(jnp.int32, (8, n), 1)
     work = [
@@ -98,7 +98,7 @@
         d = {(i, j): row_of(cols[j], i) for j in range(8) for i in range(j, 8)}
         up = [row_of(rows, j) for j in range(8)]
         inv = [row_of(ident, j) for j in range(8)]
-        last = min(panels - 1, (k // per + 1) * per - 1)
+        last = min(panels - 1, (k // per + 1) * per - 1 + ahead)
         below = {
             b: [lane_of(work[b][0], 8 * k + j) for j in range(8)]
             for b in range(k + 1, last + 1)
@@ -126,7 +126,8 @@
             w = jnp.where(sub == j, inv[j], w)
         out.append(w)
         held.append((u, w))
-        if k % per == per - 1 and k + 1 < panels:
+        first = k + 1 + ahead
+        if k % per == per - 1 and first < panels:
             us = jnp.concatenate([p[0] for p in held], 0)
             ws = jnp.concatenate([p[1] for p in held], 0)
             uh, um, ul = parts(us)
@@ -139,11 +140,12 @@
                 1,
             ).astype(BF16)
             left = jnp.concatenate([uh, uh, uh, um, um, ul], 0).T
-            left = left[8 * (k + 1) :, :].astype(BF16)
+            left = left[8 * first :, :].astype(BF16)
             change = jnp.dot(left, right, preferred_element_type=F32)
-            for b in range(k + 1, panels):
-                part = change[8 * (b - k - 1) : 8 * (b - k), :]
+            for b in range(first, panels):
+                part = change[8 * (b - first) : 8 * (b - first + 1), :]
                 work[b] = [work[b][0] - part[:, :n], work[b][1] - part[:, n:]]
+        if k % per == per - 1:
             held = []
     return jnp.concatenate(out, 0)
 
@@ -191,15 +193,54 @@
 
 
 def add_band_blocks(ref, blocks, width):
-    tile = blocks[0].shape[1]
-    for owner in range(2):
-        for b in blocks:
-            tag = b[2 * tile + 8 * owner : 2 * tile + 8 * owner + 8, :]
-            add_block(ref, b[owner * tile : (owner + 1) * tile, :], place_of(tag), tile, owner * width)
-
-
-def sort_kernel(owner, slot, updates, out_ref, pay_ref):
+    for b in blocks:
+        tile = b.shape[2]
+        for i in range(b.shape[0]):
+            for owner in range(2):
+                tag = b[i, 2 * tile + 8 * owner : 2 * tile + 8 * owner + 8, :]
+                block = b[i, owner * tile : (owner + 1) * tile, :]
+                add_block(ref, block, place_of(tag), tile, owner * width)
+
+
+def square_ids(n):
+    return lax.broadcasted_iota(jnp.int32, (n, n), 0), lax.broadcasted_iota(jnp.int32, (n, n), 1)
+
+
+def pack(ref, s):
+    n = s.shape[0] // 2
+    row, col = square_ids(n)
+    ref[:n, :] = jnp.where(row >= col, s[:n, :n], s[n:, n:])
+    ref[n : 2 * n, :] = s[n:, :n]
+    diag = jnp.sum(jnp.where(row == col, s[n:, n:], 0.0), 0, keepdims=True)
+    ref[2 * n : 2 * n + 8, :] = jnp.broadcast_to(diag, (8, n))
+
+
+def unpack(ref):
+    n = ref.shape[1]
+    row, col = square_ids(n)
+    both, low = ref[:n, :], ref[n : 2 * n, :]
+    turned = both.T
+    s00 = jnp.where(row >= col, both, turned)
+    s11 = jnp.where(row < col, both, jnp.where(row > col, turned, ref[2 * n : 2 * n + 1, :]))
+    return jnp.concatenate(
+        [jnp.concatenate([s00, low.T], 1), jnp.concatenate([low, s11], 1)], 0
+    )
+
+
+def put_rows(ref, start, rows):
+    n = ref.shape[1]
+    ref[start : start + n, :] = rows[:, :n]
+    ref[start + n : start + 2 * n, :] = rows[:, n:]
+
+
+def get_rows(ref, start):
+    n = ref.shape[1]
+    return jnp.concatenate([ref[start : start + n, :], ref[start + n : start + 2 * n, :]], 1)
+
+
+def sort_kernel(owner, slot, info, updates, front, out_ref, pay_ref, diag_ref):
     sends, tile = updates.shape[:2]
+    width = front.shape[1]
     out_ref[...] = jnp.zeros_like(out_ref)
     for j in range(sends):
         out_ref[owner[j], :tile, :] = updates[j]
@@ -208,87 +249,101 @@
         pay_ref[o * tile : (o + 1) * tile, :] = out_ref[o, :tile, :]
         pay_ref[2 * tile + 8 * o : 2 * tile + 8 * o + 8, :] = out_ref[o, tile:, :]
 
-
-def matched_kernel(info, front, turned, *refs):
-    blocks, out_ref, band = refs[:-2], refs[-2], refs[-1]
+    @pl.when(info[3] == 0)
+    def _():
+        pack(diag_ref, front[:width, :])
+        put_rows(diag_ref, width + 8, front[width : width + tile, :])
+
+    @pl.when(info[3] == 1)
+    def _():
+        pack(diag_ref, front[width:, :])
+        put_rows(diag_ref, width + 8, front[:width, tile:].T)
+
+
+def rows_kernel(info, front, turned, diag, d1, d2, d3, here, there, diag_ref, out_ref, band, part):
     width = front.shape[1]
-
-    @pl.when(info[0] == info[1])
+    tile = width // 2
+    group, layer, core = info[0], info[1], info[2]
+
+    @pl.when((group == 0) | (group == layer))
     def _():
         band[...] = jnp.zeros_like(band)
-        add_band_blocks(band, blocks, width)
-        start = pl.multiple_of(info[2] * width, width)
-        own = jnp.where(info[0] == 0, front[...], turned[...])
-        out_ref[...] = own.T + band[pl.ds(start, width), :]
-
-
-def pack(ref, blocks):
-    w11, w21, w22 = blocks
-    n = w11.shape[0]
-    row = lax.broadcasted_iota(jnp.int32, (n, n), 0)
-    col = lax.broadcasted_iota(jnp.int32, (n, n), 1)
-    ref[:n, :] = jnp.where(row >= col, w11, w22.T)
-    ref[n : 2 * n, :] = w21
-    diag = jnp.sum(jnp.where(row == col, w22, 0.0), 0, keepdims=True)
-    ref[2 * n :, :] = jnp.broadcast_to(diag, (8, n))
-
-
-def unpack(ref):
-    n = ref.shape[1]
-    row = lax.broadcasted_iota(jnp.int32, (n, n), 0)
-    col = lax.broadcasted_iota(jnp.int32, (n, n), 1)
-    both, zero = ref[:n, :], jnp.zeros((n, n), F32)
-    w11 = jnp.where(row >= col, both, 0.0)
-    w22 = jnp.where(row > col, both.T, jnp.where(row == col, ref[2 * n : 2 * n + 1, :], 0.0))
-    return jnp.concatenate(
-        [jnp.concatenate([w11, zero], 1), jnp.concatenate([ref[n : 2 * n, :], w22], 1)], 0
-    )
-
-
-def first_kernel(info, matched, w_ref):
-    width = matched.shape[0]
-
-    @pl.when(info[3] == 0)
-    def _():
-        pack(w_ref, factor_pair(symmetric(matched[:, :width])))
-
-
-def second_kernel(info, below, w1, w_ref):
-    width = below.shape[0]
-
-    @pl.when(info[3] == 0)
-    def _():
-        lower = dot_t(below[:, :width], unpack(w1))
-        pack(w_ref, factor_pair(symmetric(below[:, width:] - dot_t(lower, lower))))
-
-
-def middle_kernel(info, shard, arrived, piece, piece2, matched, m1, m2, m3, diag, diag2, w, w2, *refs):
-    blocks = refs[:8]
-    out_ref, q_ref, n_ref, band, line, square, tri = refs[8:]
+        add_band_blocks(band, (here, there), width)
+
+    @pl.when(group == 0)
+    def _():
+        for z, d in enumerate((diag, d1, d2, d3)):
+
+            @pl.when(layer == z)
+            def _(d=d):
+                diag_ref[...] = d[...]
+
+        @pl.when(core == 0)
+        def _():
+            pack(part, symmetric(band[:width, :width]))
+            put_rows(part, width + 8, band[width : width + tile, :width])
+
+        @pl.when(core == 1)
+        def _():
+            pack(part, symmetric(band[width:, width:]))
+            put_rows(part, width + 8, band[width + tile :, :width])
+
+        diag_ref[...] += part[...]
+
+    @pl.when((group == layer) & (group > 0))
+    def _():
+        start = pl.multiple_of(core * width, width)
+        out_ref[...] = turned[...].T + band[pl.ds(start, width), :]
+
+
+def first_kernel(info, here, there, w_ref, l_ref, top, bottom):
+    tile = here.shape[1]
+    width = 2 * tile
+
+    @pl.when(info[2] == 0)
+    def _():
+        top[...] = here[...]
+        bottom[...] = there[...]
+
+    @pl.when(info[2] == 1)
+    def _():
+        top[...] = there[...]
+        bottom[...] = here[...]
+
+    store_inverse(w_ref, factor_pair(unpack(top)))
+    w = w_ref[...]
+    l_ref[:tile, :] = dot_t(get_rows(top, width + 8), w)
+    l_ref[tile:, :] = dot_t(get_rows(bottom, width + 8), w)
+
+
+def second_kernel(info, here, there, lower, w_ref, bottom):
+    @pl.when(info[2] == 0)
+    def _():
+        bottom[...] = there[...]
+
+    @pl.when(info[2] == 1)
+    def _():
+        bottom[...] = here[...]
+
+    store_inverse(w_ref, factor_pair(unpack(bottom) - dot_t(lower[...], lower[...])))
+
+
+def middle_kernel(
+    info, shard, arrived, piece, piece2, matched, m1, m2, m3, w, lower, here, there, out_ref, q_ref, n_ref, band, line
+):
     tile = arrived.shape[2]
     nrows, width = shard.shape
     group, layer, core, column = info[0], info[1], info[2], info[4]
     out_ref[...] = shard[...]
     for i in range(arrived.shape[0]):
         add_block(out_ref, arrived[i, :tile, :], place_of(arrived[i, tile:, :]), tile)
-    @pl.when(core == 1)
-    def _():
-        square[...] = diag[...]
-        tri[...] = w[...]
-
-    @pl.when(core == 0)
-    def _():
-        square[...] = diag2[...]
-        tri[...] = w2[...]
-
     for k, m in enumerate((matched, m1, m2, m3)):
 
         @pl.when((group ^ layer) == k)
         def _(m=m):
             line[...] = m[...]
 
-    w1 = unpack(tri)
-    l21 = dot_t(square[...], w1)
+    w1, l21 = w[...], lower[...]
     by_rows = ((group >= 2) & (layer >= 2)) | (group == layer)
     for c, (same, swapped) in enumerate(((piece, piece2), (piece2, piece))):
 
@@ -308,7 +363,7 @@
         def _(c=c, p=swapped):
             band[:, c * width : (c + 1) * width] = p[...]
 
-    add_band_blocks(band, blocks, width)
+    add_band_blocks(band, (here, there), width)
 
     @pl.when(column == 0)
     def _():
@@ -340,39 +395,23 @@
             q_ref[...] = band[:, width:] - dot_t(q_ref[...], l21)
 
 
-def last_kernel(info, out1, q, n, w, w2, out_ref, tri):
+def last_kernel(info, out1, q, n, w, out_ref):
     nrows, width = out1.shape
-    group, core, column = info[0], info[2], info[4]
-
-    @pl.when(core == 0)
-    def _():
-        tri[...] = w[...]
-
-    @pl.when(core == 1)
-    def _():
-        tri[...] = w2[...]
-
-    @pl.when(column == 0)
+    group, column = info[0], info[4]
+
+    @pl.when((column == 0) | ((column > 1) & (group == 0)))
     def _():
         out_ref[...] = out1[...]
 
-    @pl.when(column > 0)
-    def _():
-        inverse = unpack(tri)
-        second = dot_t(q[...], inverse)
-
-        @pl.when(column == 1)
-        def _():
-            rows = group * nrows + lax.broadcasted_iota(jnp.int32, (nrows, width), 0)
-            out_ref[...] = jnp.where(rows >= width, second, out1[...])
-
-        @pl.when((column > 1) & (group == 0))
-        def _():
-            out_ref[...] = out1[...]
-
-        @pl.when((column > 1) & (group > 0))
-        def _():
-            out_ref[...] = out1[...] - dot_t(second, dot_t(n[...], inverse))
+    @pl.when(column == 1)
+    def _():
+        rows = group * nrows + lax.broadcasted_iota(jnp.int32, (nrows, width), 0)
+        out_ref[...] = jnp.where(rows >= width, dot_t(q[...], w[...]), out1[...])
+
+    @pl.when((column > 1) & (group > 0))
+    def _():
+        second = dot_t(q[...], w[...])
+        out_ref[...] = out1[...] - dot_t(second, dot_t(n[...], w[...]))
 
 
 def kernel(body, outs, args, smem=1, scratch=(), flops=1 << 20):
@@ -409,69 +448,60 @@
     both = range(2)
     swap = [(dev(g, z, c), dev(g, z, 1 - c)) for g in groups for z in layers for c in both]
 
-    outgoing, payload = kernel(
+    packed = out(2 * width + 8, tile)
+    outgoing, payload, diag = kernel(
         sort_kernel,
-        (out(nfront, tile + 8, tile), out(2 * tile + 16, tile)),
-        (target_owner, target_slot, updates),
-        smem=2,
-    )
-    blocks = [payload]
-    for s in layers[1:]:
-        pairs = [(dev(g, z, c), dev(g, z ^ s, c)) for g in groups for z in layers for c in both]
-        blocks.append(send(payload, pairs))
-    blocks += [send(b, swap) for b in blocks]
-
+        (out(nfront, tile + 8, tile), out(2 * tile + 16, tile), packed),
+        (target_owner, target_slot, info, updates, front),
+        smem=3,
+    )
+    diags = [send(diag, [(dev(0, 0, c), dev(0, s, c)) for c in both]) for s in layers[1:]]
     turned = send(front, [(dev(0, z, c), dev(z, z, c)) for z in layers[1:] for c in both])
-    matched = kernel(
-        matched_kernel, out(width, 2 * width), (info, front, turned, *blocks), scratch=[(nrows, 2 * width)]
-    )
-    below = send(matched, [(dev(0, 0, 1), dev(0, 0, 0))])
+    near = send(
+        front, [(dev(g, 0, c), dev(g, z, c)) for g, z in ((1, 2), (2, 1), (3, 1)) for c in both]
+    )
+    here = lax.all_gather(
+        payload, "front", axis_index_groups=[[2 * z + c for z in layers] for c in both]
+    )
+    there = send(here, swap)
+
+    diag, matched = kernel(
+        rows_kernel,
+        (packed, out(width, 2 * width)),
+        (info, front, turned, diag, *diags, here, there),
+        scratch=[(nrows, 2 * width), packed.shape],
+    )
+    got = [
+        send(diag, [(dev(0, z, c), dev(s, z, c)) for z in layers for c in both]) for s in groups[1:]
+    ]
     away = [
-        send(
-            matched,
-            [(dev(z, z, c), dev(z ^ s, z, c)) for z in layers for c in both if (z, c) != (0, 0)],
-        )
+        send(matched, [(dev(z, z, c), dev(z ^ s, z, c)) for z in layers[1:] for c in both])
         for s in groups[1:]
     ]
-    diag = jnp.where(group == 0, matched, away[0] + away[1] + away[2])[:, :width]
-    moved = [send(diag, [(dev(g, 0, 1), dev(g, s, 1)) for g in groups]) for s in layers[1:]]
-    diag = jnp.where(layer == 0, diag, moved[0] + moved[1] + moved[2])
-    diag2 = send(diag, [(dev(g, z, 1), dev(g, z, 0)) for g in groups for z in layers])
-
-    near = send(
-        front, [(dev(g, 0, c), dev(g, z, c)) for g, z in ((1, 2), (2, 1), (3, 1)) for c in both]
-    )
+    diag = jnp.where(group == 0, diag, got[0] + got[1] + got[2])
+    diag2 = send(diag, swap)
+
     far = send(
         jnp.where(group == layer, turned, near),
         [(dev(g, z, c), dev(g, 5 - z, c)) for g, z in ((1, 2), (2, 2), (3, 3)) for c in both],
     )
     piece = jnp.where(layer == 0, front, jnp.where(group == layer, turned, near + far))
     piece2 = send(piece, swap)
-
-    def share(x, c):
-        got = [send(x, [(dev(0, 0, c), dev(0, s, c))]) for s in layers[1:]]
-        x = jnp.where(layer == 0, x, got[0] + got[1] + got[2])
-        got = [send(x, [(dev(0, z, c), dev(s, z, c)) for z in layers]) for s in groups[1:]]
-        x = jnp.where(group == 0, x, got[0] + got[1] + got[2])
-        return x, send(x, [(dev(g, z, c), dev(g, z, 1 - c)) for g in groups for z in layers])
-
-    packed = out(2 * tile + 8, tile)
-    w1 = kernel(first_kernel, packed, (info, matched), flops=1 << 32)
-    w2 = kernel(second_kernel, packed, (info, below, w1), flops=1 << 32)
-    w1, w1x = share(send(w1, [(dev(0, 0, 0), dev(0, 0, 1))]), 1)
-    w2, w2x = share(w2, 0)
-
     arrived = lax.all_to_all(outgoing, "front", split_axis=0, concat_axis=0, tiled=True)
+
+    square = out(width, width)
+    w1, l21 = kernel(
+        first_kernel, (square, square), (info, diag, diag2), scratch=[packed.shape] * 2, flops=1 << 32
+    )
+    w2 = kernel(second_kernel, square, (info, diag, diag2, l21), scratch=[packed.shape], flops=1 << 32)
     out1, q, n = kernel(
         middle_kernel,
-        (out(nrows, width), out(nrows, width), out(width, width)),
-        (info, front, arrived, piece, piece2, matched, *away, diag, diag2, w1, w1x, *blocks),
-        scratch=[(nrows, 2 * width), (width, 2 * width), (width, width), (2 * tile + 8, tile)],
+        (out(nrows, width), out(nrows, width), square),
+        (info, front, arrived, piece, piece2, matched, *away, w1, l21, here, there),
+        scratch=[(nrows, 2 * width), (width, 2 * width)],
         flops=1 << 31,
     )
-    return kernel(
-        last_kernel, out(nrows, width), (info, out1, q, n, w2, w2x), scratch=[(2 * tile + 8, tile)], flops=1 << 30
-    )
+    return kernel(last_kernel, out(nrows, width), (info, out1, q, n, w2), flops=1 << 30)
 
 
 def solution(mesh):

time: 108 us -> 101 us (0.935)
  the two profiles are of different devices: /device:TPU:0 before, /device:TPU:11 now
where the time goes in v3:
time: 101 us
  starting transfers between devices  45.7 us (45%)
  Pallas kernels  27.5 us (27%)
  blocking collectives  17.7 us (18%)
  local copies, waits for them, and re-layouts  6.2 us (6%)
  other arithmetic  3.23 us (3%)
    ppermute x15, starting transfers between devices, send(): return lax.ppermute(x, AXES, pairs)  38.6 us
    pallas_call x6, Pallas kernels, kernel(): pl.pallas_call(body, out_shape=outs, in_specs=spec, scratch_shapes=[pltpu...  27.5 us
    all_gather x1, blocking collectives, aligned(): lax.all_gather(payload, 'front', axis_index_groups=[[2 * z + c for z in l...  17.7 us
    all_to_all x1, starting transfers between devices, aligned(): lax.all_to_all(outgoing, 'front', split_axis=0, concat_axis=0, tiled=True)  7.09 us
    unnamed x18, local copies, waits for them, and re-layouts  6.12 us
  transfers between devices with their start and end apart: 16, of which 0 were waited for; matrix products, arithmetic and copies ran while one was open for 3% of the time, Pallas kernels for 17%

profile of v3, /device:TPU:11, one launch (start us, length us, event | category | flops | bytes accessed | tf_op | source)
XLA Modules:
  0.0 100.6 jit_solution(7385450066341574030)
XLA Ops:
  0.0 1.5 %collective-permute-start.1 = (f32[512,256]{1,0:T(8,128)}, f32[512,256]{1,0:T(8,128)}, u32[]{:S(2)}, u32[]{:S(2)}) collective-permute-start(f32[512,256]{1,0:T(8,128)} %shard.1), channel_id=1, source_target_pairs={{8,12},{9,13},{16,18},{17,19},{24,26},{25,27}} | collective-permute-start | bytes 1572872 | tf_op jit(solution)/shard_map/ppermute | solution.py:443
  1.5 1.3 %collective-permute-start = (f32[512,256]{1,0:T(8,128)}, f32[512,256]{1,0:T(8,128)S(1)}, u32[]{:S(2)}, u32[]{:S(2)}) collective-permute-start(f32[512,256]{1,0:T(8,128)} %shard.1), channel_id=1, source_target_pairs={{2,10},{3,11},{4,20},{5,21},{6,30},{7,31}} | collective-permute-start | bytes 1572872 | tf_op jit(solution)/shard_map/ppermute | solution.py:443
  2.9 0.6 copy-done.3
  3.5 1.0 %copy-done = f32[512,256]{1,0:T(8,128)S(1)} copy-done((f32[512,256]{1,0:T(8,128)S(1)}, f32[512,256]{1,0:T(8,128)}, u32[]{:S(2)}) %copy-start) | copy-done | bytes 524312
  4.5 0.9 copy-done.2
  5.5 1.5 %shard_map.46 = (f32[8,136,128]{2,1,0:T(8,128)}, f32[272,128]{1,0:T(8,128)S(1)}, f32[520,128]{1,0:T(8,128)S(1)}) custom-call(s32[4]{0:T(128)S(1)} %copy-done.3, s32[4]{0:T(128)S(1)} %copy-done.4, s32[5]{0:T(128)S(1)} %stack.23.info, f32[4,128,128]{2,1,0:T(8,128)S(1)} %copy-done.2, f32[512,256]{1,0:T(8,128)S(1)} %copy-done), custom_call_target="tpu_custom_call" | custom-call | flops 1048576 | bytes 1048576 | tf_op jit(solution)/shard_map/pallas_call | solution.py:420
  6.9 17.7 %all-gather = f32[1088,128]{1,0:T(8,128)S(1)} all-gather(f32[272,128]{1,0:T(8,128)S(1)} %get-tuple-element.17), channel_id=2, replica_groups={{0,2,4,6},{1,3,5,7},{8,10,12,14},{9,11,13,15},{16,18,20,22},{17,19,21,2..., dimensions={0}, use_global_device_ids=true | all-gather | bytes 696320 | tf_op jit(solution)/shard_map/all_gather | solution.py:463
  24.6 4.3 %collective-permute-start.7 = (f32[4,272,128]{2,1,0:T(8,128)S(1)}, f32[4,272,128]{2,1,0:T(8,128)S(1)}, u32[]{:S(2)}, u32[]{:S(2)}) collective-permute-start(f32[4,272,128]{2,1,0:T(8,128)S(1)} %bitcast.6), channel_id=1, source_target_pairs={{0,1},{1,0},{2,3},{3,2},{4,5},{5,4},{6,7},{7,6},{8,9},{9,8},{10,11... | collective-permute-start | bytes 1671176 | tf_op jit(solution)/shard_map/ppermute | solution.py:443
  28.9 0.7 collective-permute-start.6
  29.6 0.7 collective-permute-start.5
  30.3 0.7 collective-permute-start.4
  31.0 0.9 broadcast_select_fusion
  32.1 1.9 %shard_map.47 = (f32[520,128]{1,0:T(8,128)S(1)}, f32[256,512]{1,0:T(8,128)}) custom-call(s32[5]{0:T(128)S(1)} %stack.23.info, f32[512,256]{1,0:T(8,128)S(1)} %copy-done.1, f32[512,256]{1,0:T(8,128)S(1)} %collective-permute-done.turned, f32[520,128]{1,0:T(8,128)S(1)} %get-tuple-element.16.diag, f32[520,128]{1,0:T(8,128)S(1)} %collective-permute-done.4.d1, ...), custom_call_target="tpu_custom_call" | custom-call | flops 1048576 | bytes 1048576 | tf_op jit(solution)/shard_map/pallas_call | solution.py:420
  34.0 0.7 collective-permute-start.13
  34.7 1.5 %collective-permute-start.2 = (f32[512,256]{1,0:T(8,128)}, f32[512,256]{1,0:T(8,128)}, u32[]{:S(2)}, u32[]{:S(2)}) collective-permute-start(f32[512,256]{1,0:T(8,128)} %broadcast_select_fusion), channel_id=1, source_target_pairs={{12,14},{13,15},{20,22},{21,23},{30,28},{31,29}} | collective-permute-start | bytes 1572872 | tf_op jit(solution)/shard_map/ppermute | solution.py:443
  36.2 0.7 collective-permute-start.12
  36.9 1.3 %collective-permute-start.11 = (f32[520,128]{1,0:T(8,128)S(1)}, f32[520,128]{1,0:T(8,128)}, u32[]{:S(2)}, u32[]{:S(2)}) collective-permute-start(f32[520,128]{1,0:T(8,128)S(1)} %get-tuple-element.19), channel_id=1, source_target_pairs={{0,8},{1,9},{2,10},{3,11},{4,12},{5,13},{6,14},{7,15}} | collective-permute-start | bytes 798728 | tf_op jit(solution)/shard_map/ppermute | solution.py:443
  38.2 7.1 %all-to-all-start = ((f32[8,136,128]{2,1,0:T(8,128)}), f32[8,136,128]{2,1,0:T(8,128)S(1)}, u32[]{:S(2)}, u32[]{:S(2)}) async-start(f32[8,136,128]{2,1,0:T(8,128)} %get-tuple-element.15), calls=%async_computation | async-start | bytes 1114112 | tf_op jit(solution)/shard_map/all_to_all | solution.py:490
  45.2 3.8 %collective-permute-start.10 = (f32[256,512]{1,0:T(8,128)}, f32[256,512]{1,0:T(8,128)}, u32[]{:S(2)}, u32[]{:S(2)}) collective-permute-start(f32[256,512]{1,0:T(8,128)} %get-tuple-element.18.matched), channel_id=1, source_target_pairs={{10,18},{11,19},{20,12},{21,13},{30,6},{31,7}} | collective-permute-start | bytes 1572872 | tf_op jit(solution)/shard_map/ppermute | solution.py:443
  49.1 14.8 %collective-permute-start.9 = (f32[256,512]{1,0:T(8,128)}, f32[256,512]{1,0:T(8,128)}, u32[]{:S(2)}, u32[]{:S(2)}) collective-permute-start(f32[256,512]{1,0:T(8,128)} %get-tuple-element.18.matched), channel_id=1, source_target_pairs={{10,26},{11,27},{20,4},{21,5},{30,14},{31,15}} | collective-permute-start | bytes 1572872 | tf_op jit(solution)/shard_map/ppermute | solution.py:443
  63.8 5.9 %collective-permute-start.8 = (f32[256,512]{1,0:T(8,128)}, f32[256,512]{1,0:T(8,128)}, u32[]{:S(2)}, u32[]{:S(2)}) collective-permute-start(f32[256,512]{1,0:T(8,128)} %get-tuple-element.18.matched), channel_id=1, source_target_pairs={{10,2},{11,3},{20,28},{21,29},{30,22},{31,23}} | collective-permute-start | bytes 1572872 | tf_op jit(solution)/shard_map/ppermute | solution.py:443
  69.7 1.0 %add_select_fusion.here = f32[520,128]{1,0:T(8,128)S(1)} fusion(f32[520,128]{1,0:T(8,128)S(1)} %get-tuple-element.19, f32[520,128]{1,0:T(8,128)S(1)} %collective-permute-done.13, f32[520,128]{1,0:T(8,128)} %collective-permute-done.11, f32[520,128]{1,0:T(8,128)S(1)} %collective-permute-done.12, pred[]{:T(512)S(6)} %eq.14), kind=kLoop, calls=%fused_computation.1 | loop fusion | flops 199680 | bytes 1331201 | tf_op jit(solution)/shard_map/jit(_where)/select_n | solution.py:481
  70.7 0.8 collective-permute-start.14
  71.6 1.3 %select_select_fusion.piece = f32[512,256]{1,0:T(8,128)S(1)} fusion(f32[512,256]{1,0:T(8,128)S(1)} %copy-done.1, f32[512,256]{1,0:T(8,128)S(1)} %collective-permute-done.turned, f32[512,256]{1,0:T(8,128)} %collective-permute-done.1, f32[512,256]{1,0:T(8,128)} %collective-permute-done.2, pred[]{:T(512)S(6)} %eq.13, pred[]{:T(512)S(6)} %eq.12), kind=kLoop, calls=%fused_computation | loop fusion | flops 393216 | bytes 2621442 | tf_op jit(solution)/shard_map/jit(_where)/select_n | solution.py:488
  73.0 8.0 %shard_map.48 = (f32[256,256]{1,0:T(8,128)S(1)}, f32[256,256]{1,0:T(8,128)S(1)}) custom-call(s32[5]{0:T(128)S(1)} %stack.23.info, f32[520,128]{1,0:T(8,128)S(1)} %add_select_fusion.here, f32[520,128]{1,0:T(8,128)S(1)} %collective-permute-done.14.there), custom_call_target="tpu_custom_call" | custom-call | flops 4294967296 | bytes 1048576 | tf_op jit(solution)/shard_map/pallas_call | solution.py:420
  81.0 0.7 copy-done.5
  81.7 8.0 %shard_map.50.w = f32[256,256]{1,0:T(8,128)S(1)} custom-call(s32[5]{0:T(128)S(1)} %stack.23.info, f32[520,128]{1,0:T(8,128)S(1)} %add_select_fusion.here, f32[520,128]{1,0:T(8,128)S(1)} %collective-permute-done.14.there, f32[256,256]{1,0:T(8,128)S(1)} %get-tuple-element.21.lower), custom_call_target="tpu_custom_call" | custom-call | flops 4294967296 | bytes 1048576 | tf_op jit(solution)/shard_map/pallas_call | solution.py:420
  89.8 0.7 copy-done.7
  90.5 0.9 copy-done.6
  91.5 0.9 copy-done.8
  92.4 4.9 %shard_map.49 = (f32[512,256]{1,0:T(8,128)S(1)}, f32[512,256]{1,0:T(8,128)S(1)}, f32[256,256]{1,0:T(8,128)S(1)}) custom-call(s32[5]{0:T(128)S(1)} %stack.23.info, f32[512,256]{1,0:T(8,128)S(1)} %copy-done.1, f32[8,136,128]{2,1,0:T(8,128)S(1)} %all-to-all-done.arrived, f32[512,256]{1,0:T(8,128)S(1)} %select_select_fusion.piece, ...), custom_call_target="tpu_custom_call" | custom-call | flops 2147483648 | bytes 1048576 | tf_op jit(solution)/shard_map/pallas_call | solution.py:420
  97.3 3.2 %shard_map.51 = f32[512,256]{1,0:T(8,128)} custom-call(s32[5]{0:T(128)S(1)} %stack.23.info, f32[512,256]{1,0:T(8,128)S(1)} %get-tuple-element.22.out1, f32[512,256]{1,0:T(8,128)S(1)} %get-tuple-element.23.q, f32[256,256]{1,0:T(8,128)S(1)} %get-tuple-element.24.n, f32[256,256]{1,0:T(8,128)S(1)} %shard_map.50.w), custom_call_target="tpu_custom_call" | custom-call | flops 1073741824 | bytes 1048576 | tf_op jit(solution)/shard_map/pallas_call | solution.py:420
  (29 shorter events, 0.5 us)
Async XLA Ops:
  0.0 30.3 %collective-permute-start.1 = (f32[512,256]{1,0:T(8,128)}, f32[512,256]{1,0:T(8,128)}, u32[]{:S(2)}, u32[]{:S(2)}) collective-permute-start(f32[512,256]{1,0:T(8,128)} %shard.1), channel_id=1, source_target_pairs={{8,12},{9,13},{16,18},{17,19},{24,26},{25,27}} | collective-permute-start | bytes 1572872 | tf_op jit(solution)/shard_map/ppermute | solution.py:443
  1.5 29.5 %collective-permute-start = (f32[512,256]{1,0:T(8,128)}, f32[512,256]{1,0:T(8,128)S(1)}, u32[]{:S(2)}, u32[]{:S(2)}) collective-permute-start(f32[512,256]{1,0:T(8,128)} %shard.1), channel_id=1, source_target_pairs={{2,10},{3,11},{4,20},{5,21},{6,30},{7,31}} | collective-permute-start | bytes 1572872 | tf_op jit(solution)/shard_map/ppermute | solution.py:443
  2.8 0.7 copy-start.3
  2.8 0.7 copy-start.4
  3.5 1.0 %copy-start = (f32[512,256]{1,0:T(8,128)S(1)}, f32[512,256]{1,0:T(8,128)}, u32[]{:S(2)}) copy-start(f32[512,256]{1,0:T(8,128)} %shard.1) | copy-start | bytes 1572868
  4.5 0.9 copy-start.2
  24.6 7.3 %collective-permute-start.7 = (f32[4,272,128]{2,1,0:T(8,128)S(1)}, f32[4,272,128]{2,1,0:T(8,128)S(1)}, u32[]{:S(2)}, u32[]{:S(2)}) collective-permute-start(f32[4,272,128]{2,1,0:T(8,128)S(1)} %bitcast.6), channel_id=1, source_target_pairs={{0,1},{1,0},{2,3},{3,2},{4,5},{5,4},{6,7},{7,6},{8,9},{9,8},{10,11... | collective-permute-start | bytes 1671176 | tf_op jit(solution)/shard_map/ppermute | solution.py:443
  28.9 3.0 %collective-permute-start.6 = (f32[520,128]{1,0:T(8,128)S(1)}, f32[520,128]{1,0:T(8,128)S(1)}, u32[]{:S(2)}, u32[]{:S(2)}) collective-permute-start(f32[520,128]{1,0:T(8,128)S(1)} %get-tuple-element.16.diag), channel_id=1, source_target_pairs={{0,6},{1,7}} | collective-permute-start | bytes 798728 | tf_op jit(solution)/shard_map/ppermute | solution.py:443
  29.6 2.3 %collective-permute-start.5 = (f32[520,128]{1,0:T(8,128)S(1)}, f32[520,128]{1,0:T(8,128)S(1)}, u32[]{:S(2)}, u32[]{:S(2)}) collective-permute-start(f32[520,128]{1,0:T(8,128)S(1)} %get-tuple-element.16.diag), channel_id=1, source_target_pairs={{0,4},{1,5}} | collective-permute-start | bytes 798728 | tf_op jit(solution)/shard_map/ppermute | solution.py:443
  30.3 1.6 %collective-permute-start.4 = (f32[520,128]{1,0:T(8,128)S(1)}, f32[520,128]{1,0:T(8,128)S(1)}, u32[]{:S(2)}, u32[]{:S(2)}) collective-permute-start(f32[520,128]{1,0:T(8,128)S(1)} %get-tuple-element.16.diag), channel_id=1, source_target_pairs={{0,2},{1,3}} | collective-permute-start | bytes 798728 | tf_op jit(solution)/shard_map/ppermute | solution.py:443
  31.0 1.2 %copy-start.1 = (f32[512,256]{1,0:T(8,128)S(1)}, f32[512,256]{1,0:T(8,128)}, u32[]{:S(2)}) copy-start(f32[512,256]{1,0:T(8,128)} %shard.1) | copy-start | bytes 1572868
  34.0 15.0 %collective-permute-start.13 = (f32[520,128]{1,0:T(8,128)S(1)}, f32[520,128]{1,0:T(8,128)S(1)}, u32[]{:S(2)}, u32[]{:S(2)}) collective-permute-start(f32[520,128]{1,0:T(8,128)S(1)} %get-tuple-element.19), channel_id=1, source_target_pairs={{0,24},{1,25},{2,26},{3,27},{4,28},{5,29},{6,30},{7,31}} | collective-permute-start | bytes 798728 | tf_op jit(solution)/shard_map/ppermute | solution.py:443
  34.7 36.9 %collective-permute-start.2 = (f32[512,256]{1,0:T(8,128)}, f32[512,256]{1,0:T(8,128)}, u32[]{:S(2)}, u32[]{:S(2)}) collective-permute-start(f32[512,256]{1,0:T(8,128)} %broadcast_select_fusion), channel_id=1, source_target_pairs={{12,14},{13,15},{20,22},{21,23},{30,28},{31,29}} | collective-permute-start | bytes 1572872 | tf_op jit(solution)/shard_map/ppermute | solution.py:443
  36.2 27.7 %collective-permute-start.12 = (f32[520,128]{1,0:T(8,128)S(1)}, f32[520,128]{1,0:T(8,128)S(1)}, u32[]{:S(2)}, u32[]{:S(2)}) collective-permute-start(f32[520,128]{1,0:T(8,128)S(1)} %get-tuple-element.19), channel_id=1, source_target_pairs={{0,16},{1,17},{2,18},{3,19},{4,20},{5,21},{6,22},{7,23}} | collective-permute-start | bytes 798728 | tf_op jit(solution)/shard_map/ppermute | solution.py:443
  36.9 32.8 %collective-permute-start.11 = (f32[520,128]{1,0:T(8,128)S(1)}, f32[520,128]{1,0:T(8,128)}, u32[]{:S(2)}, u32[]{:S(2)}) collective-permute-start(f32[520,128]{1,0:T(8,128)S(1)} %get-tuple-element.19), channel_id=1, source_target_pairs={{0,8},{1,9},{2,10},{3,11},{4,12},{5,13},{6,14},{7,15}} | collective-permute-start | bytes 798728 | tf_op jit(solution)/shard_map/ppermute | solution.py:443
  38.2 52.3 %all-to-all-start = ((f32[8,136,128]{2,1,0:T(8,128)}), f32[8,136,128]{2,1,0:T(8,128)S(1)}, u32[]{:S(2)}, u32[]{:S(2)}) async-start(f32[8,136,128]{2,1,0:T(8,128)} %get-tuple-element.15), calls=%async_computation | async-start | bytes 1114112 | tf_op jit(solution)/shard_map/all_to_all | solution.py:490
  45.2 45.2 %collective-permute-start.10 = (f32[256,512]{1,0:T(8,128)}, f32[256,512]{1,0:T(8,128)}, u32[]{:S(2)}, u32[]{:S(2)}) collective-permute-start(f32[256,512]{1,0:T(8,128)} %get-tuple-element.18.matched), channel_id=1, source_target_pairs={{10,18},{11,19},{20,12},{21,13},{30,6},{31,7}} | collective-permute-start | bytes 1572872 | tf_op jit(solution)/shard_map/ppermute | solution.py:443
  49.1 41.4 %collective-permute-start.9 = (f32[256,512]{1,0:T(8,128)}, f32[256,512]{1,0:T(8,128)}, u32[]{:S(2)}, u32[]{:S(2)}) collective-permute-start(f32[256,512]{1,0:T(8,128)} %get-tuple-element.18.matched), channel_id=1, source_target_pairs={{10,26},{11,27},{20,4},{21,5},{30,14},{31,15}} | collective-permute-start | bytes 1572872 | tf_op jit(solution)/shard_map/ppermute | solution.py:443
  63.8 26.6 %collective-permute-start.8 = (f32[256,512]{1,0:T(8,128)}, f32[256,512]{1,0:T(8,128)}, u32[]{:S(2)}, u32[]{:S(2)}) collective-permute-start(f32[256,512]{1,0:T(8,128)} %get-tuple-element.18.matched), channel_id=1, source_target_pairs={{10,2},{11,3},{20,28},{21,29},{30,22},{31,23}} | collective-permute-start | bytes 1572872 | tf_op jit(solution)/shard_map/ppermute | solution.py:443
  70.7 2.3 %collective-permute-start.14 = (f32[520,128]{1,0:T(8,128)S(1)}, f32[520,128]{1,0:T(8,128)S(1)}, u32[]{:S(2)}, u32[]{:S(2)}) collective-permute-start(f32[520,128]{1,0:T(8,128)S(1)} %add_select_fusion.here), channel_id=1, source_target_pairs={{0,1},{1,0},{2,3},{3,2},{4,5},{5,4},{6,7},{7,6},{8,9},{9,8},{10,11... | collective-permute-start | bytes 798728 | tf_op jit(solution)/shard_map/ppermute | solution.py:443
  72.9 17.6 %collective-permute-start.3 = (f32[512,256]{1,0:T(8,128)S(1)}, f32[512,256]{1,0:T(8,128)S(1)}, u32[]{:S(2)}, u32[]{:S(2)}) collective-permute-start(f32[512,256]{1,0:T(8,128)S(1)} %select_select_fusion.piece), channel_id=1, source_target_pairs={{0,1},{1,0},{2,3},{3,2},{4,5},{5,4},{6,7},{7,6},{8,9},{9,8},{10,11... | collective-permute-start | bytes 1572872 | tf_op jit(solution)/shard_map/ppermute | solution.py:443
  81.0 0.7 copy-start.5
  89.7 0.7 copy-start.7
  90.5 1.0 copy-start.6
  91.5 0.9 copy-start.8

commit v4 on v3

--- a/solution.py
+++ b/solution.py
@@ -193,13 +193,12 @@
 
 
 def add_band_blocks(ref, blocks, width):
-    for b in blocks:
-        tile = b.shape[2]
-        for i in range(b.shape[0]):
-            for owner in range(2):
-                tag = b[i, 2 * tile + 8 * owner : 2 * tile + 8 * owner + 8, :]
-                block = b[i, owner * tile : (owner + 1) * tile, :]
-                add_block(ref, block, place_of(tag), tile, owner * width)
+    tile = blocks.shape[2]
+    for i in range(blocks.shape[0]):
+        for owner in range(2):
+            tag = blocks[i, 2 * tile + 8 * owner : 2 * tile + 8 * owner + 8, :]
+            block = blocks[i, owner * tile : (owner + 1) * tile, :]
+            add_block(ref, block, place_of(tag), tile, owner * width)
 
 
 def square_ids(n):
@@ -260,7 +259,7 @@
         put_rows(diag_ref, width + 8, front[:width, tile:].T)
 
 
-def rows_kernel(info, front, turned, diag, d1, d2, d3, here, there, diag_ref, out_ref, band, part):
+def rows_kernel(info, front, turned, diag, d1, d2, d3, blocks, diag_ref, out_ref, band, part):
     width = front.shape[1]
     tile = width // 2
     group, layer, core = info[0], info[1], info[2]
@@ -268,7 +267,7 @@
     @pl.when((group == 0) | (group == layer))
     def _():
         band[...] = jnp.zeros_like(band)
-        add_band_blocks(band, (here, there), width)
+        add_band_blocks(band, blocks, width)
 
     @pl.when(group == 0)
     def _():
@@ -329,7 +328,7 @@
 
 
 def middle_kernel(
-    info, shard, arrived, piece, piece2, matched, m1, m2, m3, w, lower, here, there, out_ref, q_ref, n_ref, band, line
+    info, shard, arrived, piece, piece2, matched, m1, m2, m3, w, lower, blocks, out_ref, q_ref, n_ref, band, line
 ):
     tile = arrived.shape[2]
     nrows, width = shard.shape
@@ -363,7 +362,7 @@
         def _(c=c, p=swapped):
             band[:, c * width : (c + 1) * width] = p[...]
 
-    add_band_blocks(band, (here, there), width)
+    add_band_blocks(band, blocks, width)
 
     @pl.when(column == 0)
     def _():
@@ -460,15 +459,16 @@
     near = send(
         front, [(dev(g, 0, c), dev(g, z, c)) for g, z in ((1, 2), (2, 1), (3, 1)) for c in both]
     )
-    here = lax.all_gather(
-        payload, "front", axis_index_groups=[[2 * z + c for z in layers] for c in both]
-    )
-    there = send(here, swap)
+    blocks = lax.all_gather(payload, "front")
+    arrived = lax.all_to_all(outgoing, "front", split_axis=0, concat_axis=0, tiled=True)
+    blocks, turned, near, arrived, *diags = lax.optimization_barrier(
+        (blocks, turned, near, arrived, *diags)
+    )
 
     diag, matched = kernel(
         rows_kernel,
         (packed, out(width, 2 * width)),
-        (info, front, turned, diag, *diags, here, there),
+        (info, front, turned, diag, *diags, blocks),
         scratch=[(nrows, 2 * width), packed.shape],
     )
     got = [
@@ -478,16 +478,16 @@
         send(matched, [(dev(z, z, c), dev(z ^ s, z, c)) for z in layers[1:] for c in both])
         for s in groups[1:]
     ]
-    diag = jnp.where(group == 0, diag, got[0] + got[1] + got[2])
-    diag2 = send(diag, swap)
-
     far = send(
         jnp.where(group == layer, turned, near),
         [(dev(g, z, c), dev(g, 5 - z, c)) for g, z in ((1, 2), (2, 2), (3, 3)) for c in both],
     )
+    diag = jnp.where(group == 0, diag, got[0] + got[1] + got[2])
+    diag2 = send(diag, swap)
+    diag, diag2, far = lax.optimization_barrier((diag, diag2, far))
+
     piece = jnp.where(layer == 0, front, jnp.where(group == layer, turned, near + far))
     piece2 = send(piece, swap)
-    arrived = lax.all_to_all(outgoing, "front", split_axis=0, concat_axis=0, tiled=True)
 
     square = out(width, width)
     w1, l21 = kernel(
@@ -497,7 +497,7 @@
     out1, q, n = kernel(
         middle_kernel,
         (out(nrows, width), out(nrows, width), square),
-        (info, front, arrived, piece, piece2, matched, *away, w1, l21, here, there),
+        (info, front, arrived, piece, piece2, matched, *away, w1, l21, blocks),
         scratch=[(nrows, 2 * width), (width, 2 * width)],
         flops=1 << 31,
     )

time: 101 us -> 111 us (1.099)
  waiting for transfers between devices: 0.04 us -> 43.6 us
  starting transfers between devices: 45.7 us -> 19.7 us
  blocking collectives: 17.7 us -> 0 us
  between operations: 0.22 us -> 13.6 us
  Pallas kernels: 27.5 us -> 25.8 us
  local copies, waits for them, and re-layouts: 6.2 us -> 4.65 us
    ppermute x15 -> x14, waiting for transfers between devices: 0.04 us -> 26.7 us  [send(): return lax.ppermute(x, AXES, pairs)]
    ppermute x15 -> x14, starting transfers between devices: 38.6 us -> 14 us  [send(): return lax.ppermute(x, AXES, pairs)]
    all_gather x1 -> x0, blocking collectives: 17.7 us -> none  [aligned(): lax.all_gather(payload, 'front', axis_index_groups=[[2 * z + c for z in l...]
    all_to_all x1, waiting for transfers between devices: 0.01 us -> 16.9 us  [aligned(): lax.all_to_all(outgoing, 'front', split_axis=0, concat_axis=0, tiled=True)]
    pallas_call x6, Pallas kernels: 27.5 us -> 25.8 us  [kernel(): pl.pallas_call(body, out_shape=outs, in_specs=spec, scratch_shapes=[pltpu...]
    unnamed x18, local copies, waits for them, and re-layouts: 6.12 us -> 4.57 us
    all_to_all x1, starting transfers between devices: 7.09 us -> 5.65 us  [aligned(): lax.all_to_all(outgoing, 'front', split_axis=0, concat_axis=0, tiled=True)]
  transfers between devices with their start and end apart: 16 -> 16, of which waited for: 0 -> 4; matrix products, arithmetic and copies ran while one was open for 3% -> 3% of each run, Pallas kernels for 17% -> 14%
where the time goes in v4:
time: 111 us
  waiting for transfers between devices  43.6 us (39%)
  Pallas kernels  25.8 us (23%)
  starting transfers between devices  19.7 us (18%)
  between operations  13.6 us (12%)
  local copies, waits for them, and re-layouts  4.65 us (4%)
  other arithmetic  3.26 us (3%)
    ppermute x14, waiting for transfers between devices, send(): return lax.ppermute(x, AXES, pairs)  26.7 us
    pallas_call x6, Pallas kernels, kernel(): pl.pallas_call(body, out_shape=outs, in_specs=spec, scratch_shapes=[pltpu...  25.8 us
    all_to_all x1, waiting for transfers between devices, aligned(): lax.all_to_all(outgoing, 'front', split_axis=0, concat_axis=0, tiled=True)  16.9 us
    ppermute x14, starting transfers between devices, send(): return lax.ppermute(x, AXES, pairs)  14 us
    all_to_all x1, starting transfers between devices, aligned(): lax.all_to_all(outgoing, 'front', split_axis=0, concat_axis=0, tiled=True)  5.65 us
    unnamed x18, local copies, waits for them, and re-layouts  4.57 us
  transfers between devices with their start and end apart: 16, of which 4 were waited for; matrix products, arithmetic and copies ran while one was open for 3% of the time, Pallas kernels for 14%

profile of v4, /device:TPU:11, one launch (start us, length us, event | category | flops | bytes accessed | tf_op | source)
XLA Modules:
  0.0 110.6 jit_solution(11966890042046240128)
XLA Ops:
  6.6 1.0 copy-done
  7.7 0.9 copy-done.4
  8.6 0.7 copy-done.5
  9.3 0.7 copy-done.6
  9.9 1.5 %shard_map.46 = (f32[8,136,128]{2,1,0:T(8,128)}, f32[272,128]{1,0:T(8,128)}, f32[520,128]{1,0:T(8,128)S(1)}) custom-call(s32[4]{0:T(128)S(1)} %copy-done.5, s32[4]{0:T(128)S(1)} %copy-done.6, s32[5]{0:T(128)S(1)} %stack.23.info, f32[4,128,128]{2,1,0:T(8,128)S(1)} %copy-done.4, f32[512,256]{1,0:T(8,128)S(1)} %copy-done), custom_call_target="tpu_custom_call" | custom-call | flops 1048576 | bytes 1048576 | tf_op jit(solution)/shard_map/pallas_call | solution.py:419
  11.4 5.6 %all-to-all-start = ((f32[8,136,128]{2,1,0:T(8,128)}), f32[8,136,128]{2,1,0:T(8,128)S(1)}, u32[]{:S(2)}, u32[]{:S(2)}) async-start(f32[8,136,128]{2,1,0:T(8,128)} %get-tuple-element.26), calls=%async_computation | async-start | bytes 1114112 | tf_op jit(solution)/shard_map/all_to_all | solution.py:463
  17.1 0.7 collective-permute-start.1
  17.8 1.3 %collective-permute-start = (f32[512,256]{1,0:T(8,128)S(1)}, f32[512,256]{1,0:T(8,128)S(1)}, u32[]{:S(2)}, u32[]{:S(2)}) collective-permute-start(f32[512,256]{1,0:T(8,128)S(1)} %copy-done.1), channel_id=1, source_target_pairs={{2,10},{3,11},{4,20},{5,21},{6,30},{7,31}} | collective-permute-start | bytes 1572872 | tf_op jit(solution)/shard_map/ppermute | solution.py:442
  19.1 0.7 collective-permute-start.4
  19.8 0.7 collective-permute-start.3
  20.4 0.7 collective-permute-start.2
  21.2 11.7 %collective-permute-done.turned = f32[512,256]{1,0:T(8,128)S(1)} collective-permute-done((f32[512,256]{1,0:T(8,128)S(1)}, f32[512,256]{1,0:T(8,128)S(1)}, u32[]{:S(2)}, u32[]{:S(2)}) %collective-permute-start) | collective-permute-done | bytes 524320 | tf_op jit(solution)/shard_map/ppermute | solution.py:442
  32.9 16.9 %all-to-all-done.arrived = f32[8,136,128]{2,1,0:T(8,128)S(1)} async-done(((f32[8,136,128]{2,1,0:T(8,128)}), f32[8,136,128]{2,1,0:T(8,128)S(1)}, u32[]{:S(2)}, u32[]{:S(2)}) %all-to-all-start) | async-done | bytes 557088 | tf_op jit(solution)/shard_map/all_to_all | solution.py:463
  49.8 1.2 %copy-done.2 = f32[2176,128]{1,0:T(8,128)S(1)} copy-done((f32[2176,128]{1,0:T(8,128)S(1)}, f32[2176,128]{1,0:T(8,128)}, u32[]{:S(2)}) %copy-start.2) | copy-done | bytes 1114136
  51.0 1.1 shard_map.47
  52.1 0.7 collective-permute-start.7
  52.8 1.4 %collective-permute-start.6 = (f32[520,128]{1,0:T(8,128)S(1)}, f32[520,128]{1,0:T(8,128)}, u32[]{:S(2)}, u32[]{:S(2)}) collective-permute-start(f32[520,128]{1,0:T(8,128)S(1)} %get-tuple-element.35), channel_id=1, source_target_pairs={{0,16},{1,17},{2,18},{3,19},{4,20},{5,21},{6,22},{7,23}} | collective-permute-start | bytes 798728 | tf_op jit(solution)/shard_map/ppermute | solution.py:442
  54.2 1.3 %collective-permute-start.5 = (f32[520,128]{1,0:T(8,128)S(1)}, f32[520,128]{1,0:T(8,128)}, u32[]{:S(2)}, u32[]{:S(2)}) collective-permute-start(f32[520,128]{1,0:T(8,128)S(1)} %get-tuple-element.35), channel_id=1, source_target_pairs={{0,8},{1,9},{2,10},{3,11},{4,12},{5,13},{6,14},{7,15}} | collective-permute-start | bytes 798728 | tf_op jit(solution)/shard_map/ppermute | solution.py:442
  55.5 0.9 broadcast_select_fusion
  56.4 1.5 %collective-permute-start.9 = (f32[512,256]{1,0:T(8,128)}, f32[512,256]{1,0:T(8,128)}, u32[]{:S(2)}, u32[]{:S(2)}) collective-permute-start(f32[512,256]{1,0:T(8,128)} %broadcast_select_fusion), channel_id=1, source_target_pairs={{12,14},{13,15},{20,22},{21,23},{30,28},{31,29}} | collective-permute-start | bytes 1572872 | tf_op jit(solution)/shard_map/ppermute | solution.py:442
  57.8 12.3 %collective-permute-done.5 = f32[520,128]{1,0:T(8,128)} collective-permute-done((f32[520,128]{1,0:T(8,128)S(1)}, f32[520,128]{1,0:T(8,128)}, u32[]{:S(2)}, u32[]{:S(2)}) %collective-permute-start.5) | collective-permute-done | bytes 266272 | tf_op jit(solution)/shard_map/ppermute | solution.py:442
  70.2 1.1 %add_select_fusion.here = f32[520,128]{1,0:T(8,128)S(1)} fusion(f32[520,128]{1,0:T(8,128)S(1)} %get-tuple-element.35, f32[520,128]{1,0:T(8,128)S(1)} %collective-permute-done.7, f32[520,128]{1,0:T(8,128)} %collective-permute-done.5, f32[520,128]{1,0:T(8,128)} %collective-permute-done.6, pred[]{:T(512)S(6)} %eq.14), kind=kLoop, calls=%fused_computation.1 | loop fusion | flops 199680 | bytes 1331201 | tf_op jit(solution)/shard_map/jit(_where)/select_n | solution.py:485
  71.3 1.2 %collective-permute-start.8 = (f32[520,128]{1,0:T(8,128)S(1)}, f32[520,128]{1,0:T(8,128)S(1)}, u32[]{:S(2)}, u32[]{:S(2)}) collective-permute-start(f32[520,128]{1,0:T(8,128)S(1)} %add_select_fusion.here), channel_id=1, source_target_pairs={{0,1},{1,0},{2,3},{3,2},{4,5},{5,4},{6,7},{7,6},{8,9},{9,8},{10,11... | collective-permute-start | bytes 798728 | tf_op jit(solution)/shard_map/ppermute | solution.py:442
  72.5 1.3 %collective-permute-start.13 = (f32[256,512]{1,0:T(8,128)S(1)}, f32[256,512]{1,0:T(8,128)S(1)}, u32[]{:S(2)}, u32[]{:S(2)}) collective-permute-start(f32[256,512]{1,0:T(8,128)S(1)} %get-tuple-element.37.matched), channel_id=1, source_target_pairs={{10,18},{11,19},{20,12},{21,13},{30,6},{31,7}} | collective-permute-start | bytes 1572872 | tf_op jit(solution)/shard_map/ppermute | solution.py:442
  73.8 1.3 %collective-permute-start.12 = (f32[256,512]{1,0:T(8,128)S(1)}, f32[256,512]{1,0:T(8,128)S(1)}, u32[]{:S(2)}, u32[]{:S(2)}) collective-permute-start(f32[256,512]{1,0:T(8,128)S(1)} %get-tuple-element.37.matched), channel_id=1, source_target_pairs={{10,26},{11,27},{20,4},{21,5},{30,14},{31,15}} | collective-permute-start | bytes 1572872 | tf_op jit(solution)/shard_map/ppermute | solution.py:442
  75.1 1.3 %collective-permute-start.11 = (f32[256,512]{1,0:T(8,128)S(1)}, f32[256,512]{1,0:T(8,128)S(1)}, u32[]{:S(2)}, u32[]{:S(2)}) collective-permute-start(f32[256,512]{1,0:T(8,128)S(1)} %get-tuple-element.37.matched), channel_id=1, source_target_pairs={{10,2},{11,3},{20,28},{21,29},{30,22},{31,23}} | collective-permute-start | bytes 1572872 | tf_op jit(solution)/shard_map/ppermute | solution.py:442
  76.5 1.3 %select_select_fusion.piece = f32[512,256]{1,0:T(8,128)S(1)} fusion(f32[512,256]{1,0:T(8,128)S(1)} %copy-done.1, f32[512,256]{1,0:T(8,128)S(1)} %collective-permute-done.turned, f32[512,256]{1,0:T(8,128)S(1)} %copy-done.8, f32[512,256]{1,0:T(8,128)} %collective-permute-done.9, pred[]{:T(512)S(6)} %eq.13, pred[]{:T(512)S(6)} %eq.12), kind=kLoop, calls=%fused_computation | loop fusion | flops 393216 | bytes 2621442 | tf_op jit(solution)/shard_map/jit(_where)/select_n | solution.py:489
  77.8 8.0 %shard_map.48 = (f32[256,256]{1,0:T(8,128)S(1)}, f32[256,256]{1,0:T(8,128)S(1)}) custom-call(s32[5]{0:T(128)S(1)} %stack.23.info, f32[520,128]{1,0:T(8,128)S(1)} %add_select_fusion.here, f32[520,128]{1,0:T(8,128)S(1)} %collective-permute-done.8.there), custom_call_target="tpu_custom_call" | custom-call | flops 4294967296 | bytes 1048576 | tf_op jit(solution)/shard_map/pallas_call | solution.py:419
  85.9 8.0 %shard_map.50.w = f32[256,256]{1,0:T(8,128)S(1)} custom-call(s32[5]{0:T(128)S(1)} %stack.23.info, f32[520,128]{1,0:T(8,128)S(1)} %add_select_fusion.here, f32[520,128]{1,0:T(8,128)S(1)} %collective-permute-done.8.there, f32[256,256]{1,0:T(8,128)S(1)} %get-tuple-element.41.lower), custom_call_target="tpu_custom_call" | custom-call | flops 4294967296 | bytes 1048576 | tf_op jit(solution)/shard_map/pallas_call | solution.py:419
  93.9 2.6 %collective-permute-done.11.m1 = f32[256,512]{1,0:T(8,128)S(1)} collective-permute-done((f32[256,512]{1,0:T(8,128)S(1)}, f32[256,512]{1,0:T(8,128)S(1)}, u32[]{:S(2)}, u32[]{:S(2)}) %collective-permute-start.11) | collective-permute-done | bytes 524320 | tf_op jit(solution)/shard_map/ppermute | solution.py:442
  96.5 4.0 %shard_map.49 = (f32[512,256]{1,0:T(8,128)S(1)}, f32[512,256]{1,0:T(8,128)S(1)}, f32[256,256]{1,0:T(8,128)S(1)}) custom-call(s32[5]{0:T(128)S(1)} %stack.23.info, f32[512,256]{1,0:T(8,128)S(1)} %copy-done.1, f32[8,136,128]{2,1,0:T(8,128)S(1)} %all-to-all-done.arrived, f32[512,256]{1,0:T(8,128)S(1)} %select_select_fusion.piece, ...), custom_call_target="tpu_custom_call" | custom-call | flops 2147483648 | bytes 1048576 | tf_op jit(solution)/shard_map/pallas_call | solution.py:419
  100.5 3.2 %shard_map.51 = f32[512,256]{1,0:T(8,128)} custom-call(s32[5]{0:T(128)S(1)} %stack.23.info, f32[512,256]{1,0:T(8,128)S(1)} %get-tuple-element.42.out1, f32[512,256]{1,0:T(8,128)S(1)} %get-tuple-element.43.q, f32[256,256]{1,0:T(8,128)S(1)} %get-tuple-element.44.n, f32[256,256]{1,0:T(8,128)S(1)} %shard_map.50.w), custom_call_target="tpu_custom_call" | custom-call | flops 1073741824 | bytes 1048576 | tf_op jit(solution)/shard_map/pallas_call | solution.py:419
  (29 shorter events, 0.3 us)
Async XLA Ops:
  6.5 43.2 %all-gather.3.cloned.1.call-start = ((), (), s32[]{:S(2)}) async-start(), calls=%async_computation.1 | async-start | bytes 1253376 | tf_op jit(solution)/shard_map/all_gather | solution.py:462
  6.6 1.0 copy-start
  7.7 0.9 copy-start.4
  8.6 0.7 copy-start.5
  9.3 0.7 copy-start.6
  9.9 7.2 %copy-start.1 = (f32[512,256]{1,0:T(8,128)S(1)}, f32[512,256]{1,0:T(8,128)}, u32[]{:S(2)}) copy-start(f32[512,256]{1,0:T(8,128)} %shard.1) | copy-start | bytes 1572868
  11.4 38.3 %all-to-all-start = ((f32[8,136,128]{2,1,0:T(8,128)}), f32[8,136,128]{2,1,0:T(8,128)S(1)}, u32[]{:S(2)}, u32[]{:S(2)}) async-start(f32[8,136,128]{2,1,0:T(8,128)} %get-tuple-element.26), calls=%async_computation | async-start | bytes 1114112 | tf_op jit(solution)/shard_map/all_to_all | solution.py:463
  17.1 4.1 %collective-permute-start.1 = (f32[512,256]{1,0:T(8,128)S(1)}, f32[512,256]{1,0:T(8,128)S(1)}, u32[]{:S(2)}, u32[]{:S(2)}) collective-permute-start(f32[512,256]{1,0:T(8,128)S(1)} %copy-done.1), channel_id=1, source_target_pairs={{8,12},{9,13},{16,18},{17,19},{24,26},{25,27}} | collective-permute-start | bytes 1572872 | tf_op jit(solution)/shard_map/ppermute | solution.py:442
  17.8 15.1 %collective-permute-start = (f32[512,256]{1,0:T(8,128)S(1)}, f32[512,256]{1,0:T(8,128)S(1)}, u32[]{:S(2)}, u32[]{:S(2)}) collective-permute-start(f32[512,256]{1,0:T(8,128)S(1)} %copy-done.1), channel_id=1, source_target_pairs={{2,10},{3,11},{4,20},{5,21},{6,30},{7,31}} | collective-permute-start | bytes 1572872 | tf_op jit(solution)/shard_map/ppermute | solution.py:442
  19.1 2.1 %collective-permute-start.4 = (f32[520,128]{1,0:T(8,128)S(1)}, f32[520,128]{1,0:T(8,128)S(1)}, u32[]{:S(2)}, u32[]{:S(2)}) collective-permute-start(f32[520,128]{1,0:T(8,128)S(1)} %get-tuple-element.27.diag), channel_id=1, source_target_pairs={{0,6},{1,7}} | collective-permute-start | bytes 798728 | tf_op jit(solution)/shard_map/ppermute | solution.py:442
  19.8 1.4 %collective-permute-start.3 = (f32[520,128]{1,0:T(8,128)S(1)}, f32[520,128]{1,0:T(8,128)S(1)}, u32[]{:S(2)}, u32[]{:S(2)}) collective-permute-start(f32[520,128]{1,0:T(8,128)S(1)} %get-tuple-element.27.diag), channel_id=1, source_target_pairs={{0,4},{1,5}} | collective-permute-start | bytes 798728 | tf_op jit(solution)/shard_map/ppermute | solution.py:442
  20.4 0.7 collective-permute-start.2
  21.2 28.6 %copy-start.7 = (f32[512,256]{1,0:T(8,128)}, f32[512,256]{1,0:T(8,128)S(1)}, u32[]{:S(2)}) copy-start(f32[512,256]{1,0:T(8,128)S(1)} %collective-permute-done.1) | copy-start | bytes 1572868
  49.8 1.2 %copy-start.2 = (f32[2176,128]{1,0:T(8,128)S(1)}, f32[2176,128]{1,0:T(8,128)}, u32[]{:S(2)}) copy-start(f32[2176,128]{1,0:T(8,128)} %all-gather.3.cloned.1.call-done) | copy-start | bytes 3342340
  52.1 5.7 %collective-permute-start.7 = (f32[520,128]{1,0:T(8,128)S(1)}, f32[520,128]{1,0:T(8,128)S(1)}, u32[]{:S(2)}, u32[]{:S(2)}) collective-permute-start(f32[520,128]{1,0:T(8,128)S(1)} %get-tuple-element.35), channel_id=1, source_target_pairs={{0,24},{1,25},{2,26},{3,27},{4,28},{5,29},{6,30},{7,31}} | collective-permute-start | bytes 798728 | tf_op jit(solution)/shard_map/ppermute | solution.py:442
  52.8 5.0 %collective-permute-start.6 = (f32[520,128]{1,0:T(8,128)S(1)}, f32[520,128]{1,0:T(8,128)}, u32[]{:S(2)}, u32[]{:S(2)}) collective-permute-start(f32[520,128]{1,0:T(8,128)S(1)} %get-tuple-element.35), channel_id=1, source_target_pairs={{0,16},{1,17},{2,18},{3,19},{4,20},{5,21},{6,22},{7,23}} | collective-permute-start | bytes 798728 | tf_op jit(solution)/shard_map/ppermute | solution.py:442
  54.2 16.0 %collective-permute-start.5 = (f32[520,128]{1,0:T(8,128)S(1)}, f32[520,128]{1,0:T(8,128)}, u32[]{:S(2)}, u32[]{:S(2)}) collective-permute-start(f32[520,128]{1,0:T(8,128)S(1)} %get-tuple-element.35), channel_id=1, source_target_pairs={{0,8},{1,9},{2,10},{3,11},{4,12},{5,13},{6,14},{7,15}} | collective-permute-start | bytes 798728 | tf_op jit(solution)/shard_map/ppermute | solution.py:442
  55.5 21.0 %copy-start.8 = (f32[512,256]{1,0:T(8,128)S(1)}, f32[512,256]{1,0:T(8,128)}, u32[]{:S(2)}) copy-start(f32[512,256]{1,0:T(8,128)} %copy-done.7) | copy-start | bytes 1572868
  56.4 20.1 %collective-permute-start.9 = (f32[512,256]{1,0:T(8,128)}, f32[512,256]{1,0:T(8,128)}, u32[]{:S(2)}, u32[]{:S(2)}) collective-permute-start(f32[512,256]{1,0:T(8,128)} %broadcast_select_fusion), channel_id=1, source_target_pairs={{12,14},{13,15},{20,22},{21,23},{30,28},{31,29}} | collective-permute-start | bytes 1572872 | tf_op jit(solution)/shard_map/ppermute | solution.py:442
  71.3 5.2 %collective-permute-start.8 = (f32[520,128]{1,0:T(8,128)S(1)}, f32[520,128]{1,0:T(8,128)S(1)}, u32[]{:S(2)}, u32[]{:S(2)}) collective-permute-start(f32[520,128]{1,0:T(8,128)S(1)} %add_select_fusion.here), channel_id=1, source_target_pairs={{0,1},{1,0},{2,3},{3,2},{4,5},{5,4},{6,7},{7,6},{8,9},{9,8},{10,11... | collective-permute-start | bytes 798728 | tf_op jit(solution)/shard_map/ppermute | solution.py:442
  72.5 21.4 %collective-permute-start.13 = (f32[256,512]{1,0:T(8,128)S(1)}, f32[256,512]{1,0:T(8,128)S(1)}, u32[]{:S(2)}, u32[]{:S(2)}) collective-permute-start(f32[256,512]{1,0:T(8,128)S(1)} %get-tuple-element.37.matched), channel_id=1, source_target_pairs={{10,18},{11,19},{20,12},{21,13},{30,6},{31,7}} | collective-permute-start | bytes 1572872 | tf_op jit(solution)/shard_map/ppermute | solution.py:442
  73.8 20.1 %collective-permute-start.12 = (f32[256,512]{1,0:T(8,128)S(1)}, f32[256,512]{1,0:T(8,128)S(1)}, u32[]{:S(2)}, u32[]{:S(2)}) collective-permute-start(f32[256,512]{1,0:T(8,128)S(1)} %get-tuple-element.37.matched), channel_id=1, source_target_pairs={{10,26},{11,27},{20,4},{21,5},{30,14},{31,15}} | collective-permute-start | bytes 1572872 | tf_op jit(solution)/shard_map/ppermute | solution.py:442
  75.1 21.4 %collective-permute-start.11 = (f32[256,512]{1,0:T(8,128)S(1)}, f32[256,512]{1,0:T(8,128)S(1)}, u32[]{:S(2)}, u32[]{:S(2)}) collective-permute-start(f32[256,512]{1,0:T(8,128)S(1)} %get-tuple-element.37.matched), channel_id=1, source_target_pairs={{10,2},{11,3},{20,28},{21,29},{30,22},{31,23}} | collective-permute-start | bytes 1572872 | tf_op jit(solution)/shard_map/ppermute | solution.py:442
  77.7 18.8 %collective-permute-start.10 = (f32[512,256]{1,0:T(8,128)S(1)}, f32[512,256]{1,0:T(8,128)S(1)}, u32[]{:S(2)}, u32[]{:S(2)}) collective-permute-start(f32[512,256]{1,0:T(8,128)S(1)} %select_select_fusion.piece), channel_id=1, source_target_pairs={{0,1},{1,0},{2,3},{3,2},{4,5},{5,4},{6,7},{7,6},{8,9},{9,8},{10,11... | collective-permute-start | bytes 1572872 | tf_op jit(solution)/shard_map/ppermute | solution.py:442
  85.9 10.6 %copy-start.3 = (f32[2176,128]{1,0:T(8,128)S(1)}, f32[2176,128]{1,0:T(8,128)}, u32[]{:S(2)}) copy-start(f32[2176,128]{1,0:T(8,128)} %all-gather.3.cloned.1.call-done) | copy-start | bytes 3342340
Sparse Core Ops, SparseCore 0:
  11.6 38.0 all-gather.2

commit v5 on v4

--- a/solution.py
+++ b/solution.py
@@ -295,7 +295,7 @@
         out_ref[...] = turned[...].T + band[pl.ds(start, width), :]
 
 
-def first_kernel(info, here, there, w_ref, l_ref, top, bottom):
+def factor_kernel(info, here, there, w_ref, l_ref, v_ref, top, bottom):
     tile = here.shape[1]
     width = 2 * tile
 
@@ -313,22 +313,12 @@
     w = w_ref[...]
     l_ref[:tile, :] = dot_t(get_rows(top, width + 8), w)
     l_ref[tile:, :] = dot_t(get_rows(bottom, width + 8), w)
-
-
-def second_kernel(info, here, there, lower, w_ref, bottom):
-    @pl.when(info[2] == 0)
-    def _():
-        bottom[...] = there[...]
-
-    @pl.when(info[2] == 1)
-    def _():
-        bottom[...] = here[...]
-
-    store_inverse(w_ref, factor_pair(unpack(bottom) - dot_t(lower[...], lower[...])))
-
-
-def middle_kernel(
-    info, shard, arrived, piece, piece2, matched, m1, m2, m3, w, lower, blocks, out_ref, q_ref, n_ref, band, line
+    lower = l_ref[...]
+    store_inverse(v_ref, factor_pair(unpack(bottom) - dot_t(lower, lower)))
+
+
+def last_kernel(
+    info, shard, arrived, piece, piece2, matched, m1, m2, m3, w, lower, v, blocks, out_ref, band, line, work
 ):
     tile = arrived.shape[2]
     nrows, width = shard.shape
@@ -343,7 +333,7 @@
             line[...] = m[...]
 
     w1, l21 = w[...], lower[...]
-    by_rows = ((group >= 2) & (layer >= 2)) | (group == layer)
+    by_rows = (layer > 0) & (((group == 1) & (layer < 3)) | ((group > 1) & (layer > 1)))
     for c, (same, swapped) in enumerate(((piece, piece2), (piece2, piece))):
 
         @pl.when(by_rows & (core == 0))
@@ -362,55 +352,42 @@
         def _(c=c, p=swapped):
             band[:, c * width : (c + 1) * width] = p[...]
 
-    add_band_blocks(band, blocks, width)
+    @pl.when(group > 0)
+    def _():
+        add_band_blocks(band, blocks, width)
 
     @pl.when(column == 0)
     def _():
         out_ref[...] = dot_t(out_ref[...], w1)
-        q_ref[...] = jnp.zeros_like(q_ref)
-        n_ref[...] = jnp.zeros_like(n_ref)
 
     @pl.when(column > 0)
     def _():
         @pl.when(group == 0)
         def _():
-            q_ref[:width, :] = jnp.zeros((width, width), F32)
-            q_ref[width:, :] = l21
+            work[:width, :] = jnp.zeros((width, width), F32)
+            work[width:, :] = l21
 
         @pl.when(group > 0)
         def _():
-            q_ref[...] = dot_t(band[:, :width], w1)
+            work[...] = dot_t(band[:, :width], w1)
+
+        first = work[...]
 
         @pl.when(column == 1)
         def _():
-            q_ref[...] = out_ref[...] - dot_t(q_ref[...], l21)
-            n_ref[...] = jnp.zeros_like(n_ref)
+            rows = group * nrows + lax.broadcasted_iota(jnp.int32, (nrows, width), 0)
+            own = out_ref[...]
+            out_ref[...] = jnp.where(rows >= width, dot_t(own - dot_t(first, l21), v[...]), own)
 
         @pl.when(column > 1)
         def _():
             mine = dot_t(line[:, :width], w1)
-            n_ref[...] = line[:, width:] - dot_t(mine, l21)
-            out_ref[...] = out_ref[...] - dot_t(q_ref[...], mine)
-            q_ref[...] = band[:, width:] - dot_t(q_ref[...], l21)
-
-
-def last_kernel(info, out1, q, n, w, out_ref):
-    nrows, width = out1.shape
-    group, column = info[0], info[4]
-
-    @pl.when((column == 0) | ((column > 1) & (group == 0)))
-    def _():
-        out_ref[...] = out1[...]
-
-    @pl.when(column == 1)
-    def _():
-        rows = group * nrows + lax.broadcasted_iota(jnp.int32, (nrows, width), 0)
-        out_ref[...] = jnp.where(rows >= width, dot_t(q[...], w[...]), out1[...])
-
-    @pl.when((column > 1) & (group > 0))
-    def _():
-        second = dot_t(q[...], w[...])
-        out_ref[...] = out1[...] - dot_t(second, dot_t(n[...], w[...]))
+            out_ref[...] -= dot_t(first, mine)
+
+            @pl.when(group > 0)
+            def _():
+                second = dot_t(band[:, width:] - dot_t(first, l21), v[...])
+                out_ref[...] -= dot_t(second, dot_t(line[:, width:] - dot_t(mine, l21), v[...]))
 
 
 def kernel(body, outs, args, smem=1, scratch=(), flops=1 << 20):
@@ -457,13 +434,15 @@
     diags = [send(diag, [(dev(0, 0, c), dev(0, s, c)) for c in both]) for s in layers[1:]]
     turned = send(front, [(dev(0, z, c), dev(z, z, c)) for z in layers[1:] for c in both])
     near = send(
-        front, [(dev(g, 0, c), dev(g, z, c)) for g, z in ((1, 2), (2, 1), (3, 1)) for c in both]
+        front, [(dev(g, 0, c), dev(g, z, c)) for g, z in ((1, 3), (2, 1), (3, 1)) for c in both]
     )
     blocks = lax.all_gather(payload, "front")
+    far = send(
+        turned,
+        [(dev(g, z, c), dev(g, y, c)) for g, z, y in ((1, 1, 2), (2, 2, 3), (3, 3, 2)) for c in both],
+    )
+    outgoing, blocks, turned, *diags = lax.optimization_barrier((outgoing, blocks, turned, *diags))
     arrived = lax.all_to_all(outgoing, "front", split_axis=0, concat_axis=0, tiled=True)
-    blocks, turned, near, arrived, *diags = lax.optimization_barrier(
-        (blocks, turned, near, arrived, *diags)
-    )
 
     diag, matched = kernel(
         rows_kernel,
@@ -478,30 +457,23 @@
         send(matched, [(dev(z, z, c), dev(z ^ s, z, c)) for z in layers[1:] for c in both])
         for s in groups[1:]
     ]
-    far = send(
-        jnp.where(group == layer, turned, near),
-        [(dev(g, z, c), dev(g, 5 - z, c)) for g, z in ((1, 2), (2, 2), (3, 3)) for c in both],
-    )
     diag = jnp.where(group == 0, diag, got[0] + got[1] + got[2])
     diag2 = send(diag, swap)
-    diag, diag2, far = lax.optimization_barrier((diag, diag2, far))
 
     piece = jnp.where(layer == 0, front, jnp.where(group == layer, turned, near + far))
     piece2 = send(piece, swap)
 
     square = out(width, width)
-    w1, l21 = kernel(
-        first_kernel, (square, square), (info, diag, diag2), scratch=[packed.shape] * 2, flops=1 << 32
-    )
-    w2 = kernel(second_kernel, square, (info, diag, diag2, l21), scratch=[packed.shape], flops=1 << 32)
-    out1, q, n = kernel(
-        middle_kernel,
-        (out(nrows, width), out(nrows, width), square),
-        (info, front, arrived, piece, piece2, matched, *away, w1, l21, blocks),
-        scratch=[(nrows, 2 * width), (width, 2 * width)],
+    w1, l21, w2 = kernel(
+        factor_kernel, (square,) * 3, (info, diag, diag2), scratch=[packed.shape] * 2, flops=1 << 33
+    )
+    return kernel(
+        last_kernel,
+        out(nrows, width),
+        (info, front, arrived, piece, piece2, matched, *away, w1, l21, w2, blocks),
+        scratch=[(nrows, 2 * width), (width, 2 * width), (nrows, width)],
         flops=1 << 31,
     )
-    return kernel(last_kernel, out(nrows, width), (info, out1, q, n, w2), flops=1 << 30)
 
 
 def solution(mesh):

time: 111 us -> 117 us (1.054)
  waiting for transfers between devices: 43.6 us -> 22.9 us
  starting transfers between devices: 19.7 us -> 38.1 us
  local copies, waits for them, and re-layouts: 4.65 us -> 15.3 us
  other arithmetic: 3.26 us -> 1.41 us
    ppermute x14, starting transfers between devices: 14 us -> 33.2 us  [send(): return lax.ppermute(x, AXES, pairs)]
    all_to_all x1, waiting for transfers between devices: 16.9 us -> 0.01 us  [aligned(): lax.all_to_all(outgoing, 'front', split_axis=0, concat_axis=0, tiled=True)]
    ppermute x14, waiting for transfers between devices: 26.7 us -> 13.6 us  [send(): return lax.ppermute(x, AXES, pairs)]
    unnamed x18 -> x38, local copies, waits for them, and re-layouts: 4.57 us -> 15.2 us
    all_gather x1, waiting for transfers between devices: 0.01 us -> 9.26 us  [aligned(): blocks = lax.all_gather(payload, 'front')]
    pallas_call x6 -> x4, Pallas kernels: 25.8 us -> 24.9 us  [kernel(): pl.pallas_call(body, out_shape=outs, in_specs=spec, scratch_shapes=[pltpu...]
  transfers between devices with their start and end apart: 16 -> 16, of which waited for: 4 -> 3; matrix products, arithmetic and copies ran while one was open for 3% -> 1% of each run, Pallas kernels for 14% -> 13%
where the time goes in v5:
time: 117 us; the launch traced here: 116 us
  starting transfers between devices  38.1 us (33%)
  Pallas kernels  24.9 us (21%)
  waiting for transfers between devices  22.9 us (20%)
  local copies, waits for them, and re-layouts  15.3 us (13%)
  between operations  13.6 us (12%)
  other arithmetic  1.41 us (1%)
    ppermute x14, starting transfers between devices, send(): return lax.ppermute(x, AXES, pairs)  33.2 us
    pallas_call x4, Pallas kernels, kernel(): pl.pallas_call(body, out_shape=outs, in_specs=spec, scratch_shapes=[pltpu...  24.9 us
    unnamed x38, local copies, waits for them, and re-layouts  15.2 us
    ppermute x14, waiting for transfers between devices, send(): return lax.ppermute(x, AXES, pairs)  13.6 us
    all_gather x1, waiting for transfers between devices, aligned(): blocks = lax.all_gather(payload, 'front')  9.26 us
    all_to_all x1, starting transfers between devices, aligned(): lax.all_to_all(outgoing, 'front', split_axis=0, concat_axis=0, tiled=True)  4.91 us
  transfers between devices with their start and end apart: 16, of which 3 were waited for; matrix products, arithmetic and copies ran while one was open for 1% of the time, Pallas kernels for 13%

profile of v5, /device:TPU:11, one launch (start us, length us, event | category | flops | bytes accessed | tf_op | source)
XLA Modules:
  0.0 116.2 jit_solution(17308665100369299667)
XLA Ops:
  6.6 1.0 copy-done
  7.7 0.9 copy-done.4
  9.9 1.5 %shard_map.46 = (f32[8,136,128]{2,1,0:T(8,128)}, f32[272,128]{1,0:T(8,128)}, f32[520,128]{1,0:T(8,128)S(1)}) custom-call(s32[4]{0:T(128)S(1)} %copy-done.5, s32[4]{0:T(128)S(1)} %copy-done.6, s32[5]{0:T(128)S(1)} %stack.23.info, f32[4,128,128]{2,1,0:T(8,128)S(1)} %copy-done.4, f32[512,256]{1,0:T(8,128)S(1)} %copy-done), custom_call_target="tpu_custom_call" | custom-call | flops 1048576 | bytes 1048576 | tf_op jit(solution)/shard_map/pallas_call | solution.py:396
  11.4 1.3 %collective-permute-start = (f32[512,256]{1,0:T(8,128)}, f32[512,256]{1,0:T(8,128)S(1)}, u32[]{:S(2)}, u32[]{:S(2)}) collective-permute-start(f32[512,256]{1,0:T(8,128)} %shard.1), channel_id=1, source_target_pairs={{2,10},{3,11},{4,20},{5,21},{6,30},{7,31}} | collective-permute-start | bytes 1572872 | tf_op jit(solution)/shard_map/ppermute | solution.py:419
  14.8 11.5 %collective-permute-done.turned = f32[512,256]{1,0:T(8,128)S(1)} collective-permute-done((f32[512,256]{1,0:T(8,128)}, f32[512,256]{1,0:T(8,128)S(1)}, u32[]{:S(2)}, u32[]{:S(2)}) %collective-permute-start) | collective-permute-done | bytes 524320 | tf_op jit(solution)/shard_map/ppermute | solution.py:419
  26.3 9.3 %all-gather.3.cloned.1.call-done = f32[2176,128]{1,0:T(8,128)} async-done(((f32[272,128]{1,0:T(8,128)}), f32[2176,128]{1,0:T(8,128)}) %all-gather.3.cloned.1.call-update) | async-done | bytes 1114128 | tf_op jit(solution)/shard_map/all_gather | solution.py:439
  35.6 1.2 %copy-done.2 = f32[2176,128]{1,0:T(8,128)S(1)} copy-done((f32[2176,128]{1,0:T(8,128)S(1)}, f32[2176,128]{1,0:T(8,128)}, u32[]{:S(2)}) %copy-start.2) | copy-done | bytes 1114136
  36.8 1.1 shard_map.47
  38.6 1.5 %collective-permute-start.4 = (f32[512,256]{1,0:T(8,128)S(1)}, f32[512,256]{1,0:T(8,128)}, u32[]{:S(2)}, u32[]{:S(2)}) collective-permute-start(f32[512,256]{1,0:T(8,128)S(1)} %copy-done.1), channel_id=1, source_target_pairs={{8,14},{9,15},{16,18},{17,19},{24,26},{25,27}} | collective-permute-start | bytes 1572872 | tf_op jit(solution)/shard_map/ppermute | solution.py:419
  40.7 3.0 %collective-permute-start.5 = (f32[512,256]{1,0:T(8,128)S(1)}, f32[512,256]{1,0:T(8,128)}, u32[]{:S(2)}, u32[]{:S(2)}) collective-permute-start(f32[512,256]{1,0:T(8,128)S(1)} %collective-permute-done.turned), channel_id=1, source_target_pairs={{10,12},{11,13},{20,22},{21,23},{30,28},{31,29}} | collective-permute-start | bytes 1572872 | tf_op jit(solution)/shard_map/ppermute | solution.py:419
  43.8 1.3 %collective-permute-start.10 = (f32[520,128]{1,0:T(8,128)S(1)}, f32[520,128]{1,0:T(8,128)S(1)}, u32[]{:S(2)}, u32[]{:S(2)}) collective-permute-start(f32[520,128]{1,0:T(8,128)S(1)} %get-tuple-element.29), channel_id=1, source_target_pairs={{0,8},{1,9},{2,10},{3,11},{4,12},{5,13},{6,14},{7,15}} | collective-permute-start | bytes 798728 | tf_op jit(solution)/shard_map/ppermute | solution.py:419
  45.1 4.9 %all-to-all-start = ((f32[8,136,128]{2,1,0:T(8,128)}), f32[8,136,128]{2,1,0:T(8,128)S(1)}, u32[]{:S(2)}, u32[]{:S(2)}) async-start(f32[8,136,128]{2,1,0:T(8,128)} %get-tuple-element.22), calls=%async_computation | async-start | bytes 1114112 | tf_op jit(solution)/shard_map/all_to_all | solution.py:445
  50.0 2.7 %collective-permute-start.9 = (f32[256,512]{1,0:T(8,128)S(1)}, f32[256,512]{1,0:T(8,128)S(1)}, u32[]{:S(2)}, u32[]{:S(2)}) collective-permute-start(f32[256,512]{1,0:T(8,128)S(1)} %get-tuple-element.28.matched), channel_id=1, source_target_pairs={{10,18},{11,19},{20,12},{21,13},{30,6},{31,7}} | collective-permute-start | bytes 1572872 | tf_op jit(solution)/shard_map/ppermute | solution.py:419
  52.8 8.3 %collective-permute-start.8 = (f32[256,512]{1,0:T(8,128)S(1)}, f32[256,512]{1,0:T(8,128)S(1)}, u32[]{:S(2)}, u32[]{:S(2)}) collective-permute-start(f32[256,512]{1,0:T(8,128)S(1)} %get-tuple-element.28.matched), channel_id=1, source_target_pairs={{10,26},{11,27},{20,4},{21,5},{30,14},{31,15}} | collective-permute-start | bytes 1572872 | tf_op jit(solution)/shard_map/ppermute | solution.py:419
  61.1 2.0 %collective-permute-done.10 = f32[520,128]{1,0:T(8,128)S(1)} collective-permute-done((f32[520,128]{1,0:T(8,128)S(1)}, f32[520,128]{1,0:T(8,128)S(1)}, u32[]{:S(2)}, u32[]{:S(2)}) %collective-permute-start.10) | collective-permute-done | bytes 266272 | tf_op jit(solution)/shard_map/ppermute | solution.py:419
  63.1 10.8 %collective-permute-start.7 = (f32[256,512]{1,0:T(8,128)S(1)}, f32[256,512]{1,0:T(8,128)S(1)}, u32[]{:S(2)}, u32[]{:S(2)}) collective-permute-start(f32[256,512]{1,0:T(8,128)S(1)} %get-tuple-element.28.matched), channel_id=1, source_target_pairs={{10,2},{11,3},{20,28},{21,29},{30,22},{31,23}} | collective-permute-start | bytes 1572872 | tf_op jit(solution)/shard_map/ppermute | solution.py:419
  74.0 0.8 collective-permute-start.13
  74.8 1.3 %select_select_fusion.piece = f32[512,256]{1,0:T(8,128)S(1)} fusion(f32[512,256]{1,0:T(8,128)S(1)} %copy-done.1, f32[512,256]{1,0:T(8,128)S(1)} %collective-permute-done.turned, f32[512,256]{1,0:T(8,128)} %collective-permute-done.4, f32[512,256]{1,0:T(8,128)} %collective-permute-done.5, pred[]{:T(512)S(6)} %eq.12, pred[]{:T(512)S(6)} %eq.11), kind=kLoop, calls=%fused_computation | loop fusion | flops 393216 | bytes 2621442 | tf_op jit(solution)/shard_map/jit(_where)/select_n | solution.py:463
  76.2 15.4 %shard_map.48 = (f32[256,256]{1,0:T(8,128)S(1)}, f32[256,256]{1,0:T(8,128)S(1)}, f32[256,256]{1,0:T(8,128)S(1)}) custom-call(s32[5]{0:T(128)S(1)} %stack.23.info, f32[520,128]{1,0:T(8,128)S(1)} %add_select_fusion.here, f32[520,128]{1,0:T(8,128)S(1)} %collective-permute-done.13.there), custom_call_target="tpu_custom_call" | custom-call | flops 8589934592 | bytes 1048576 | tf_op jit(solution)/shard_map/pallas_call | solution.py:396
  91.7 0.7 copy-done.15
  92.4 0.7 copy-done.17
  93.1 0.8 copy-done.7
  93.9 0.8 copy-done.9
  94.7 0.8 copy-done.11
  95.5 0.8 copy-done.13
  96.3 1.0 copy-done.8
  97.3 1.0 copy-done.10
  98.4 1.0 copy-done.12
  99.4 1.0 copy-done.14
  100.5 0.9 copy-done.16
  101.4 0.9 copy-done.18
  102.4 7.0 %shard_map.49 = f32[512,256]{1,0:T(8,128)} custom-call(s32[5]{0:T(128)S(1)} %stack.23.info, f32[512,256]{1,0:T(8,128)S(1)} %copy-done.1, f32[8,136,128]{2,1,0:T(8,128)S(1)} %all-to-all-done.arrived, f32[512,256]{1,0:T(8,128)S(1)} %select_select_fusion.piece, f32[512,256]{1,0:T(8,128)S(1)} %copy-done.14, f32[256,512]{1,0:T(8,128)S(1)} %get-tuple-element.28.matched, ...), custom_call_target="tpu_custom_call" | custom-call | flops 2147483648 | bytes 1048576 | tf_op jit(solution)/shard_map/pallas_call | solution.py:396
  (46 shorter events, 5.0 us)
Async XLA Ops:
  6.5 29.0 %all-gather.3.cloned.1.call-start = ((), (), s32[]{:S(2)}) async-start(), calls=%async_computation.1 | async-start | bytes 1253376 | tf_op jit(solution)/shard_map/all_gather | solution.py:439
  6.6 1.0 copy-start
  7.7 0.9 copy-start.4
  9.9 25.7 %copy-start.1 = (f32[512,256]{1,0:T(8,128)S(1)}, f32[512,256]{1,0:T(8,128)}, u32[]{:S(2)}) copy-start(f32[512,256]{1,0:T(8,128)} %shard.1) | copy-start | bytes 1572868
  11.4 14.9 %collective-permute-start = (f32[512,256]{1,0:T(8,128)}, f32[512,256]{1,0:T(8,128)S(1)}, u32[]{:S(2)}, u32[]{:S(2)}) collective-permute-start(f32[512,256]{1,0:T(8,128)} %shard.1), channel_id=1, source_target_pairs={{2,10},{3,11},{4,20},{5,21},{6,30},{7,31}} | collective-permute-start | bytes 1572872 | tf_op jit(solution)/shard_map/ppermute | solution.py:419
  12.7 2.1 %collective-permute-start.3 = (f32[520,128]{1,0:T(8,128)S(1)}, f32[520,128]{1,0:T(8,128)S(1)}, u32[]{:S(2)}, u32[]{:S(2)}) collective-permute-start(f32[520,128]{1,0:T(8,128)S(1)} %get-tuple-element.21.diag), channel_id=1, source_target_pairs={{0,6},{1,7}} | collective-permute-start | bytes 798728 | tf_op jit(solution)/shard_map/ppermute | solution.py:419
  13.4 1.4 %collective-permute-start.2 = (f32[520,128]{1,0:T(8,128)S(1)}, f32[520,128]{1,0:T(8,128)S(1)}, u32[]{:S(2)}, u32[]{:S(2)}) collective-permute-start(f32[520,128]{1,0:T(8,128)S(1)} %get-tuple-element.21.diag), channel_id=1, source_target_pairs={{0,4},{1,5}} | collective-permute-start | bytes 798728 | tf_op jit(solution)/shard_map/ppermute | solution.py:419
  14.1 0.7 collective-permute-start.1
  35.6 1.2 %copy-start.2 = (f32[2176,128]{1,0:T(8,128)S(1)}, f32[2176,128]{1,0:T(8,128)}, u32[]{:S(2)}) copy-start(f32[2176,128]{1,0:T(8,128)} %all-gather.3.cloned.1.call-done) | copy-start | bytes 3342340
  37.9 12.1 %collective-permute-start.12 = (f32[520,128]{1,0:T(8,128)S(1)}, f32[520,128]{1,0:T(8,128)S(1)}, u32[]{:S(2)}, u32[]{:S(2)}) collective-permute-start(f32[520,128]{1,0:T(8,128)S(1)} %get-tuple-element.29), channel_id=1, source_target_pairs={{0,24},{1,25},{2,26},{3,27},{4,28},{5,29},{6,30},{7,31}} | collective-permute-start | bytes 798728 | tf_op jit(solution)/shard_map/ppermute | solution.py:419
  38.6 35.4 %collective-permute-start.4 = (f32[512,256]{1,0:T(8,128)S(1)}, f32[512,256]{1,0:T(8,128)}, u32[]{:S(2)}, u32[]{:S(2)}) collective-permute-start(f32[512,256]{1,0:T(8,128)S(1)} %copy-done.1), channel_id=1, source_target_pairs={{8,14},{9,15},{16,18},{17,19},{24,26},{25,27}} | collective-permute-start | bytes 1572872 | tf_op jit(solution)/shard_map/ppermute | solution.py:419
  40.1 12.7 %collective-permute-start.11 = (f32[520,128]{1,0:T(8,128)S(1)}, f32[520,128]{1,0:T(8,128)S(1)}, u32[]{:S(2)}, u32[]{:S(2)}) collective-permute-start(f32[520,128]{1,0:T(8,128)S(1)} %get-tuple-element.29), channel_id=1, source_target_pairs={{0,16},{1,17},{2,18},{3,19},{4,20},{5,21},{6,22},{7,23}} | collective-permute-start | bytes 798728 | tf_op jit(solution)/shard_map/ppermute | solution.py:419
  40.7 34.1 %collective-permute-start.5 = (f32[512,256]{1,0:T(8,128)S(1)}, f32[512,256]{1,0:T(8,128)}, u32[]{:S(2)}, u32[]{:S(2)}) collective-permute-start(f32[512,256]{1,0:T(8,128)S(1)} %collective-permute-done.turned), channel_id=1, source_target_pairs={{10,12},{11,13},{20,22},{21,23},{30,28},{31,29}} | collective-permute-start | bytes 1572872 | tf_op jit(solution)/shard_map/ppermute | solution.py:419
  43.8 19.3 %collective-permute-start.10 = (f32[520,128]{1,0:T(8,128)S(1)}, f32[520,128]{1,0:T(8,128)S(1)}, u32[]{:S(2)}, u32[]{:S(2)}) collective-permute-start(f32[520,128]{1,0:T(8,128)S(1)} %get-tuple-element.29), channel_id=1, source_target_pairs={{0,8},{1,9},{2,10},{3,11},{4,12},{5,13},{6,14},{7,15}} | collective-permute-start | bytes 798728 | tf_op jit(solution)/shard_map/ppermute | solution.py:419
  45.1 51.2 %all-to-all-start = ((f32[8,136,128]{2,1,0:T(8,128)}), f32[8,136,128]{2,1,0:T(8,128)S(1)}, u32[]{:S(2)}, u32[]{:S(2)}) async-start(f32[8,136,128]{2,1,0:T(8,128)} %get-tuple-element.22), calls=%async_computation | async-start | bytes 1114112 | tf_op jit(solution)/shard_map/all_to_all | solution.py:445
  50.0 43.1 %collective-permute-start.9 = (f32[256,512]{1,0:T(8,128)S(1)}, f32[256,512]{1,0:T(8,128)S(1)}, u32[]{:S(2)}, u32[]{:S(2)}) collective-permute-start(f32[256,512]{1,0:T(8,128)S(1)} %get-tuple-element.28.matched), channel_id=1, source_target_pairs={{10,18},{11,19},{20,12},{21,13},{30,6},{31,7}} | collective-permute-start | bytes 1572872 | tf_op jit(solution)/shard_map/ppermute | solution.py:419
  52.8 41.1 %collective-permute-start.8 = (f32[256,512]{1,0:T(8,128)S(1)}, f32[256,512]{1,0:T(8,128)S(1)}, u32[]{:S(2)}, u32[]{:S(2)}) collective-permute-start(f32[256,512]{1,0:T(8,128)S(1)} %get-tuple-element.28.matched), channel_id=1, source_target_pairs={{10,26},{11,27},{20,4},{21,5},{30,14},{31,15}} | collective-permute-start | bytes 1572872 | tf_op jit(solution)/shard_map/ppermute | solution.py:419
  63.1 31.6 %collective-permute-start.7 = (f32[256,512]{1,0:T(8,128)S(1)}, f32[256,512]{1,0:T(8,128)S(1)}, u32[]{:S(2)}, u32[]{:S(2)}) collective-permute-start(f32[256,512]{1,0:T(8,128)S(1)} %get-tuple-element.28.matched), channel_id=1, source_target_pairs={{10,2},{11,3},{20,28},{21,29},{30,22},{31,23}} | collective-permute-start | bytes 1572872 | tf_op jit(solution)/shard_map/ppermute | solution.py:419
  74.0 2.3 %collective-permute-start.13 = (f32[520,128]{1,0:T(8,128)S(1)}, f32[520,128]{1,0:T(8,128)S(1)}, u32[]{:S(2)}, u32[]{:S(2)}) collective-permute-start(f32[520,128]{1,0:T(8,128)S(1)} %add_select_fusion.here), channel_id=1, source_target_pairs={{0,1},{1,0},{2,3},{3,2},{4,5},{5,4},{6,7},{7,6},{8,9},{9,8},{10,11... | collective-permute-start | bytes 798728 | tf_op jit(solution)/shard_map/ppermute | solution.py:419
  76.1 20.2 %copy-start.3 = (f32[2176,128]{1,0:T(8,128)S(1)}, f32[2176,128]{1,0:T(8,128)}, u32[]{:S(2)}) copy-start(f32[2176,128]{1,0:T(8,128)} %all-gather.3.cloned.1.call-done) | copy-start | bytes 3342340
  76.1 19.3 %collective-permute-start.6 = (f32[512,256]{1,0:T(8,128)S(1)}, f32[512,256]{1,0:T(8,128)S(1)}, u32[]{:S(2)}, u32[]{:S(2)}) collective-permute-start(f32[512,256]{1,0:T(8,128)S(1)} %select_select_fusion.piece), channel_id=1, source_target_pairs={{0,1},{1,0},{2,3},{3,2},{4,5},{5,4},{6,7},{7,6},{8,9},{9,8},{10,11... | collective-permute-start | bytes 1572872 | tf_op jit(solution)/shard_map/ppermute | solution.py:419
  91.6 0.7 copy-start.15
  93.1 0.8 copy-start.7
  93.9 0.8 copy-start.9
  94.7 0.8 copy-start.11
  95.5 0.8 copy-start.13
  96.3 1.0 copy-start.8
  97.3 1.0 copy-start.10
  98.4 1.0 copy-start.12
  99.4 1.0 copy-start.14
  100.5 0.9 copy-start.16
  101.4 0.9 copy-start.18
  (3 other events, 2.0 us)
Sparse Core Ops, SparseCore 0:
  11.5 23.9 all-gather.2

commit v6 on v5

--- a/solution.py
+++ b/solution.py
@@ -1,4 +1,4 @@
-import functools
+import math
 
 import jax
 import jax.numpy as jnp
@@ -11,7 +11,6 @@
 BF16 = jnp.bfloat16
 AXES = ("leaf", "front")
 EXACT = lax.Precision.HIGHEST
-VMEM_LIMIT = 40 * 1024 * 1024
 
 
 def spread(value, axis, source):
@@ -160,6 +159,16 @@
     )
 
 
+def dot3_t(a, b):
+    ah, bh = a.astype(BF16), b.astype(BF16)
+    al, bl = (a - ah.astype(F32)).astype(BF16), (b - bh.astype(F32)).astype(BF16)
+
+    def product(x, y):
+        return lax.dot_general(x, y, (((1,), (1,)), ((), ())), preferred_element_type=F32)
+
+    return product(ah, bl) + product(al, bh) + product(ah, bh)
+
+
 def factor_pair(a):
     h = a.shape[0] // 2
     w11 = factor_inverse(a[:h, :h])
@@ -193,11 +202,11 @@
 
 
 def add_band_blocks(ref, blocks, width):
-    tile = blocks.shape[2]
-    for i in range(blocks.shape[0]):
+    for b in blocks:
+        tile = b.shape[1]
         for owner in range(2):
-            tag = blocks[i, 2 * tile + 8 * owner : 2 * tile + 8 * owner + 8, :]
-            block = blocks[i, owner * tile : (owner + 1) * tile, :]
+            tag = b[2 * tile + 8 * owner : 2 * tile + 8 * owner + 8, :]
+            block = b[owner * tile : (owner + 1) * tile, :]
             add_block(ref, block, place_of(tag), tile, owner * width)
 
 
@@ -259,7 +268,8 @@
         put_rows(diag_ref, width + 8, front[:width, tile:].T)
 
 
-def rows_kernel(info, front, turned, diag, d1, d2, d3, blocks, diag_ref, out_ref, band, part):
+def rows_kernel(info, front, turned, diag, hop1, hop2, *refs):
+    blocks, (diag_ref, out_ref, band, part) = refs[:8], refs[8:]
     width = front.shape[1]
     tile = width // 2
     group, layer, core = info[0], info[1], info[2]
@@ -271,7 +281,7 @@
 
     @pl.when(group == 0)
     def _():
-        for z, d in enumerate((diag, d1, d2, d3)):
+        for z, d in enumerate((diag, hop2, hop1, hop2)):
 
             @pl.when(layer == z)
             def _(d=d):
@@ -317,9 +327,8 @@
     store_inverse(v_ref, factor_pair(unpack(bottom) - dot_t(lower, lower)))
 
 
-def last_kernel(
-    info, shard, arrived, piece, piece2, matched, m1, m2, m3, w, lower, v, blocks, out_ref, band, line, work
-):
+def last_kernel(info, shard, arrived, piece, piece2, matched, m1, m2, m3, w, lower, v, *refs):
+    blocks, (out_ref, band, line, work) = refs[:8], refs[8:]
     tile = arrived.shape[2]
     nrows, width = shard.shape
     group, layer, core, column = info[0], info[1], info[2], info[4]
@@ -358,7 +367,7 @@
 
     @pl.when(column == 0)
     def _():
-        out_ref[...] = dot_t(out_ref[...], w1)
+        out_ref[...] = dot3_t(out_ref[...], w1)
 
     @pl.when(column > 0)
     def _():
@@ -369,7 +378,7 @@
 
         @pl.when(group > 0)
         def _():
-            work[...] = dot_t(band[:, :width], w1)
+            work[...] = dot3_t(band[:, :width], w1)
 
         first = work[...]
 
@@ -377,28 +386,30 @@
         def _():
             rows = group * nrows + lax.broadcasted_iota(jnp.int32, (nrows, width), 0)
             own = out_ref[...]
-            out_ref[...] = jnp.where(rows >= width, dot_t(own - dot_t(first, l21), v[...]), own)
+            out_ref[...] = jnp.where(rows >= width, dot3_t(own - dot3_t(first, l21), v[...]), own)
 
         @pl.when(column > 1)
         def _():
-            mine = dot_t(line[:, :width], w1)
-            out_ref[...] -= dot_t(first, mine)
+            mine = dot3_t(line[:, :width], w1)
+            out_ref[...] -= dot3_t(first, mine)
 
             @pl.when(group > 0)
             def _():
-                second = dot_t(band[:, width:] - dot_t(first, l21), v[...])
-                out_ref[...] -= dot_t(second, dot_t(line[:, width:] - dot_t(mine, l21), v[...]))
+                second = dot3_t(band[:, width:] - dot3_t(first, l21), v[...])
+                out_ref[...] -= dot3_t(second, dot3_t(line[:, width:] - dot3_t(mine, l21), v[...]))
 
 
 def kernel(body, outs, args, smem=1, scratch=(), flops=1 << 20):
     spec = [pl.BlockSpec(memory_space=pltpu.SMEM)] * smem
     spec += [pl.BlockSpec(memory_space=pltpu.VMEM)] * (len(args) - smem)
+    sizes = [a.size for a in args[smem:]] + [o.size for o in jax.tree.leaves(outs)]
+    need = 4 * (sum(sizes) + sum(math.prod(s) for s in scratch)) + (6 << 20)
     return pl.pallas_call(
         body,
         out_shape=outs,
         in_specs=spec,
         scratch_shapes=[pltpu.VMEM(s, F32) for s in scratch],
-        compiler_params=pltpu.CompilerParams(vmem_limit_bytes=VMEM_LIMIT),
+        compiler_params=pltpu.CompilerParams(vmem_limit_bytes=need),
         cost_estimate=pl.CostEstimate(flops=flops, bytes_accessed=1 << 20, transcendentals=0),
     )(*args)
 
@@ -431,25 +442,33 @@
         (target_owner, target_slot, info, updates, front),
         smem=3,
     )
-    diags = [send(diag, [(dev(0, 0, c), dev(0, s, c)) for c in both]) for s in layers[1:]]
-    turned = send(front, [(dev(0, z, c), dev(z, z, c)) for z in layers[1:] for c in both])
+    blocks = [payload]
+    for s in layers[1:]:
+        pairs = [(dev(g, z, c), dev(g, z ^ s, c)) for g in groups for z in layers for c in both]
+        blocks.append(send(payload, pairs))
+    blocks += [send(b, swap) for b in blocks]
+    hop1 = send(diag, [(dev(0, 0, c), dev(0, 2, c)) for c in both])
+    hop2 = send(
+        jnp.where(layer == 0, diag, hop1), [(dev(0, z, c), dev(0, z + 1, c)) for z in (0, 2) for c in both]
+    )
+    early, outgoing, info = lax.optimization_barrier((front, outgoing, info))
+    turned = send(early, [(dev(0, z, c), dev(z, z, c)) for z in layers[1:] for c in both])
     near = send(
-        front, [(dev(g, 0, c), dev(g, z, c)) for g, z in ((1, 3), (2, 1), (3, 1)) for c in both]
-    )
-    blocks = lax.all_gather(payload, "front")
+        early, [(dev(g, 0, c), dev(g, z, c)) for g, z in ((1, 3), (2, 1), (3, 1)) for c in both]
+    )
     far = send(
         turned,
         [(dev(g, z, c), dev(g, y, c)) for g, z, y in ((1, 1, 2), (2, 2, 3), (3, 3, 2)) for c in both],
     )
-    outgoing, blocks, turned, *diags = lax.optimization_barrier((outgoing, blocks, turned, *diags))
-    arrived = lax.all_to_all(outgoing, "front", split_axis=0, concat_axis=0, tiled=True)
 
     diag, matched = kernel(
         rows_kernel,
         (packed, out(width, 2 * width)),
-        (info, front, turned, diag, *diags, blocks),
+        (info, front, turned, diag, hop1, hop2, *blocks),
         scratch=[(nrows, 2 * width), packed.shape],
     )
+    diag, outgoing = lax.optimization_barrier((diag, outgoing))
+    arrived = lax.all_to_all(outgoing, "front", split_axis=0, concat_axis=0, tiled=True)
     got = [
         send(diag, [(dev(0, z, c), dev(s, z, c)) for z in layers for c in both]) for s in groups[1:]
     ]
@@ -470,7 +489,7 @@
     return kernel(
         last_kernel,
         out(nrows, width),
-        (info, front, arrived, piece, piece2, matched, *away, w1, l21, w2, blocks),
+        (info, front, arrived, piece, piece2, matched, *away, w1, l21, w2, *blocks),
         scratch=[(nrows, 2 * width), (width, 2 * width), (nrows, width)],
         flops=1 << 31,
     )

time: 117 us -> 90.5 us (0.77)
  between operations: 13.6 us -> 0.15 us
  waiting for transfers between devices: 22.9 us -> 13.2 us
  local copies, waits for them, and re-layouts: 15.3 us -> 10.4 us
    all_gather x1 -> x0, waiting for transfers between devices: 9.26 us -> none  [aligned(): blocks = lax.all_gather(payload, 'front')]
    unnamed x38 -> x26, local copies, waits for them, and re-layouts: 15.2 us -> 10.4 us
    ppermute x14 -> x20, waiting for transfers between devices: 13.6 us -> 13.2 us  [send(): return lax.ppermute(x, AXES, pairs)]
    ppermute x14 -> x20, starting transfers between devices: 33.2 us -> 33.4 us  [send(): return lax.ppermute(x, AXES, pairs)]
  transfers between devices with their start and end apart: 16 -> 21, of which waited for: 3 -> 6; matrix products, arithmetic and copies ran while one was open for 1% -> 3% of each run, Pallas kernels for 13% -> 17%
where the time goes in v6:
time: 90.5 us; the launch traced here: 88.7 us
  starting transfers between devices  38 us (42%)
  Pallas kernels  24.5 us (27%)
  waiting for transfers between devices  13.2 us (15%)
  local copies, waits for them, and re-layouts  10.4 us (11%)
  other arithmetic  2.49 us (3%)
    ppermute x20, starting transfers between devices, send(): return lax.ppermute(x, AXES, pairs)  33.4 us
    pallas_call x4, Pallas kernels, kernel(): pl.pallas_call(body, out_shape=outs, in_specs=spec, scratch_shapes=[pltpu...  24.5 us
    ppermute x20, waiting for transfers between devices, send(): return lax.ppermute(x, AXES, pairs)  13.2 us
    unnamed x26, local copies, waits for them, and re-layouts  10.4 us
    all_to_all x1, starting transfers between devices, aligned(): lax.all_to_all(outgoing, 'front', split_axis=0, concat_axis=0, tiled=True)  4.54 us
  transfers between devices with their start and end apart: 21, of which 6 were waited for; matrix products, arithmetic and copies ran while one was open for 3% of the time, Pallas kernels for 17%

profile of v6, /device:TPU:11, one launch (start us, length us, event | category | flops | bytes accessed | tf_op | source)
XLA Modules:
  0.0 88.7 jit_solution(17798439098844456276)
XLA Ops:
  0.7 0.9 %copy-done = f32[4,128,128]{2,1,0:T(8,128)S(1)} copy-done((f32[4,128,128]{2,1,0:T(8,128)S(1)}, f32[4,128,128]{2,1,0:T(8,128)}, u32[]{:S(2)}) %copy-start) | copy-done | bytes 262168
  1.6 1.9 %shard_map.46 = (f32[8,136,128]{2,1,0:T(8,128)}, f32[272,128]{1,0:T(8,128)S(1)}, f32[520,128]{1,0:T(8,128)S(1)}) custom-call(s32[4]{0:T(128)S(1)} %copy-done.1, s32[4]{0:T(128)S(1)} %copy-done.2, s32[5]{0:T(128)S(1)} %stack.23.info, f32[4,128,128]{2,1,0:T(8,128)S(1)} %copy-done, f32[512,256]{1,0:T(8,128)} %shard.1), custom_call_target="tpu_custom_call" | custom-call | flops 1048576 | bytes 1048576 | tf_op jit(solution)/shard_map/pallas_call | solution.py:407
  4.2 1.3 %collective-permute-start = (f32[512,256]{1,0:T(8,128)}, f32[512,256]{1,0:T(8,128)S(1)}, u32[]{:S(2)}, u32[]{:S(2)}) collective-permute-start(f32[512,256]{1,0:T(8,128)} %shard.1), channel_id=1, source_target_pairs={{2,10},{3,11},{4,20},{5,21},{6,30},{7,31}} | collective-permute-start | bytes 1572872 | tf_op jit(solution)/shard_map/ppermute | solution.py:430
  5.6 1.9 %collective-permute-start.4 = (f32[272,128]{1,0:T(8,128)S(1)}, f32[272,128]{1,0:T(8,128)S(1)}, u32[]{:S(2)}, u32[]{:S(2)}) collective-permute-start(f32[272,128]{1,0:T(8,128)S(1)} %get-tuple-element.22.refs_0_), channel_id=1, source_target_pairs={{0,4},{1,5},{2,6},{3,7},{4,0},{5,1},{6,2},{7,3},{8,12},{9,13},{10,... | collective-permute-start | bytes 417800 | tf_op jit(solution)/shard_map/ppermute | solution.py:430
  8.2 1.5 %collective-permute-start.6 = (f32[272,128]{1,0:T(8,128)S(1)}, f32[272,128]{1,0:T(8,128)S(1)}, u32[]{:S(2)}, u32[]{:S(2)}) collective-permute-start(f32[272,128]{1,0:T(8,128)S(1)} %get-tuple-element.22.refs_0_), channel_id=1, source_target_pairs={{0,1},{1,0},{2,3},{3,2},{4,5},{5,4},{6,7},{7,6},{8,9},{9,8},{10,11... | collective-permute-start | bytes 417800 | tf_op jit(solution)/shard_map/ppermute | solution.py:430
  10.8 2.7 %collective-permute-done.4.refs_2_ = f32[272,128]{1,0:T(8,128)S(1)} collective-permute-done((f32[272,128]{1,0:T(8,128)S(1)}, f32[272,128]{1,0:T(8,128)S(1)}, u32[]{:S(2)}, u32[]{:S(2)}) %collective-permute-start.4) | collective-permute-done | bytes 139296 | tf_op jit(solution)/shard_map/ppermute | solution.py:430
  13.5 5.1 %collective-permute-start.7 = (f32[272,128]{1,0:T(8,128)S(1)}, f32[272,128]{1,0:T(8,128)S(1)}, u32[]{:S(2)}, u32[]{:S(2)}) collective-permute-start(f32[272,128]{1,0:T(8,128)S(1)} %collective-permute-done.3.refs_1_), channel_id=1, source_target_pairs={{0,1},{1,0},{2,3},{3,2},{4,5},{5,4},{6,7},{7,6},{8,9},{9,8},{10,11... | collective-permute-start | bytes 417800 | tf_op jit(solution)/shard_map/ppermute | solution.py:430
  18.7 1.6 %collective-permute-done.5.refs_3_ = f32[272,128]{1,0:T(8,128)S(1)} collective-permute-done((f32[272,128]{1,0:T(8,128)S(1)}, f32[272,128]{1,0:T(8,128)S(1)}, u32[]{:S(2)}, u32[]{:S(2)}) %collective-permute-start.5) | collective-permute-done | bytes 139296 | tf_op jit(solution)/shard_map/ppermute | solution.py:430
  20.2 1.6 %collective-permute-start.8 = (f32[272,128]{1,0:T(8,128)S(1)}, f32[272,128]{1,0:T(8,128)S(1)}, u32[]{:S(2)}, u32[]{:S(2)}) collective-permute-start(f32[272,128]{1,0:T(8,128)S(1)} %collective-permute-done.4.refs_2_), channel_id=1, source_target_pairs={{0,1},{1,0},{2,3},{3,2},{4,5},{5,4},{6,7},{7,6},{8,9},{9,8},{10,11... | collective-permute-start | bytes 417800 | tf_op jit(solution)/shard_map/ppermute | solution.py:430
  21.9 1.0 %collective-permute-done.8.refs_6_ = f32[272,128]{1,0:T(8,128)S(1)} collective-permute-done((f32[272,128]{1,0:T(8,128)S(1)}, f32[272,128]{1,0:T(8,128)S(1)}, u32[]{:S(2)}, u32[]{:S(2)}) %collective-permute-start.8) | collective-permute-done | bytes 139296 | tf_op jit(solution)/shard_map/ppermute | solution.py:430
  23.2 1.6 %shard_map.47 = (f32[520,128]{1,0:T(8,128)S(1)}, f32[256,512]{1,0:T(8,128)S(1)}) custom-call(s32[5]{0:T(128)S(1)} %stack.23.info, f32[512,256]{1,0:T(8,128)} %shard.1, f32[512,256]{1,0:T(8,128)S(1)} %collective-permute-done.turned, f32[520,128]{1,0:T(8,128)S(1)} %get-tuple-element.21.diag, f32[520,128]{1,0:T(8,128)S(1)} %collective-permute-done.1.hop1, ...), custom_call_target="tpu_custom_call" | custom-call | flops 1048576 | bytes 1048576 | tf_op jit(solution)/shard_map/pallas_call | solution.py:407
  25.5 1.5 %collective-permute-start.10 = (f32[512,256]{1,0:T(8,128)}, f32[512,256]{1,0:T(8,128)}, u32[]{:S(2)}, u32[]{:S(2)}) collective-permute-start(f32[512,256]{1,0:T(8,128)} %shard.1), channel_id=1, source_target_pairs={{8,14},{9,15},{16,18},{17,19},{24,26},{25,27}} | collective-permute-start | bytes 1572872 | tf_op jit(solution)/shard_map/ppermute | solution.py:430
  27.0 1.3 %collective-permute-start.16 = (f32[520,128]{1,0:T(8,128)S(1)}, f32[520,128]{1,0:T(8,128)}, u32[]{:S(2)}, u32[]{:S(2)}) collective-permute-start(f32[520,128]{1,0:T(8,128)S(1)} %get-tuple-element.27), channel_id=1, source_target_pairs={{0,8},{1,9},{2,10},{3,11},{4,12},{5,13},{6,14},{7,15}} | collective-permute-start | bytes 798728 | tf_op jit(solution)/shard_map/ppermute | solution.py:430
  28.3 2.9 %collective-permute-start.11 = (f32[512,256]{1,0:T(8,128)S(1)}, f32[512,256]{1,0:T(8,128)}, u32[]{:S(2)}, u32[]{:S(2)}) collective-permute-start(f32[512,256]{1,0:T(8,128)S(1)} %collective-permute-done.turned), channel_id=1, source_target_pairs={{10,12},{11,13},{20,22},{21,23},{30,28},{31,29}} | collective-permute-start | bytes 1572872 | tf_op jit(solution)/shard_map/ppermute | solution.py:430
  31.2 1.4 %collective-permute-start.17 = (f32[520,128]{1,0:T(8,128)S(1)}, f32[520,128]{1,0:T(8,128)}, u32[]{:S(2)}, u32[]{:S(2)}) collective-permute-start(f32[520,128]{1,0:T(8,128)S(1)} %get-tuple-element.27), channel_id=1, source_target_pairs={{0,16},{1,17},{2,18},{3,19},{4,20},{5,21},{6,22},{7,23}} | collective-permute-start | bytes 798728 | tf_op jit(solution)/shard_map/ppermute | solution.py:430
  32.5 4.5 %all-to-all-start = ((f32[8,136,128]{2,1,0:T(8,128)}), f32[8,136,128]{2,1,0:T(8,128)S(1)}, u32[]{:S(2)}, u32[]{:S(2)}) async-start(f32[8,136,128]{2,1,0:T(8,128)} %get-tuple-element.25), calls=%async_computation | async-start | bytes 1114112 | tf_op jit(solution)/shard_map/all_to_all | solution.py:471
  37.1 8.0 %collective-permute-start.13 = (f32[256,512]{1,0:T(8,128)S(1)}, f32[256,512]{1,0:T(8,128)S(1)}, u32[]{:S(2)}, u32[]{:S(2)}) collective-permute-start(f32[256,512]{1,0:T(8,128)S(1)} %get-tuple-element.26.matched), channel_id=1, source_target_pairs={{10,2},{11,3},{20,28},{21,29},{30,22},{31,23}} | collective-permute-start | bytes 1572872 | tf_op jit(solution)/shard_map/ppermute | solution.py:430
  45.1 1.3 %collective-permute-start.14 = (f32[256,512]{1,0:T(8,128)S(1)}, f32[256,512]{1,0:T(8,128)S(1)}, u32[]{:S(2)}, u32[]{:S(2)}) collective-permute-start(f32[256,512]{1,0:T(8,128)S(1)} %get-tuple-element.26.matched), channel_id=1, source_target_pairs={{10,26},{11,27},{20,4},{21,5},{30,14},{31,15}} | collective-permute-start | bytes 1572872 | tf_op jit(solution)/shard_map/ppermute | solution.py:430
  46.4 1.3 %collective-permute-start.15 = (f32[256,512]{1,0:T(8,128)S(1)}, f32[256,512]{1,0:T(8,128)S(1)}, u32[]{:S(2)}, u32[]{:S(2)}) collective-permute-start(f32[256,512]{1,0:T(8,128)S(1)} %get-tuple-element.26.matched), channel_id=1, source_target_pairs={{10,18},{11,19},{20,12},{21,13},{30,6},{31,7}} | collective-permute-start | bytes 1572872 | tf_op jit(solution)/shard_map/ppermute | solution.py:430
  47.8 1.1 %add_select_fusion.here = f32[520,128]{1,0:T(8,128)S(1)} fusion(f32[520,128]{1,0:T(8,128)S(1)} %get-tuple-element.27, f32[520,128]{1,0:T(8,128)S(1)} %collective-permute-done.18, f32[520,128]{1,0:T(8,128)} %collective-permute-done.16, f32[520,128]{1,0:T(8,128)} %collective-permute-done.17, pred[]{:T(512)S(6)} %eq.14), kind=kLoop, calls=%fused_computation.1 | loop fusion | flops 199680 | bytes 1331201 | tf_op jit(solution)/shard_map/jit(_where)/select_n | solution.py:479
  48.9 0.9 %collective-permute-start.19 = (f32[520,128]{1,0:T(8,128)S(1)}, f32[520,128]{1,0:T(8,128)S(1)}, u32[]{:S(2)}, u32[]{:S(2)}) collective-permute-start(f32[520,128]{1,0:T(8,128)S(1)} %add_select_fusion.here), channel_id=1, source_target_pairs={{0,1},{1,0},{2,3},{3,2},{4,5},{5,4},{6,7},{7,6},{8,9},{9,8},{10,11... | collective-permute-start | bytes 798728 | tf_op jit(solution)/shard_map/ppermute | solution.py:430
  49.8 7.2 %collective-permute-done.11 = f32[512,256]{1,0:T(8,128)} collective-permute-done((f32[512,256]{1,0:T(8,128)S(1)}, f32[512,256]{1,0:T(8,128)}, u32[]{:S(2)}, u32[]{:S(2)}) %collective-permute-start.11) | collective-permute-done | bytes 524320 | tf_op jit(solution)/shard_map/ppermute | solution.py:430
  57.0 1.3 %select_select_fusion.piece = f32[512,256]{1,0:T(8,128)S(1)} fusion(f32[512,256]{1,0:T(8,128)} %shard.1, f32[512,256]{1,0:T(8,128)S(1)} %collective-permute-done.turned, f32[512,256]{1,0:T(8,128)} %collective-permute-done.10, f32[512,256]{1,0:T(8,128)} %collective-permute-done.11, pred[]{:T(512)S(6)} %eq.13, pred[]{:T(512)S(6)} %eq.12), kind=kLoop, calls=%fused_computation | loop fusion | flops 393216 | bytes 2621442 | tf_op jit(solution)/shard_map/jit(_where)/select_n | solution.py:482
  58.9 15.4 %shard_map.48 = (f32[256,256]{1,0:T(8,128)S(1)}, f32[256,256]{1,0:T(8,128)S(1)}, f32[256,256]{1,0:T(8,128)S(1)}) custom-call(s32[5]{0:T(128)S(1)} %stack.23.info, f32[520,128]{1,0:T(8,128)S(1)} %add_select_fusion.here, f32[520,128]{1,0:T(8,128)S(1)} %collective-permute-done.19.there), custom_call_target="tpu_custom_call" | custom-call | flops 8589934592 | bytes 1048576 | tf_op jit(solution)/shard_map/pallas_call | solution.py:407
  76.5 0.8 copy-done.5
  77.3 0.8 copy-done.7
  78.1 1.0 %copy-done.4 = f32[256,512]{1,0:T(8,128)S(1)} copy-done((f32[256,512]{1,0:T(8,128)S(1)}, f32[256,512]{1,0:T(8,128)}, u32[]{:S(2)}) %copy-start.4) | copy-done | bytes 524312
  79.2 1.0 %copy-done.6 = f32[256,512]{1,0:T(8,128)S(1)} copy-done((f32[256,512]{1,0:T(8,128)S(1)}, f32[256,512]{1,0:T(8,128)}, u32[]{:S(2)}) %copy-start.6) | copy-done | bytes 524312
  80.2 1.0 %copy-done.8 = f32[256,512]{1,0:T(8,128)S(1)} copy-done((f32[256,512]{1,0:T(8,128)S(1)}, f32[256,512]{1,0:T(8,128)}, u32[]{:S(2)}) %copy-start.8) | copy-done | bytes 524312
  81.3 0.9 %copy-done.10 = f32[256,256]{1,0:T(8,128)S(1)} copy-done((f32[256,256]{1,0:T(8,128)S(1)}, f32[256,256]{1,0:T(8,128)}, u32[]{:S(2)}) %copy-start.10) | copy-done | bytes 262168
  82.2 0.9 %copy-done.12 = f32[256,256]{1,0:T(8,128)S(1)} copy-done((f32[256,256]{1,0:T(8,128)S(1)}, f32[256,256]{1,0:T(8,128)}, u32[]{:S(2)}) %copy-start.12) | copy-done | bytes 262168
  83.2 5.6 %shard_map.49 = f32[512,256]{1,0:T(8,128)} custom-call(s32[5]{0:T(128)S(1)} %stack.23.info, f32[512,256]{1,0:T(8,128)} %shard.1, f32[8,136,128]{2,1,0:T(8,128)S(1)} %all-to-all-done.arrived, f32[512,256]{1,0:T(8,128)S(1)} %select_select_fusion.piece, f32[512,256]{1,0:T(8,128)S(1)} %collective-permute-done.12.piece2, ...), custom_call_target="tpu_custom_call" | custom-call | flops 2147483648 | bytes 1048576 | tf_op jit(solution)/shard_map/pallas_call | solution.py:407
  (44 shorter events, 7.1 us)
Async XLA Ops:
  0.7 0.9 %copy-start = (f32[4,128,128]{2,1,0:T(8,128)S(1)}, f32[4,128,128]{2,1,0:T(8,128)}, u32[]{:S(2)}) copy-start(f32[4,128,128]{2,1,0:T(8,128)} %updates.1) | copy-start | bytes 786436
  3.6 4.7 %collective-permute-start.1 = (f32[520,128]{1,0:T(8,128)S(1)}, f32[520,128]{1,0:T(8,128)S(1)}, u32[]{:S(2)}, u32[]{:S(2)}) collective-permute-start(f32[520,128]{1,0:T(8,128)S(1)} %get-tuple-element.21.diag), channel_id=1, source_target_pairs={{0,4},{1,5}} | collective-permute-start | bytes 798728 | tf_op jit(solution)/shard_map/ppermute | solution.py:430
  4.2 19.0 %collective-permute-start = (f32[512,256]{1,0:T(8,128)}, f32[512,256]{1,0:T(8,128)S(1)}, u32[]{:S(2)}, u32[]{:S(2)}) collective-permute-start(f32[512,256]{1,0:T(8,128)} %shard.1), channel_id=1, source_target_pairs={{2,10},{3,11},{4,20},{5,21},{6,30},{7,31}} | collective-permute-start | bytes 1572872 | tf_op jit(solution)/shard_map/ppermute | solution.py:430
  5.5 4.6 %collective-permute-start.3 = (f32[272,128]{1,0:T(8,128)S(1)}, f32[272,128]{1,0:T(8,128)S(1)}, u32[]{:S(2)}, u32[]{:S(2)}) collective-permute-start(f32[272,128]{1,0:T(8,128)S(1)} %get-tuple-element.22.refs_0_), channel_id=1, source_target_pairs={{0,2},{1,3},{2,0},{3,1},{4,6},{5,7},{6,4},{7,5},{8,10},{9,11},{10,... | collective-permute-start | bytes 417800 | tf_op jit(solution)/shard_map/ppermute | solution.py:430
  5.6 7.9 %collective-permute-start.4 = (f32[272,128]{1,0:T(8,128)S(1)}, f32[272,128]{1,0:T(8,128)S(1)}, u32[]{:S(2)}, u32[]{:S(2)}) collective-permute-start(f32[272,128]{1,0:T(8,128)S(1)} %get-tuple-element.22.refs_0_), channel_id=1, source_target_pairs={{0,4},{1,5},{2,6},{3,7},{4,0},{5,1},{6,2},{7,3},{8,12},{9,13},{10,... | collective-permute-start | bytes 417800 | tf_op jit(solution)/shard_map/ppermute | solution.py:430
  7.5 12.7 %collective-permute-start.5 = (f32[272,128]{1,0:T(8,128)S(1)}, f32[272,128]{1,0:T(8,128)S(1)}, u32[]{:S(2)}, u32[]{:S(2)}) collective-permute-start(f32[272,128]{1,0:T(8,128)S(1)} %get-tuple-element.22.refs_0_), channel_id=1, source_target_pairs={{0,6},{1,7},{2,4},{3,5},{4,2},{5,3},{6,0},{7,1},{8,14},{9,15},{10,... | collective-permute-start | bytes 417800 | tf_op jit(solution)/shard_map/ppermute | solution.py:430
  8.2 13.6 %collective-permute-start.6 = (f32[272,128]{1,0:T(8,128)S(1)}, f32[272,128]{1,0:T(8,128)S(1)}, u32[]{:S(2)}, u32[]{:S(2)}) collective-permute-start(f32[272,128]{1,0:T(8,128)S(1)} %get-tuple-element.22.refs_0_), channel_id=1, source_target_pairs={{0,1},{1,0},{2,3},{3,2},{4,5},{5,4},{6,7},{7,6},{8,9},{9,8},{10,11... | collective-permute-start | bytes 417800 | tf_op jit(solution)/shard_map/ppermute | solution.py:430
  10.1 13.1 %collective-permute-start.2 = (f32[520,128]{1,0:T(8,128)S(1)}, f32[520,128]{1,0:T(8,128)S(1)}, u32[]{:S(2)}, u32[]{:S(2)}) collective-permute-start(f32[520,128]{1,0:T(8,128)S(1)} %broadcast_select_fusion), channel_id=1, source_target_pairs={{0,2},{1,3},{4,6},{5,7}} | collective-permute-start | bytes 798728 | tf_op jit(solution)/shard_map/ppermute | solution.py:430
  13.5 8.3 %collective-permute-start.7 = (f32[272,128]{1,0:T(8,128)S(1)}, f32[272,128]{1,0:T(8,128)S(1)}, u32[]{:S(2)}, u32[]{:S(2)}) collective-permute-start(f32[272,128]{1,0:T(8,128)S(1)} %collective-permute-done.3.refs_1_), channel_id=1, source_target_pairs={{0,1},{1,0},{2,3},{3,2},{4,5},{5,4},{6,7},{7,6},{8,9},{9,8},{10,11... | collective-permute-start | bytes 417800 | tf_op jit(solution)/shard_map/ppermute | solution.py:430
  20.2 2.6 %collective-permute-start.8 = (f32[272,128]{1,0:T(8,128)S(1)}, f32[272,128]{1,0:T(8,128)S(1)}, u32[]{:S(2)}, u32[]{:S(2)}) collective-permute-start(f32[272,128]{1,0:T(8,128)S(1)} %collective-permute-done.4.refs_2_), channel_id=1, source_target_pairs={{0,1},{1,0},{2,3},{3,2},{4,5},{5,4},{6,7},{7,6},{8,9},{9,8},{10,11... | collective-permute-start | bytes 417800 | tf_op jit(solution)/shard_map/ppermute | solution.py:430
  21.9 1.4 %collective-permute-start.9 = (f32[272,128]{1,0:T(8,128)S(1)}, f32[272,128]{1,0:T(8,128)S(1)}, u32[]{:S(2)}, u32[]{:S(2)}) collective-permute-start(f32[272,128]{1,0:T(8,128)S(1)} %collective-permute-done.5.refs_3_), channel_id=1, source_target_pairs={{0,1},{1,0},{2,3},{3,2},{4,5},{5,4},{6,7},{7,6},{8,9},{9,8},{10,11... | collective-permute-start | bytes 417800 | tf_op jit(solution)/shard_map/ppermute | solution.py:430
  24.8 12.3 %collective-permute-start.18 = (f32[520,128]{1,0:T(8,128)S(1)}, f32[520,128]{1,0:T(8,128)S(1)}, u32[]{:S(2)}, u32[]{:S(2)}) collective-permute-start(f32[520,128]{1,0:T(8,128)S(1)} %get-tuple-element.27), channel_id=1, source_target_pairs={{0,24},{1,25},{2,26},{3,27},{4,28},{5,29},{6,30},{7,31}} | collective-permute-start | bytes 798728 | tf_op jit(solution)/shard_map/ppermute | solution.py:430
  25.5 23.4 %collective-permute-start.10 = (f32[512,256]{1,0:T(8,128)}, f32[512,256]{1,0:T(8,128)}, u32[]{:S(2)}, u32[]{:S(2)}) collective-permute-start(f32[512,256]{1,0:T(8,128)} %shard.1), channel_id=1, source_target_pairs={{8,14},{9,15},{16,18},{17,19},{24,26},{25,27}} | collective-permute-start | bytes 1572872 | tf_op jit(solution)/shard_map/ppermute | solution.py:430
  27.0 18.1 %collective-permute-start.16 = (f32[520,128]{1,0:T(8,128)S(1)}, f32[520,128]{1,0:T(8,128)}, u32[]{:S(2)}, u32[]{:S(2)}) collective-permute-start(f32[520,128]{1,0:T(8,128)S(1)} %get-tuple-element.27), channel_id=1, source_target_pairs={{0,8},{1,9},{2,10},{3,11},{4,12},{5,13},{6,14},{7,15}} | collective-permute-start | bytes 798728 | tf_op jit(solution)/shard_map/ppermute | solution.py:430
  28.3 28.7 %collective-permute-start.11 = (f32[512,256]{1,0:T(8,128)S(1)}, f32[512,256]{1,0:T(8,128)}, u32[]{:S(2)}, u32[]{:S(2)}) collective-permute-start(f32[512,256]{1,0:T(8,128)S(1)} %collective-permute-done.turned), channel_id=1, source_target_pairs={{10,12},{11,13},{20,22},{21,23},{30,28},{31,29}} | collective-permute-start | bytes 1572872 | tf_op jit(solution)/shard_map/ppermute | solution.py:430
  31.2 15.3 %collective-permute-start.17 = (f32[520,128]{1,0:T(8,128)S(1)}, f32[520,128]{1,0:T(8,128)}, u32[]{:S(2)}, u32[]{:S(2)}) collective-permute-start(f32[520,128]{1,0:T(8,128)S(1)} %get-tuple-element.27), channel_id=1, source_target_pairs={{0,16},{1,17},{2,18},{3,19},{4,20},{5,21},{6,22},{7,23}} | collective-permute-start | bytes 798728 | tf_op jit(solution)/shard_map/ppermute | solution.py:430
  32.5 45.6 %all-to-all-start = ((f32[8,136,128]{2,1,0:T(8,128)}), f32[8,136,128]{2,1,0:T(8,128)S(1)}, u32[]{:S(2)}, u32[]{:S(2)}) async-start(f32[8,136,128]{2,1,0:T(8,128)} %get-tuple-element.25), calls=%async_computation | async-start | bytes 1114112 | tf_op jit(solution)/shard_map/all_to_all | solution.py:471
  37.1 38.6 %collective-permute-start.13 = (f32[256,512]{1,0:T(8,128)S(1)}, f32[256,512]{1,0:T(8,128)S(1)}, u32[]{:S(2)}, u32[]{:S(2)}) collective-permute-start(f32[256,512]{1,0:T(8,128)S(1)} %get-tuple-element.26.matched), channel_id=1, source_target_pairs={{10,2},{11,3},{20,28},{21,29},{30,22},{31,23}} | collective-permute-start | bytes 1572872 | tf_op jit(solution)/shard_map/ppermute | solution.py:430
  45.1 31.4 %collective-permute-start.14 = (f32[256,512]{1,0:T(8,128)S(1)}, f32[256,512]{1,0:T(8,128)S(1)}, u32[]{:S(2)}, u32[]{:S(2)}) collective-permute-start(f32[256,512]{1,0:T(8,128)S(1)} %get-tuple-element.26.matched), channel_id=1, source_target_pairs={{10,26},{11,27},{20,4},{21,5},{30,14},{31,15}} | collective-permute-start | bytes 1572872 | tf_op jit(solution)/shard_map/ppermute | solution.py:430
  46.4 30.9 %collective-permute-start.15 = (f32[256,512]{1,0:T(8,128)S(1)}, f32[256,512]{1,0:T(8,128)S(1)}, u32[]{:S(2)}, u32[]{:S(2)}) collective-permute-start(f32[256,512]{1,0:T(8,128)S(1)} %get-tuple-element.26.matched), channel_id=1, source_target_pairs={{10,18},{11,19},{20,12},{21,13},{30,6},{31,7}} | collective-permute-start | bytes 1572872 | tf_op jit(solution)/shard_map/ppermute | solution.py:430
  48.9 10.0 %collective-permute-start.19 = (f32[520,128]{1,0:T(8,128)S(1)}, f32[520,128]{1,0:T(8,128)S(1)}, u32[]{:S(2)}, u32[]{:S(2)}) collective-permute-start(f32[520,128]{1,0:T(8,128)S(1)} %add_select_fusion.here), channel_id=1, source_target_pairs={{0,1},{1,0},{2,3},{3,2},{4,5},{5,4},{6,7},{7,6},{8,9},{9,8},{10,11... | collective-permute-start | bytes 798728 | tf_op jit(solution)/shard_map/ppermute | solution.py:430
  58.3 19.8 %collective-permute-start.12 = (f32[512,256]{1,0:T(8,128)S(1)}, f32[512,256]{1,0:T(8,128)S(1)}, u32[]{:S(2)}, u32[]{:S(2)}) collective-permute-start(f32[512,256]{1,0:T(8,128)S(1)} %select_select_fusion.piece), channel_id=1, source_target_pairs={{0,1},{1,0},{2,3},{3,2},{4,5},{5,4},{6,7},{7,6},{8,9},{9,8},{10,11... | collective-permute-start | bytes 1572872 | tf_op jit(solution)/shard_map/ppermute | solution.py:430
  74.3 0.7 copy-start.9
  75.0 0.7 copy-start.11
  75.7 0.8 copy-start.3
  76.5 0.8 copy-start.5
  77.3 0.8 copy-start.7
  78.1 1.0 %copy-start.4 = (f32[256,512]{1,0:T(8,128)S(1)}, f32[256,512]{1,0:T(8,128)}, u32[]{:S(2)}) copy-start(f32[256,512]{1,0:T(8,128)} %copy-done.3) | copy-start | bytes 1572868
  79.2 1.0 %copy-start.6 = (f32[256,512]{1,0:T(8,128)S(1)}, f32[256,512]{1,0:T(8,128)}, u32[]{:S(2)}) copy-start(f32[256,512]{1,0:T(8,128)} %copy-done.5) | copy-start | bytes 1572868
  80.2 1.0 %copy-start.8 = (f32[256,512]{1,0:T(8,128)S(1)}, f32[256,512]{1,0:T(8,128)}, u32[]{:S(2)}) copy-start(f32[256,512]{1,0:T(8,128)} %copy-done.7) | copy-start | bytes 1572868
  81.3 0.9 %copy-start.10 = (f32[256,256]{1,0:T(8,128)S(1)}, f32[256,256]{1,0:T(8,128)}, u32[]{:S(2)}) copy-start(f32[256,256]{1,0:T(8,128)} %copy-done.9) | copy-start | bytes 786436
  82.2 0.9 %copy-start.12 = (f32[256,256]{1,0:T(8,128)S(1)}, f32[256,256]{1,0:T(8,128)}, u32[]{:S(2)}) copy-start(f32[256,256]{1,0:T(8,128)} %copy-done.11) | copy-start | bytes 786436
  (2 other events, 1.3 us)

commit v7 on v6

--- a/solution.py
+++ b/solution.py
@@ -246,29 +246,47 @@
     return jnp.concatenate([ref[start : start + n, :], ref[start + n : start + 2 * n, :]], 1)
 
 
-def sort_kernel(owner, slot, info, updates, front, out_ref, pay_ref, diag_ref):
+def sort_kernel(owner, slot, info, updates, front, out_ref, pay_ref, diag_ref, square, sems, side):
     sends, tile = updates.shape[:2]
     width = front.shape[1]
+    near_diag = info[3] < 2
+    corner = pltpu.make_async_copy(front, square, side)
+
+    @pl.when(near_diag)
+    def _():
+        corner.start()
+
     out_ref[...] = jnp.zeros_like(out_ref)
+    copies = [
+        pltpu.make_async_copy(updates.at[j], out_ref.at[owner[j], pl.ds(0, tile), :], sems.at[j])
+        for j in range(sends)
+    ]
     for j in range(sends):
-        out_ref[owner[j], :tile, :] = updates[j]
+        copies[j].start()
         out_ref[owner[j], tile:, :] = jnp.full((8, tile), slot[j].astype(F32))
+
+    @pl.when(near_diag)
+    def _():
+        corner.wait()
+
+    @pl.when(info[3] == 0)
+    def _():
+        pack(diag_ref, square[:width, :])
+        put_rows(diag_ref, width + 8, square[width : width + tile, :])
+
+    @pl.when(info[3] == 1)
+    def _():
+        pack(diag_ref, square[width:, :])
+        put_rows(diag_ref, width + 8, square[:width, tile:].T)
+
+    for c in copies:
+        c.wait()
     for o in range(2):
         pay_ref[o * tile : (o + 1) * tile, :] = out_ref[o, :tile, :]
         pay_ref[2 * tile + 8 * o : 2 * tile + 8 * o + 8, :] = out_ref[o, tile:, :]
 
-    @pl.when(info[3] == 0)
-    def _():
-        pack(diag_ref, front[:width, :])
-        put_rows(diag_ref, width + 8, front[width : width + tile, :])
-
-    @pl.when(info[3] == 1)
-    def _():
-        pack(diag_ref, front[width:, :])
-        put_rows(diag_ref, width + 8, front[:width, tile:].T)
-
-
-def rows_kernel(info, front, turned, diag, hop1, hop2, *refs):
+
+def rows_kernel(info, front, direct, diag, hop1, hop2, *refs):
     blocks, (diag_ref, out_ref, band, part) = refs[:8], refs[8:]
     width = front.shape[1]
     tile = width // 2
@@ -302,7 +320,7 @@
     @pl.when((group == layer) & (group > 0))
     def _():
         start = pl.multiple_of(core * width, width)
-        out_ref[...] = turned[...].T + band[pl.ds(start, width), :]
+        out_ref[...] = direct[...].T + band[pl.ds(start, width), :]
 
 
 def factor_kernel(info, here, there, w_ref, l_ref, v_ref, top, bottom):
@@ -327,43 +345,63 @@
     store_inverse(v_ref, factor_pair(unpack(bottom) - dot_t(lower, lower)))
 
 
-def last_kernel(info, shard, arrived, piece, piece2, matched, m1, m2, m3, w, lower, v, *refs):
-    blocks, (out_ref, band, line, work) = refs[:8], refs[8:]
-    tile = arrived.shape[2]
-    nrows, width = shard.shape
+def last_kernel(info, *refs):
+    (shard, arrived, piece, piece2, matched, m1, m2, m3, w, lower, v), blocks = refs[:11], refs[11:19]
+    out_ref, band, line, work, halves, came, pays, tri, sems = refs[19:]
+    tile = came.shape[2]
+    nrows, width = out_ref.shape
     group, layer, core, column = info[0], info[1], info[2], info[4]
-    out_ref[...] = shard[...]
-    for i in range(arrived.shape[0]):
-        add_block(out_ref, arrived[i, :tile, :], place_of(arrived[i, tile:, :]), tile)
+    copies = [
+        pltpu.make_async_copy(src, dst, sems.at[i])
+        for i, (src, dst) in enumerate(
+            [
+                (shard, out_ref),
+                (arrived, came),
+                (piece, halves.at[0]),
+                (piece2, halves.at[1]),
+                (w, tri.at[0]),
+                (lower, tri.at[1]),
+                (v, tri.at[2]),
+            ]
+            + [(b, pays.at[i]) for i, b in enumerate(blocks)]
+        )
+    ]
+    last = len(copies)
+    for c in copies:
+        c.start()
     for k, m in enumerate((matched, m1, m2, m3)):
 
         @pl.when((group ^ layer) == k)
         def _(m=m):
-            line[...] = m[...]
-
-    w1, l21 = w[...], lower[...]
+            pltpu.make_async_copy(m, line, sems.at[last]).start()
+
+    copies[0].wait()
+    copies[1].wait()
+    for i in range(came.shape[0]):
+        add_block(out_ref, came[i, :tile, :], place_of(came[i, tile:, :]), tile)
+    copies[2].wait()
+    copies[3].wait()
     by_rows = (layer > 0) & (((group == 1) & (layer < 3)) | ((group > 1) & (layer > 1)))
-    for c, (same, swapped) in enumerate(((piece, piece2), (piece2, piece))):
-
-        @pl.when(by_rows & (core == 0))
-        def _(c=c, p=same):
-            band[c * width : (c + 1) * width, :] = p[...].T
-
-        @pl.when(by_rows & (core == 1))
-        def _(c=c, p=swapped):
-            band[c * width : (c + 1) * width, :] = p[...].T
-
-        @pl.when(~by_rows & (core == 0))
-        def _(c=c, p=same):
-            band[:, c * width : (c + 1) * width] = p[...]
-
-        @pl.when(~by_rows & (core == 1))
-        def _(c=c, p=swapped):
-            band[:, c * width : (c + 1) * width] = p[...]
+    for c in range(2):
+        side = jnp.where(core == 0, c, 1 - c)
+
+        @pl.when(by_rows)
+        def _(c=c, side=side):
+            band[c * width : (c + 1) * width, :] = halves[side].T
+
+        @pl.when(~by_rows)
+        def _(c=c, side=side):
+            band[:, c * width : (c + 1) * width] = halves[side]
+
+    for c in copies[4:]:
+        c.wait()
+    pltpu.make_async_copy(matched, line, sems.at[last]).wait()
 
     @pl.when(group > 0)
     def _():
-        add_band_blocks(band, blocks, width)
+        add_band_blocks(band, [pays.at[i] for i in range(len(blocks))], width)
+
+    w1, l21, v = tri[0], tri[1], tri.at[2]
 
     @pl.when(column == 0)
     def _():
@@ -399,17 +437,20 @@
                 out_ref[...] -= dot3_t(second, dot3_t(line[:, width:] - dot3_t(mine, l21), v[...]))
 
 
-def kernel(body, outs, args, smem=1, scratch=(), flops=1 << 20):
+def kernel(body, outs, args, smem=1, scratch=(), flops=1 << 20, sems=(), away=False):
+    space = pl.ANY if away else pltpu.VMEM
     spec = [pl.BlockSpec(memory_space=pltpu.SMEM)] * smem
-    spec += [pl.BlockSpec(memory_space=pltpu.VMEM)] * (len(args) - smem)
-    sizes = [a.size for a in args[smem:]] + [o.size for o in jax.tree.leaves(outs)]
-    need = 4 * (sum(sizes) + sum(math.prod(s) for s in scratch)) + (6 << 20)
+    spec += [pl.BlockSpec(memory_space=space)] * (len(args) - smem)
+    sizes = [o.size for o in jax.tree.leaves(outs)] + [math.prod(s) for s in scratch]
+    if not away:
+        sizes += [a.size for a in args[smem:]]
     return pl.pallas_call(
         body,
         out_shape=outs,
         in_specs=spec,
-        scratch_shapes=[pltpu.VMEM(s, F32) for s in scratch],
-        compiler_params=pltpu.CompilerParams(vmem_limit_bytes=need),
+        scratch_shapes=[pltpu.VMEM(s, F32) for s in scratch]
+        + [pltpu.SemaphoreType.DMA(s) for s in sems],
+        compiler_params=pltpu.CompilerParams(vmem_limit_bytes=4 * sum(sizes) + (6 << 20)),
         cost_estimate=pl.CostEstimate(flops=flops, bytes_accessed=1 << 20, transcendentals=0),
     )(*args)
 
@@ -441,6 +482,9 @@
         (out(nfront, tile + 8, tile), out(2 * tile + 16, tile), packed),
         (target_owner, target_slot, info, updates, front),
         smem=3,
+        scratch=[(nrows, width)],
+        sems=[(updates.shape[0],), ()],
+        away=True,
     )
     blocks = [payload]
     for s in layers[1:]:
@@ -451,20 +495,21 @@
     hop2 = send(
         jnp.where(layer == 0, diag, hop1), [(dev(0, z, c), dev(0, z + 1, c)) for z in (0, 2) for c in both]
     )
-    early, outgoing, info = lax.optimization_barrier((front, outgoing, info))
-    turned = send(early, [(dev(0, z, c), dev(z, z, c)) for z in layers[1:] for c in both])
-    near = send(
-        early, [(dev(g, 0, c), dev(g, z, c)) for g, z in ((1, 3), (2, 1), (3, 1)) for c in both]
-    )
-    far = send(
-        turned,
+    early, info = lax.optimization_barrier((front, info))
+    direct = send(
+        early,
+        [(dev(0, z, c), dev(z, z, c)) for z in layers[1:] for c in both]
+        + [(dev(g, 0, c), dev(g, z, c)) for g, z in ((1, 3), (2, 1), (3, 1)) for c in both],
+    )
+    on = send(
+        direct,
         [(dev(g, z, c), dev(g, y, c)) for g, z, y in ((1, 1, 2), (2, 2, 3), (3, 3, 2)) for c in both],
     )
 
     diag, matched = kernel(
         rows_kernel,
         (packed, out(width, 2 * width)),
-        (info, front, turned, diag, hop1, hop2, *blocks),
+        (info, front, direct, diag, hop1, hop2, *blocks),
         scratch=[(nrows, 2 * width), packed.shape],
     )
     diag, outgoing = lax.optimization_barrier((diag, outgoing))
@@ -479,7 +524,7 @@
     diag = jnp.where(group == 0, diag, got[0] + got[1] + got[2])
     diag2 = send(diag, swap)
 
-    piece = jnp.where(layer == 0, front, jnp.where(group == layer, turned, near + far))
+    piece = jnp.where(layer == 0, front, direct + on)
     piece2 = send(piece, swap)
 
     square = out(width, width)
@@ -490,8 +535,18 @@
         last_kernel,
         out(nrows, width),
         (info, front, arrived, piece, piece2, matched, *away, w1, l21, w2, *blocks),
-        scratch=[(nrows, 2 * width), (width, 2 * width), (nrows, width)],
+        scratch=[
+            (nrows, 2 * width),
+            (width, 2 * width),
+            (nrows, width),
+            (2, nrows, width),
+            arrived.shape,
+            (8,) + payload.shape,
+            (3, width, width),
+        ],
         flops=1 << 31,
+        sems=[(16,)],
+        away=True,
     )
 
 

time: 90.5 us -> 88.9 us (0.982)
  the two profiles are of different devices: /device:TPU:11 before, /device:TPU:19 now
where the time goes in v7:
time: 88.9 us; the launch traced here: 88.2 us
  starting transfers between devices  44.9 us (51%)
  Pallas kernels  25.1 us (28%)
  local copies, waits for them, and re-layouts  10.4 us (12%)
  waiting for transfers between devices  5.19 us (6%)
  other arithmetic  2.3 us (3%)
    ppermute x19, starting transfers between devices, send(): return lax.ppermute(x, AXES, pairs)  37.6 us
    pallas_call x4, Pallas kernels, kernel(): pl.pallas_call(body, out_shape=outs, in_specs=spec, scratch_shapes=[pltpu...  25.1 us
    unnamed x26, local copies, waits for them, and re-layouts  10.4 us
    all_to_all x1, starting transfers between devices, aligned(): lax.all_to_all(outgoing, 'front', split_axis=0, concat_axis=0, tiled=True)  7.32 us
    ppermute x19, waiting for transfers between devices, send(): return lax.ppermute(x, AXES, pairs)  5.19 us
  transfers between devices with their start and end apart: 20, of which 3 were waited for; matrix products, arithmetic and copies ran while one was open for 3% of the time, Pallas kernels for 17%

profile of v7, /device:TPU:19, one launch (start us, length us, event | category | flops | bytes accessed | tf_op | source)
XLA Modules:
  0.0 88.2 jit_solution(831514744403610336)
XLA Ops:
  0.7 0.9 %copy-done = f32[4,128,128]{2,1,0:T(8,128)S(1)} copy-done((f32[4,128,128]{2,1,0:T(8,128)S(1)}, f32[4,128,128]{2,1,0:T(8,128)}, u32[]{:S(2)}) %copy-start) | copy-done | bytes 262168
  1.6 1.8 %shard_map.46 = (f32[8,136,128]{2,1,0:T(8,128)}, f32[272,128]{1,0:T(8,128)S(1)}, f32[520,128]{1,0:T(8,128)S(1)}) custom-call(s32[4]{0:T(128)S(1)} %copy-done.1, s32[4]{0:T(128)S(1)} %copy-done.2, s32[5]{0:T(128)S(1)} %stack.23.info, f32[4,128,128]{2,1,0:T(8,128)S(1)} %copy-done, f32[512,256]{1,0:T(8,128)} %refs_0_.1), custom_call_target="tpu_custom_call" | custom-call | flops 1048576 | bytes 1048576 | tf_op jit(solution)/shard_map/pallas_call | solution.py:447
  4.1 0.7 collective-permute-start
  4.8 0.7 collective-permute-start.6
  5.6 0.8 collective-permute-start.5
  6.4 4.1 %collective-permute-start.4 = (f32[272,128]{1,0:T(8,128)S(1)}, f32[272,128]{1,0:T(8,128)S(1)}, u32[]{:S(2)}, u32[]{:S(2)}) collective-permute-start(f32[272,128]{1,0:T(8,128)S(1)} %get-tuple-element.20.refs_0_.refs_11_), channel_id=1, source_target_pairs={{0,4},{1,5},{2,6},{3,7},{4,0},{5,1},{6,2},{7,3},{8,12},{9,13},{10,... | collective-permute-start | bytes 417800 | tf_op jit(solution)/shard_map/ppermute | solution.py:471
  10.5 1.2 %collective-permute-start.3 = (f32[272,128]{1,0:T(8,128)S(1)}, f32[272,128]{1,0:T(8,128)S(1)}, u32[]{:S(2)}, u32[]{:S(2)}) collective-permute-start(f32[272,128]{1,0:T(8,128)S(1)} %get-tuple-element.20.refs_0_.refs_11_), channel_id=1, source_target_pairs={{0,2},{1,3},{2,0},{3,1},{4,6},{5,7},{6,4},{7,5},{8,10},{9,11},{10,... | collective-permute-start | bytes 417800 | tf_op jit(solution)/shard_map/ppermute | solution.py:471
  12.4 16.2 %collective-permute-start.9 = (f32[272,128]{1,0:T(8,128)S(1)}, f32[272,128]{1,0:T(8,128)S(1)}, u32[]{:S(2)}, u32[]{:S(2)}) collective-permute-start(f32[272,128]{1,0:T(8,128)S(1)} %collective-permute-done.5.refs_3_.refs_14_), channel_id=1, source_target_pairs={{0,1},{1,0},{2,3},{3,2},{4,5},{5,4},{6,7},{7,6},{8,9},{9,8},{10,11... | collective-permute-start | bytes 417800 | tf_op jit(solution)/shard_map/ppermute | solution.py:471
  28.6 1.0 %collective-permute-start.8 = (f32[272,128]{1,0:T(8,128)S(1)}, f32[272,128]{1,0:T(8,128)S(1)}, u32[]{:S(2)}, u32[]{:S(2)}) collective-permute-start(f32[272,128]{1,0:T(8,128)S(1)} %collective-permute-done.4.refs_2_.refs_13_), channel_id=1, source_target_pairs={{0,1},{1,0},{2,3},{3,2},{4,5},{5,4},{6,7},{7,6},{8,9},{9,8},{10,11... | collective-permute-start | bytes 417800 | tf_op jit(solution)/shard_map/ppermute | solution.py:471
  29.7 1.0 %collective-permute-done.8.refs_6_.refs_17_ = f32[272,128]{1,0:T(8,128)S(1)} collective-permute-done((f32[272,128]{1,0:T(8,128)S(1)}, f32[272,128]{1,0:T(8,128)S(1)}, u32[]{:S(2)}, u32[]{:S(2)}) %collective-permute-start.8) | collective-permute-done | bytes 139296 | tf_op jit(solution)/shard_map/ppermute | solution.py:471
  31.0 1.1 %shard_map.47 = (f32[520,128]{1,0:T(8,128)S(1)}, f32[256,512]{1,0:T(8,128)S(1)}) custom-call(s32[5]{0:T(128)S(1)} %stack.23.info, f32[512,256]{1,0:T(8,128)} %refs_0_.1, f32[512,256]{1,0:T(8,128)S(1)} %collective-permute-done.direct, f32[520,128]{1,0:T(8,128)S(1)} %get-tuple-element.19.diag, f32[520,128]{1,0:T(8,128)S(1)} %collective-permute-done.1.hop1, ...), custom_call_target="tpu_custom_call" | custom-call | flops 1048576 | bytes 1048576 | tf_op jit(solution)/shard_map/pallas_call | solution.py:447
  32.8 1.3 %collective-permute-start.10 = (f32[512,256]{1,0:T(8,128)S(1)}, f32[512,256]{1,0:T(8,128)}, u32[]{:S(2)}, u32[]{:S(2)}) collective-permute-start(f32[512,256]{1,0:T(8,128)S(1)} %collective-permute-done.direct), channel_id=1, source_target_pairs={{10,12},{11,13},{20,22},{21,23},{30,28},{31,29}} | collective-permute-start | bytes 1572872 | tf_op jit(solution)/shard_map/ppermute | solution.py:471
  34.1 1.4 %collective-permute-start.16 = (f32[520,128]{1,0:T(8,128)S(1)}, f32[520,128]{1,0:T(8,128)}, u32[]{:S(2)}, u32[]{:S(2)}) collective-permute-start(f32[520,128]{1,0:T(8,128)S(1)} %get-tuple-element.25), channel_id=1, source_target_pairs={{0,16},{1,17},{2,18},{3,19},{4,20},{5,21},{6,22},{7,23}} | collective-permute-start | bytes 798728 | tf_op jit(solution)/shard_map/ppermute | solution.py:471
  35.5 1.3 %collective-permute-start.15 = (f32[520,128]{1,0:T(8,128)S(1)}, f32[520,128]{1,0:T(8,128)}, u32[]{:S(2)}, u32[]{:S(2)}) collective-permute-start(f32[520,128]{1,0:T(8,128)S(1)} %get-tuple-element.25), channel_id=1, source_target_pairs={{0,8},{1,9},{2,10},{3,11},{4,12},{5,13},{6,14},{7,15}} | collective-permute-start | bytes 798728 | tf_op jit(solution)/shard_map/ppermute | solution.py:471
  36.8 7.3 %all-to-all-start = ((f32[8,136,128]{2,1,0:T(8,128)}), f32[8,136,128]{2,1,0:T(8,128)S(1)}, u32[]{:S(2)}, u32[]{:S(2)}) async-start(f32[8,136,128]{2,1,0:T(8,128)} %get-tuple-element.23), calls=%async_computation | async-start | bytes 1114112 | tf_op jit(solution)/shard_map/all_to_all | solution.py:516
  44.1 1.3 %collective-permute-start.14 = (f32[256,512]{1,0:T(8,128)S(1)}, f32[256,512]{1,0:T(8,128)S(1)}, u32[]{:S(2)}, u32[]{:S(2)}) collective-permute-start(f32[256,512]{1,0:T(8,128)S(1)} %get-tuple-element.24.refs_4_), channel_id=1, source_target_pairs={{10,18},{11,19},{20,12},{21,13},{30,6},{31,7}} | collective-permute-start | bytes 1572872 | tf_op jit(solution)/shard_map/ppermute | solution.py:471
  46.8 1.1 %add_select_fusion.1.here = f32[520,128]{1,0:T(8,128)S(1)} fusion(f32[520,128]{1,0:T(8,128)S(1)} %get-tuple-element.25, f32[520,128]{1,0:T(8,128)S(1)} %collective-permute-done.17, f32[520,128]{1,0:T(8,128)} %collective-permute-done.15, f32[520,128]{1,0:T(8,128)} %collective-permute-done.16, pred[]{:T(512)S(6)} %eq.10), kind=kLoop, calls=%fused_computation.1 | loop fusion | flops 199680 | bytes 1331201 | tf_op jit(solution)/shard_map/jit(_where)/select_n | solution.py:524
  47.9 0.8 collective-permute-start.18
  48.7 3.8 %collective-permute-done.10 = f32[512,256]{1,0:T(8,128)} collective-permute-done((f32[512,256]{1,0:T(8,128)S(1)}, f32[512,256]{1,0:T(8,128)}, u32[]{:S(2)}, u32[]{:S(2)}) %collective-permute-start.10) | collective-permute-done | bytes 524320 | tf_op jit(solution)/shard_map/ppermute | solution.py:471
  52.5 1.1 %add_select_fusion.refs_2_ = f32[512,256]{1,0:T(8,128)S(1)} fusion(f32[512,256]{1,0:T(8,128)} %refs_0_.1, f32[512,256]{1,0:T(8,128)S(1)} %collective-permute-done.direct, f32[512,256]{1,0:T(8,128)} %collective-permute-done.10, pred[]{:T(512)S(6)} %eq.9), kind=kLoop, calls=%fused_computation | loop fusion | flops 262144 | bytes 2097153 | tf_op jit(solution)/shard_map/jit(_where)/select_n | solution.py:527
  53.6 3.4 %collective-permute-start.11 = (f32[512,256]{1,0:T(8,128)S(1)}, f32[512,256]{1,0:T(8,128)S(1)}, u32[]{:S(2)}, u32[]{:S(2)}) collective-permute-start(f32[512,256]{1,0:T(8,128)S(1)} %add_select_fusion.refs_2_), channel_id=1, source_target_pairs={{0,1},{1,0},{2,3},{3,2},{4,5},{5,4},{6,7},{7,6},{8,9},{9,8},{10,11... | collective-permute-start | bytes 1572872 | tf_op jit(solution)/shard_map/ppermute | solution.py:471
  57.0 15.4 %shard_map.48 = (f32[256,256]{1,0:T(8,128)S(1)}, f32[256,256]{1,0:T(8,128)S(1)}, f32[256,256]{1,0:T(8,128)S(1)}) custom-call(s32[5]{0:T(128)S(1)} %stack.23.info, f32[520,128]{1,0:T(8,128)S(1)} %add_select_fusion.1.here, f32[520,128]{1,0:T(8,128)S(1)} %collective-permute-done.18.there), custom_call_target="tpu_custom_call" | custom-call | flops 8589934592 | bytes 1048576 | tf_op jit(solution)/shard_map/pallas_call | solution.py:447
  73.1 0.7 copy-done.11
  73.8 0.8 copy-done.3
  74.6 0.8 copy-done.5
  75.4 0.8 copy-done.7
  76.2 1.0 %copy-done.4 = f32[256,512]{1,0:T(8,128)S(1)} copy-done((f32[256,512]{1,0:T(8,128)S(1)}, f32[256,512]{1,0:T(8,128)}, u32[]{:S(2)}) %copy-start.4) | copy-done | bytes 524312
  77.3 1.0 %copy-done.6 = f32[256,512]{1,0:T(8,128)S(1)} copy-done((f32[256,512]{1,0:T(8,128)S(1)}, f32[256,512]{1,0:T(8,128)}, u32[]{:S(2)}) %copy-start.6) | copy-done | bytes 524312
  78.3 1.0 %copy-done.8 = f32[256,512]{1,0:T(8,128)S(1)} copy-done((f32[256,512]{1,0:T(8,128)S(1)}, f32[256,512]{1,0:T(8,128)}, u32[]{:S(2)}) %copy-start.8) | copy-done | bytes 524312
  79.4 0.9 %copy-done.10 = f32[256,256]{1,0:T(8,128)S(1)} copy-done((f32[256,256]{1,0:T(8,128)S(1)}, f32[256,256]{1,0:T(8,128)}, u32[]{:S(2)}) %copy-start.10) | copy-done | bytes 262168
  80.3 0.9 %copy-done.12 = f32[256,256]{1,0:T(8,128)S(1)} copy-done((f32[256,256]{1,0:T(8,128)S(1)}, f32[256,256]{1,0:T(8,128)}, u32[]{:S(2)}) %copy-start.12) | copy-done | bytes 262168
  81.3 6.8 %shard_map.49 = f32[512,256]{1,0:T(8,128)} custom-call(s32[5]{0:T(128)S(1)} %stack.23.info, f32[512,256]{1,0:T(8,128)} %refs_0_.1, f32[8,136,128]{2,1,0:T(8,128)S(1)} %all-to-all-done.refs_1_, f32[512,256]{1,0:T(8,128)S(1)} %add_select_fusion.refs_2_, f32[512,256]{1,0:T(8,128)S(1)} %collective-permute-done.11.refs_3_, ...), custom_call_target="tpu_custom_call" | custom-call | flops 2147483648 | bytes 1048576 | tf_op jit(solution)/shard_map/pallas_call | solution.py:447
  (42 shorter events, 5.3 us)
Async XLA Ops:
  0.0 0.7 copy-start.2
  0.7 0.9 %copy-start = (f32[4,128,128]{2,1,0:T(8,128)S(1)}, f32[4,128,128]{2,1,0:T(8,128)}, u32[]{:S(2)}) copy-start(f32[4,128,128]{2,1,0:T(8,128)} %updates.1) | copy-start | bytes 786436
  3.4 7.0 %collective-permute-start.1 = (f32[520,128]{1,0:T(8,128)S(1)}, f32[520,128]{1,0:T(8,128)S(1)}, u32[]{:S(2)}, u32[]{:S(2)}) collective-permute-start(f32[520,128]{1,0:T(8,128)S(1)} %get-tuple-element.19.diag), channel_id=1, source_target_pairs={{0,4},{1,5}} | collective-permute-start | bytes 798728 | tf_op jit(solution)/shard_map/ppermute | solution.py:471
  4.1 26.9 %collective-permute-start = (f32[512,256]{1,0:T(8,128)}, f32[512,256]{1,0:T(8,128)S(1)}, u32[]{:S(2)}, u32[]{:S(2)}) collective-permute-start(f32[512,256]{1,0:T(8,128)} %refs_0_.1), channel_id=1, source_target_pairs={{2,10},{3,11},{4,20},{5,21},{6,30},{7,31},{8,14},{9,15},{16,18},{1... | collective-permute-start | bytes 1572872 | tf_op jit(solution)/shard_map/ppermute | solution.py:471
  4.8 6.9 %collective-permute-start.6 = (f32[272,128]{1,0:T(8,128)S(1)}, f32[272,128]{1,0:T(8,128)S(1)}, u32[]{:S(2)}, u32[]{:S(2)}) collective-permute-start(f32[272,128]{1,0:T(8,128)S(1)} %get-tuple-element.20.refs_0_.refs_11_), channel_id=1, source_target_pairs={{0,1},{1,0},{2,3},{3,2},{4,5},{5,4},{6,7},{7,6},{8,9},{9,8},{10,11... | collective-permute-start | bytes 417800 | tf_op jit(solution)/shard_map/ppermute | solution.py:471
  5.6 6.8 %collective-permute-start.5 = (f32[272,128]{1,0:T(8,128)S(1)}, f32[272,128]{1,0:T(8,128)S(1)}, u32[]{:S(2)}, u32[]{:S(2)}) collective-permute-start(f32[272,128]{1,0:T(8,128)S(1)} %get-tuple-element.20.refs_0_.refs_11_), channel_id=1, source_target_pairs={{0,6},{1,7},{2,4},{3,5},{4,2},{5,3},{6,0},{7,1},{8,14},{9,15},{10,... | collective-permute-start | bytes 417800 | tf_op jit(solution)/shard_map/ppermute | solution.py:471
  6.4 22.3 %collective-permute-start.4 = (f32[272,128]{1,0:T(8,128)S(1)}, f32[272,128]{1,0:T(8,128)S(1)}, u32[]{:S(2)}, u32[]{:S(2)}) collective-permute-start(f32[272,128]{1,0:T(8,128)S(1)} %get-tuple-element.20.refs_0_.refs_11_), channel_id=1, source_target_pairs={{0,4},{1,5},{2,6},{3,7},{4,0},{5,1},{6,2},{7,3},{8,12},{9,13},{10,... | collective-permute-start | bytes 417800 | tf_op jit(solution)/shard_map/ppermute | solution.py:471
  10.5 19.2 %collective-permute-start.3 = (f32[272,128]{1,0:T(8,128)S(1)}, f32[272,128]{1,0:T(8,128)S(1)}, u32[]{:S(2)}, u32[]{:S(2)}) collective-permute-start(f32[272,128]{1,0:T(8,128)S(1)} %get-tuple-element.20.refs_0_.refs_11_), channel_id=1, source_target_pairs={{0,2},{1,3},{2,0},{3,1},{4,6},{5,7},{6,4},{7,5},{8,10},{9,11},{10,... | collective-permute-start | bytes 417800 | tf_op jit(solution)/shard_map/ppermute | solution.py:471
  11.7 19.3 %collective-permute-start.2 = (f32[520,128]{1,0:T(8,128)S(1)}, f32[520,128]{1,0:T(8,128)S(1)}, u32[]{:S(2)}, u32[]{:S(2)}) collective-permute-start(f32[520,128]{1,0:T(8,128)S(1)} %broadcast_select_fusion), channel_id=1, source_target_pairs={{0,2},{1,3},{4,6},{5,7}} | collective-permute-start | bytes 798728 | tf_op jit(solution)/shard_map/ppermute | solution.py:471
  12.4 17.2 %collective-permute-start.9 = (f32[272,128]{1,0:T(8,128)S(1)}, f32[272,128]{1,0:T(8,128)S(1)}, u32[]{:S(2)}, u32[]{:S(2)}) collective-permute-start(f32[272,128]{1,0:T(8,128)S(1)} %collective-permute-done.5.refs_3_.refs_14_), channel_id=1, source_target_pairs={{0,1},{1,0},{2,3},{3,2},{4,5},{5,4},{6,7},{7,6},{8,9},{9,8},{10,11... | collective-permute-start | bytes 417800 | tf_op jit(solution)/shard_map/ppermute | solution.py:471
  28.6 2.0 %collective-permute-start.8 = (f32[272,128]{1,0:T(8,128)S(1)}, f32[272,128]{1,0:T(8,128)S(1)}, u32[]{:S(2)}, u32[]{:S(2)}) collective-permute-start(f32[272,128]{1,0:T(8,128)S(1)} %collective-permute-done.4.refs_2_.refs_13_), channel_id=1, source_target_pairs={{0,1},{1,0},{2,3},{3,2},{4,5},{5,4},{6,7},{7,6},{8,9},{9,8},{10,11... | collective-permute-start | bytes 417800 | tf_op jit(solution)/shard_map/ppermute | solution.py:471
  29.7 1.4 %collective-permute-start.7 = (f32[272,128]{1,0:T(8,128)S(1)}, f32[272,128]{1,0:T(8,128)S(1)}, u32[]{:S(2)}, u32[]{:S(2)}) collective-permute-start(f32[272,128]{1,0:T(8,128)S(1)} %collective-permute-done.3.refs_1_.refs_12_), channel_id=1, source_target_pairs={{0,1},{1,0},{2,3},{3,2},{4,5},{5,4},{6,7},{7,6},{8,9},{9,8},{10,11... | collective-permute-start | bytes 417800 | tf_op jit(solution)/shard_map/ppermute | solution.py:471
  32.1 13.3 %collective-permute-start.17 = (f32[520,128]{1,0:T(8,128)S(1)}, f32[520,128]{1,0:T(8,128)S(1)}, u32[]{:S(2)}, u32[]{:S(2)}) collective-permute-start(f32[520,128]{1,0:T(8,128)S(1)} %get-tuple-element.25), channel_id=1, source_target_pairs={{0,24},{1,25},{2,26},{3,27},{4,28},{5,29},{6,30},{7,31}} | collective-permute-start | bytes 798728 | tf_op jit(solution)/shard_map/ppermute | solution.py:471
  32.8 19.7 %collective-permute-start.10 = (f32[512,256]{1,0:T(8,128)S(1)}, f32[512,256]{1,0:T(8,128)}, u32[]{:S(2)}, u32[]{:S(2)}) collective-permute-start(f32[512,256]{1,0:T(8,128)S(1)} %collective-permute-done.direct), channel_id=1, source_target_pairs={{10,12},{11,13},{20,22},{21,23},{30,28},{31,29}} | collective-permute-start | bytes 1572872 | tf_op jit(solution)/shard_map/ppermute | solution.py:471
  34.1 12.0 %collective-permute-start.16 = (f32[520,128]{1,0:T(8,128)S(1)}, f32[520,128]{1,0:T(8,128)}, u32[]{:S(2)}, u32[]{:S(2)}) collective-permute-start(f32[520,128]{1,0:T(8,128)S(1)} %get-tuple-element.25), channel_id=1, source_target_pairs={{0,16},{1,17},{2,18},{3,19},{4,20},{5,21},{6,22},{7,23}} | collective-permute-start | bytes 798728 | tf_op jit(solution)/shard_map/ppermute | solution.py:471
  35.5 11.3 %collective-permute-start.15 = (f32[520,128]{1,0:T(8,128)S(1)}, f32[520,128]{1,0:T(8,128)}, u32[]{:S(2)}, u32[]{:S(2)}) collective-permute-start(f32[520,128]{1,0:T(8,128)S(1)} %get-tuple-element.25), channel_id=1, source_target_pairs={{0,8},{1,9},{2,10},{3,11},{4,12},{5,13},{6,14},{7,15}} | collective-permute-start | bytes 798728 | tf_op jit(solution)/shard_map/ppermute | solution.py:471
  36.8 39.5 %all-to-all-start = ((f32[8,136,128]{2,1,0:T(8,128)}), f32[8,136,128]{2,1,0:T(8,128)S(1)}, u32[]{:S(2)}, u32[]{:S(2)}) async-start(f32[8,136,128]{2,1,0:T(8,128)} %get-tuple-element.23), calls=%async_computation | async-start | bytes 1114112 | tf_op jit(solution)/shard_map/all_to_all | solution.py:516
  44.1 29.7 %collective-permute-start.14 = (f32[256,512]{1,0:T(8,128)S(1)}, f32[256,512]{1,0:T(8,128)S(1)}, u32[]{:S(2)}, u32[]{:S(2)}) collective-permute-start(f32[256,512]{1,0:T(8,128)S(1)} %get-tuple-element.24.refs_4_), channel_id=1, source_target_pairs={{10,18},{11,19},{20,12},{21,13},{30,6},{31,7}} | collective-permute-start | bytes 1572872 | tf_op jit(solution)/shard_map/ppermute | solution.py:471
  45.4 29.2 %collective-permute-start.13 = (f32[256,512]{1,0:T(8,128)S(1)}, f32[256,512]{1,0:T(8,128)S(1)}, u32[]{:S(2)}, u32[]{:S(2)}) collective-permute-start(f32[256,512]{1,0:T(8,128)S(1)} %get-tuple-element.24.refs_4_), channel_id=1, source_target_pairs={{10,26},{11,27},{20,4},{21,5},{30,14},{31,15}} | collective-permute-start | bytes 1572872 | tf_op jit(solution)/shard_map/ppermute | solution.py:471
  46.1 29.3 %collective-permute-start.12 = (f32[256,512]{1,0:T(8,128)S(1)}, f32[256,512]{1,0:T(8,128)S(1)}, u32[]{:S(2)}, u32[]{:S(2)}) collective-permute-start(f32[256,512]{1,0:T(8,128)S(1)} %get-tuple-element.24.refs_4_), channel_id=1, source_target_pairs={{10,2},{11,3},{20,28},{21,29},{30,22},{31,23}} | collective-permute-start | bytes 1572872 | tf_op jit(solution)/shard_map/ppermute | solution.py:471
  47.9 9.1 %collective-permute-start.18 = (f32[520,128]{1,0:T(8,128)S(1)}, f32[520,128]{1,0:T(8,128)S(1)}, u32[]{:S(2)}, u32[]{:S(2)}) collective-permute-start(f32[520,128]{1,0:T(8,128)S(1)} %add_select_fusion.1.here), channel_id=1, source_target_pairs={{0,1},{1,0},{2,3},{3,2},{4,5},{5,4},{6,7},{7,6},{8,9},{9,8},{10,11... | collective-permute-start | bytes 798728 | tf_op jit(solution)/shard_map/ppermute | solution.py:471
  53.6 22.6 %collective-permute-start.11 = (f32[512,256]{1,0:T(8,128)S(1)}, f32[512,256]{1,0:T(8,128)S(1)}, u32[]{:S(2)}, u32[]{:S(2)}) collective-permute-start(f32[512,256]{1,0:T(8,128)S(1)} %add_select_fusion.refs_2_), channel_id=1, source_target_pairs={{0,1},{1,0},{2,3},{3,2},{4,5},{5,4},{6,7},{7,6},{8,9},{9,8},{10,11... | collective-permute-start | bytes 1572872 | tf_op jit(solution)/shard_map/ppermute | solution.py:471
  72.4 0.7 copy-start.9
  73.1 0.7 copy-start.11
  73.8 0.8 copy-start.3
  74.6 0.8 copy-start.5
  75.4 0.8 copy-start.7
  76.2 1.0 %copy-start.4 = (f32[256,512]{1,0:T(8,128)S(1)}, f32[256,512]{1,0:T(8,128)}, u32[]{:S(2)}) copy-start(f32[256,512]{1,0:T(8,128)} %copy-done.3) | copy-start | bytes 1572868
  77.3 1.0 %copy-start.6 = (f32[256,512]{1,0:T(8,128)S(1)}, f32[256,512]{1,0:T(8,128)}, u32[]{:S(2)}) copy-start(f32[256,512]{1,0:T(8,128)} %copy-done.5) | copy-start | bytes 1572868
  78.3 1.0 %copy-start.8 = (f32[256,512]{1,0:T(8,128)S(1)}, f32[256,512]{1,0:T(8,128)}, u32[]{:S(2)}) copy-start(f32[256,512]{1,0:T(8,128)} %copy-done.7) | copy-start | bytes 1572868
  79.4 0.9 %copy-start.10 = (f32[256,256]{1,0:T(8,128)S(1)}, f32[256,256]{1,0:T(8,128)}, u32[]{:S(2)}) copy-start(f32[256,256]{1,0:T(8,128)} %copy-done.9) | copy-start | bytes 786436
  80.3 0.9 %copy-start.12 = (f32[256,256]{1,0:T(8,128)S(1)}, f32[256,256]{1,0:T(8,128)}, u32[]{:S(2)}) copy-start(f32[256,256]{1,0:T(8,128)} %copy-done.11) | copy-start | bytes 786436
  (1 other events, 0.7 us)

commit v8 on v7

--- a/solution.py
+++ b/solution.py
@@ -286,40 +286,43 @@
         pay_ref[2 * tile + 8 * o : 2 * tile + 8 * o + 8, :] = out_ref[o, tile:, :]
 
 
-def rows_kernel(info, front, direct, diag, hop1, hop2, *refs):
-    blocks, (diag_ref, out_ref, band, part) = refs[:8], refs[8:]
-    width = front.shape[1]
-    tile = width // 2
-    group, layer, core = info[0], info[1], info[2]
-
-    @pl.when((group == 0) | (group == layer))
+def diagonal_kernel(info, diag, hop1, hop2, *refs):
+    blocks, (diag_ref, band, part) = refs[:8], refs[8:]
+    tile = diag.shape[1]
+    width = 2 * tile
+
+    @pl.when(info[0] == 0)
     def _():
         band[...] = jnp.zeros_like(band)
         add_band_blocks(band, blocks, width)
-
-    @pl.when(group == 0)
-    def _():
         for z, d in enumerate((diag, hop2, hop1, hop2)):
 
-            @pl.when(layer == z)
+            @pl.when(info[1] == z)
             def _(d=d):
                 diag_ref[...] = d[...]
 
-        @pl.when(core == 0)
+        @pl.when(info[2] == 0)
         def _():
             pack(part, symmetric(band[:width, :width]))
             put_rows(part, width + 8, band[width : width + tile, :width])
 
-        @pl.when(core == 1)
+        @pl.when(info[2] == 1)
         def _():
             pack(part, symmetric(band[width:, width:]))
             put_rows(part, width + 8, band[width + tile :, :width])
 
         diag_ref[...] += part[...]
 
-    @pl.when((group == layer) & (group > 0))
-    def _():
-        start = pl.multiple_of(core * width, width)
+
+def matched_kernel(info, direct, *refs):
+    blocks, (out_ref, band) = refs[:8], refs[8:]
+    width = direct.shape[1]
+
+    @pl.when((info[0] == info[1]) & (info[0] > 0))
+    def _():
+        band[...] = jnp.zeros_like(band)
+        add_band_blocks(band, blocks, width)
+        start = pl.multiple_of(info[2] * width, width)
         out_ref[...] = direct[...].T + band[pl.ds(start, width), :]
 
 
@@ -438,9 +441,11 @@
 
 
 def kernel(body, outs, args, smem=1, scratch=(), flops=1 << 20, sems=(), away=False):
-    space = pl.ANY if away else pltpu.VMEM
+    space = pltpu.HBM if away else pltpu.VMEM
     spec = [pl.BlockSpec(memory_space=pltpu.SMEM)] * smem
     spec += [pl.BlockSpec(memory_space=space)] * (len(args) - smem)
+    if away:
+        args = args[:smem] + tuple(pltpu.with_memory_space_constraint(a, pltpu.HBM) for a in args[smem:])
     sizes = [o.size for o in jax.tree.leaves(outs)] + [math.prod(s) for s in scratch]
     if not away:
         sizes += [a.size for a in args[smem:]]
@@ -490,12 +495,12 @@
     for s in layers[1:]:
         pairs = [(dev(g, z, c), dev(g, z ^ s, c)) for g in groups for z in layers for c in both]
         blocks.append(send(payload, pairs))
+    early, *blocks = lax.optimization_barrier((front, *blocks))
     blocks += [send(b, swap) for b in blocks]
     hop1 = send(diag, [(dev(0, 0, c), dev(0, 2, c)) for c in both])
     hop2 = send(
         jnp.where(layer == 0, diag, hop1), [(dev(0, z, c), dev(0, z + 1, c)) for z in (0, 2) for c in both]
     )
-    early, info = lax.optimization_barrier((front, info))
     direct = send(
         early,
         [(dev(0, z, c), dev(z, z, c)) for z in layers[1:] for c in both]
@@ -506,24 +511,28 @@
         [(dev(g, z, c), dev(g, y, c)) for g, z, y in ((1, 1, 2), (2, 2, 3), (3, 3, 2)) for c in both],
     )
 
-    diag, matched = kernel(
-        rows_kernel,
-        (packed, out(width, 2 * width)),
-        (info, front, direct, diag, hop1, hop2, *blocks),
+    diag = kernel(
+        diagonal_kernel,
+        packed,
+        (info, diag, hop1, hop2, *blocks),
         scratch=[(nrows, 2 * width), packed.shape],
     )
     diag, outgoing = lax.optimization_barrier((diag, outgoing))
-    arrived = lax.all_to_all(outgoing, "front", split_axis=0, concat_axis=0, tiled=True)
     got = [
         send(diag, [(dev(0, z, c), dev(s, z, c)) for z in layers for c in both]) for s in groups[1:]
     ]
+    arrived = lax.all_to_all(outgoing, "front", split_axis=0, concat_axis=0, tiled=True)
+    diag = jnp.where(group == 0, diag, got[0] + got[1] + got[2])
+    diag2 = send(diag, swap)
+
+    rows, diag = lax.optimization_barrier((direct, diag))
+    matched = kernel(
+        matched_kernel, out(width, 2 * width), (info, rows, *blocks), scratch=[(nrows, 2 * width)]
+    )
     away = [
         send(matched, [(dev(z, z, c), dev(z ^ s, z, c)) for z in layers[1:] for c in both])
         for s in groups[1:]
     ]
-    diag = jnp.where(group == 0, diag, got[0] + got[1] + got[2])
-    diag2 = send(diag, swap)
-
     piece = jnp.where(layer == 0, front, direct + on)
     piece2 = send(piece, swap)
 

time: 88.9 us -> 88.7 us (level)
  the two profiles are of different devices: /device:TPU:19 before, /device:TPU:21 now
where the time goes in v8:
time: 88.7 us; the launch traced here: 88.2 us
  starting transfers between devices  34.2 us (39%)
  Pallas kernels  26.1 us (29%)
  waiting for transfers between devices  19.9 us (22%)
  local copies, waits for them, and re-layouts  5.39 us (6%)
  other arithmetic  2.22 us (3%)
    ppermute x19, starting transfers between devices, send(): return lax.ppermute(x, AXES, pairs)  26.3 us
    pallas_call x5, Pallas kernels, kernel(): pl.pallas_call(body, out_shape=outs, in_specs=spec, scratch_shapes=[pltpu...  26.1 us
    ppermute x19, waiting for transfers between devices, send(): return lax.ppermute(x, AXES, pairs)  19.9 us
    all_to_all x1, starting transfers between devices, aligned(): lax.all_to_all(outgoing, 'front', split_axis=0, concat_axis=0, tiled=True)  7.92 us
    unnamed x40, local copies, waits for them, and re-layouts  5.31 us
  transfers between devices with their start and end apart: 20, of which 7 were waited for; matrix products, arithmetic and copies ran while one was open for 3% of the time, Pallas kernels for 19%

profile of v8, /device:TPU:21, one launch (start us, length us, event | category | flops | bytes accessed | tf_op | source)
XLA Modules:
  0.0 88.2 jit_solution(9789726410761340033)
XLA Ops:
  0.1 0.6 copy-done.9
  0.7 2.4 %shard_map.46 = (f32[8,136,128]{2,1,0:T(8,128)}, f32[272,128]{1,0:T(8,128)S(1)}, f32[520,128]{1,0:T(8,128)S(1)}) custom-call(s32[4]{0:T(128)S(1)} %copy-done.9, s32[4]{0:T(128)S(1)} %copy-done.10, s32[5]{0:T(128)S(1)} %stack.23.info, f32[4,128,128]{2,1,0:T(8,128)} %updates.1, f32[512,256]{1,0:T(8,128)} %refs_0_.1), custom_call_target="tpu_custom_call" | custom-call | flops 1048576 | bytes 1048576 | tf_op jit(solution)/shard_map/pallas_call | solution.py:452
  3.1 0.7 collective-permute-start
  4.0 3.2 %collective-permute-start.3 = (f32[272,128]{1,0:T(8,128)S(1)}, f32[272,128]{1,0:T(8,128)S(1)}, u32[]{:S(2)}, u32[]{:S(2)}) collective-permute-start(f32[272,128]{1,0:T(8,128)S(1)} %get-tuple-element.22.refs_0_.refs_11_), channel_id=1, source_target_pairs={{0,4},{1,5},{2,6},{3,7},{4,0},{5,1},{6,2},{7,3},{8,12},{9,13},{10,... | collective-permute-start | bytes 417800 | tf_op jit(solution)/shard_map/ppermute | solution.py:476
  7.2 4.9 %collective-permute-done.4.refs_3_.refs_14_ = f32[272,128]{1,0:T(8,128)S(1)} collective-permute-done((f32[272,128]{1,0:T(8,128)S(1)}, f32[272,128]{1,0:T(8,128)S(1)}, u32[]{:S(2)}, u32[]{:S(2)}) %collective-permute-start.4) | collective-permute-done | bytes 139296 | tf_op jit(solution)/shard_map/ppermute | solution.py:476
  12.1 3.4 %collective-permute-done.3.refs_2_.refs_13_ = f32[272,128]{1,0:T(8,128)S(1)} collective-permute-done((f32[272,128]{1,0:T(8,128)S(1)}, f32[272,128]{1,0:T(8,128)S(1)}, u32[]{:S(2)}, u32[]{:S(2)}) %collective-permute-start.3) | collective-permute-done | bytes 139296 | tf_op jit(solution)/shard_map/ppermute | solution.py:476
  15.5 1.3 %collective-permute-start.9 = (f32[512,256]{1,0:T(8,128)S(1)}, f32[512,256]{1,0:T(8,128)S(1)}, u32[]{:S(2)}, u32[]{:S(2)}) collective-permute-start(f32[512,256]{1,0:T(8,128)S(1)} %copy-done.14), channel_id=1, source_target_pairs={{2,10},{3,11},{4,20},{5,21},{6,30},{7,31},{8,14},{9,15},{16,18},{1... | collective-permute-start | bytes 1572872 | tf_op jit(solution)/shard_map/ppermute | solution.py:476
  16.8 1.7 %collective-permute-start.5 = (f32[272,128]{1,0:T(8,128)S(1)}, f32[272,128]{1,0:T(8,128)S(1)}, u32[]{:S(2)}, u32[]{:S(2)}) collective-permute-start(f32[272,128]{1,0:T(8,128)S(1)} %get-tuple-element.22.refs_0_.refs_11_), channel_id=1, source_target_pairs={{0,1},{1,0},{2,3},{3,2},{4,5},{5,4},{6,7},{7,6},{8,9},{9,8},{10,11... | collective-permute-start | bytes 417800 | tf_op jit(solution)/shard_map/ppermute | solution.py:476
  18.5 0.7 collective-permute-start.1
  19.8 0.8 collective-permute-done.6.refs_5_.refs_16_
  21.7 0.7 collective-permute-start.14
  22.4 1.3 %collective-permute-start.13 = (f32[520,128]{1,0:T(8,128)S(1)}, f32[520,128]{1,0:T(8,128)S(1)}, u32[]{:S(2)}, u32[]{:S(2)}) collective-permute-start(f32[520,128]{1,0:T(8,128)S(1)} %shard_map.47), channel_id=1, source_target_pairs={{0,16},{1,17},{2,18},{3,19},{4,20},{5,21},{6,22},{7,23}} | collective-permute-start | bytes 798728 | tf_op jit(solution)/shard_map/ppermute | solution.py:476
  23.7 1.4 %collective-permute-start.12 = (f32[520,128]{1,0:T(8,128)S(1)}, f32[520,128]{1,0:T(8,128)}, u32[]{:S(2)}, u32[]{:S(2)}) collective-permute-start(f32[520,128]{1,0:T(8,128)S(1)} %shard_map.47), channel_id=1, source_target_pairs={{0,8},{1,9},{2,10},{3,11},{4,12},{5,13},{6,14},{7,15}} | collective-permute-start | bytes 798728 | tf_op jit(solution)/shard_map/ppermute | solution.py:476
  25.0 5.2 %collective-permute-done.9.direct = f32[512,256]{1,0:T(8,128)S(1)} collective-permute-done((f32[512,256]{1,0:T(8,128)S(1)}, f32[512,256]{1,0:T(8,128)S(1)}, u32[]{:S(2)}, u32[]{:S(2)}) %collective-permute-start.9) | collective-permute-done | bytes 524320 | tf_op jit(solution)/shard_map/ppermute | solution.py:476
  30.2 2.1 %collective-permute-start.10 = (f32[512,256]{1,0:T(8,128)S(1)}, f32[512,256]{1,0:T(8,128)}, u32[]{:S(2)}, u32[]{:S(2)}) collective-permute-start(f32[512,256]{1,0:T(8,128)S(1)} %collective-permute-done.9.direct), channel_id=1, source_target_pairs={{10,12},{11,13},{20,22},{21,23},{30,28},{31,29}} | collective-permute-start | bytes 1572872 | tf_op jit(solution)/shard_map/ppermute | solution.py:476
  32.3 7.9 %all-to-all-start = ((f32[8,136,128]{2,1,0:T(8,128)}), f32[8,136,128]{2,1,0:T(8,128)S(1)}, u32[]{:S(2)}, u32[]{:S(2)}) async-start(f32[8,136,128]{2,1,0:T(8,128)} %get-tuple-element.27), calls=%async_computation | async-start | bytes 1114112 | tf_op jit(solution)/shard_map/all_to_all | solution.py:524
  40.2 5.1 %collective-permute-done.13 = f32[520,128]{1,0:T(8,128)S(1)} collective-permute-done((f32[520,128]{1,0:T(8,128)S(1)}, f32[520,128]{1,0:T(8,128)S(1)}, u32[]{:S(2)}, u32[]{:S(2)}) %collective-permute-start.13) | collective-permute-done | bytes 266272 | tf_op jit(solution)/shard_map/ppermute | solution.py:476
  45.4 1.0 %add_select_fusion.1.here = f32[520,128]{1,0:T(8,128)S(1)} fusion(f32[520,128]{1,0:T(8,128)S(1)} %shard_map.47, f32[520,128]{1,0:T(8,128)S(1)} %collective-permute-done.14, f32[520,128]{1,0:T(8,128)} %collective-permute-done.12, f32[520,128]{1,0:T(8,128)S(1)} %collective-permute-done.13, pred[]{:T(512)S(6)} %eq.10), kind=kLoop, calls=%fused_computation.1 | loop fusion | flops 199680 | bytes 1331201 | tf_op jit(solution)/shard_map/jit(_where)/select_n | solution.py:525
  46.4 1.4 %collective-permute-start.18 = (f32[520,128]{1,0:T(8,128)S(1)}, f32[520,128]{1,0:T(8,128)S(1)}, u32[]{:S(2)}, u32[]{:S(2)}) collective-permute-start(f32[520,128]{1,0:T(8,128)S(1)} %add_select_fusion.1.here), channel_id=1, source_target_pairs={{0,1},{1,0},{2,3},{3,2},{4,5},{5,4},{6,7},{7,6},{8,9},{9,8},{10,11... | collective-permute-start | bytes 798728 | tf_op jit(solution)/shard_map/ppermute | solution.py:476
  47.9 1.0 %shard_map.48.refs_4_ = f32[256,512]{1,0:T(8,128)S(1)} custom-call(s32[5]{0:T(128)S(1)} %stack.23.info, f32[512,256]{1,0:T(8,128)S(1)} %collective-permute-done.9.direct, f32[272,128]{1,0:T(8,128)S(1)} %get-tuple-element.22.refs_0_.refs_11_, f32[272,128]{1,0:T(8,128)S(1)} %collective-permute-done.2.refs_1_.refs_12_, ...), custom_call_target="tpu_custom_call" | custom-call | flops 1048576 | bytes 1048576 | tf_op jit(solution)/shard_map/pallas_call | solution.py:452
  48.9 7.2 %collective-permute-start.17 = (f32[256,512]{1,0:T(8,128)S(1)}, f32[256,512]{1,0:T(8,128)S(1)}, u32[]{:S(2)}, u32[]{:S(2)}) collective-permute-start(f32[256,512]{1,0:T(8,128)S(1)} %shard_map.48.refs_4_), channel_id=1, source_target_pairs={{10,18},{11,19},{20,12},{21,13},{30,6},{31,7}} | collective-permute-start | bytes 1572872 | tf_op jit(solution)/shard_map/ppermute | solution.py:476
  56.1 1.3 %collective-permute-start.16 = (f32[256,512]{1,0:T(8,128)S(1)}, f32[256,512]{1,0:T(8,128)S(1)}, u32[]{:S(2)}, u32[]{:S(2)}) collective-permute-start(f32[256,512]{1,0:T(8,128)S(1)} %shard_map.48.refs_4_), channel_id=1, source_target_pairs={{10,26},{11,27},{20,4},{21,5},{30,14},{31,15}} | collective-permute-start | bytes 1572872 | tf_op jit(solution)/shard_map/ppermute | solution.py:476
  57.4 2.1 %collective-permute-start.15 = (f32[256,512]{1,0:T(8,128)S(1)}, f32[256,512]{1,0:T(8,128)}, u32[]{:S(2)}, u32[]{:S(2)}) collective-permute-start(f32[256,512]{1,0:T(8,128)S(1)} %shard_map.48.refs_4_), channel_id=1, source_target_pairs={{10,2},{11,3},{20,28},{21,29},{30,22},{31,23}} | collective-permute-start | bytes 1572872 | tf_op jit(solution)/shard_map/ppermute | solution.py:476
  59.5 1.2 %add_select_fusion.refs_2_ = f32[512,256]{1,0:T(8,128)S(1)} fusion(f32[512,256]{1,0:T(8,128)S(1)} %copy-done.14, f32[512,256]{1,0:T(8,128)S(1)} %collective-permute-done.9.direct, f32[512,256]{1,0:T(8,128)} %collective-permute-done.10, pred[]{:T(512)S(6)} %eq.9), kind=kLoop, calls=%fused_computation | loop fusion | flops 262144 | bytes 2097153 | tf_op jit(solution)/shard_map/jit(_where)/select_n | solution.py:536
  61.1 15.4 %shard_map.49 = (f32[256,256]{1,0:T(8,128)S(1)}, f32[256,256]{1,0:T(8,128)S(1)}, f32[256,256]{1,0:T(8,128)S(1)}) custom-call(s32[5]{0:T(128)S(1)} %stack.23.info, f32[520,128]{1,0:T(8,128)S(1)} %add_select_fusion.1.here, f32[520,128]{1,0:T(8,128)S(1)} %collective-permute-done.18.there), custom_call_target="tpu_custom_call" | custom-call | flops 8589934592 | bytes 1048576 | tf_op jit(solution)/shard_map/pallas_call | solution.py:452
  76.6 0.7 copy-done.11
  77.2 0.7 copy-done.12
  78.0 0.7 copy-done.13
  78.7 0.8 copy-done.17
  79.5 0.8 copy-done.18
  80.3 0.8 copy-done.15
  81.3 6.8 %shard_map.50 = f32[512,256]{1,0:T(8,128)} custom-call(s32[5]{0:T(128)S(1)} %stack.23.info, f32[512,256]{1,0:T(8,128)} %refs_0_.1, f32[8,136,128]{2,1,0:T(8,128)} %copy-done.15, f32[512,256]{1,0:T(8,128)} %copy-done.16, f32[512,256]{1,0:T(8,128)} %copy-done.19, f32[256,512]{1,0:T(8,128)} %copy-done.8, f32[256,512]{1,0:T(8,128)} %collective-permute-done.15.refs_5_, ...), custom_call_target="tpu_custom_call" | custom-call | flops 2147483648 | bytes 1048576 | tf_op jit(solution)/shard_map/pallas_call | solution.py:452
  (57 shorter events, 2.7 us)
Async XLA Ops:
  0.0 15.5 %copy-start.14 = (f32[512,256]{1,0:T(8,128)S(1)}, f32[512,256]{1,0:T(8,128)}, u32[]{:S(2)}) copy-start(f32[512,256]{1,0:T(8,128)} %refs_0_.1) | copy-start | bytes 1572868
  3.1 44.8 %copy-start = (f32[272,128]{1,0:T(8,128)}, f32[272,128]{1,0:T(8,128)S(1)}, u32[]{:S(2)}) copy-start(f32[272,128]{1,0:T(8,128)S(1)} %get-tuple-element.22.refs_0_.refs_11_) | copy-start | bytes 417796
  3.1 15.4 %collective-permute-start = (f32[520,128]{1,0:T(8,128)S(1)}, f32[520,128]{1,0:T(8,128)S(1)}, u32[]{:S(2)}, u32[]{:S(2)}) collective-permute-start(f32[520,128]{1,0:T(8,128)S(1)} %get-tuple-element.20.diag), channel_id=1, source_target_pairs={{0,4},{1,5}} | collective-permute-start | bytes 798728 | tf_op jit(solution)/shard_map/ppermute | solution.py:476
  3.8 8.3 %collective-permute-start.4 = (f32[272,128]{1,0:T(8,128)S(1)}, f32[272,128]{1,0:T(8,128)S(1)}, u32[]{:S(2)}, u32[]{:S(2)}) collective-permute-start(f32[272,128]{1,0:T(8,128)S(1)} %get-tuple-element.22.refs_0_.refs_11_), channel_id=1, source_target_pairs={{0,6},{1,7},{2,4},{3,5},{4,2},{5,3},{6,0},{7,1},{8,14},{9,15},{10,... | collective-permute-start | bytes 417800 | tf_op jit(solution)/shard_map/ppermute | solution.py:476
  4.0 11.5 %collective-permute-start.3 = (f32[272,128]{1,0:T(8,128)S(1)}, f32[272,128]{1,0:T(8,128)S(1)}, u32[]{:S(2)}, u32[]{:S(2)}) collective-permute-start(f32[272,128]{1,0:T(8,128)S(1)} %get-tuple-element.22.refs_0_.refs_11_), channel_id=1, source_target_pairs={{0,4},{1,5},{2,6},{3,7},{4,0},{5,1},{6,2},{7,3},{8,12},{9,13},{10,... | collective-permute-start | bytes 417800 | tf_op jit(solution)/shard_map/ppermute | solution.py:476
  7.2 8.3 %collective-permute-start.2 = (f32[272,128]{1,0:T(8,128)S(1)}, f32[272,128]{1,0:T(8,128)S(1)}, u32[]{:S(2)}, u32[]{:S(2)}) collective-permute-start(f32[272,128]{1,0:T(8,128)S(1)} %get-tuple-element.22.refs_0_.refs_11_), channel_id=1, source_target_pairs={{0,2},{1,3},{2,0},{3,1},{4,6},{5,7},{6,4},{7,5},{8,10},{9,11},{10,... | collective-permute-start | bytes 417800 | tf_op jit(solution)/shard_map/ppermute | solution.py:476
  12.1 35.8 %copy-start.1 = (f32[272,128]{1,0:T(8,128)}, f32[272,128]{1,0:T(8,128)S(1)}, u32[]{:S(2)}) copy-start(f32[272,128]{1,0:T(8,128)S(1)} %collective-permute-done.4.refs_3_.refs_14_) | copy-start | bytes 417796
  15.5 32.4 %copy-start.2 = (f32[272,128]{1,0:T(8,128)}, f32[272,128]{1,0:T(8,128)S(1)}, u32[]{:S(2)}) copy-start(f32[272,128]{1,0:T(8,128)S(1)} %collective-permute-done.3.refs_2_.refs_13_) | copy-start | bytes 417796
  15.5 32.4 %copy-start.3 = (f32[272,128]{1,0:T(8,128)}, f32[272,128]{1,0:T(8,128)S(1)}, u32[]{:S(2)}) copy-start(f32[272,128]{1,0:T(8,128)S(1)} %collective-permute-done.2.refs_1_.refs_12_) | copy-start | bytes 417796
  15.5 14.7 %collective-permute-start.9 = (f32[512,256]{1,0:T(8,128)S(1)}, f32[512,256]{1,0:T(8,128)S(1)}, u32[]{:S(2)}, u32[]{:S(2)}) collective-permute-start(f32[512,256]{1,0:T(8,128)S(1)} %copy-done.14), channel_id=1, source_target_pairs={{2,10},{3,11},{4,20},{5,21},{6,30},{7,31},{8,14},{9,15},{16,18},{1... | collective-permute-start | bytes 1572872 | tf_op jit(solution)/shard_map/ppermute | solution.py:476
  16.8 3.0 %collective-permute-start.5 = (f32[272,128]{1,0:T(8,128)S(1)}, f32[272,128]{1,0:T(8,128)S(1)}, u32[]{:S(2)}, u32[]{:S(2)}) collective-permute-start(f32[272,128]{1,0:T(8,128)S(1)} %get-tuple-element.22.refs_0_.refs_11_), channel_id=1, source_target_pairs={{0,1},{1,0},{2,3},{3,2},{4,5},{5,4},{6,7},{7,6},{8,9},{9,8},{10,11... | collective-permute-start | bytes 417800 | tf_op jit(solution)/shard_map/ppermute | solution.py:476
  18.5 2.6 %collective-permute-start.1 = (f32[520,128]{1,0:T(8,128)S(1)}, f32[520,128]{1,0:T(8,128)S(1)}, u32[]{:S(2)}, u32[]{:S(2)}) collective-permute-start(f32[520,128]{1,0:T(8,128)S(1)} %broadcast_select_fusion), channel_id=1, source_target_pairs={{0,2},{1,3},{4,6},{5,7}} | collective-permute-start | bytes 798728 | tf_op jit(solution)/shard_map/ppermute | solution.py:476
  19.2 1.4 %collective-permute-start.6 = (f32[272,128]{1,0:T(8,128)S(1)}, f32[272,128]{1,0:T(8,128)S(1)}, u32[]{:S(2)}, u32[]{:S(2)}) collective-permute-start(f32[272,128]{1,0:T(8,128)S(1)} %collective-permute-done.2.refs_1_.refs_12_), channel_id=1, source_target_pairs={{0,1},{1,0},{2,3},{3,2},{4,5},{5,4},{6,7},{7,6},{8,9},{9,8},{10,11... | collective-permute-start | bytes 417800 | tf_op jit(solution)/shard_map/ppermute | solution.py:476
  19.3 1.5 %collective-permute-start.7 = (f32[272,128]{1,0:T(8,128)S(1)}, f32[272,128]{1,0:T(8,128)S(1)}, u32[]{:S(2)}, u32[]{:S(2)}) collective-permute-start(f32[272,128]{1,0:T(8,128)S(1)} %collective-permute-done.3.refs_2_.refs_13_), channel_id=1, source_target_pairs={{0,1},{1,0},{2,3},{3,2},{4,5},{5,4},{6,7},{7,6},{8,9},{9,8},{10,11... | collective-permute-start | bytes 417800 | tf_op jit(solution)/shard_map/ppermute | solution.py:476
  19.7 28.1 %copy-start.4 = (f32[272,128]{1,0:T(8,128)}, f32[272,128]{1,0:T(8,128)S(1)}, u32[]{:S(2)}) copy-start(f32[272,128]{1,0:T(8,128)S(1)} %collective-permute-done.5.refs_4_.refs_15_) | copy-start | bytes 417796
  19.7 1.4 %collective-permute-start.8 = (f32[272,128]{1,0:T(8,128)S(1)}, f32[272,128]{1,0:T(8,128)S(1)}, u32[]{:S(2)}, u32[]{:S(2)}) collective-permute-start(f32[272,128]{1,0:T(8,128)S(1)} %collective-permute-done.4.refs_3_.refs_14_), channel_id=1, source_target_pairs={{0,1},{1,0},{2,3},{3,2},{4,5},{5,4},{6,7},{7,6},{8,9},{9,8},{10,11... | collective-permute-start | bytes 417800 | tf_op jit(solution)/shard_map/ppermute | solution.py:476
  20.6 27.3 %copy-start.5 = (f32[272,128]{1,0:T(8,128)}, f32[272,128]{1,0:T(8,128)S(1)}, u32[]{:S(2)}) copy-start(f32[272,128]{1,0:T(8,128)S(1)} %collective-permute-done.6.refs_5_.refs_16_) | copy-start | bytes 417796
  20.8 27.1 %copy-start.6 = (f32[272,128]{1,0:T(8,128)}, f32[272,128]{1,0:T(8,128)S(1)}, u32[]{:S(2)}) copy-start(f32[272,128]{1,0:T(8,128)S(1)} %collective-permute-done.7.refs_6_.refs_17_) | copy-start | bytes 417796
  21.1 26.8 %copy-start.7 = (f32[272,128]{1,0:T(8,128)}, f32[272,128]{1,0:T(8,128)S(1)}, u32[]{:S(2)}) copy-start(f32[272,128]{1,0:T(8,128)S(1)} %collective-permute-done.8.refs_7_.refs_18_) | copy-start | bytes 417796
  21.7 18.6 %collective-permute-start.14 = (f32[520,128]{1,0:T(8,128)S(1)}, f32[520,128]{1,0:T(8,128)S(1)}, u32[]{:S(2)}, u32[]{:S(2)}) collective-permute-start(f32[520,128]{1,0:T(8,128)S(1)} %shard_map.47), channel_id=1, source_target_pairs={{0,24},{1,25},{2,26},{3,27},{4,28},{5,29},{6,30},{7,31}} | collective-permute-start | bytes 798728 | tf_op jit(solution)/shard_map/ppermute | solution.py:476
  22.4 23.0 %collective-permute-start.13 = (f32[520,128]{1,0:T(8,128)S(1)}, f32[520,128]{1,0:T(8,128)S(1)}, u32[]{:S(2)}, u32[]{:S(2)}) collective-permute-start(f32[520,128]{1,0:T(8,128)S(1)} %shard_map.47), channel_id=1, source_target_pairs={{0,16},{1,17},{2,18},{3,19},{4,20},{5,21},{6,22},{7,23}} | collective-permute-start | bytes 798728 | tf_op jit(solution)/shard_map/ppermute | solution.py:476
  23.7 21.7 %collective-permute-start.12 = (f32[520,128]{1,0:T(8,128)S(1)}, f32[520,128]{1,0:T(8,128)}, u32[]{:S(2)}, u32[]{:S(2)}) collective-permute-start(f32[520,128]{1,0:T(8,128)S(1)} %shard_map.47), channel_id=1, source_target_pairs={{0,8},{1,9},{2,10},{3,11},{4,12},{5,13},{6,14},{7,15}} | collective-permute-start | bytes 798728 | tf_op jit(solution)/shard_map/ppermute | solution.py:476
  30.2 29.3 %collective-permute-start.10 = (f32[512,256]{1,0:T(8,128)S(1)}, f32[512,256]{1,0:T(8,128)}, u32[]{:S(2)}, u32[]{:S(2)}) collective-permute-start(f32[512,256]{1,0:T(8,128)S(1)} %collective-permute-done.9.direct), channel_id=1, source_target_pairs={{10,12},{11,13},{20,22},{21,23},{30,28},{31,29}} | collective-permute-start | bytes 1572872 | tf_op jit(solution)/shard_map/ppermute | solution.py:476
  32.3 48.0 %all-to-all-start = ((f32[8,136,128]{2,1,0:T(8,128)}), f32[8,136,128]{2,1,0:T(8,128)S(1)}, u32[]{:S(2)}, u32[]{:S(2)}) async-start(f32[8,136,128]{2,1,0:T(8,128)} %get-tuple-element.27), calls=%async_computation | async-start | bytes 1114112 | tf_op jit(solution)/shard_map/all_to_all | solution.py:524
  46.4 14.7 %collective-permute-start.18 = (f32[520,128]{1,0:T(8,128)S(1)}, f32[520,128]{1,0:T(8,128)S(1)}, u32[]{:S(2)}, u32[]{:S(2)}) collective-permute-start(f32[520,128]{1,0:T(8,128)S(1)} %add_select_fusion.1.here), channel_id=1, source_target_pairs={{0,1},{1,0},{2,3},{3,2},{4,5},{5,4},{6,7},{7,6},{8,9},{9,8},{10,11... | collective-permute-start | bytes 798728 | tf_op jit(solution)/shard_map/ppermute | solution.py:476
  48.9 11.8 %copy-start.8 = (f32[256,512]{1,0:T(8,128)}, f32[256,512]{1,0:T(8,128)S(1)}, u32[]{:S(2)}) copy-start(f32[256,512]{1,0:T(8,128)S(1)} %shard_map.48.refs_4_) | copy-start | bytes 1572868
  48.9 29.8 %collective-permute-start.17 = (f32[256,512]{1,0:T(8,128)S(1)}, f32[256,512]{1,0:T(8,128)S(1)}, u32[]{:S(2)}, u32[]{:S(2)}) collective-permute-start(f32[256,512]{1,0:T(8,128)S(1)} %shard_map.48.refs_4_), channel_id=1, source_target_pairs={{10,18},{11,19},{20,12},{21,13},{30,6},{31,7}} | collective-permute-start | bytes 1572872 | tf_op jit(solution)/shard_map/ppermute | solution.py:476
  56.1 22.6 %collective-permute-start.16 = (f32[256,512]{1,0:T(8,128)S(1)}, f32[256,512]{1,0:T(8,128)S(1)}, u32[]{:S(2)}, u32[]{:S(2)}) collective-permute-start(f32[256,512]{1,0:T(8,128)S(1)} %shard_map.48.refs_4_), channel_id=1, source_target_pairs={{10,26},{11,27},{20,4},{21,5},{30,14},{31,15}} | collective-permute-start | bytes 1572872 | tf_op jit(solution)/shard_map/ppermute | solution.py:476
  57.4 22.9 %collective-permute-start.15 = (f32[256,512]{1,0:T(8,128)S(1)}, f32[256,512]{1,0:T(8,128)}, u32[]{:S(2)}, u32[]{:S(2)}) collective-permute-start(f32[256,512]{1,0:T(8,128)S(1)} %shard_map.48.refs_4_), channel_id=1, source_target_pairs={{10,2},{11,3},{20,28},{21,29},{30,22},{31,23}} | collective-permute-start | bytes 1572872 | tf_op jit(solution)/shard_map/ppermute | solution.py:476
  60.7 15.8 %copy-start.16 = (f32[512,256]{1,0:T(8,128)}, f32[512,256]{1,0:T(8,128)S(1)}, u32[]{:S(2)}) copy-start(f32[512,256]{1,0:T(8,128)S(1)} %add_select_fusion.refs_2_) | copy-start | bytes 1572868
  60.7 19.6 %collective-permute-start.11 = (f32[512,256]{1,0:T(8,128)S(1)}, f32[512,256]{1,0:T(8,128)S(1)}, u32[]{:S(2)}, u32[]{:S(2)}) collective-permute-start(f32[512,256]{1,0:T(8,128)S(1)} %add_select_fusion.refs_2_), channel_id=1, source_target_pairs={{0,1},{1,0},{2,3},{3,2},{4,5},{5,4},{6,7},{7,6},{8,9},{9,8},{10,11... | collective-permute-start | bytes 1572872 | tf_op jit(solution)/shard_map/ppermute | solution.py:476
  80.3 1.0 %copy-start.19 = (f32[512,256]{1,0:T(8,128)}, f32[512,256]{1,0:T(8,128)S(1)}, u32[]{:S(2)}) copy-start(f32[512,256]{1,0:T(8,128)S(1)} %collective-permute-done.11.refs_3_) | copy-start | bytes 1572868
  (8 other events, 5.9 us)

commit v9 on v8

--- a/solution.py
+++ b/solution.py
@@ -314,19 +314,19 @@
         diag_ref[...] += part[...]
 
 
-def matched_kernel(info, direct, *refs):
+def matched_kernel(info, turned, *refs):
     blocks, (out_ref, band) = refs[:8], refs[8:]
-    width = direct.shape[1]
+    width = turned.shape[1]
 
     @pl.when((info[0] == info[1]) & (info[0] > 0))
     def _():
         band[...] = jnp.zeros_like(band)
         add_band_blocks(band, blocks, width)
         start = pl.multiple_of(info[2] * width, width)
-        out_ref[...] = direct[...].T + band[pl.ds(start, width), :]
-
-
-def factor_kernel(info, here, there, w_ref, l_ref, v_ref, top, bottom):
+        out_ref[...] = turned[...].T + band[pl.ds(start, width), :]
+
+
+def factor_kernel(info, here, there, out_ref, top, bottom, done, sems):
     tile = here.shape[1]
     width = 2 * tile
 
@@ -340,17 +340,24 @@
         top[...] = there[...]
         bottom[...] = here[...]
 
+    w_ref, l_ref = done.at[0], done.at[1]
+    copies = [pltpu.make_async_copy(done.at[i], out_ref.at[i], sems.at[i]) for i in range(3)]
     store_inverse(w_ref, factor_pair(unpack(top)))
+    copies[0].start()
     w = w_ref[...]
     l_ref[:tile, :] = dot_t(get_rows(top, width + 8), w)
     l_ref[tile:, :] = dot_t(get_rows(bottom, width + 8), w)
+    copies[1].start()
     lower = l_ref[...]
-    store_inverse(v_ref, factor_pair(unpack(bottom) - dot_t(lower, lower)))
+    store_inverse(done.at[2], factor_pair(unpack(bottom) - dot_t(lower, lower)))
+    copies[2].start()
+    for c in copies:
+        c.wait()
 
 
 def last_kernel(info, *refs):
-    (shard, arrived, piece, piece2, matched, m1, m2, m3, w, lower, v), blocks = refs[:11], refs[11:19]
-    out_ref, band, line, work, halves, came, pays, tri, sems = refs[19:]
+    (shard, arrived, piece, piece2, matched, m1, m2, m3, factors), blocks = refs[:9], refs[9:17]
+    out_ref, band, line, work, halves, came, pays, tri, sems = refs[17:]
     tile = came.shape[2]
     nrows, width = out_ref.shape
     group, layer, core, column = info[0], info[1], info[2], info[4]
@@ -362,9 +369,7 @@
                 (arrived, came),
                 (piece, halves.at[0]),
                 (piece2, halves.at[1]),
-                (w, tri.at[0]),
-                (lower, tri.at[1]),
-                (v, tri.at[2]),
+                (factors, tri),
             ]
             + [(b, pays.at[i]) for i, b in enumerate(blocks)]
         )
@@ -384,7 +389,7 @@
         add_block(out_ref, came[i, :tile, :], place_of(came[i, tile:, :]), tile)
     copies[2].wait()
     copies[3].wait()
-    by_rows = (layer > 0) & (((group == 1) & (layer < 3)) | ((group > 1) & (layer > 1)))
+    by_rows = (layer > 0) & ((group == 1) | (layer > 1))
     for c in range(2):
         side = jnp.where(core == 0, c, 1 - c)
 
@@ -443,16 +448,18 @@
 def kernel(body, outs, args, smem=1, scratch=(), flops=1 << 20, sems=(), away=False):
     space = pltpu.HBM if away else pltpu.VMEM
     spec = [pl.BlockSpec(memory_space=pltpu.SMEM)] * smem
+    out_space = pltpu.HBM if isinstance(outs, type(pltpu.HBM((8, 128), F32))) else pltpu.VMEM
     spec += [pl.BlockSpec(memory_space=space)] * (len(args) - smem)
     if away:
         args = args[:smem] + tuple(pltpu.with_memory_space_constraint(a, pltpu.HBM) for a in args[smem:])
-    sizes = [o.size for o in jax.tree.leaves(outs)] + [math.prod(s) for s in scratch]
+    sizes = [math.prod(o.shape) for o in jax.tree.leaves(outs)] + [math.prod(s) for s in scratch]
     if not away:
         sizes += [a.size for a in args[smem:]]
     return pl.pallas_call(
         body,
         out_shape=outs,
         in_specs=spec,
+        out_specs=jax.tree.map(lambda o: pl.BlockSpec(memory_space=out_space), outs),
         scratch_shapes=[pltpu.VMEM(s, F32) for s in scratch]
         + [pltpu.SemaphoreType.DMA(s) for s in sems],
         compiler_params=pltpu.CompilerParams(vmem_limit_bytes=4 * sum(sizes) + (6 << 20)),
@@ -495,21 +502,14 @@
     for s in layers[1:]:
         pairs = [(dev(g, z, c), dev(g, z ^ s, c)) for g in groups for z in layers for c in both]
         blocks.append(send(payload, pairs))
-    early, *blocks = lax.optimization_barrier((front, *blocks))
     blocks += [send(b, swap) for b in blocks]
     hop1 = send(diag, [(dev(0, 0, c), dev(0, 2, c)) for c in both])
     hop2 = send(
         jnp.where(layer == 0, diag, hop1), [(dev(0, z, c), dev(0, z + 1, c)) for z in (0, 2) for c in both]
     )
-    direct = send(
-        early,
-        [(dev(0, z, c), dev(z, z, c)) for z in layers[1:] for c in both]
-        + [(dev(g, 0, c), dev(g, z, c)) for g, z in ((1, 3), (2, 1), (3, 1)) for c in both],
-    )
-    on = send(
-        direct,
-        [(dev(g, z, c), dev(g, y, c)) for g, z, y in ((1, 1, 2), (2, 2, 3), (3, 3, 2)) for c in both],
-    )
+    early, outgoing, info = lax.optimization_barrier((front, outgoing, info))
+    turned = send(early, [(dev(0, z, c), dev(z, z, c)) for z in layers[1:] for c in both])
+    diag, turned = lax.optimization_barrier((diag, turned))
 
     diag = kernel(
         diagonal_kernel,
@@ -517,7 +517,7 @@
         (info, diag, hop1, hop2, *blocks),
         scratch=[(nrows, 2 * width), packed.shape],
     )
-    diag, outgoing = lax.optimization_barrier((diag, outgoing))
+    diag, outgoing, early, turned = lax.optimization_barrier((diag, outgoing, early, turned))
     got = [
         send(diag, [(dev(0, z, c), dev(s, z, c)) for z in layers for c in both]) for s in groups[1:]
     ]
@@ -525,25 +525,41 @@
     diag = jnp.where(group == 0, diag, got[0] + got[1] + got[2])
     diag2 = send(diag, swap)
 
-    rows, diag = lax.optimization_barrier((direct, diag))
+    far = send(
+        turned,
+        [(dev(g, z, c), dev(g, y, c)) for g, z, y in ((1, 1, 2), (2, 2, 3), (3, 3, 2)) for c in both],
+    )
+
     matched = kernel(
-        matched_kernel, out(width, 2 * width), (info, rows, *blocks), scratch=[(nrows, 2 * width)]
+        matched_kernel, out(width, 2 * width), (info, turned, *blocks), scratch=[(nrows, 2 * width)]
+    )
+    matched, early, diag = lax.optimization_barrier((matched, early, diag))
+    near = send(
+        early,
+        [(dev(g, 0, c), dev(g, 1, c)) for g in (2, 3) for c in both]
+        + [(dev(0, 1, c), dev(1, 3, c)) for c in both],
     )
     away = [
         send(matched, [(dev(z, z, c), dev(z ^ s, z, c)) for z in layers[1:] for c in both])
         for s in groups[1:]
     ]
-    piece = jnp.where(layer == 0, front, direct + on)
+
+    diag, diag2, far = lax.optimization_barrier((diag, diag2, far))
+    factors = kernel(
+        factor_kernel,
+        pltpu.HBM((3, width, width), F32),
+        (info, diag, diag2),
+        scratch=[packed.shape] * 2 + [(3, width, width)],
+        flops=1 << 33,
+        sems=[(3,)],
+    )
+    factors, near, far = lax.optimization_barrier((factors, near, far))
+    piece = jnp.where(layer == 0, front, jnp.where(group == layer, turned, near + far))
     piece2 = send(piece, swap)
-
-    square = out(width, width)
-    w1, l21, w2 = kernel(
-        factor_kernel, (square,) * 3, (info, diag, diag2), scratch=[packed.shape] * 2, flops=1 << 33
-    )
     return kernel(
         last_kernel,
         out(nrows, width),
-        (info, front, arrived, piece, piece2, matched, *away, w1, l21, w2, *blocks),
+        (info, front, arrived, piece, piece2, matched, *away, factors, *blocks),
         scratch=[
             (nrows, 2 * width),
             (width, 2 * width),

time: 88.7 us -> 84.1 us (0.948)
  the two profiles are of different devices: /device:TPU:21 before, /device:TPU:11 now
where the time goes in v9:
time: 84.1 us; the launch traced here: 82.4 us
  starting transfers between devices  33.8 us (40%)
  Pallas kernels  26.8 us (32%)
  waiting for transfers between devices  16.1 us (19%)
  local copies, waits for them, and re-layouts  3.07 us (4%)
  other arithmetic  2.22 us (3%)
    ppermute x20, starting transfers between devices, send(): return lax.ppermute(x, AXES, pairs)  29.7 us
    pallas_call x5, Pallas kernels, kernel(): pl.pallas_call(body, out_shape=outs, in_specs=spec, out_specs=jax.tree.ma...  26.8 us
    ppermute x20, waiting for transfers between devices, send(): return lax.ppermute(x, AXES, pairs)  16.1 us
    all_to_all x1, starting transfers between devices, aligned(): lax.all_to_all(outgoing, 'front', split_axis=0, concat_axis=0, tiled=True)  4.14 us
    unnamed x32, local copies, waits for them, and re-layouts  2.98 us
  transfers between devices with their start and end apart: 21, of which 6 were waited for; matrix products, arithmetic and copies ran while one was open for 3% of the time, Pallas kernels for 21%

profile of v9, /device:TPU:11, one launch (start us, length us, event | category | flops | bytes accessed | tf_op | source)
XLA Modules:
  0.0 82.4 jit_solution(14521970982360557715)
XLA Ops:
  0.7 2.4 %shard_map.46 = (f32[8,136,128]{2,1,0:T(8,128)}, f32[272,128]{1,0:T(8,128)S(1)}, f32[520,128]{1,0:T(8,128)S(1)}) custom-call(s32[4]{0:T(128)S(1)} %copy-done.9, s32[4]{0:T(128)S(1)} %copy-done.10, s32[5]{0:T(128)S(1)} %stack.23.info, f32[4,128,128]{2,1,0:T(8,128)} %updates.1, f32[512,256]{1,0:T(8,128)} %refs_0_.1), custom_call_target="tpu_custom_call" | custom-call | flops 1048576 | bytes 1048576 | tf_op jit(solution)/shard_map/pallas_call | solution.py:458
  3.1 0.7 collective-permute-start.1
  3.8 1.3 %collective-permute-start = (f32[512,256]{1,0:T(8,128)S(1)}, f32[512,256]{1,0:T(8,128)S(1)}, u32[]{:S(2)}, u32[]{:S(2)}) collective-permute-start(f32[512,256]{1,0:T(8,128)S(1)} %copy-done.11), channel_id=1, source_target_pairs={{2,10},{3,11},{4,20},{5,21},{6,30},{7,31}} | collective-permute-start | bytes 1572872 | tf_op jit(solution)/shard_map/ppermute | solution.py:483
  5.1 1.9 %collective-permute-start.4 = (f32[272,128]{1,0:T(8,128)S(1)}, f32[272,128]{1,0:T(8,128)S(1)}, u32[]{:S(2)}, u32[]{:S(2)}) collective-permute-start(f32[272,128]{1,0:T(8,128)S(1)} %get-tuple-element.31.refs_0_.refs_9_), channel_id=1, source_target_pairs={{0,4},{1,5},{2,6},{3,7},{4,0},{5,1},{6,2},{7,3},{8,12},{9,13},{10,... | collective-permute-start | bytes 417800 | tf_op jit(solution)/shard_map/ppermute | solution.py:483
  7.0 0.8 collective-permute-start.5
  7.8 0.7 collective-permute-start.2
  8.5 1.2 %collective-permute-done.3.refs_1_.refs_10_ = f32[272,128]{1,0:T(8,128)S(1)} collective-permute-done((f32[272,128]{1,0:T(8,128)S(1)}, f32[272,128]{1,0:T(8,128)S(1)}, u32[]{:S(2)}, u32[]{:S(2)}) %collective-permute-start.3) | collective-permute-done | bytes 139296 | tf_op jit(solution)/shard_map/ppermute | solution.py:483
  9.7 2.7 %collective-permute-start.6 = (f32[272,128]{1,0:T(8,128)S(1)}, f32[272,128]{1,0:T(8,128)S(1)}, u32[]{:S(2)}, u32[]{:S(2)}) collective-permute-start(f32[272,128]{1,0:T(8,128)S(1)} %get-tuple-element.31.refs_0_.refs_9_), channel_id=1, source_target_pairs={{0,1},{1,0},{2,3},{3,2},{4,5},{5,4},{6,7},{7,6},{8,9},{9,8},{10,11... | collective-permute-start | bytes 417800 | tf_op jit(solution)/shard_map/ppermute | solution.py:483
  12.4 0.7 collective-permute-done.4.refs_2_.refs_11_
  13.1 5.1 %collective-permute-start.7 = (f32[272,128]{1,0:T(8,128)S(1)}, f32[272,128]{1,0:T(8,128)S(1)}, u32[]{:S(2)}, u32[]{:S(2)}) collective-permute-start(f32[272,128]{1,0:T(8,128)S(1)} %collective-permute-done.3.refs_1_.refs_10_), channel_id=1, source_target_pairs={{0,1},{1,0},{2,3},{3,2},{4,5},{5,4},{6,7},{7,6},{8,9},{9,8},{10,11... | collective-permute-start | bytes 417800 | tf_op jit(solution)/shard_map/ppermute | solution.py:483
  18.2 1.6 %collective-permute-done.5.refs_3_.refs_12_ = f32[272,128]{1,0:T(8,128)S(1)} collective-permute-done((f32[272,128]{1,0:T(8,128)S(1)}, f32[272,128]{1,0:T(8,128)S(1)}, u32[]{:S(2)}, u32[]{:S(2)}) %collective-permute-start.5) | collective-permute-done | bytes 139296 | tf_op jit(solution)/shard_map/ppermute | solution.py:483
  19.7 1.6 %collective-permute-start.8 = (f32[272,128]{1,0:T(8,128)S(1)}, f32[272,128]{1,0:T(8,128)S(1)}, u32[]{:S(2)}, u32[]{:S(2)}) collective-permute-start(f32[272,128]{1,0:T(8,128)S(1)} %collective-permute-done.4.refs_2_.refs_11_), channel_id=1, source_target_pairs={{0,1},{1,0},{2,3},{3,2},{4,5},{5,4},{6,7},{7,6},{8,9},{9,8},{10,11... | collective-permute-start | bytes 417800 | tf_op jit(solution)/shard_map/ppermute | solution.py:483
  21.5 0.9 %collective-permute-done.8.refs_6_.refs_15_ = f32[272,128]{1,0:T(8,128)S(1)} collective-permute-done((f32[272,128]{1,0:T(8,128)S(1)}, f32[272,128]{1,0:T(8,128)S(1)}, u32[]{:S(2)}, u32[]{:S(2)}) %collective-permute-start.8) | collective-permute-done | bytes 139296 | tf_op jit(solution)/shard_map/ppermute | solution.py:483
  23.3 0.7 collective-permute-start.12
  24.0 1.3 %collective-permute-start.10 = (f32[520,128]{1,0:T(8,128)S(1)}, f32[520,128]{1,0:T(8,128)S(1)}, u32[]{:S(2)}, u32[]{:S(2)}) collective-permute-start(f32[520,128]{1,0:T(8,128)S(1)} %shard_map.47), channel_id=1, source_target_pairs={{0,8},{1,9},{2,10},{3,11},{4,12},{5,13},{6,14},{7,15}} | collective-permute-start | bytes 798728 | tf_op jit(solution)/shard_map/ppermute | solution.py:483
  25.3 1.4 %collective-permute-start.11 = (f32[520,128]{1,0:T(8,128)S(1)}, f32[520,128]{1,0:T(8,128)}, u32[]{:S(2)}, u32[]{:S(2)}) collective-permute-start(f32[520,128]{1,0:T(8,128)S(1)} %shard_map.47), channel_id=1, source_target_pairs={{0,16},{1,17},{2,18},{3,19},{4,20},{5,21},{6,22},{7,23}} | collective-permute-start | bytes 798728 | tf_op jit(solution)/shard_map/ppermute | solution.py:483
  26.7 3.4 %collective-permute-start.14 = (f32[512,256]{1,0:T(8,128)S(1)}, f32[512,256]{1,0:T(8,128)}, u32[]{:S(2)}, u32[]{:S(2)}) collective-permute-start(f32[512,256]{1,0:T(8,128)S(1)} %collective-permute-done.turned), channel_id=1, source_target_pairs={{10,12},{11,13},{20,22},{21,23},{30,28},{31,29}} | collective-permute-start | bytes 1572872 | tf_op jit(solution)/shard_map/ppermute | solution.py:483
  30.1 11.3 %collective-permute-done.10 = f32[520,128]{1,0:T(8,128)S(1)} collective-permute-done((f32[520,128]{1,0:T(8,128)S(1)}, f32[520,128]{1,0:T(8,128)S(1)}, u32[]{:S(2)}, u32[]{:S(2)}) %collective-permute-start.10) | collective-permute-done | bytes 266272 | tf_op jit(solution)/shard_map/ppermute | solution.py:483
  41.4 1.0 %add_select_fusion.here = f32[520,128]{1,0:T(8,128)S(1)} fusion(f32[520,128]{1,0:T(8,128)S(1)} %shard_map.47, f32[520,128]{1,0:T(8,128)S(1)} %collective-permute-done.12, f32[520,128]{1,0:T(8,128)S(1)} %collective-permute-done.10, f32[520,128]{1,0:T(8,128)} %collective-permute-done.11, pred[]{:T(512)S(6)} %eq.14), kind=kLoop, calls=%fused_computation.1 | loop fusion | flops 199680 | bytes 1331201 | tf_op jit(solution)/shard_map/jit(_where)/select_n | solution.py:525
  42.4 2.3 %collective-permute-start.13 = (f32[520,128]{1,0:T(8,128)S(1)}, f32[520,128]{1,0:T(8,128)S(1)}, u32[]{:S(2)}, u32[]{:S(2)}) collective-permute-start(f32[520,128]{1,0:T(8,128)S(1)} %add_select_fusion.here), channel_id=1, source_target_pairs={{0,1},{1,0},{2,3},{3,2},{4,5},{5,4},{6,7},{7,6},{8,9},{9,8},{10,11... | collective-permute-start | bytes 798728 | tf_op jit(solution)/shard_map/ppermute | solution.py:483
  44.7 4.1 %all-to-all-start = ((f32[8,136,128]{2,1,0:T(8,128)}), f32[8,136,128]{2,1,0:T(8,128)}, u32[]{:S(2)}, u32[]{:S(2)}) async-start(f32[8,136,128]{2,1,0:T(8,128)} %get-tuple-element.34), calls=%async_computation | async-start | bytes 1114112 | tf_op jit(solution)/shard_map/all_to_all | solution.py:524
  48.9 1.0 %shard_map.48.refs_4_ = f32[256,512]{1,0:T(8,128)S(1)} custom-call(s32[5]{0:T(128)S(1)} %stack.23.info, f32[512,256]{1,0:T(8,128)S(1)} %collective-permute-done.turned, f32[272,128]{1,0:T(8,128)S(1)} %get-tuple-element.31.refs_0_.refs_9_, f32[272,128]{1,0:T(8,128)S(1)} %collective-permute-done.3.refs_1_.refs_10_, ...), custom_call_target="tpu_custom_call" | custom-call | flops 1048576 | bytes 1048576 | tf_op jit(solution)/shard_map/pallas_call | solution.py:458
  49.9 1.3 %collective-permute-start.17 = (f32[256,512]{1,0:T(8,128)S(1)}, f32[256,512]{1,0:T(8,128)S(1)}, u32[]{:S(2)}, u32[]{:S(2)}) collective-permute-start(f32[256,512]{1,0:T(8,128)S(1)} %shard_map.48.refs_4_), channel_id=1, source_target_pairs={{10,2},{11,3},{20,28},{21,29},{30,22},{31,23}} | collective-permute-start | bytes 1572872 | tf_op jit(solution)/shard_map/ppermute | solution.py:483
  51.2 1.3 %collective-permute-start.18 = (f32[256,512]{1,0:T(8,128)S(1)}, f32[256,512]{1,0:T(8,128)S(1)}, u32[]{:S(2)}, u32[]{:S(2)}) collective-permute-start(f32[256,512]{1,0:T(8,128)S(1)} %shard_map.48.refs_4_), channel_id=1, source_target_pairs={{10,26},{11,27},{20,4},{21,5},{30,14},{31,15}} | collective-permute-start | bytes 1572872 | tf_op jit(solution)/shard_map/ppermute | solution.py:483
  52.5 2.1 %collective-permute-start.19 = (f32[256,512]{1,0:T(8,128)S(1)}, f32[256,512]{1,0:T(8,128)}, u32[]{:S(2)}, u32[]{:S(2)}) collective-permute-start(f32[256,512]{1,0:T(8,128)S(1)} %shard_map.48.refs_4_), channel_id=1, source_target_pairs={{10,18},{11,19},{20,12},{21,13},{30,6},{31,7}} | collective-permute-start | bytes 1572872 | tf_op jit(solution)/shard_map/ppermute | solution.py:483
  54.6 0.7 collective-permute-start.15
  55.3 16.1 %shard_map.49.refs_8_ = f32[3,256,256]{2,1,0:T(8,128)} custom-call(s32[5]{0:T(128)S(1)} %stack.23.info, f32[520,128]{1,0:T(8,128)S(1)} %add_select_fusion.here, f32[520,128]{1,0:T(8,128)S(1)} %collective-permute-done.13.there), custom_call_target="tpu_custom_call" | custom-call | flops 8589934592 | bytes 1048576 | tf_op jit(solution)/shard_map/pallas_call | solution.py:458
  71.5 1.2 %select_select_fusion.refs_2_ = f32[512,256]{1,0:T(8,128)S(1)} fusion(f32[512,256]{1,0:T(8,128)S(1)} %copy-done.11, f32[512,256]{1,0:T(8,128)S(1)} %collective-permute-done.turned, f32[512,256]{1,0:T(8,128)S(1)} %collective-permute-done.15, f32[512,256]{1,0:T(8,128)} %collective-permute-done.14, pred[]{:T(512)S(6)} %eq.13, pred[]{:T(512)S(6)} %eq.12), kind=kLoop, calls=%fused_computation | loop fusion | flops 393216 | bytes 2621442 | tf_op jit(solution)/shard_map/jit(_where)/select_n | solution.py:557
  73.1 0.8 copy-done.13
  73.8 0.8 copy-done.14
  74.7 0.8 copy-done.15
  75.5 6.8 %shard_map.50 = f32[512,256]{1,0:T(8,128)} custom-call(s32[5]{0:T(128)S(1)} %stack.23.info, f32[512,256]{1,0:T(8,128)} %refs_0_.1, f32[8,136,128]{2,1,0:T(8,128)} %all-to-all-done.refs_1_, f32[512,256]{1,0:T(8,128)} %copy-done.12, f32[512,256]{1,0:T(8,128)} %copy-done.15, f32[256,512]{1,0:T(8,128)} %copy-done.8, f32[256,512]{1,0:T(8,128)} %copy-done.13, ...), custom_call_target="tpu_custom_call" | custom-call | flops 2147483648 | bytes 1048576 | tf_op jit(solution)/shard_map/pallas_call | solution.py:458
  (51 shorter events, 2.2 us)
Async XLA Ops:
  0.0 3.7 %copy-start.11 = (f32[512,256]{1,0:T(8,128)S(1)}, f32[512,256]{1,0:T(8,128)}, u32[]{:S(2)}) copy-start(f32[512,256]{1,0:T(8,128)} %refs_0_.1) | copy-start | bytes 1572868
  3.0 45.8 %copy-start = (f32[272,128]{1,0:T(8,128)}, f32[272,128]{1,0:T(8,128)S(1)}, u32[]{:S(2)}) copy-start(f32[272,128]{1,0:T(8,128)S(1)} %get-tuple-element.31.refs_0_.refs_9_) | copy-start | bytes 417796
  3.1 4.7 %collective-permute-start.1 = (f32[520,128]{1,0:T(8,128)S(1)}, f32[520,128]{1,0:T(8,128)S(1)}, u32[]{:S(2)}, u32[]{:S(2)}) collective-permute-start(f32[520,128]{1,0:T(8,128)S(1)} %get-tuple-element.30.diag), channel_id=1, source_target_pairs={{0,4},{1,5}} | collective-permute-start | bytes 798728 | tf_op jit(solution)/shard_map/ppermute | solution.py:483
  3.8 17.6 %collective-permute-start = (f32[512,256]{1,0:T(8,128)S(1)}, f32[512,256]{1,0:T(8,128)S(1)}, u32[]{:S(2)}, u32[]{:S(2)}) collective-permute-start(f32[512,256]{1,0:T(8,128)S(1)} %copy-done.11), channel_id=1, source_target_pairs={{2,10},{3,11},{4,20},{5,21},{6,30},{7,31}} | collective-permute-start | bytes 1572872 | tf_op jit(solution)/shard_map/ppermute | solution.py:483
  5.1 4.6 %collective-permute-start.3 = (f32[272,128]{1,0:T(8,128)S(1)}, f32[272,128]{1,0:T(8,128)S(1)}, u32[]{:S(2)}, u32[]{:S(2)}) collective-permute-start(f32[272,128]{1,0:T(8,128)S(1)} %get-tuple-element.31.refs_0_.refs_9_), channel_id=1, source_target_pairs={{0,2},{1,3},{2,0},{3,1},{4,6},{5,7},{6,4},{7,5},{8,10},{9,11},{10,... | collective-permute-start | bytes 417800 | tf_op jit(solution)/shard_map/ppermute | solution.py:483
  5.1 7.9 %collective-permute-start.4 = (f32[272,128]{1,0:T(8,128)S(1)}, f32[272,128]{1,0:T(8,128)S(1)}, u32[]{:S(2)}, u32[]{:S(2)}) collective-permute-start(f32[272,128]{1,0:T(8,128)S(1)} %get-tuple-element.31.refs_0_.refs_9_), channel_id=1, source_target_pairs={{0,4},{1,5},{2,6},{3,7},{4,0},{5,1},{6,2},{7,3},{8,12},{9,13},{10,... | collective-permute-start | bytes 417800 | tf_op jit(solution)/shard_map/ppermute | solution.py:483
  7.0 12.7 %collective-permute-start.5 = (f32[272,128]{1,0:T(8,128)S(1)}, f32[272,128]{1,0:T(8,128)S(1)}, u32[]{:S(2)}, u32[]{:S(2)}) collective-permute-start(f32[272,128]{1,0:T(8,128)S(1)} %get-tuple-element.31.refs_0_.refs_9_), channel_id=1, source_target_pairs={{0,6},{1,7},{2,4},{3,5},{4,2},{5,3},{6,0},{7,1},{8,14},{9,15},{10,... | collective-permute-start | bytes 417800 | tf_op jit(solution)/shard_map/ppermute | solution.py:483
  7.8 15.0 %collective-permute-start.2 = (f32[520,128]{1,0:T(8,128)S(1)}, f32[520,128]{1,0:T(8,128)S(1)}, u32[]{:S(2)}, u32[]{:S(2)}) collective-permute-start(f32[520,128]{1,0:T(8,128)S(1)} %broadcast_select_fusion), channel_id=1, source_target_pairs={{0,2},{1,3},{4,6},{5,7}} | collective-permute-start | bytes 798728 | tf_op jit(solution)/shard_map/ppermute | solution.py:483
  9.7 39.2 %copy-start.1 = (f32[272,128]{1,0:T(8,128)}, f32[272,128]{1,0:T(8,128)S(1)}, u32[]{:S(2)}) copy-start(f32[272,128]{1,0:T(8,128)S(1)} %collective-permute-done.3.refs_1_.refs_10_) | copy-start | bytes 417796
  9.7 11.8 %collective-permute-start.6 = (f32[272,128]{1,0:T(8,128)S(1)}, f32[272,128]{1,0:T(8,128)S(1)}, u32[]{:S(2)}, u32[]{:S(2)}) collective-permute-start(f32[272,128]{1,0:T(8,128)S(1)} %get-tuple-element.31.refs_0_.refs_9_), channel_id=1, source_target_pairs={{0,1},{1,0},{2,3},{3,2},{4,5},{5,4},{6,7},{7,6},{8,9},{9,8},{10,11... | collective-permute-start | bytes 417800 | tf_op jit(solution)/shard_map/ppermute | solution.py:483
  13.1 35.8 %copy-start.2 = (f32[272,128]{1,0:T(8,128)}, f32[272,128]{1,0:T(8,128)S(1)}, u32[]{:S(2)}) copy-start(f32[272,128]{1,0:T(8,128)S(1)} %collective-permute-done.4.refs_2_.refs_11_) | copy-start | bytes 417796
  13.1 8.4 %collective-permute-start.7 = (f32[272,128]{1,0:T(8,128)S(1)}, f32[272,128]{1,0:T(8,128)S(1)}, u32[]{:S(2)}, u32[]{:S(2)}) collective-permute-start(f32[272,128]{1,0:T(8,128)S(1)} %collective-permute-done.3.refs_1_.refs_10_), channel_id=1, source_target_pairs={{0,1},{1,0},{2,3},{3,2},{4,5},{5,4},{6,7},{7,6},{8,9},{9,8},{10,11... | collective-permute-start | bytes 417800 | tf_op jit(solution)/shard_map/ppermute | solution.py:483
  19.7 29.1 %copy-start.3 = (f32[272,128]{1,0:T(8,128)}, f32[272,128]{1,0:T(8,128)S(1)}, u32[]{:S(2)}) copy-start(f32[272,128]{1,0:T(8,128)S(1)} %collective-permute-done.5.refs_3_.refs_12_) | copy-start | bytes 417796
  19.7 2.6 %collective-permute-start.8 = (f32[272,128]{1,0:T(8,128)S(1)}, f32[272,128]{1,0:T(8,128)S(1)}, u32[]{:S(2)}, u32[]{:S(2)}) collective-permute-start(f32[272,128]{1,0:T(8,128)S(1)} %collective-permute-done.4.refs_2_.refs_11_), channel_id=1, source_target_pairs={{0,1},{1,0},{2,3},{3,2},{4,5},{5,4},{6,7},{7,6},{8,9},{9,8},{10,11... | collective-permute-start | bytes 417800 | tf_op jit(solution)/shard_map/ppermute | solution.py:483
  21.4 1.4 %collective-permute-start.9 = (f32[272,128]{1,0:T(8,128)S(1)}, f32[272,128]{1,0:T(8,128)S(1)}, u32[]{:S(2)}, u32[]{:S(2)}) collective-permute-start(f32[272,128]{1,0:T(8,128)S(1)} %collective-permute-done.5.refs_3_.refs_12_), channel_id=1, source_target_pairs={{0,1},{1,0},{2,3},{3,2},{4,5},{5,4},{6,7},{7,6},{8,9},{9,8},{10,11... | collective-permute-start | bytes 417800 | tf_op jit(solution)/shard_map/ppermute | solution.py:483
  21.5 27.4 %copy-start.4 = (f32[272,128]{1,0:T(8,128)}, f32[272,128]{1,0:T(8,128)S(1)}, u32[]{:S(2)}) copy-start(f32[272,128]{1,0:T(8,128)S(1)} %collective-permute-done.6.refs_4_.refs_13_) | copy-start | bytes 417796
  21.5 27.4 %copy-start.5 = (f32[272,128]{1,0:T(8,128)}, f32[272,128]{1,0:T(8,128)S(1)}, u32[]{:S(2)}) copy-start(f32[272,128]{1,0:T(8,128)S(1)} %collective-permute-done.7.refs_5_.refs_14_) | copy-start | bytes 417796
  22.4 26.5 %copy-start.6 = (f32[272,128]{1,0:T(8,128)}, f32[272,128]{1,0:T(8,128)S(1)}, u32[]{:S(2)}) copy-start(f32[272,128]{1,0:T(8,128)S(1)} %collective-permute-done.8.refs_6_.refs_15_) | copy-start | bytes 417796
  22.8 26.1 %copy-start.7 = (f32[272,128]{1,0:T(8,128)}, f32[272,128]{1,0:T(8,128)S(1)}, u32[]{:S(2)}) copy-start(f32[272,128]{1,0:T(8,128)S(1)} %collective-permute-done.9.refs_7_.refs_16_) | copy-start | bytes 417796
  23.3 6.8 %collective-permute-start.12 = (f32[520,128]{1,0:T(8,128)S(1)}, f32[520,128]{1,0:T(8,128)S(1)}, u32[]{:S(2)}, u32[]{:S(2)}) collective-permute-start(f32[520,128]{1,0:T(8,128)S(1)} %shard_map.47), channel_id=1, source_target_pairs={{0,24},{1,25},{2,26},{3,27},{4,28},{5,29},{6,30},{7,31}} | collective-permute-start | bytes 798728 | tf_op jit(solution)/shard_map/ppermute | solution.py:483
  24.0 17.4 %collective-permute-start.10 = (f32[520,128]{1,0:T(8,128)S(1)}, f32[520,128]{1,0:T(8,128)S(1)}, u32[]{:S(2)}, u32[]{:S(2)}) collective-permute-start(f32[520,128]{1,0:T(8,128)S(1)} %shard_map.47), channel_id=1, source_target_pairs={{0,8},{1,9},{2,10},{3,11},{4,12},{5,13},{6,14},{7,15}} | collective-permute-start | bytes 798728 | tf_op jit(solution)/shard_map/ppermute | solution.py:483
  25.3 16.1 %collective-permute-start.11 = (f32[520,128]{1,0:T(8,128)S(1)}, f32[520,128]{1,0:T(8,128)}, u32[]{:S(2)}, u32[]{:S(2)}) collective-permute-start(f32[520,128]{1,0:T(8,128)S(1)} %shard_map.47), channel_id=1, source_target_pairs={{0,16},{1,17},{2,18},{3,19},{4,20},{5,21},{6,22},{7,23}} | collective-permute-start | bytes 798728 | tf_op jit(solution)/shard_map/ppermute | solution.py:483
  26.7 27.9 %collective-permute-start.14 = (f32[512,256]{1,0:T(8,128)S(1)}, f32[512,256]{1,0:T(8,128)}, u32[]{:S(2)}, u32[]{:S(2)}) collective-permute-start(f32[512,256]{1,0:T(8,128)S(1)} %collective-permute-done.turned), channel_id=1, source_target_pairs={{10,12},{11,13},{20,22},{21,23},{30,28},{31,29}} | collective-permute-start | bytes 1572872 | tf_op jit(solution)/shard_map/ppermute | solution.py:483
  42.4 12.9 %collective-permute-start.13 = (f32[520,128]{1,0:T(8,128)S(1)}, f32[520,128]{1,0:T(8,128)S(1)}, u32[]{:S(2)}, u32[]{:S(2)}) collective-permute-start(f32[520,128]{1,0:T(8,128)S(1)} %add_select_fusion.here), channel_id=1, source_target_pairs={{0,1},{1,0},{2,3},{3,2},{4,5},{5,4},{6,7},{7,6},{8,9},{9,8},{10,11... | collective-permute-start | bytes 798728 | tf_op jit(solution)/shard_map/ppermute | solution.py:483
  44.7 30.0 %all-to-all-start = ((f32[8,136,128]{2,1,0:T(8,128)}), f32[8,136,128]{2,1,0:T(8,128)}, u32[]{:S(2)}, u32[]{:S(2)}) async-start(f32[8,136,128]{2,1,0:T(8,128)} %get-tuple-element.34), calls=%async_computation | async-start | bytes 1114112 | tf_op jit(solution)/shard_map/all_to_all | solution.py:524
  49.8 21.6 %copy-start.8 = (f32[256,512]{1,0:T(8,128)}, f32[256,512]{1,0:T(8,128)S(1)}, u32[]{:S(2)}) copy-start(f32[256,512]{1,0:T(8,128)S(1)} %shard_map.48.refs_4_) | copy-start | bytes 1572868
  49.9 23.2 %collective-permute-start.17 = (f32[256,512]{1,0:T(8,128)S(1)}, f32[256,512]{1,0:T(8,128)S(1)}, u32[]{:S(2)}, u32[]{:S(2)}) collective-permute-start(f32[256,512]{1,0:T(8,128)S(1)} %shard_map.48.refs_4_), channel_id=1, source_target_pairs={{10,2},{11,3},{20,28},{21,29},{30,22},{31,23}} | collective-permute-start | bytes 1572872 | tf_op jit(solution)/shard_map/ppermute | solution.py:483
  51.2 21.9 %collective-permute-start.18 = (f32[256,512]{1,0:T(8,128)S(1)}, f32[256,512]{1,0:T(8,128)S(1)}, u32[]{:S(2)}, u32[]{:S(2)}) collective-permute-start(f32[256,512]{1,0:T(8,128)S(1)} %shard_map.48.refs_4_), channel_id=1, source_target_pairs={{10,26},{11,27},{20,4},{21,5},{30,14},{31,15}} | collective-permute-start | bytes 1572872 | tf_op jit(solution)/shard_map/ppermute | solution.py:483
  52.5 22.1 %collective-permute-start.19 = (f32[256,512]{1,0:T(8,128)S(1)}, f32[256,512]{1,0:T(8,128)}, u32[]{:S(2)}, u32[]{:S(2)}) collective-permute-start(f32[256,512]{1,0:T(8,128)S(1)} %shard_map.48.refs_4_), channel_id=1, source_target_pairs={{10,18},{11,19},{20,12},{21,13},{30,6},{31,7}} | collective-permute-start | bytes 1572872 | tf_op jit(solution)/shard_map/ppermute | solution.py:483
  54.6 16.9 %collective-permute-start.15 = (f32[512,256]{1,0:T(8,128)S(1)}, f32[512,256]{1,0:T(8,128)S(1)}, u32[]{:S(2)}, u32[]{:S(2)}) collective-permute-start(f32[512,256]{1,0:T(8,128)S(1)} %copy-done.11), channel_id=1, source_target_pairs={{16,18},{17,19},{24,26},{25,27},{2,14},{3,15}} | collective-permute-start | bytes 1572872 | tf_op jit(solution)/shard_map/ppermute | solution.py:483
  72.7 2.0 %copy-start.12 = (f32[512,256]{1,0:T(8,128)}, f32[512,256]{1,0:T(8,128)S(1)}, u32[]{:S(2)}) copy-start(f32[512,256]{1,0:T(8,128)S(1)} %select_select_fusion.refs_2_) | copy-start | bytes 1572868
  72.7 2.0 %collective-permute-start.16 = (f32[512,256]{1,0:T(8,128)S(1)}, f32[512,256]{1,0:T(8,128)S(1)}, u32[]{:S(2)}, u32[]{:S(2)}) collective-permute-start(f32[512,256]{1,0:T(8,128)S(1)} %select_select_fusion.refs_2_), channel_id=1, source_target_pairs={{0,1},{1,0},{2,3},{3,2},{4,5},{5,4},{6,7},{7,6},{8,9},{9,8},{10,11... | collective-permute-start | bytes 1572872 | tf_op jit(solution)/shard_map/ppermute | solution.py:483
  (5 other events, 3.7 us)

commit v10 on v9

--- a/solution.py
+++ b/solution.py
@@ -159,23 +159,24 @@
     )
 
 
-def dot3_t(a, b):
-    ah, bh = a.astype(BF16), b.astype(BF16)
-    al, bl = (a - ah.astype(F32)).astype(BF16), (b - bh.astype(F32)).astype(BF16)
-
-    def product(x, y):
-        return lax.dot_general(x, y, (((1,), (1,)), ((), ())), preferred_element_type=F32)
-
-    return product(ah, bl) + product(al, bh) + product(ah, bh)
-
-
-def factor_pair(a):
-    h = a.shape[0] // 2
-    w11 = factor_inverse(a[:h, :h])
-    l21 = dot_t(a[h:, :h], w11)
-    w22 = factor_inverse(a[h:, h:] - dot_t(l21, l21))
-    w21 = -dot(w22, dot(l21, w11))
-    return w11, w21, w22
+def two_parts(a):
+    high = a.astype(BF16)
+    return high, (a - high.astype(F32)).astype(BF16)
+
+
+def wide(a):
+    high, low = two_parts(a)
+    return jnp.concatenate([high, low, high], 1)
+
+
+def times(a, b):
+    high, low = two_parts(b)
+    return lax.dot_general(
+        a,
+        jnp.concatenate([high, high, low], 1),
+        (((1,), (1,)), ((), ())),
+        preferred_element_type=F32,
+    )
 
 
 def store_inverse(ref, blocks):
@@ -340,16 +341,25 @@
         top[...] = there[...]
         bottom[...] = here[...]
 
-    w_ref, l_ref = done.at[0], done.at[1]
     copies = [pltpu.make_async_copy(done.at[i], out_ref.at[i], sems.at[i]) for i in range(3)]
-    store_inverse(w_ref, factor_pair(unpack(top)))
+    a = unpack(top)
+    d = jnp.concatenate([get_rows(top, width + 8), get_rows(bottom, width + 8)], 0)
+    w11 = factor_inverse(a[:tile, :tile])
+    low = dot_t(a[tile:, :tile], w11)
+    left = dot_t(d[:, :tile], w11)
+    w22 = factor_inverse(a[tile:, tile:] - dot_t(low, low))
+    rest = d[:, tile:] - dot_t(left, low)
+    s = unpack(bottom) - dot_t(left, left)
+    right = dot_t(rest, w22)
+    store_inverse(done.at[0], (w11, -dot(w22, dot(low, w11)), w22))
+    done[1] = jnp.concatenate([left, right], 1)
     copies[0].start()
-    w = w_ref[...]
-    l_ref[:tile, :] = dot_t(get_rows(top, width + 8), w)
-    l_ref[tile:, :] = dot_t(get_rows(bottom, width + 8), w)
     copies[1].start()
-    lower = l_ref[...]
-    store_inverse(done.at[2], factor_pair(unpack(bottom) - dot_t(lower, lower)))
+    upper, lower = right[:tile, :], right[tile:, :]
+    w11 = factor_inverse(s[:tile, :tile] - dot_t(upper, upper))
+    low = dot_t(s[tile:, :tile] - dot_t(lower, upper), w11)
+    w22 = factor_inverse(s[tile:, tile:] - dot_t(lower, lower) - dot_t(low, low))
+    store_inverse(done.at[2], (w11, -dot(w22, dot(low, w11)), w22))
     copies[2].start()
     for c in copies:
         c.wait()
@@ -377,9 +387,11 @@
     last = len(copies)
     for c in copies:
         c.start()
+    way = jnp.where(group == 0, 3, jnp.where((group == 2) | ((group == 3) & (layer == 2)), 1, 2))
+    way = jnp.where(group == layer, 0, way)
     for k, m in enumerate((matched, m1, m2, m3)):
 
-        @pl.when((group ^ layer) == k)
+        @pl.when(way == k)
         def _(m=m):
             pltpu.make_async_copy(m, line, sems.at[last]).start()
 
@@ -409,11 +421,11 @@
     def _():
         add_band_blocks(band, [pays.at[i] for i in range(len(blocks))], width)
 
-    w1, l21, v = tri[0], tri[1], tri.at[2]
+    w1, l21, v = tri[0], tri[1], tri[2]
 
     @pl.when(column == 0)
     def _():
-        out_ref[...] = dot3_t(out_ref[...], w1)
+        out_ref[...] = times(wide(out_ref[...]), w1)
 
     @pl.when(column > 0)
     def _():
@@ -424,34 +436,41 @@
 
         @pl.when(group > 0)
         def _():
-            work[...] = dot3_t(band[:, :width], w1)
-
-        first = work[...]
+            work[...] = times(wide(band[:, :width]), w1)
+
+        first = wide(work[...])
 
         @pl.when(column == 1)
         def _():
             rows = group * nrows + lax.broadcasted_iota(jnp.int32, (nrows, width), 0)
             own = out_ref[...]
-            out_ref[...] = jnp.where(rows >= width, dot3_t(own - dot3_t(first, l21), v[...]), own)
-
-        @pl.when(column > 1)
+            second = times(wide(own - times(first, l21)), v)
+            out_ref[...] = jnp.where(rows >= width, second, own)
+
+        @pl.when((column > 1) & (group == 0))
         def _():
-            mine = dot3_t(line[:, :width], w1)
-            out_ref[...] -= dot3_t(first, mine)
-
-            @pl.when(group > 0)
-            def _():
-                second = dot3_t(band[:, width:] - dot3_t(first, l21), v[...])
-                out_ref[...] -= dot3_t(second, dot3_t(line[:, width:] - dot3_t(mine, l21), v[...]))
-
-
-def kernel(body, outs, args, smem=1, scratch=(), flops=1 << 20, sems=(), away=False):
+            out_ref[...] -= times(first, times(wide(line[:, :width]), w1))
+
+        @pl.when((column > 1) & (group > 0))
+        def _():
+            mine = times(wide(line[:, :width]), w1)
+            rest = times(wide(line[:, width:] - times(wide(mine), l21)), v)
+            second = times(wide(band[:, width:] - times(first, l21)), v)
+            out_ref[...] = out_ref[...] - times(first, mine) - times(wide(second), rest)
+
+
+def kernel(body, outs, args, smem=1, scratch=(), flops=1 << 20, sems=(), away=False, anywhere=()):
     space = pltpu.HBM if away else pltpu.VMEM
     spec = [pl.BlockSpec(memory_space=pltpu.SMEM)] * smem
     out_space = pltpu.HBM if isinstance(outs, type(pltpu.HBM((8, 128), F32))) else pltpu.VMEM
-    spec += [pl.BlockSpec(memory_space=space)] * (len(args) - smem)
+    spec += [
+        pl.BlockSpec(memory_space=pl.ANY if i in anywhere else space) for i in range(len(args) - smem)
+    ]
     if away:
-        args = args[:smem] + tuple(pltpu.with_memory_space_constraint(a, pltpu.HBM) for a in args[smem:])
+        args = args[:smem] + tuple(
+            a if i in anywhere else pltpu.with_memory_space_constraint(a, pltpu.HBM)
+            for i, a in enumerate(args[smem:])
+        )
     sizes = [math.prod(o.shape) for o in jax.tree.leaves(outs)] + [math.prod(s) for s in scratch]
     if not away:
         sizes += [a.size for a in args[smem:]]
@@ -540,8 +559,8 @@
         + [(dev(0, 1, c), dev(1, 3, c)) for c in both],
     )
     away = [
-        send(matched, [(dev(z, z, c), dev(z ^ s, z, c)) for z in layers[1:] for c in both])
-        for s in groups[1:]
+        send(matched, [(dev(z, z, c), dev(g, z, c)) for z, g in pairs for c in both])
+        for pairs in (((1, 2), (2, 3), (3, 2)), ((1, 3), (2, 1), (3, 1)), ((1, 0), (2, 0), (3, 0)))
     ]
 
     diag, diag2, far = lax.optimization_barrier((diag, diag2, far))
@@ -572,6 +591,7 @@
         flops=1 << 31,
         sems=[(16,)],
         away=True,
+        anywhere=(2, 3, 5, 6, 7),
     )
 
 

time: 84.1 us -> 80.9 us (0.962)
  the two profiles are of different devices: /device:TPU:11 before, /device:TPU:27 now
where the time goes in v10:
time: 80.9 us; the launch traced here: 80.4 us
  starting transfers between devices  29.4 us (36%)
  Pallas kernels  25.2 us (31%)
  waiting for transfers between devices  23.4 us (29%)
  other arithmetic  1.29 us (2%)
    pallas_call x5, Pallas kernels, kernel(): pl.pallas_call(body, out_shape=outs, in_specs=spec, out_specs=jax.tree.ma...  25.2 us
    ppermute x20, starting transfers between devices, send(): return lax.ppermute(x, AXES, pairs)  23.7 us
    ppermute x20, waiting for transfers between devices, send(): return lax.ppermute(x, AXES, pairs)  23.4 us
    all_to_all x1, starting transfers between devices, aligned(): lax.all_to_all(outgoing, 'front', split_axis=0, concat_axis=0, tiled=True)  5.74 us
  transfers between devices with their start and end apart: 21, of which 7 were waited for; matrix products, arithmetic and copies ran while one was open for 2% of the time, Pallas kernels for 21%

profile of v10, /device:TPU:27, one launch (start us, length us, event | category | flops | bytes accessed | tf_op | source)
XLA Modules:
  0.0 80.4 jit_solution(8082542087492713830)
XLA Ops:
  0.1 0.6 copy-done.9
  0.7 2.4 %shard_map.46 = (f32[8,136,128]{2,1,0:T(8,128)}, f32[272,128]{1,0:T(8,128)S(1)}, f32[520,128]{1,0:T(8,128)S(1)}) custom-call(s32[4]{0:T(128)S(1)} %copy-done.9, s32[4]{0:T(128)S(1)} %copy-done.10, s32[5]{0:T(128)S(1)} %stack.23.info, f32[4,128,128]{2,1,0:T(8,128)} %updates.1, f32[512,256]{1,0:T(8,128)} %refs_0_.1), custom_call_target="tpu_custom_call" | custom-call | flops 1048576 | bytes 1048576 | tf_op jit(solution)/shard_map/pallas_call | solution.py:477
  3.1 0.7 collective-permute-start.1
  3.8 0.7 collective-permute-start
  4.7 0.6 collective-permute-start.4
  5.3 2.8 %collective-permute-start.5 = (f32[272,128]{1,0:T(8,128)S(1)}, f32[272,128]{1,0:T(8,128)S(1)}, u32[]{:S(2)}, u32[]{:S(2)}) collective-permute-start(f32[272,128]{1,0:T(8,128)S(1)} %get-tuple-element.31.refs_0_.refs_9_), channel_id=1, source_target_pairs={{0,6},{1,7},{2,4},{3,5},{4,2},{5,3},{6,0},{7,1},{8,14},{9,15},{10,... | collective-permute-start | bytes 417800 | tf_op jit(solution)/shard_map/ppermute | solution.py:502
  8.1 0.7 collective-permute-start.2
  8.8 2.0 %collective-permute-done.3.refs_1_.refs_10_ = f32[272,128]{1,0:T(8,128)S(1)} collective-permute-done((f32[272,128]{1,0:T(8,128)S(1)}, f32[272,128]{1,0:T(8,128)S(1)}, u32[]{:S(2)}, u32[]{:S(2)}) %collective-permute-start.3) | collective-permute-done | bytes 139296 | tf_op jit(solution)/shard_map/ppermute | solution.py:502
  10.8 1.8 %collective-permute-start.6 = (f32[272,128]{1,0:T(8,128)S(1)}, f32[272,128]{1,0:T(8,128)S(1)}, u32[]{:S(2)}, u32[]{:S(2)}) collective-permute-start(f32[272,128]{1,0:T(8,128)S(1)} %get-tuple-element.31.refs_0_.refs_9_), channel_id=1, source_target_pairs={{0,1},{1,0},{2,3},{3,2},{4,5},{5,4},{6,7},{7,6},{8,9},{9,8},{10,11... | collective-permute-start | bytes 417800 | tf_op jit(solution)/shard_map/ppermute | solution.py:502
  12.6 6.3 %collective-permute-start.7 = (f32[272,128]{1,0:T(8,128)S(1)}, f32[272,128]{1,0:T(8,128)S(1)}, u32[]{:S(2)}, u32[]{:S(2)}) collective-permute-start(f32[272,128]{1,0:T(8,128)S(1)} %collective-permute-done.3.refs_1_.refs_10_), channel_id=1, source_target_pairs={{0,1},{1,0},{2,3},{3,2},{4,5},{5,4},{6,7},{7,6},{8,9},{9,8},{10,11... | collective-permute-start | bytes 417800 | tf_op jit(solution)/shard_map/ppermute | solution.py:502
  19.1 0.4 collective-permute-start.9
  19.5 0.5 collective-permute-done.7.refs_5_.refs_14_
  20.0 0.4 collective-permute-done.8.refs_6_.refs_15_
  20.5 0.5 shard_map.47
  21.1 0.7 collective-permute-start.12
  21.8 1.3 %collective-permute-start.10 = (f32[520,128]{1,0:T(8,128)S(1)}, f32[520,128]{1,0:T(8,128)S(1)}, u32[]{:S(2)}, u32[]{:S(2)}) collective-permute-start(f32[520,128]{1,0:T(8,128)S(1)} %shard_map.47), channel_id=1, source_target_pairs={{0,8},{1,9},{2,10},{3,11},{4,12},{5,13},{6,14},{7,15}} | collective-permute-start | bytes 798728 | tf_op jit(solution)/shard_map/ppermute | solution.py:502
  23.1 0.7 collective-permute-start.11
  23.8 1.5 %collective-permute-start.14 = (f32[512,256]{1,0:T(8,128)S(1)}, f32[512,256]{1,0:T(8,128)}, u32[]{:S(2)}, u32[]{:S(2)}) collective-permute-start(f32[512,256]{1,0:T(8,128)S(1)} %collective-permute-done.turned), channel_id=1, source_target_pairs={{10,12},{11,13},{20,22},{21,23},{30,28},{31,29}} | collective-permute-start | bytes 1572872 | tf_op jit(solution)/shard_map/ppermute | solution.py:502
  25.2 15.8 %collective-permute-done.10 = f32[520,128]{1,0:T(8,128)S(1)} collective-permute-done((f32[520,128]{1,0:T(8,128)S(1)}, f32[520,128]{1,0:T(8,128)S(1)}, u32[]{:S(2)}, u32[]{:S(2)}) %collective-permute-start.10) | collective-permute-done | bytes 266272 | tf_op jit(solution)/shard_map/ppermute | solution.py:502
  41.1 0.8 collective-permute-start.13
  41.9 5.7 %all-to-all-start = ((f32[8,136,128]{2,1,0:T(8,128)}), f32[8,136,128]{2,1,0:T(8,128)}, u32[]{:S(2)}, u32[]{:S(2)}) async-start(f32[8,136,128]{2,1,0:T(8,128)} %get-tuple-element.34), calls=%async_computation | async-start | bytes 1114112 | tf_op jit(solution)/shard_map/all_to_all | solution.py:543
  47.7 0.6 shard_map.48.refs_4_
  48.3 0.7 collective-permute-start.17
  49.0 1.3 %collective-permute-start.18 = (f32[256,512]{1,0:T(8,128)S(1)}, f32[256,512]{1,0:T(8,128)S(1)}, u32[]{:S(2)}, u32[]{:S(2)}) collective-permute-start(f32[256,512]{1,0:T(8,128)S(1)} %shard_map.48.refs_4_), channel_id=1, source_target_pairs={{10,26},{11,27},{20,12},{21,13},{30,14},{31,15}} | collective-permute-start | bytes 1572872 | tf_op jit(solution)/shard_map/ppermute | solution.py:502
  50.3 0.7 collective-permute-start.19
  51.0 1.3 %collective-permute-start.15 = (f32[512,256]{1,0:T(8,128)S(1)}, f32[512,256]{1,0:T(8,128)S(1)}, u32[]{:S(2)}, u32[]{:S(2)}) collective-permute-start(f32[512,256]{1,0:T(8,128)S(1)} %copy-done.12), channel_id=1, source_target_pairs={{16,18},{17,19},{24,26},{25,27},{2,14},{3,15}} | collective-permute-start | bytes 1572872 | tf_op jit(solution)/shard_map/ppermute | solution.py:502
  52.3 15.9 %shard_map.49.refs_8_ = f32[3,256,256]{2,1,0:T(8,128)} custom-call(s32[5]{0:T(128)S(1)} %stack.23.info, f32[520,128]{1,0:T(8,128)S(1)} %add_select_fusion.here, f32[520,128]{1,0:T(8,128)} %collective-permute-done.13.there), custom_call_target="tpu_custom_call" | custom-call | flops 8589934592 | bytes 1048576 | tf_op jit(solution)/shard_map/pallas_call | solution.py:477
  68.3 3.0 %collective-permute-done.15 = f32[512,256]{1,0:T(8,128)S(1)} collective-permute-done((f32[512,256]{1,0:T(8,128)S(1)}, f32[512,256]{1,0:T(8,128)S(1)}, u32[]{:S(2)}, u32[]{:S(2)}) %collective-permute-start.15) | collective-permute-done | bytes 524320 | tf_op jit(solution)/shard_map/ppermute | solution.py:502
  71.2 1.2 %select_select_fusion.refs_2_ = f32[512,256]{1,0:T(8,128)S(1)} fusion(f32[512,256]{1,0:T(8,128)S(1)} %copy-done.12, f32[512,256]{1,0:T(8,128)S(1)} %collective-permute-done.turned, f32[512,256]{1,0:T(8,128)S(1)} %collective-permute-done.15, f32[512,256]{1,0:T(8,128)} %collective-permute-done.14, pred[]{:T(512)S(6)} %eq.13, pred[]{:T(512)S(6)} %eq.12), kind=kLoop, calls=%fused_computation | loop fusion | flops 393216 | bytes 2621442 | tf_op jit(solution)/shard_map/jit(_where)/select_n | solution.py:576
  72.4 0.5 collective-permute-start.16
  73.0 1.5 %collective-permute-done.16.refs_3_ = f32[512,256]{1,0:T(8,128)S(1)} collective-permute-done((f32[512,256]{1,0:T(8,128)S(1)}, f32[512,256]{1,0:T(8,128)S(1)}, u32[]{:S(2)}, u32[]{:S(2)}) %collective-permute-start.16) | collective-permute-done | bytes 524320 | tf_op jit(solution)/shard_map/ppermute | solution.py:502
  74.5 5.8 %shard_map.50 = f32[512,256]{1,0:T(8,128)} custom-call(s32[5]{0:T(128)S(1)} %stack.23.info, f32[512,256]{1,0:T(8,128)} %refs_0_.1, f32[8,136,128]{2,1,0:T(8,128)} %all-to-all-done.refs_1_, f32[512,256]{1,0:T(8,128)S(1)} %select_select_fusion.refs_2_, f32[512,256]{1,0:T(8,128)S(1)} %collective-permute-done.16.refs_3_, f32[256,512]{1,0:T(8,128)} %copy-done.8, ...), custom_call_target="tpu_custom_call" | custom-call | flops 2147483648 | bytes 1048576 | tf_op jit(solution)/shard_map/pallas_call | solution.py:477
  (45 shorter events, 0.8 us)
Async XLA Ops:
  0.0 3.7 %copy-start.11 = (f32[512,256]{1,0:T(8,128)S(1)}, f32[512,256]{1,0:T(8,128)}, u32[]{:S(2)}) copy-start(f32[512,256]{1,0:T(8,128)} %refs_0_.1) | copy-start | bytes 1572868
  3.0 44.6 %copy-start = (f32[272,128]{1,0:T(8,128)}, f32[272,128]{1,0:T(8,128)S(1)}, u32[]{:S(2)}) copy-start(f32[272,128]{1,0:T(8,128)S(1)} %get-tuple-element.31.refs_0_.refs_9_) | copy-start | bytes 417796
  3.1 5.0 %collective-permute-start.1 = (f32[520,128]{1,0:T(8,128)S(1)}, f32[520,128]{1,0:T(8,128)S(1)}, u32[]{:S(2)}, u32[]{:S(2)}) collective-permute-start(f32[520,128]{1,0:T(8,128)S(1)} %get-tuple-element.30.diag), channel_id=1, source_target_pairs={{0,4},{1,5}} | collective-permute-start | bytes 798728 | tf_op jit(solution)/shard_map/ppermute | solution.py:502
  3.8 15.3 %collective-permute-start = (f32[512,256]{1,0:T(8,128)S(1)}, f32[512,256]{1,0:T(8,128)S(1)}, u32[]{:S(2)}, u32[]{:S(2)}) collective-permute-start(f32[512,256]{1,0:T(8,128)S(1)} %copy-done.11), channel_id=1, source_target_pairs={{2,10},{3,11},{4,20},{5,21},{6,30},{7,31}} | collective-permute-start | bytes 1572872 | tf_op jit(solution)/shard_map/ppermute | solution.py:502
  4.5 6.4 %collective-permute-start.3 = (f32[272,128]{1,0:T(8,128)S(1)}, f32[272,128]{1,0:T(8,128)S(1)}, u32[]{:S(2)}, u32[]{:S(2)}) collective-permute-start(f32[272,128]{1,0:T(8,128)S(1)} %get-tuple-element.31.refs_0_.refs_9_), channel_id=1, source_target_pairs={{0,2},{1,3},{2,0},{3,1},{4,6},{5,7},{6,4},{7,5},{8,10},{9,11},{10,... | collective-permute-start | bytes 417800 | tf_op jit(solution)/shard_map/ppermute | solution.py:502
  4.7 7.9 %collective-permute-start.4 = (f32[272,128]{1,0:T(8,128)S(1)}, f32[272,128]{1,0:T(8,128)S(1)}, u32[]{:S(2)}, u32[]{:S(2)}) collective-permute-start(f32[272,128]{1,0:T(8,128)S(1)} %get-tuple-element.31.refs_0_.refs_9_), channel_id=1, source_target_pairs={{0,4},{1,5},{2,6},{3,7},{4,0},{5,1},{6,2},{7,3},{8,12},{9,13},{10,... | collective-permute-start | bytes 417800 | tf_op jit(solution)/shard_map/ppermute | solution.py:502
  5.3 13.7 %collective-permute-start.5 = (f32[272,128]{1,0:T(8,128)S(1)}, f32[272,128]{1,0:T(8,128)S(1)}, u32[]{:S(2)}, u32[]{:S(2)}) collective-permute-start(f32[272,128]{1,0:T(8,128)S(1)} %get-tuple-element.31.refs_0_.refs_9_), channel_id=1, source_target_pairs={{0,6},{1,7},{2,4},{3,5},{4,2},{5,3},{6,0},{7,1},{8,14},{9,15},{10,... | collective-permute-start | bytes 417800 | tf_op jit(solution)/shard_map/ppermute | solution.py:502
  8.1 12.4 %collective-permute-start.2 = (f32[520,128]{1,0:T(8,128)S(1)}, f32[520,128]{1,0:T(8,128)S(1)}, u32[]{:S(2)}, u32[]{:S(2)}) collective-permute-start(f32[520,128]{1,0:T(8,128)S(1)} %broadcast_select_fusion), channel_id=1, source_target_pairs={{0,2},{1,3},{4,6},{5,7}} | collective-permute-start | bytes 798728 | tf_op jit(solution)/shard_map/ppermute | solution.py:502
  10.8 36.8 %copy-start.1 = (f32[272,128]{1,0:T(8,128)}, f32[272,128]{1,0:T(8,128)S(1)}, u32[]{:S(2)}) copy-start(f32[272,128]{1,0:T(8,128)S(1)} %collective-permute-done.3.refs_1_.refs_10_) | copy-start | bytes 417796
  10.8 8.7 %collective-permute-start.6 = (f32[272,128]{1,0:T(8,128)S(1)}, f32[272,128]{1,0:T(8,128)S(1)}, u32[]{:S(2)}, u32[]{:S(2)}) collective-permute-start(f32[272,128]{1,0:T(8,128)S(1)} %get-tuple-element.31.refs_0_.refs_9_), channel_id=1, source_target_pairs={{0,1},{1,0},{2,3},{3,2},{4,5},{5,4},{6,7},{7,6},{8,9},{9,8},{10,11... | collective-permute-start | bytes 417800 | tf_op jit(solution)/shard_map/ppermute | solution.py:502
  12.6 35.0 %copy-start.2 = (f32[272,128]{1,0:T(8,128)}, f32[272,128]{1,0:T(8,128)S(1)}, u32[]{:S(2)}) copy-start(f32[272,128]{1,0:T(8,128)S(1)} %collective-permute-done.4.refs_2_.refs_11_) | copy-start | bytes 417796
  12.6 7.3 %collective-permute-start.7 = (f32[272,128]{1,0:T(8,128)S(1)}, f32[272,128]{1,0:T(8,128)S(1)}, u32[]{:S(2)}, u32[]{:S(2)}) collective-permute-start(f32[272,128]{1,0:T(8,128)S(1)} %collective-permute-done.3.refs_1_.refs_10_), channel_id=1, source_target_pairs={{0,1},{1,0},{2,3},{3,2},{4,5},{5,4},{6,7},{7,6},{8,9},{9,8},{10,11... | collective-permute-start | bytes 417800 | tf_op jit(solution)/shard_map/ppermute | solution.py:502
  19.0 28.7 %copy-start.3 = (f32[272,128]{1,0:T(8,128)}, f32[272,128]{1,0:T(8,128)S(1)}, u32[]{:S(2)}) copy-start(f32[272,128]{1,0:T(8,128)S(1)} %collective-permute-done.5.refs_3_.refs_12_) | copy-start | bytes 417796
  19.0 1.4 %collective-permute-start.8 = (f32[272,128]{1,0:T(8,128)S(1)}, f32[272,128]{1,0:T(8,128)S(1)}, u32[]{:S(2)}, u32[]{:S(2)}) collective-permute-start(f32[272,128]{1,0:T(8,128)S(1)} %collective-permute-done.4.refs_2_.refs_11_), channel_id=1, source_target_pairs={{0,1},{1,0},{2,3},{3,2},{4,5},{5,4},{6,7},{7,6},{8,9},{9,8},{10,11... | collective-permute-start | bytes 417800 | tf_op jit(solution)/shard_map/ppermute | solution.py:502
  19.1 1.5 %collective-permute-start.9 = (f32[272,128]{1,0:T(8,128)S(1)}, f32[272,128]{1,0:T(8,128)S(1)}, u32[]{:S(2)}, u32[]{:S(2)}) collective-permute-start(f32[272,128]{1,0:T(8,128)S(1)} %collective-permute-done.5.refs_3_.refs_12_), channel_id=1, source_target_pairs={{0,1},{1,0},{2,3},{3,2},{4,5},{5,4},{6,7},{7,6},{8,9},{9,8},{10,11... | collective-permute-start | bytes 417800 | tf_op jit(solution)/shard_map/ppermute | solution.py:502
  19.5 28.1 %copy-start.4 = (f32[272,128]{1,0:T(8,128)}, f32[272,128]{1,0:T(8,128)S(1)}, u32[]{:S(2)}) copy-start(f32[272,128]{1,0:T(8,128)S(1)} %collective-permute-done.6.refs_4_.refs_13_) | copy-start | bytes 417796
  20.0 27.7 %copy-start.5 = (f32[272,128]{1,0:T(8,128)}, f32[272,128]{1,0:T(8,128)S(1)}, u32[]{:S(2)}) copy-start(f32[272,128]{1,0:T(8,128)S(1)} %collective-permute-done.7.refs_5_.refs_14_) | copy-start | bytes 417796
  20.3 27.3 %copy-start.6 = (f32[272,128]{1,0:T(8,128)}, f32[272,128]{1,0:T(8,128)S(1)}, u32[]{:S(2)}) copy-start(f32[272,128]{1,0:T(8,128)S(1)} %collective-permute-done.8.refs_6_.refs_15_) | copy-start | bytes 417796
  20.5 27.1 %copy-start.7 = (f32[272,128]{1,0:T(8,128)}, f32[272,128]{1,0:T(8,128)S(1)}, u32[]{:S(2)}) copy-start(f32[272,128]{1,0:T(8,128)S(1)} %collective-permute-done.9.refs_7_.refs_16_) | copy-start | bytes 417796
  21.1 4.1 %collective-permute-start.12 = (f32[520,128]{1,0:T(8,128)S(1)}, f32[520,128]{1,0:T(8,128)S(1)}, u32[]{:S(2)}, u32[]{:S(2)}) collective-permute-start(f32[520,128]{1,0:T(8,128)S(1)} %shard_map.47), channel_id=1, source_target_pairs={{0,24},{1,25},{2,26},{3,27},{4,28},{5,29},{6,30},{7,31}} | collective-permute-start | bytes 798728 | tf_op jit(solution)/shard_map/ppermute | solution.py:502
  21.8 19.2 %collective-permute-start.10 = (f32[520,128]{1,0:T(8,128)S(1)}, f32[520,128]{1,0:T(8,128)S(1)}, u32[]{:S(2)}, u32[]{:S(2)}) collective-permute-start(f32[520,128]{1,0:T(8,128)S(1)} %shard_map.47), channel_id=1, source_target_pairs={{0,8},{1,9},{2,10},{3,11},{4,12},{5,13},{6,14},{7,15}} | collective-permute-start | bytes 798728 | tf_op jit(solution)/shard_map/ppermute | solution.py:502
  23.1 17.9 %collective-permute-start.11 = (f32[520,128]{1,0:T(8,128)S(1)}, f32[520,128]{1,0:T(8,128)S(1)}, u32[]{:S(2)}, u32[]{:S(2)}) collective-permute-start(f32[520,128]{1,0:T(8,128)S(1)} %shard_map.47), channel_id=1, source_target_pairs={{0,16},{1,17},{2,18},{3,19},{4,20},{5,21},{6,22},{7,23}} | collective-permute-start | bytes 798728 | tf_op jit(solution)/shard_map/ppermute | solution.py:502
  23.8 27.2 %collective-permute-start.14 = (f32[512,256]{1,0:T(8,128)S(1)}, f32[512,256]{1,0:T(8,128)}, u32[]{:S(2)}, u32[]{:S(2)}) collective-permute-start(f32[512,256]{1,0:T(8,128)S(1)} %collective-permute-done.turned), channel_id=1, source_target_pairs={{10,12},{11,13},{20,22},{21,23},{30,28},{31,29}} | collective-permute-start | bytes 1572872 | tf_op jit(solution)/shard_map/ppermute | solution.py:502
  41.1 11.2 %collective-permute-start.13 = (f32[520,128]{1,0:T(8,128)S(1)}, f32[520,128]{1,0:T(8,128)}, u32[]{:S(2)}, u32[]{:S(2)}) collective-permute-start(f32[520,128]{1,0:T(8,128)S(1)} %add_select_fusion.here), channel_id=1, source_target_pairs={{0,1},{1,0},{2,3},{3,2},{4,5},{5,4},{6,7},{7,6},{8,9},{9,8},{10,11... | collective-permute-start | bytes 798728 | tf_op jit(solution)/shard_map/ppermute | solution.py:502
  41.9 31.1 %all-to-all-start = ((f32[8,136,128]{2,1,0:T(8,128)}), f32[8,136,128]{2,1,0:T(8,128)}, u32[]{:S(2)}, u32[]{:S(2)}) async-start(f32[8,136,128]{2,1,0:T(8,128)} %get-tuple-element.34), calls=%async_computation | async-start | bytes 1114112 | tf_op jit(solution)/shard_map/all_to_all | solution.py:543
  47.7 3.3 %copy-start.12 = (f32[512,256]{1,0:T(8,128)S(1)}, f32[512,256]{1,0:T(8,128)}, u32[]{:S(2)}) copy-start(f32[512,256]{1,0:T(8,128)} %refs_0_.1) | copy-start | bytes 1572868
  48.3 20.0 %copy-start.8 = (f32[256,512]{1,0:T(8,128)}, f32[256,512]{1,0:T(8,128)S(1)}, u32[]{:S(2)}) copy-start(f32[256,512]{1,0:T(8,128)S(1)} %shard_map.48.refs_4_) | copy-start | bytes 1572868
  48.3 24.7 %collective-permute-start.17 = (f32[256,512]{1,0:T(8,128)S(1)}, f32[256,512]{1,0:T(8,128)S(1)}, u32[]{:S(2)}, u32[]{:S(2)}) collective-permute-start(f32[256,512]{1,0:T(8,128)S(1)} %shard_map.48.refs_4_), channel_id=1, source_target_pairs={{10,18},{11,19},{20,28},{21,29},{30,22},{31,23}} | collective-permute-start | bytes 1572872 | tf_op jit(solution)/shard_map/ppermute | solution.py:502
  49.0 24.0 %collective-permute-start.18 = (f32[256,512]{1,0:T(8,128)S(1)}, f32[256,512]{1,0:T(8,128)S(1)}, u32[]{:S(2)}, u32[]{:S(2)}) collective-permute-start(f32[256,512]{1,0:T(8,128)S(1)} %shard_map.48.refs_4_), channel_id=1, source_target_pairs={{10,26},{11,27},{20,12},{21,13},{30,14},{31,15}} | collective-permute-start | bytes 1572872 | tf_op jit(solution)/shard_map/ppermute | solution.py:502
  50.3 22.7 %collective-permute-start.19 = (f32[256,512]{1,0:T(8,128)S(1)}, f32[256,512]{1,0:T(8,128)S(1)}, u32[]{:S(2)}, u32[]{:S(2)}) collective-permute-start(f32[256,512]{1,0:T(8,128)S(1)} %shard_map.48.refs_4_), channel_id=1, source_target_pairs={{10,2},{11,3},{20,4},{21,5},{30,6},{31,7}} | collective-permute-start | bytes 1572872 | tf_op jit(solution)/shard_map/ppermute | solution.py:502
  51.0 20.3 %collective-permute-start.15 = (f32[512,256]{1,0:T(8,128)S(1)}, f32[512,256]{1,0:T(8,128)S(1)}, u32[]{:S(2)}, u32[]{:S(2)}) collective-permute-start(f32[512,256]{1,0:T(8,128)S(1)} %copy-done.12), channel_id=1, source_target_pairs={{16,18},{17,19},{24,26},{25,27},{2,14},{3,15}} | collective-permute-start | bytes 1572872 | tf_op jit(solution)/shard_map/ppermute | solution.py:502
  72.4 2.0 %collective-permute-start.16 = (f32[512,256]{1,0:T(8,128)S(1)}, f32[512,256]{1,0:T(8,128)S(1)}, u32[]{:S(2)}, u32[]{:S(2)}) collective-permute-start(f32[512,256]{1,0:T(8,128)S(1)} %select_select_fusion.refs_2_), channel_id=1, source_target_pairs={{0,1},{1,0},{2,3},{3,2},{4,5},{5,4},{6,7},{7,6},{8,9},{9,8},{10,11... | collective-permute-start | bytes 1572872 | tf_op jit(solution)/shard_map/ppermute | solution.py:502
  (2 other events, 1.3 us)

commit v11 on v10

--- a/solution.py
+++ b/solution.py
@@ -93,36 +93,41 @@
     out, held = [], []
     for k in range(panels):
         rows, ident = work[k]
-        cols = [lane_of(rows, 8 * k + j) for j in range(8)]
-        d = {(i, j): row_of(cols[j], i) for j in range(8) for i in range(j, 8)}
-        up = [row_of(rows, j) for j in range(8)]
-        inv = [row_of(ident, j) for j in range(8)]
-        last = min(panels - 1, (k // per + 1) * per - 1 + ahead)
+        if k == 0:
+            cols = [lane_of(rows, j) for j in range(8)]
+        last = min(panels - 1, max(k + 1, (k // per + 1) * per - 1 + ahead))
         below = {
             b: [lane_of(work[b][0], 8 * k + j) for j in range(8)]
             for b in range(k + 1, last + 1)
         }
+        if k + 1 < panels:
+            following = [lane_of(work[k + 1][0], 8 * k + 8 + j) for j in range(8)]
+        scale = jnp.zeros((8, n), F32)
         for j in range(8):
-            r = lax.rsqrt(d[j, j])
-            for i in range(j + 1, 8):
-                d[i, j] = d[i, j] * r
-            for i in range(j + 1, 8):
-                for m in range(j + 1, i + 1):
-                    d[i, m] = d[i, m] - d[i, j] * d[m, j]
-            up[j] = up[j] * r
-            inv[j] = inv[j] * r
-            for i in range(j + 1, 8):
-                up[i] = up[i] - d[i, j] * up[j]
-                inv[i] = inv[i] - d[i, j] * inv[j]
+            s = {i: row_of(cols[j], i) for i in range(j, 8)}
+            r = lax.rsqrt(s[j])
+            inverse = r * r
+            ratio = {i: s[i] * inverse for i in range(j + 1, 8)}
+            if j < 7:
+                cols[j + 1] = cols[j + 1] - (cols[j] * s[j + 1]) * inverse
+            for i in range(j + 2, 8):
+                cols[i] = cols[i] - cols[j] * ratio[i]
+            up, ue = row_of(rows, j), row_of(ident, j)
+            if j < 7:
+                part = jnp.where(sub > j, cols[j] * inverse, 0.0)
+                rows, ident = rows - part * up, ident - part * ue
+            scale = jnp.where(sub == j, r, scale)
             for b, c in below.items():
-                c[j] = c[j] * r
+                cj = c[j] * inverse
+                if b == k + 1:
+                    for i in range(8):
+                        following[i] = following[i] - cj * row_of(c[j], i)
                 for i in range(j + 1, 8):
-                    c[i] = c[i] - d[i, j] * c[j]
-                work[b] = [work[b][0] - c[j] * up[j], work[b][1] - c[j] * inv[j]]
-        u, w = up[0], inv[0]
-        for j in range(1, 8):
-            u = jnp.where(sub == j, up[j], u)
-            w = jnp.where(sub == j, inv[j], w)
+                    c[i] = c[i] - c[j] * ratio[i]
+                work[b] = [work[b][0] - cj * up, work[b][1] - cj * ue]
+        if k + 1 < panels:
+            cols = following
+        u, w = rows * scale, ident * scale
         out.append(w)
         held.append((u, w))
         first = k + 1 + ahead
@@ -401,7 +406,7 @@
         add_block(out_ref, came[i, :tile, :], place_of(came[i, tile:, :]), tile)
     copies[2].wait()
     copies[3].wait()
-    by_rows = (layer > 0) & ((group == 1) | (layer > 1))
+    by_rows = (layer > 0) & (((group == 1) & (layer < 3)) | ((group > 1) & (layer > 1)))
     for c in range(2):
         side = jnp.where(core == 0, c, 1 - c)
 
@@ -540,24 +545,19 @@
     got = [
         send(diag, [(dev(0, z, c), dev(s, z, c)) for z in layers for c in both]) for s in groups[1:]
     ]
-    arrived = lax.all_to_all(outgoing, "front", split_axis=0, concat_axis=0, tiled=True)
     diag = jnp.where(group == 0, diag, got[0] + got[1] + got[2])
     diag2 = send(diag, swap)
 
+    hops = ((1, 0, 3), (2, 0, 1), (3, 0, 1), (1, 1, 2), (2, 2, 3), (3, 3, 2))
     far = send(
-        turned,
-        [(dev(g, z, c), dev(g, y, c)) for g, z, y in ((1, 1, 2), (2, 2, 3), (3, 3, 2)) for c in both],
+        jnp.where(layer == 0, early, turned), [(dev(g, z, c), dev(g, y, c)) for g, z, y in hops for c in both]
     )
 
     matched = kernel(
         matched_kernel, out(width, 2 * width), (info, turned, *blocks), scratch=[(nrows, 2 * width)]
     )
-    matched, early, diag = lax.optimization_barrier((matched, early, diag))
-    near = send(
-        early,
-        [(dev(g, 0, c), dev(g, 1, c)) for g in (2, 3) for c in both]
-        + [(dev(0, 1, c), dev(1, 3, c)) for c in both],
-    )
+    matched, diag, outgoing = lax.optimization_barrier((matched, diag, outgoing))
+    arrived = lax.all_to_all(outgoing, "front", split_axis=0, concat_axis=0, tiled=True)
     away = [
         send(matched, [(dev(z, z, c), dev(g, z, c)) for z, g in pairs for c in both])
         for pairs in (((1, 2), (2, 3), (3, 2)), ((1, 3), (2, 1), (3, 1)), ((1, 0), (2, 0), (3, 0)))
@@ -572,8 +572,8 @@
         flops=1 << 33,
         sems=[(3,)],
     )
-    factors, near, far = lax.optimization_barrier((factors, near, far))
-    piece = jnp.where(layer == 0, front, jnp.where(group == layer, turned, near + far))
+    factors, far = lax.optimization_barrier((factors, far))
+    piece = jnp.where(layer == 0, front, jnp.where(group == layer, turned, far))
     piece2 = send(piece, swap)
     return kernel(
         last_kernel,

time: 80.9 us -> 78 us (0.964)
  the two profiles are of different devices: /device:TPU:27 before, /device:TPU:13 now
where the time goes in v11:
time: 78 us; the launch traced here: 77.5 us
  starting transfers between devices  30.5 us (39%)
  Pallas kernels  22.9 us (29%)
  waiting for transfers between devices  20 us (26%)
  other arithmetic  3.05 us (4%)
    pallas_call x5, Pallas kernels, kernel(): pl.pallas_call(body, out_shape=outs, in_specs=spec, out_specs=jax.tree.ma...  22.9 us
    ppermute x19, starting transfers between devices, send(): return lax.ppermute(x, AXES, pairs)  20.7 us
    ppermute x19, waiting for transfers between devices, send(): return lax.ppermute(x, AXES, pairs)  20 us
    all_to_all x1, starting transfers between devices, aligned(): lax.all_to_all(outgoing, 'front', split_axis=0, concat_axis=0, tiled=True)  9.76 us
  transfers between devices with their start and end apart: 20, of which 7 were waited for; matrix products, arithmetic and copies ran while one was open for 4% of the time, Pallas kernels for 18%

profile of v11, /device:TPU:13, one launch (start us, length us, event | category | flops | bytes accessed | tf_op | source)
XLA Modules:
  0.0 77.5 jit_solution(17677065395220492056)
XLA Ops:
  0.1 0.6 copy-done.9
  0.7 2.4 %shard_map.46 = (f32[8,136,128]{2,1,0:T(8,128)}, f32[272,128]{1,0:T(8,128)S(1)}, f32[520,128]{1,0:T(8,128)S(1)}) custom-call(s32[4]{0:T(128)S(1)} %copy-done.9, s32[4]{0:T(128)S(1)} %copy-done.10, s32[5]{0:T(128)S(1)} %stack.23.info, f32[4,128,128]{2,1,0:T(8,128)} %updates.1, f32[512,256]{1,0:T(8,128)} %refs_0_.1), custom_call_target="tpu_custom_call" | custom-call | flops 1048576 | bytes 1048576 | tf_op jit(solution)/shard_map/pallas_call | solution.py:482
  3.1 0.7 collective-permute-start.1
  3.8 0.7 collective-permute-start
  4.7 2.9 %collective-permute-start.4 = (f32[272,128]{1,0:T(8,128)S(1)}, f32[272,128]{1,0:T(8,128)S(1)}, u32[]{:S(2)}, u32[]{:S(2)}) collective-permute-start(f32[272,128]{1,0:T(8,128)S(1)} %get-tuple-element.30.refs_0_.refs_9_), channel_id=1, source_target_pairs={{0,4},{1,5},{2,6},{3,7},{4,0},{5,1},{6,2},{7,3},{8,12},{9,13},{10,... | collective-permute-start | bytes 417800 | tf_op jit(solution)/shard_map/ppermute | solution.py:507
  7.7 0.7 collective-permute-start.2
  8.3 0.7 collective-permute-done.3.refs_1_.refs_10_
  9.1 2.2 %collective-permute-start.6 = (f32[272,128]{1,0:T(8,128)S(1)}, f32[272,128]{1,0:T(8,128)S(1)}, u32[]{:S(2)}, u32[]{:S(2)}) collective-permute-start(f32[272,128]{1,0:T(8,128)S(1)} %get-tuple-element.30.refs_0_.refs_9_), channel_id=1, source_target_pairs={{0,1},{1,0},{2,3},{3,2},{4,5},{5,4},{6,7},{7,6},{8,9},{9,8},{10,11... | collective-permute-start | bytes 417800 | tf_op jit(solution)/shard_map/ppermute | solution.py:507
  11.3 4.8 %collective-permute-done.4.refs_2_.refs_11_ = f32[272,128]{1,0:T(8,128)S(1)} collective-permute-done((f32[272,128]{1,0:T(8,128)S(1)}, f32[272,128]{1,0:T(8,128)S(1)}, u32[]{:S(2)}, u32[]{:S(2)}) %collective-permute-start.4) | collective-permute-done | bytes 139296 | tf_op jit(solution)/shard_map/ppermute | solution.py:507
  16.1 2.4 %collective-permute-start.7 = (f32[272,128]{1,0:T(8,128)S(1)}, f32[272,128]{1,0:T(8,128)S(1)}, u32[]{:S(2)}, u32[]{:S(2)}) collective-permute-start(f32[272,128]{1,0:T(8,128)S(1)} %collective-permute-done.3.refs_1_.refs_10_), channel_id=1, source_target_pairs={{0,1},{1,0},{2,3},{3,2},{4,5},{5,4},{6,7},{7,6},{8,9},{9,8},{10,11... | collective-permute-start | bytes 417800 | tf_op jit(solution)/shard_map/ppermute | solution.py:507
  18.4 0.7 collective-permute-done.5.refs_3_.refs_12_
  19.2 1.6 %collective-permute-start.8 = (f32[272,128]{1,0:T(8,128)S(1)}, f32[272,128]{1,0:T(8,128)S(1)}, u32[]{:S(2)}, u32[]{:S(2)}) collective-permute-start(f32[272,128]{1,0:T(8,128)S(1)} %collective-permute-done.4.refs_2_.refs_11_), channel_id=1, source_target_pairs={{0,1},{1,0},{2,3},{3,2},{4,5},{5,4},{6,7},{7,6},{8,9},{9,8},{10,11... | collective-permute-start | bytes 417800 | tf_op jit(solution)/shard_map/ppermute | solution.py:507
  20.9 0.9 %collective-permute-done.8.refs_6_.refs_15_ = f32[272,128]{1,0:T(8,128)S(1)} collective-permute-done((f32[272,128]{1,0:T(8,128)S(1)}, f32[272,128]{1,0:T(8,128)S(1)}, u32[]{:S(2)}, u32[]{:S(2)}) %collective-permute-start.8) | collective-permute-done | bytes 139296 | tf_op jit(solution)/shard_map/ppermute | solution.py:507
  22.2 0.5 shard_map.47
  22.7 0.7 collective-permute-start.12
  23.4 0.7 collective-permute-start.10
  24.1 1.3 %collective-permute-start.11 = (f32[520,128]{1,0:T(8,128)S(1)}, f32[520,128]{1,0:T(8,128)}, u32[]{:S(2)}, u32[]{:S(2)}) collective-permute-start(f32[520,128]{1,0:T(8,128)S(1)} %shard_map.47), channel_id=1, source_target_pairs={{0,16},{1,17},{2,18},{3,19},{4,20},{5,21},{6,22},{7,23}} | collective-permute-start | bytes 798728 | tf_op jit(solution)/shard_map/ppermute | solution.py:507
  25.4 0.9 %broadcast_select_fusion = f32[512,256]{1,0:T(8,128)} fusion(f32[512,256]{1,0:T(8,128)S(1)} %copy-done.11, f32[512,256]{1,0:T(8,128)S(1)} %collective-permute-done.turned, pred[]{:T(512)S(6)} %eq.13), kind=kLoop, calls=%fused_computation.2 | loop fusion | flops 131072 | bytes 1572865 | tf_op jit(solution)/shard_map/jit(_where)/select_n | solution.py:553
  26.3 1.3 %collective-permute-start.14 = (f32[512,256]{1,0:T(8,128)}, f32[512,256]{1,0:T(8,128)}, u32[]{:S(2)}, u32[]{:S(2)}) collective-permute-start(f32[512,256]{1,0:T(8,128)} %broadcast_select_fusion), channel_id=1, source_target_pairs={{8,14},{9,15},{16,18},{17,19},{24,26},{25,27},{10,12},{11,13},{20,... | collective-permute-start | bytes 1572872 | tf_op jit(solution)/shard_map/ppermute | solution.py:507
  27.6 10.8 %collective-permute-done.11 = f32[520,128]{1,0:T(8,128)} collective-permute-done((f32[520,128]{1,0:T(8,128)S(1)}, f32[520,128]{1,0:T(8,128)}, u32[]{:S(2)}, u32[]{:S(2)}) %collective-permute-start.11) | collective-permute-done | bytes 266272 | tf_op jit(solution)/shard_map/ppermute | solution.py:507
  38.4 1.0 %add_select_fusion.here = f32[520,128]{1,0:T(8,128)S(1)} fusion(f32[520,128]{1,0:T(8,128)S(1)} %shard_map.47, f32[520,128]{1,0:T(8,128)S(1)} %collective-permute-done.12, f32[520,128]{1,0:T(8,128)S(1)} %collective-permute-done.10, f32[520,128]{1,0:T(8,128)} %collective-permute-done.11, pred[]{:T(512)S(6)} %eq.14), kind=kLoop, calls=%fused_computation.1 | loop fusion | flops 199680 | bytes 1331201 | tf_op jit(solution)/shard_map/jit(_where)/select_n | solution.py:548
  39.4 2.3 %collective-permute-start.13 = (f32[520,128]{1,0:T(8,128)S(1)}, f32[520,128]{1,0:T(8,128)}, u32[]{:S(2)}, u32[]{:S(2)}) collective-permute-start(f32[520,128]{1,0:T(8,128)S(1)} %add_select_fusion.here), channel_id=1, source_target_pairs={{0,1},{1,0},{2,3},{3,2},{4,5},{5,4},{6,7},{7,6},{8,9},{9,8},{10,11... | collective-permute-start | bytes 798728 | tf_op jit(solution)/shard_map/ppermute | solution.py:507
  41.7 0.6 shard_map.48.refs_4_
  42.3 1.3 %collective-permute-start.16 = (f32[256,512]{1,0:T(8,128)S(1)}, f32[256,512]{1,0:T(8,128)S(1)}, u32[]{:S(2)}, u32[]{:S(2)}) collective-permute-start(f32[256,512]{1,0:T(8,128)S(1)} %shard_map.48.refs_4_), channel_id=1, source_target_pairs={{10,18},{11,19},{20,28},{21,29},{30,22},{31,23}} | collective-permute-start | bytes 1572872 | tf_op jit(solution)/shard_map/ppermute | solution.py:507
  43.6 0.7 collective-permute-start.17
  44.3 0.7 collective-permute-start.18
  45.0 9.8 %all-to-all-start = ((f32[8,136,128]{2,1,0:T(8,128)}), f32[8,136,128]{2,1,0:T(8,128)}, u32[]{:S(2)}, u32[]{:S(2)}) async-start(f32[8,136,128]{2,1,0:T(8,128)} %get-tuple-element.36), calls=%async_computation | async-start | bytes 1114112 | tf_op jit(solution)/shard_map/all_to_all | solution.py:560
  54.8 13.6 %shard_map.49.refs_8_ = f32[3,256,256]{2,1,0:T(8,128)} custom-call(s32[5]{0:T(128)S(1)} %stack.23.info, f32[520,128]{1,0:T(8,128)S(1)} %add_select_fusion.here, f32[520,128]{1,0:T(8,128)} %collective-permute-done.13.there), custom_call_target="tpu_custom_call" | custom-call | flops 8589934592 | bytes 1048576 | tf_op jit(solution)/shard_map/pallas_call | solution.py:482
  68.4 1.2 %select_select_fusion.refs_2_ = f32[512,256]{1,0:T(8,128)S(1)} fusion(f32[512,256]{1,0:T(8,128)S(1)} %copy-done.12, f32[512,256]{1,0:T(8,128)S(1)} %collective-permute-done.turned, f32[512,256]{1,0:T(8,128)} %collective-permute-done.14, pred[]{:T(512)S(6)} %eq.15, pred[]{:T(512)S(6)} %eq.13), kind=kLoop, calls=%fused_computation | loop fusion | flops 262144 | bytes 2097154 | tf_op jit(solution)/shard_map/jit(_where)/select_n | solution.py:576
  69.6 0.4 collective-permute-start.15
  70.0 1.5 %collective-permute-done.15.refs_3_ = f32[512,256]{1,0:T(8,128)S(1)} collective-permute-done((f32[512,256]{1,0:T(8,128)S(1)}, f32[512,256]{1,0:T(8,128)S(1)}, u32[]{:S(2)}, u32[]{:S(2)}) %collective-permute-start.15) | collective-permute-done | bytes 524320 | tf_op jit(solution)/shard_map/ppermute | solution.py:507
  71.6 5.8 %shard_map.50 = f32[512,256]{1,0:T(8,128)} custom-call(s32[5]{0:T(128)S(1)} %stack.23.info, f32[512,256]{1,0:T(8,128)} %refs_0_.1, f32[8,136,128]{2,1,0:T(8,128)} %all-to-all-done.refs_1_, f32[512,256]{1,0:T(8,128)S(1)} %select_select_fusion.refs_2_, f32[512,256]{1,0:T(8,128)S(1)} %collective-permute-done.15.refs_3_, f32[256,512]{1,0:T(8,128)} %copy-done.8, ...), custom_call_target="tpu_custom_call" | custom-call | flops 2147483648 | bytes 1048576 | tf_op jit(solution)/shard_map/pallas_call | solution.py:482
  (44 shorter events, 0.9 us)
Async XLA Ops:
  0.0 0.7 copy-start.10
  0.0 3.7 %copy-start.11 = (f32[512,256]{1,0:T(8,128)S(1)}, f32[512,256]{1,0:T(8,128)}, u32[]{:S(2)}) copy-start(f32[512,256]{1,0:T(8,128)} %refs_0_.1) | copy-start | bytes 1572868
  3.1 38.6 %copy-start = (f32[272,128]{1,0:T(8,128)}, f32[272,128]{1,0:T(8,128)S(1)}, u32[]{:S(2)}) copy-start(f32[272,128]{1,0:T(8,128)S(1)} %get-tuple-element.30.refs_0_.refs_9_) | copy-start | bytes 417796
  3.1 4.5 %collective-permute-start.1 = (f32[520,128]{1,0:T(8,128)S(1)}, f32[520,128]{1,0:T(8,128)S(1)}, u32[]{:S(2)}, u32[]{:S(2)}) collective-permute-start(f32[520,128]{1,0:T(8,128)S(1)} %get-tuple-element.29.diag), channel_id=1, source_target_pairs={{0,4},{1,5}} | collective-permute-start | bytes 798728 | tf_op jit(solution)/shard_map/ppermute | solution.py:507
  3.8 17.0 %collective-permute-start = (f32[512,256]{1,0:T(8,128)S(1)}, f32[512,256]{1,0:T(8,128)S(1)}, u32[]{:S(2)}, u32[]{:S(2)}) collective-permute-start(f32[512,256]{1,0:T(8,128)S(1)} %copy-done.11), channel_id=1, source_target_pairs={{2,10},{3,11},{4,20},{5,21},{6,30},{7,31}} | collective-permute-start | bytes 1572872 | tf_op jit(solution)/shard_map/ppermute | solution.py:507
  4.5 4.6 %collective-permute-start.3 = (f32[272,128]{1,0:T(8,128)S(1)}, f32[272,128]{1,0:T(8,128)S(1)}, u32[]{:S(2)}, u32[]{:S(2)}) collective-permute-start(f32[272,128]{1,0:T(8,128)S(1)} %get-tuple-element.30.refs_0_.refs_9_), channel_id=1, source_target_pairs={{0,2},{1,3},{2,0},{3,1},{4,6},{5,7},{6,4},{7,5},{8,10},{9,11},{10,... | collective-permute-start | bytes 417800 | tf_op jit(solution)/shard_map/ppermute | solution.py:507
  4.7 11.4 %collective-permute-start.4 = (f32[272,128]{1,0:T(8,128)S(1)}, f32[272,128]{1,0:T(8,128)S(1)}, u32[]{:S(2)}, u32[]{:S(2)}) collective-permute-start(f32[272,128]{1,0:T(8,128)S(1)} %get-tuple-element.30.refs_0_.refs_9_), channel_id=1, source_target_pairs={{0,4},{1,5},{2,6},{3,7},{4,0},{5,1},{6,2},{7,3},{8,12},{9,13},{10,... | collective-permute-start | bytes 417800 | tf_op jit(solution)/shard_map/ppermute | solution.py:507
  7.6 11.6 %collective-permute-start.5 = (f32[272,128]{1,0:T(8,128)S(1)}, f32[272,128]{1,0:T(8,128)S(1)}, u32[]{:S(2)}, u32[]{:S(2)}) collective-permute-start(f32[272,128]{1,0:T(8,128)S(1)} %get-tuple-element.30.refs_0_.refs_9_), channel_id=1, source_target_pairs={{0,6},{1,7},{2,4},{3,5},{4,2},{5,3},{6,0},{7,1},{8,14},{9,15},{10,... | collective-permute-start | bytes 417800 | tf_op jit(solution)/shard_map/ppermute | solution.py:507
  7.7 14.5 %collective-permute-start.2 = (f32[520,128]{1,0:T(8,128)S(1)}, f32[520,128]{1,0:T(8,128)S(1)}, u32[]{:S(2)}, u32[]{:S(2)}) collective-permute-start(f32[520,128]{1,0:T(8,128)S(1)} %broadcast_select_fusion.1), channel_id=1, source_target_pairs={{0,2},{1,3},{4,6},{5,7}} | collective-permute-start | bytes 798728 | tf_op jit(solution)/shard_map/ppermute | solution.py:507
  9.1 32.6 %copy-start.1 = (f32[272,128]{1,0:T(8,128)}, f32[272,128]{1,0:T(8,128)S(1)}, u32[]{:S(2)}) copy-start(f32[272,128]{1,0:T(8,128)S(1)} %collective-permute-done.3.refs_1_.refs_10_) | copy-start | bytes 417796
  9.1 11.8 %collective-permute-start.6 = (f32[272,128]{1,0:T(8,128)S(1)}, f32[272,128]{1,0:T(8,128)S(1)}, u32[]{:S(2)}, u32[]{:S(2)}) collective-permute-start(f32[272,128]{1,0:T(8,128)S(1)} %get-tuple-element.30.refs_0_.refs_9_), channel_id=1, source_target_pairs={{0,1},{1,0},{2,3},{3,2},{4,5},{5,4},{6,7},{7,6},{8,9},{9,8},{10,11... | collective-permute-start | bytes 417800 | tf_op jit(solution)/shard_map/ppermute | solution.py:507
  16.1 25.6 %copy-start.2 = (f32[272,128]{1,0:T(8,128)}, f32[272,128]{1,0:T(8,128)S(1)}, u32[]{:S(2)}) copy-start(f32[272,128]{1,0:T(8,128)S(1)} %collective-permute-done.4.refs_2_.refs_11_) | copy-start | bytes 417796
  16.1 4.8 %collective-permute-start.7 = (f32[272,128]{1,0:T(8,128)S(1)}, f32[272,128]{1,0:T(8,128)S(1)}, u32[]{:S(2)}, u32[]{:S(2)}) collective-permute-start(f32[272,128]{1,0:T(8,128)S(1)} %collective-permute-done.3.refs_1_.refs_10_), channel_id=1, source_target_pairs={{0,1},{1,0},{2,3},{3,2},{4,5},{5,4},{6,7},{7,6},{8,9},{9,8},{10,11... | collective-permute-start | bytes 417800 | tf_op jit(solution)/shard_map/ppermute | solution.py:507
  19.2 22.5 %copy-start.3 = (f32[272,128]{1,0:T(8,128)}, f32[272,128]{1,0:T(8,128)S(1)}, u32[]{:S(2)}) copy-start(f32[272,128]{1,0:T(8,128)S(1)} %collective-permute-done.5.refs_3_.refs_12_) | copy-start | bytes 417796
  19.2 2.6 %collective-permute-start.8 = (f32[272,128]{1,0:T(8,128)S(1)}, f32[272,128]{1,0:T(8,128)S(1)}, u32[]{:S(2)}, u32[]{:S(2)}) collective-permute-start(f32[272,128]{1,0:T(8,128)S(1)} %collective-permute-done.4.refs_2_.refs_11_), channel_id=1, source_target_pairs={{0,1},{1,0},{2,3},{3,2},{4,5},{5,4},{6,7},{7,6},{8,9},{9,8},{10,11... | collective-permute-start | bytes 417800 | tf_op jit(solution)/shard_map/ppermute | solution.py:507
  20.8 1.4 %collective-permute-start.9 = (f32[272,128]{1,0:T(8,128)S(1)}, f32[272,128]{1,0:T(8,128)S(1)}, u32[]{:S(2)}, u32[]{:S(2)}) collective-permute-start(f32[272,128]{1,0:T(8,128)S(1)} %collective-permute-done.5.refs_3_.refs_12_), channel_id=1, source_target_pairs={{0,1},{1,0},{2,3},{3,2},{4,5},{5,4},{6,7},{7,6},{8,9},{9,8},{10,11... | collective-permute-start | bytes 417800 | tf_op jit(solution)/shard_map/ppermute | solution.py:507
  20.9 20.8 %copy-start.4 = (f32[272,128]{1,0:T(8,128)}, f32[272,128]{1,0:T(8,128)S(1)}, u32[]{:S(2)}) copy-start(f32[272,128]{1,0:T(8,128)S(1)} %collective-permute-done.6.refs_4_.refs_13_) | copy-start | bytes 417796
  20.9 20.8 %copy-start.5 = (f32[272,128]{1,0:T(8,128)}, f32[272,128]{1,0:T(8,128)S(1)}, u32[]{:S(2)}) copy-start(f32[272,128]{1,0:T(8,128)S(1)} %collective-permute-done.7.refs_5_.refs_14_) | copy-start | bytes 417796
  21.8 19.9 %copy-start.6 = (f32[272,128]{1,0:T(8,128)}, f32[272,128]{1,0:T(8,128)S(1)}, u32[]{:S(2)}) copy-start(f32[272,128]{1,0:T(8,128)S(1)} %collective-permute-done.8.refs_6_.refs_15_) | copy-start | bytes 417796
  22.2 19.5 %copy-start.7 = (f32[272,128]{1,0:T(8,128)}, f32[272,128]{1,0:T(8,128)S(1)}, u32[]{:S(2)}) copy-start(f32[272,128]{1,0:T(8,128)S(1)} %collective-permute-done.9.refs_7_.refs_16_) | copy-start | bytes 417796
  22.7 4.8 %collective-permute-start.12 = (f32[520,128]{1,0:T(8,128)S(1)}, f32[520,128]{1,0:T(8,128)S(1)}, u32[]{:S(2)}, u32[]{:S(2)}) collective-permute-start(f32[520,128]{1,0:T(8,128)S(1)} %shard_map.47), channel_id=1, source_target_pairs={{0,24},{1,25},{2,26},{3,27},{4,28},{5,29},{6,30},{7,31}} | collective-permute-start | bytes 798728 | tf_op jit(solution)/shard_map/ppermute | solution.py:507
  23.4 4.2 %collective-permute-start.10 = (f32[520,128]{1,0:T(8,128)S(1)}, f32[520,128]{1,0:T(8,128)S(1)}, u32[]{:S(2)}, u32[]{:S(2)}) collective-permute-start(f32[520,128]{1,0:T(8,128)S(1)} %shard_map.47), channel_id=1, source_target_pairs={{0,8},{1,9},{2,10},{3,11},{4,12},{5,13},{6,14},{7,15}} | collective-permute-start | bytes 798728 | tf_op jit(solution)/shard_map/ppermute | solution.py:507
  24.1 14.3 %collective-permute-start.11 = (f32[520,128]{1,0:T(8,128)S(1)}, f32[520,128]{1,0:T(8,128)}, u32[]{:S(2)}, u32[]{:S(2)}) collective-permute-start(f32[520,128]{1,0:T(8,128)S(1)} %shard_map.47), channel_id=1, source_target_pairs={{0,16},{1,17},{2,18},{3,19},{4,20},{5,21},{6,22},{7,23}} | collective-permute-start | bytes 798728 | tf_op jit(solution)/shard_map/ppermute | solution.py:507
  26.3 28.5 %collective-permute-start.14 = (f32[512,256]{1,0:T(8,128)}, f32[512,256]{1,0:T(8,128)}, u32[]{:S(2)}, u32[]{:S(2)}) collective-permute-start(f32[512,256]{1,0:T(8,128)} %broadcast_select_fusion), channel_id=1, source_target_pairs={{8,14},{9,15},{16,18},{17,19},{24,26},{25,27},{10,12},{11,13},{20,... | collective-permute-start | bytes 1572872 | tf_op jit(solution)/shard_map/ppermute | solution.py:507
  39.4 15.4 %collective-permute-start.13 = (f32[520,128]{1,0:T(8,128)S(1)}, f32[520,128]{1,0:T(8,128)}, u32[]{:S(2)}, u32[]{:S(2)}) collective-permute-start(f32[520,128]{1,0:T(8,128)S(1)} %add_select_fusion.here), channel_id=1, source_target_pairs={{0,1},{1,0},{2,3},{3,2},{4,5},{5,4},{6,7},{7,6},{8,9},{9,8},{10,11... | collective-permute-start | bytes 798728 | tf_op jit(solution)/shard_map/ppermute | solution.py:507
  42.3 2.7 %copy-start.8 = (f32[256,512]{1,0:T(8,128)}, f32[256,512]{1,0:T(8,128)S(1)}, u32[]{:S(2)}) copy-start(f32[256,512]{1,0:T(8,128)S(1)} %shard_map.48.refs_4_) | copy-start | bytes 1572868
  42.3 27.7 %collective-permute-start.16 = (f32[256,512]{1,0:T(8,128)S(1)}, f32[256,512]{1,0:T(8,128)S(1)}, u32[]{:S(2)}, u32[]{:S(2)}) collective-permute-start(f32[256,512]{1,0:T(8,128)S(1)} %shard_map.48.refs_4_), channel_id=1, source_target_pairs={{10,18},{11,19},{20,28},{21,29},{30,22},{31,23}} | collective-permute-start | bytes 1572872 | tf_op jit(solution)/shard_map/ppermute | solution.py:507
  43.6 26.4 %collective-permute-start.17 = (f32[256,512]{1,0:T(8,128)S(1)}, f32[256,512]{1,0:T(8,128)S(1)}, u32[]{:S(2)}, u32[]{:S(2)}) collective-permute-start(f32[256,512]{1,0:T(8,128)S(1)} %shard_map.48.refs_4_), channel_id=1, source_target_pairs={{10,26},{11,27},{20,12},{21,13},{30,14},{31,15}} | collective-permute-start | bytes 1572872 | tf_op jit(solution)/shard_map/ppermute | solution.py:507
  44.3 25.7 %collective-permute-start.18 = (f32[256,512]{1,0:T(8,128)S(1)}, f32[256,512]{1,0:T(8,128)S(1)}, u32[]{:S(2)}, u32[]{:S(2)}) collective-permute-start(f32[256,512]{1,0:T(8,128)S(1)} %shard_map.48.refs_4_), channel_id=1, source_target_pairs={{10,2},{11,3},{20,4},{21,5},{30,6},{31,7}} | collective-permute-start | bytes 1572872 | tf_op jit(solution)/shard_map/ppermute | solution.py:507
  45.0 26.6 %all-to-all-start = ((f32[8,136,128]{2,1,0:T(8,128)}), f32[8,136,128]{2,1,0:T(8,128)}, u32[]{:S(2)}, u32[]{:S(2)}) async-start(f32[8,136,128]{2,1,0:T(8,128)} %get-tuple-element.36), calls=%async_computation | async-start | bytes 1114112 | tf_op jit(solution)/shard_map/all_to_all | solution.py:560
  54.8 13.7 %copy-start.12 = (f32[512,256]{1,0:T(8,128)S(1)}, f32[512,256]{1,0:T(8,128)}, u32[]{:S(2)}) copy-start(f32[512,256]{1,0:T(8,128)} %refs_0_.1) | copy-start | bytes 1572868
  69.6 2.0 %collective-permute-start.15 = (f32[512,256]{1,0:T(8,128)S(1)}, f32[512,256]{1,0:T(8,128)S(1)}, u32[]{:S(2)}, u32[]{:S(2)}) collective-permute-start(f32[512,256]{1,0:T(8,128)S(1)} %select_select_fusion.refs_2_), channel_id=1, source_target_pairs={{0,1},{1,0},{2,3},{3,2},{4,5},{5,4},{6,7},{7,6},{8,9},{9,8},{10,11... | collective-permute-start | bytes 1572872 | tf_op jit(solution)/shard_map/ppermute | solution.py:507
  (1 other events, 0.7 us)

commit v12 on v11

--- a/solution.py
+++ b/solution.py
@@ -392,7 +392,7 @@
     last = len(copies)
     for c in copies:
         c.start()
-    way = jnp.where(group == 0, 3, jnp.where((group == 2) | ((group == 3) & (layer == 2)), 1, 2))
+    way = jnp.where(group == 0, 1, jnp.where((group == 2) | ((group == 3) & (layer == 2)), 3, 2))
     way = jnp.where(group == layer, 0, way)
     for k, m in enumerate((matched, m1, m2, m3)):
 
@@ -560,10 +560,12 @@
     arrived = lax.all_to_all(outgoing, "front", split_axis=0, concat_axis=0, tiled=True)
     away = [
         send(matched, [(dev(z, z, c), dev(g, z, c)) for z, g in pairs for c in both])
-        for pairs in (((1, 2), (2, 3), (3, 2)), ((1, 3), (2, 1), (3, 1)), ((1, 0), (2, 0), (3, 0)))
+        for pairs in (((1, 0), (2, 0), (3, 0)), ((1, 3), (2, 1), (3, 1)), ((1, 2), (2, 3), (3, 2)))
     ]
 
     diag, diag2, far = lax.optimization_barrier((diag, diag2, far))
+    piece = jnp.where(layer == 0, front, jnp.where(group == layer, turned, far))
+    piece2 = send(piece, swap)
     factors = kernel(
         factor_kernel,
         pltpu.HBM((3, width, width), F32),
@@ -572,9 +574,6 @@
         flops=1 << 33,
         sems=[(3,)],
     )
-    factors, far = lax.optimization_barrier((factors, far))
-    piece = jnp.where(layer == 0, front, jnp.where(group == layer, turned, far))
-    piece2 = send(piece, swap)
     return kernel(
         last_kernel,
         out(nrows, width),

time: 78 us -> 76.1 us (0.976)
  the two profiles are of different devices: /device:TPU:13 before, /device:TPU:11 now
where the time goes in v12:
time: 76.1 us; the launch traced here: 74.9 us
  starting transfers between devices  25.7 us (34%)
  waiting for transfers between devices  23.9 us (31%)
  Pallas kernels  23 us (30%)
  other arithmetic  1.13 us (1%)
    ppermute x19, waiting for transfers between devices, send(): return lax.ppermute(x, AXES, pairs)  23.9 us
    pallas_call x5, Pallas kernels, kernel(): pl.pallas_call(body, out_shape=outs, in_specs=spec, out_specs=jax.tree.ma...  23 us
    ppermute x19, starting transfers between devices, send(): return lax.ppermute(x, AXES, pairs)  21.6 us
    all_to_all x1, starting transfers between devices, aligned(): lax.all_to_all(outgoing, 'front', split_axis=0, concat_axis=0, tiled=True)  4.15 us
  transfers between devices with their start and end apart: 20, of which 4 were waited for; matrix products, arithmetic and copies ran while one was open for 2% of the time, Pallas kernels for 19%

profile of v12, /device:TPU:11, one launch (start us, length us, event | category | flops | bytes accessed | tf_op | source)
XLA Modules:
  0.0 74.9 jit_solution(13907139500339472955)
XLA Ops:
  0.0 0.1 stack.23.info
  0.1 0.6 copy-done.9
  0.7 2.4 %shard_map.46 = (f32[8,136,128]{2,1,0:T(8,128)}, f32[272,128]{1,0:T(8,128)S(1)}, f32[520,128]{1,0:T(8,128)S(1)}) custom-call(s32[4]{0:T(128)S(1)} %copy-done.9, s32[4]{0:T(128)S(1)} %copy-done.10, s32[5]{0:T(128)S(1)} %stack.23.info, f32[4,128,128]{2,1,0:T(8,128)} %updates.1, f32[512,256]{1,0:T(8,128)} %refs_0_.1), custom_call_target="tpu_custom_call" | custom-call | flops 1048576 | bytes 1048576 | tf_op jit(solution)/shard_map/pallas_call | solution.py:482
  3.1 0.7 collective-permute-start.1
  3.8 1.3 %collective-permute-start = (f32[512,256]{1,0:T(8,128)S(1)}, f32[512,256]{1,0:T(8,128)S(1)}, u32[]{:S(2)}, u32[]{:S(2)}) collective-permute-start(f32[512,256]{1,0:T(8,128)S(1)} %copy-done.11), channel_id=1, source_target_pairs={{2,10},{3,11},{4,20},{5,21},{6,30},{7,31}} | collective-permute-start | bytes 1572872 | tf_op jit(solution)/shard_map/ppermute | solution.py:507
  5.1 0.8 %collective-permute-start.5 = (f32[272,128]{1,0:T(8,128)S(1)}, f32[272,128]{1,0:T(8,128)S(1)}, u32[]{:S(2)}, u32[]{:S(2)}) collective-permute-start(f32[272,128]{1,0:T(8,128)S(1)} %get-tuple-element.28.refs_0_.refs_9_), channel_id=1, source_target_pairs={{0,6},{1,7},{2,4},{3,5},{4,2},{5,3},{6,0},{7,1},{8,14},{9,15},{10,... | collective-permute-start | bytes 417800 | tf_op jit(solution)/shard_map/ppermute | solution.py:507
  5.8 1.1 %collective-permute-start.4 = (f32[272,128]{1,0:T(8,128)S(1)}, f32[272,128]{1,0:T(8,128)S(1)}, u32[]{:S(2)}, u32[]{:S(2)}) collective-permute-start(f32[272,128]{1,0:T(8,128)S(1)} %get-tuple-element.28.refs_0_.refs_9_), channel_id=1, source_target_pairs={{0,4},{1,5},{2,6},{3,7},{4,0},{5,1},{6,2},{7,3},{8,12},{9,13},{10,... | collective-permute-start | bytes 417800 | tf_op jit(solution)/shard_map/ppermute | solution.py:507
  6.9 1.1 %collective-permute-start.3 = (f32[272,128]{1,0:T(8,128)S(1)}, f32[272,128]{1,0:T(8,128)S(1)}, u32[]{:S(2)}, u32[]{:S(2)}) collective-permute-start(f32[272,128]{1,0:T(8,128)S(1)} %get-tuple-element.28.refs_0_.refs_9_), channel_id=1, source_target_pairs={{0,2},{1,3},{2,0},{3,1},{4,6},{5,7},{6,4},{7,5},{8,10},{9,11},{10,... | collective-permute-start | bytes 417800 | tf_op jit(solution)/shard_map/ppermute | solution.py:507
  8.1 0.7 collective-permute-start.2
  8.8 7.7 %collective-permute-done.5.refs_3_.refs_12_ = f32[272,128]{1,0:T(8,128)S(1)} collective-permute-done((f32[272,128]{1,0:T(8,128)S(1)}, f32[272,128]{1,0:T(8,128)S(1)}, u32[]{:S(2)}, u32[]{:S(2)}) %collective-permute-start.5) | collective-permute-done | bytes 139296 | tf_op jit(solution)/shard_map/ppermute | solution.py:507
  16.4 1.1 %collective-permute-start.6 = (f32[272,128]{1,0:T(8,128)S(1)}, f32[272,128]{1,0:T(8,128)S(1)}, u32[]{:S(2)}, u32[]{:S(2)}) collective-permute-start(f32[272,128]{1,0:T(8,128)S(1)} %get-tuple-element.28.refs_0_.refs_9_), channel_id=1, source_target_pairs={{0,1},{1,0},{2,3},{3,2},{4,5},{5,4},{6,7},{7,6},{8,9},{9,8},{10,11... | collective-permute-start | bytes 417800 | tf_op jit(solution)/shard_map/ppermute | solution.py:507
  17.6 1.1 %collective-permute-start.9 = (f32[272,128]{1,0:T(8,128)S(1)}, f32[272,128]{1,0:T(8,128)S(1)}, u32[]{:S(2)}, u32[]{:S(2)}) collective-permute-start(f32[272,128]{1,0:T(8,128)S(1)} %collective-permute-done.5.refs_3_.refs_12_), channel_id=1, source_target_pairs={{0,1},{1,0},{2,3},{3,2},{4,5},{5,4},{6,7},{7,6},{8,9},{9,8},{10,11... | collective-permute-start | bytes 417800 | tf_op jit(solution)/shard_map/ppermute | solution.py:507
  18.8 1.2 %collective-permute-start.7 = (f32[272,128]{1,0:T(8,128)S(1)}, f32[272,128]{1,0:T(8,128)S(1)}, u32[]{:S(2)}, u32[]{:S(2)}) collective-permute-start(f32[272,128]{1,0:T(8,128)S(1)} %collective-permute-done.3.refs_1_.refs_10_), channel_id=1, source_target_pairs={{0,1},{1,0},{2,3},{3,2},{4,5},{5,4},{6,7},{7,6},{8,9},{9,8},{10,11... | collective-permute-start | bytes 417800 | tf_op jit(solution)/shard_map/ppermute | solution.py:507
  20.1 0.9 %collective-permute-done.7.refs_5_.refs_14_ = f32[272,128]{1,0:T(8,128)S(1)} collective-permute-done((f32[272,128]{1,0:T(8,128)S(1)}, f32[272,128]{1,0:T(8,128)S(1)}, u32[]{:S(2)}, u32[]{:S(2)}) %collective-permute-start.7) | collective-permute-done | bytes 139296 | tf_op jit(solution)/shard_map/ppermute | solution.py:507
  21.0 0.5 shard_map.47
  21.6 0.7 collective-permute-start.12
  22.3 0.7 collective-permute-start.11
  22.9 1.3 %collective-permute-start.10 = (f32[520,128]{1,0:T(8,128)S(1)}, f32[520,128]{1,0:T(8,128)S(1)}, u32[]{:S(2)}, u32[]{:S(2)}) collective-permute-start(f32[520,128]{1,0:T(8,128)S(1)} %shard_map.47), channel_id=1, source_target_pairs={{0,8},{1,9},{2,10},{3,11},{4,12},{5,13},{6,14},{7,15}} | collective-permute-start | bytes 798728 | tf_op jit(solution)/shard_map/ppermute | solution.py:507
  24.2 0.9 %broadcast_select_fusion = f32[512,256]{1,0:T(8,128)} fusion(f32[512,256]{1,0:T(8,128)S(1)} %copy-done.11, f32[512,256]{1,0:T(8,128)S(1)} %collective-permute-done.turned, pred[]{:T(512)S(6)} %eq.13), kind=kLoop, calls=%fused_computation.2 | loop fusion | flops 131072 | bytes 1572865 | tf_op jit(solution)/shard_map/jit(_where)/select_n | solution.py:553
  25.1 2.7 %collective-permute-start.14 = (f32[512,256]{1,0:T(8,128)}, f32[512,256]{1,0:T(8,128)}, u32[]{:S(2)}, u32[]{:S(2)}) collective-permute-start(f32[512,256]{1,0:T(8,128)} %broadcast_select_fusion), channel_id=1, source_target_pairs={{8,14},{9,15},{16,18},{17,19},{24,26},{25,27},{10,12},{11,13},{20,... | collective-permute-start | bytes 1572872 | tf_op jit(solution)/shard_map/ppermute | solution.py:507
  27.8 13.6 %collective-permute-done.10 = f32[520,128]{1,0:T(8,128)S(1)} collective-permute-done((f32[520,128]{1,0:T(8,128)S(1)}, f32[520,128]{1,0:T(8,128)S(1)}, u32[]{:S(2)}, u32[]{:S(2)}) %collective-permute-start.10) | collective-permute-done | bytes 266272 | tf_op jit(solution)/shard_map/ppermute | solution.py:507
  41.5 2.3 %collective-permute-start.13 = (f32[520,128]{1,0:T(8,128)S(1)}, f32[520,128]{1,0:T(8,128)S(1)}, u32[]{:S(2)}, u32[]{:S(2)}) collective-permute-start(f32[520,128]{1,0:T(8,128)S(1)} %add_select_fusion.here), channel_id=1, source_target_pairs={{0,1},{1,0},{2,3},{3,2},{4,5},{5,4},{6,7},{7,6},{8,9},{9,8},{10,11... | collective-permute-start | bytes 798728 | tf_op jit(solution)/shard_map/ppermute | solution.py:507
  43.8 1.0 %shard_map.48.refs_4_ = f32[256,512]{1,0:T(8,128)S(1)} custom-call(s32[5]{0:T(128)S(1)} %stack.23.info, f32[512,256]{1,0:T(8,128)S(1)} %collective-permute-done.turned, f32[272,128]{1,0:T(8,128)S(1)} %get-tuple-element.28.refs_0_.refs_9_, f32[272,128]{1,0:T(8,128)S(1)} %collective-permute-done.3.refs_1_.refs_10_, ...), custom_call_target="tpu_custom_call" | custom-call | flops 1048576 | bytes 1048576 | tf_op jit(solution)/shard_map/pallas_call | solution.py:482
  44.8 1.3 %collective-permute-start.18 = (f32[256,512]{1,0:T(8,128)S(1)}, f32[256,512]{1,0:T(8,128)S(1)}, u32[]{:S(2)}, u32[]{:S(2)}) collective-permute-start(f32[256,512]{1,0:T(8,128)S(1)} %shard_map.48.refs_4_), channel_id=1, source_target_pairs={{10,18},{11,19},{20,28},{21,29},{30,22},{31,23}} | collective-permute-start | bytes 1572872 | tf_op jit(solution)/shard_map/ppermute | solution.py:507
  46.1 1.3 %collective-permute-start.17 = (f32[256,512]{1,0:T(8,128)S(1)}, f32[256,512]{1,0:T(8,128)S(1)}, u32[]{:S(2)}, u32[]{:S(2)}) collective-permute-start(f32[256,512]{1,0:T(8,128)S(1)} %shard_map.48.refs_4_), channel_id=1, source_target_pairs={{10,26},{11,27},{20,12},{21,13},{30,14},{31,15}} | collective-permute-start | bytes 1572872 | tf_op jit(solution)/shard_map/ppermute | solution.py:507
  47.4 2.1 %collective-permute-start.16 = (f32[256,512]{1,0:T(8,128)S(1)}, f32[256,512]{1,0:T(8,128)}, u32[]{:S(2)}, u32[]{:S(2)}) collective-permute-start(f32[256,512]{1,0:T(8,128)S(1)} %shard_map.48.refs_4_), channel_id=1, source_target_pairs={{10,2},{11,3},{20,4},{21,5},{30,6},{31,7}} | collective-permute-start | bytes 1572872 | tf_op jit(solution)/shard_map/ppermute | solution.py:507
  49.5 4.2 %all-to-all-start = ((f32[8,136,128]{2,1,0:T(8,128)}), f32[8,136,128]{2,1,0:T(8,128)}, u32[]{:S(2)}, u32[]{:S(2)}) async-start(f32[8,136,128]{2,1,0:T(8,128)} %get-tuple-element.34), calls=%async_computation | async-start | bytes 1114112 | tf_op jit(solution)/shard_map/all_to_all | solution.py:560
  53.7 0.2 select_select_fusion.refs_2_
  53.9 0.1 collective-permute-start.15
  54.0 13.2 %shard_map.49.refs_8_ = f32[3,256,256]{2,1,0:T(8,128)} custom-call(s32[5]{0:T(128)S(1)} %stack.23.info, f32[520,128]{1,0:T(8,128)S(1)} %add_select_fusion.here, f32[520,128]{1,0:T(8,128)S(1)} %collective-permute-done.13.there), custom_call_target="tpu_custom_call" | custom-call | flops 8589934592 | bytes 1048576 | tf_op jit(solution)/shard_map/pallas_call | solution.py:482
  67.2 1.7 %collective-permute-done.16.refs_5_ = f32[256,512]{1,0:T(8,128)} collective-permute-done((f32[256,512]{1,0:T(8,128)S(1)}, f32[256,512]{1,0:T(8,128)}, u32[]{:S(2)}, u32[]{:S(2)}) %collective-permute-start.16) | collective-permute-done | bytes 524320 | tf_op jit(solution)/shard_map/ppermute | solution.py:507
  68.8 6.0 %shard_map.50 = f32[512,256]{1,0:T(8,128)} custom-call(s32[5]{0:T(128)S(1)} %stack.23.info, f32[512,256]{1,0:T(8,128)} %refs_0_.1, f32[8,136,128]{2,1,0:T(8,128)} %all-to-all-done.refs_1_, f32[512,256]{1,0:T(8,128)S(1)} %select_select_fusion.refs_2_, f32[512,256]{1,0:T(8,128)S(1)} %collective-permute-done.15.refs_3_, f32[256,512]{1,0:T(8,128)} %copy-done.8, ...), custom_call_target="tpu_custom_call" | custom-call | flops 2147483648 | bytes 1048576 | tf_op jit(solution)/shard_map/pallas_call | solution.py:482
  (42 shorter events, 0.3 us)
Async XLA Ops:
  0.0 0.7 copy-start.9
  0.0 0.7 copy-start.10
  0.0 3.8 %copy-start.11 = (f32[512,256]{1,0:T(8,128)S(1)}, f32[512,256]{1,0:T(8,128)}, u32[]{:S(2)}) copy-start(f32[512,256]{1,0:T(8,128)} %refs_0_.1) | copy-start | bytes 1572868
  3.1 40.7 %copy-start = (f32[272,128]{1,0:T(8,128)}, f32[272,128]{1,0:T(8,128)S(1)}, u32[]{:S(2)}) copy-start(f32[272,128]{1,0:T(8,128)S(1)} %get-tuple-element.28.refs_0_.refs_9_) | copy-start | bytes 417796
  3.1 5.0 %collective-permute-start.1 = (f32[520,128]{1,0:T(8,128)S(1)}, f32[520,128]{1,0:T(8,128)S(1)}, u32[]{:S(2)}, u32[]{:S(2)}) collective-permute-start(f32[520,128]{1,0:T(8,128)S(1)} %get-tuple-element.27.diag), channel_id=1, source_target_pairs={{0,4},{1,5}} | collective-permute-start | bytes 798728 | tf_op jit(solution)/shard_map/ppermute | solution.py:507
  3.8 15.0 %collective-permute-start = (f32[512,256]{1,0:T(8,128)S(1)}, f32[512,256]{1,0:T(8,128)S(1)}, u32[]{:S(2)}, u32[]{:S(2)}) collective-permute-start(f32[512,256]{1,0:T(8,128)S(1)} %copy-done.11), channel_id=1, source_target_pairs={{2,10},{3,11},{4,20},{5,21},{6,30},{7,31}} | collective-permute-start | bytes 1572872 | tf_op jit(solution)/shard_map/ppermute | solution.py:507
  5.1 11.4 %collective-permute-start.5 = (f32[272,128]{1,0:T(8,128)S(1)}, f32[272,128]{1,0:T(8,128)S(1)}, u32[]{:S(2)}, u32[]{:S(2)}) collective-permute-start(f32[272,128]{1,0:T(8,128)S(1)} %get-tuple-element.28.refs_0_.refs_9_), channel_id=1, source_target_pairs={{0,6},{1,7},{2,4},{3,5},{4,2},{5,3},{6,0},{7,1},{8,14},{9,15},{10,... | collective-permute-start | bytes 417800 | tf_op jit(solution)/shard_map/ppermute | solution.py:507
  5.8 11.7 %collective-permute-start.4 = (f32[272,128]{1,0:T(8,128)S(1)}, f32[272,128]{1,0:T(8,128)S(1)}, u32[]{:S(2)}, u32[]{:S(2)}) collective-permute-start(f32[272,128]{1,0:T(8,128)S(1)} %get-tuple-element.28.refs_0_.refs_9_), channel_id=1, source_target_pairs={{0,4},{1,5},{2,6},{3,7},{4,0},{5,1},{6,2},{7,3},{8,12},{9,13},{10,... | collective-permute-start | bytes 417800 | tf_op jit(solution)/shard_map/ppermute | solution.py:507
  6.9 11.8 %collective-permute-start.3 = (f32[272,128]{1,0:T(8,128)S(1)}, f32[272,128]{1,0:T(8,128)S(1)}, u32[]{:S(2)}, u32[]{:S(2)}) collective-permute-start(f32[272,128]{1,0:T(8,128)S(1)} %get-tuple-element.28.refs_0_.refs_9_), channel_id=1, source_target_pairs={{0,2},{1,3},{2,0},{3,1},{4,6},{5,7},{6,4},{7,5},{8,10},{9,11},{10,... | collective-permute-start | bytes 417800 | tf_op jit(solution)/shard_map/ppermute | solution.py:507
  8.1 12.9 %collective-permute-start.2 = (f32[520,128]{1,0:T(8,128)S(1)}, f32[520,128]{1,0:T(8,128)S(1)}, u32[]{:S(2)}, u32[]{:S(2)}) collective-permute-start(f32[520,128]{1,0:T(8,128)S(1)} %broadcast_select_fusion.1), channel_id=1, source_target_pairs={{0,2},{1,3},{4,6},{5,7}} | collective-permute-start | bytes 798728 | tf_op jit(solution)/shard_map/ppermute | solution.py:507
  16.4 27.3 %copy-start.1 = (f32[272,128]{1,0:T(8,128)}, f32[272,128]{1,0:T(8,128)S(1)}, u32[]{:S(2)}) copy-start(f32[272,128]{1,0:T(8,128)S(1)} %collective-permute-done.5.refs_3_.refs_12_) | copy-start | bytes 417796
  16.4 3.6 %collective-permute-start.6 = (f32[272,128]{1,0:T(8,128)S(1)}, f32[272,128]{1,0:T(8,128)S(1)}, u32[]{:S(2)}, u32[]{:S(2)}) collective-permute-start(f32[272,128]{1,0:T(8,128)S(1)} %get-tuple-element.28.refs_0_.refs_9_), channel_id=1, source_target_pairs={{0,1},{1,0},{2,3},{3,2},{4,5},{5,4},{6,7},{7,6},{8,9},{9,8},{10,11... | collective-permute-start | bytes 417800 | tf_op jit(solution)/shard_map/ppermute | solution.py:507
  17.6 26.2 %copy-start.2 = (f32[272,128]{1,0:T(8,128)}, f32[272,128]{1,0:T(8,128)S(1)}, u32[]{:S(2)}) copy-start(f32[272,128]{1,0:T(8,128)S(1)} %collective-permute-done.4.refs_2_.refs_11_) | copy-start | bytes 417796
  17.6 2.4 %collective-permute-start.9 = (f32[272,128]{1,0:T(8,128)S(1)}, f32[272,128]{1,0:T(8,128)S(1)}, u32[]{:S(2)}, u32[]{:S(2)}) collective-permute-start(f32[272,128]{1,0:T(8,128)S(1)} %collective-permute-done.5.refs_3_.refs_12_), channel_id=1, source_target_pairs={{0,1},{1,0},{2,3},{3,2},{4,5},{5,4},{6,7},{7,6},{8,9},{9,8},{10,11... | collective-permute-start | bytes 417800 | tf_op jit(solution)/shard_map/ppermute | solution.py:507
  18.7 25.1 %copy-start.3 = (f32[272,128]{1,0:T(8,128)}, f32[272,128]{1,0:T(8,128)S(1)}, u32[]{:S(2)}) copy-start(f32[272,128]{1,0:T(8,128)S(1)} %collective-permute-done.3.refs_1_.refs_10_) | copy-start | bytes 417796
  18.7 1.4 %collective-permute-start.8 = (f32[272,128]{1,0:T(8,128)S(1)}, f32[272,128]{1,0:T(8,128)S(1)}, u32[]{:S(2)}, u32[]{:S(2)}) collective-permute-start(f32[272,128]{1,0:T(8,128)S(1)} %collective-permute-done.4.refs_2_.refs_11_), channel_id=1, source_target_pairs={{0,1},{1,0},{2,3},{3,2},{4,5},{5,4},{6,7},{7,6},{8,9},{9,8},{10,11... | collective-permute-start | bytes 417800 | tf_op jit(solution)/shard_map/ppermute | solution.py:507
  18.8 2.2 %collective-permute-start.7 = (f32[272,128]{1,0:T(8,128)S(1)}, f32[272,128]{1,0:T(8,128)S(1)}, u32[]{:S(2)}, u32[]{:S(2)}) collective-permute-start(f32[272,128]{1,0:T(8,128)S(1)} %collective-permute-done.3.refs_1_.refs_10_), channel_id=1, source_target_pairs={{0,1},{1,0},{2,3},{3,2},{4,5},{5,4},{6,7},{7,6},{8,9},{9,8},{10,11... | collective-permute-start | bytes 417800 | tf_op jit(solution)/shard_map/ppermute | solution.py:507
  20.0 23.8 %copy-start.4 = (f32[272,128]{1,0:T(8,128)}, f32[272,128]{1,0:T(8,128)S(1)}, u32[]{:S(2)}) copy-start(f32[272,128]{1,0:T(8,128)S(1)} %collective-permute-done.6.refs_4_.refs_13_) | copy-start | bytes 417796
  20.0 23.8 %copy-start.5 = (f32[272,128]{1,0:T(8,128)}, f32[272,128]{1,0:T(8,128)S(1)}, u32[]{:S(2)}) copy-start(f32[272,128]{1,0:T(8,128)S(1)} %collective-permute-done.9.refs_7_.refs_16_) | copy-start | bytes 417796
  20.1 23.7 %copy-start.6 = (f32[272,128]{1,0:T(8,128)}, f32[272,128]{1,0:T(8,128)S(1)}, u32[]{:S(2)}) copy-start(f32[272,128]{1,0:T(8,128)S(1)} %collective-permute-done.8.refs_6_.refs_15_) | copy-start | bytes 417796
  21.0 22.8 %copy-start.7 = (f32[272,128]{1,0:T(8,128)}, f32[272,128]{1,0:T(8,128)S(1)}, u32[]{:S(2)}) copy-start(f32[272,128]{1,0:T(8,128)S(1)} %collective-permute-done.7.refs_5_.refs_14_) | copy-start | bytes 417796
  21.6 6.2 %collective-permute-start.12 = (f32[520,128]{1,0:T(8,128)S(1)}, f32[520,128]{1,0:T(8,128)S(1)}, u32[]{:S(2)}, u32[]{:S(2)}) collective-permute-start(f32[520,128]{1,0:T(8,128)S(1)} %shard_map.47), channel_id=1, source_target_pairs={{0,24},{1,25},{2,26},{3,27},{4,28},{5,29},{6,30},{7,31}} | collective-permute-start | bytes 798728 | tf_op jit(solution)/shard_map/ppermute | solution.py:507
  22.3 5.6 %collective-permute-start.11 = (f32[520,128]{1,0:T(8,128)S(1)}, f32[520,128]{1,0:T(8,128)S(1)}, u32[]{:S(2)}, u32[]{:S(2)}) collective-permute-start(f32[520,128]{1,0:T(8,128)S(1)} %shard_map.47), channel_id=1, source_target_pairs={{0,16},{1,17},{2,18},{3,19},{4,20},{5,21},{6,22},{7,23}} | collective-permute-start | bytes 798728 | tf_op jit(solution)/shard_map/ppermute | solution.py:507
  22.9 18.5 %collective-permute-start.10 = (f32[520,128]{1,0:T(8,128)S(1)}, f32[520,128]{1,0:T(8,128)S(1)}, u32[]{:S(2)}, u32[]{:S(2)}) collective-permute-start(f32[520,128]{1,0:T(8,128)S(1)} %shard_map.47), channel_id=1, source_target_pairs={{0,8},{1,9},{2,10},{3,11},{4,12},{5,13},{6,14},{7,15}} | collective-permute-start | bytes 798728 | tf_op jit(solution)/shard_map/ppermute | solution.py:507
  25.1 28.6 %collective-permute-start.14 = (f32[512,256]{1,0:T(8,128)}, f32[512,256]{1,0:T(8,128)}, u32[]{:S(2)}, u32[]{:S(2)}) collective-permute-start(f32[512,256]{1,0:T(8,128)} %broadcast_select_fusion), channel_id=1, source_target_pairs={{8,14},{9,15},{16,18},{17,19},{24,26},{25,27},{10,12},{11,13},{20,... | collective-permute-start | bytes 1572872 | tf_op jit(solution)/shard_map/ppermute | solution.py:507
  41.5 12.2 %collective-permute-start.13 = (f32[520,128]{1,0:T(8,128)S(1)}, f32[520,128]{1,0:T(8,128)S(1)}, u32[]{:S(2)}, u32[]{:S(2)}) collective-permute-start(f32[520,128]{1,0:T(8,128)S(1)} %add_select_fusion.here), channel_id=1, source_target_pairs={{0,1},{1,0},{2,3},{3,2},{4,5},{5,4},{6,7},{7,6},{8,9},{9,8},{10,11... | collective-permute-start | bytes 798728 | tf_op jit(solution)/shard_map/ppermute | solution.py:507
  44.8 4.8 %copy-start.8 = (f32[256,512]{1,0:T(8,128)}, f32[256,512]{1,0:T(8,128)S(1)}, u32[]{:S(2)}) copy-start(f32[256,512]{1,0:T(8,128)S(1)} %shard_map.48.refs_4_) | copy-start | bytes 1572868
  44.8 22.4 %collective-permute-start.18 = (f32[256,512]{1,0:T(8,128)S(1)}, f32[256,512]{1,0:T(8,128)S(1)}, u32[]{:S(2)}, u32[]{:S(2)}) collective-permute-start(f32[256,512]{1,0:T(8,128)S(1)} %shard_map.48.refs_4_), channel_id=1, source_target_pairs={{10,18},{11,19},{20,28},{21,29},{30,22},{31,23}} | collective-permute-start | bytes 1572872 | tf_op jit(solution)/shard_map/ppermute | solution.py:507
  46.1 21.0 %collective-permute-start.17 = (f32[256,512]{1,0:T(8,128)S(1)}, f32[256,512]{1,0:T(8,128)S(1)}, u32[]{:S(2)}, u32[]{:S(2)}) collective-permute-start(f32[256,512]{1,0:T(8,128)S(1)} %shard_map.48.refs_4_), channel_id=1, source_target_pairs={{10,26},{11,27},{20,12},{21,13},{30,14},{31,15}} | collective-permute-start | bytes 1572872 | tf_op jit(solution)/shard_map/ppermute | solution.py:507
  47.4 21.4 %collective-permute-start.16 = (f32[256,512]{1,0:T(8,128)S(1)}, f32[256,512]{1,0:T(8,128)}, u32[]{:S(2)}, u32[]{:S(2)}) collective-permute-start(f32[256,512]{1,0:T(8,128)S(1)} %shard_map.48.refs_4_), channel_id=1, source_target_pairs={{10,2},{11,3},{20,4},{21,5},{30,6},{31,7}} | collective-permute-start | bytes 1572872 | tf_op jit(solution)/shard_map/ppermute | solution.py:507
  49.5 19.3 %all-to-all-start = ((f32[8,136,128]{2,1,0:T(8,128)}), f32[8,136,128]{2,1,0:T(8,128)}, u32[]{:S(2)}, u32[]{:S(2)}) async-start(f32[8,136,128]{2,1,0:T(8,128)} %get-tuple-element.34), calls=%async_computation | async-start | bytes 1114112 | tf_op jit(solution)/shard_map/all_to_all | solution.py:560
  53.9 14.9 %collective-permute-start.15 = (f32[512,256]{1,0:T(8,128)S(1)}, f32[512,256]{1,0:T(8,128)S(1)}, u32[]{:S(2)}, u32[]{:S(2)}) collective-permute-start(f32[512,256]{1,0:T(8,128)S(1)} %select_select_fusion.refs_2_), channel_id=1, source_target_pairs={{0,1},{1,0},{2,3},{3,2},{4,5},{5,4},{6,7},{7,6},{8,9},{9,8},{10,11... | collective-permute-start | bytes 1572872 | tf_op jit(solution)/shard_map/ppermute | solution.py:507

commit v13 on v12

--- a/solution.py
+++ b/solution.py
@@ -523,7 +523,7 @@
         away=True,
     )
     blocks = [payload]
-    for s in layers[1:]:
+    for s in (3, 2, 1):
         pairs = [(dev(g, z, c), dev(g, z ^ s, c)) for g in groups for z in layers for c in both]
         blocks.append(send(payload, pairs))
     blocks += [send(b, swap) for b in blocks]

time: 76.1 us -> 75.9 us (level)
  starting transfers between devices: 25.7 us -> 32.2 us
  waiting for transfers between devices: 23.9 us -> 17.5 us
    ppermute x19, waiting for transfers between devices: 23.9 us -> 17.5 us  [send(): return lax.ppermute(x, AXES, pairs)]
    ppermute x19, starting transfers between devices: 21.6 us -> 28 us  [send(): return lax.ppermute(x, AXES, pairs)]
  transfers between devices with their start and end apart: 20 -> 20, of which waited for: 4 -> 7; matrix products, arithmetic and copies ran while one was open for 2% -> 2% of each run, Pallas kernels for 19% -> 19%
where the time goes in v13:
time: 75.9 us; the launch traced here: 74.9 us
  starting transfers between devices  32.2 us (42%)
  Pallas kernels  23 us (30%)
  waiting for transfers between devices  17.5 us (23%)
  other arithmetic  1.13 us (1%)
    ppermute x19, starting transfers between devices, send(): return lax.ppermute(x, AXES, pairs)  28 us
    pallas_call x5, Pallas kernels, kernel(): pl.pallas_call(body, out_shape=outs, in_specs=spec, out_specs=jax.tree.ma...  23 us
    ppermute x19, waiting for transfers between devices, send(): return lax.ppermute(x, AXES, pairs)  17.5 us
    all_to_all x1, starting transfers between devices, aligned(): lax.all_to_all(outgoing, 'front', split_axis=0, concat_axis=0, tiled=True)  4.15 us
  transfers between devices with their start and end apart: 20, of which 7 were waited for; matrix products, arithmetic and copies ran while one was open for 2% of the time, Pallas kernels for 19%

profile of v13, /device:TPU:11, one launch (start us, length us, event | category | flops | bytes accessed | tf_op | source)
XLA Modules:
  0.0 74.9 jit_solution(18221393320872596122)
XLA Ops:
  0.1 0.6 copy-done.9
  0.7 2.4 %shard_map.46 = (f32[8,136,128]{2,1,0:T(8,128)}, f32[272,128]{1,0:T(8,128)S(1)}, f32[520,128]{1,0:T(8,128)S(1)}) custom-call(s32[4]{0:T(128)S(1)} %copy-done.9, s32[4]{0:T(128)S(1)} %copy-done.10, s32[5]{0:T(128)S(1)} %stack.23.info, f32[4,128,128]{2,1,0:T(8,128)} %updates.1, f32[512,256]{1,0:T(8,128)} %refs_0_.1), custom_call_target="tpu_custom_call" | custom-call | flops 1048576 | bytes 1048576 | tf_op jit(solution)/shard_map/pallas_call | solution.py:482
  3.1 0.7 collective-permute-start.1
  3.8 1.3 %collective-permute-start = (f32[512,256]{1,0:T(8,128)S(1)}, f32[512,256]{1,0:T(8,128)S(1)}, u32[]{:S(2)}, u32[]{:S(2)}) collective-permute-start(f32[512,256]{1,0:T(8,128)S(1)} %copy-done.11), channel_id=1, source_target_pairs={{2,10},{3,11},{4,20},{5,21},{6,30},{7,31}} | collective-permute-start | bytes 1572872 | tf_op jit(solution)/shard_map/ppermute | solution.py:507
  5.2 1.9 %collective-permute-start.4 = (f32[272,128]{1,0:T(8,128)S(1)}, f32[272,128]{1,0:T(8,128)S(1)}, u32[]{:S(2)}, u32[]{:S(2)}) collective-permute-start(f32[272,128]{1,0:T(8,128)S(1)} %get-tuple-element.28.refs_0_.refs_9_), channel_id=1, source_target_pairs={{0,4},{1,5},{2,6},{3,7},{4,0},{5,1},{6,2},{7,3},{8,12},{9,13},{10,... | collective-permute-start | bytes 417800 | tf_op jit(solution)/shard_map/ppermute | solution.py:507
  7.0 0.8 %collective-permute-start.3 = (f32[272,128]{1,0:T(8,128)S(1)}, f32[272,128]{1,0:T(8,128)S(1)}, u32[]{:S(2)}, u32[]{:S(2)}) collective-permute-start(f32[272,128]{1,0:T(8,128)S(1)} %get-tuple-element.28.refs_0_.refs_9_), channel_id=1, source_target_pairs={{0,6},{1,7},{2,4},{3,5},{4,2},{5,3},{6,0},{7,1},{8,14},{9,15},{10,... | collective-permute-start | bytes 417800 | tf_op jit(solution)/shard_map/ppermute | solution.py:507
  7.8 0.7 collective-permute-start.2
  8.5 1.2 %collective-permute-done.5.refs_3_.refs_12_ = f32[272,128]{1,0:T(8,128)S(1)} collective-permute-done((f32[272,128]{1,0:T(8,128)S(1)}, f32[272,128]{1,0:T(8,128)S(1)}, u32[]{:S(2)}, u32[]{:S(2)}) %collective-permute-start.5) | collective-permute-done | bytes 139296 | tf_op jit(solution)/shard_map/ppermute | solution.py:507
  9.7 2.7 %collective-permute-start.6 = (f32[272,128]{1,0:T(8,128)S(1)}, f32[272,128]{1,0:T(8,128)S(1)}, u32[]{:S(2)}, u32[]{:S(2)}) collective-permute-start(f32[272,128]{1,0:T(8,128)S(1)} %get-tuple-element.28.refs_0_.refs_9_), channel_id=1, source_target_pairs={{0,1},{1,0},{2,3},{3,2},{4,5},{5,4},{6,7},{7,6},{8,9},{9,8},{10,11... | collective-permute-start | bytes 417800 | tf_op jit(solution)/shard_map/ppermute | solution.py:507
  12.4 0.7 collective-permute-done.4.refs_2_.refs_11_
  13.1 5.1 %collective-permute-start.9 = (f32[272,128]{1,0:T(8,128)S(1)}, f32[272,128]{1,0:T(8,128)S(1)}, u32[]{:S(2)}, u32[]{:S(2)}) collective-permute-start(f32[272,128]{1,0:T(8,128)S(1)} %collective-permute-done.5.refs_3_.refs_12_), channel_id=1, source_target_pairs={{0,1},{1,0},{2,3},{3,2},{4,5},{5,4},{6,7},{7,6},{8,9},{9,8},{10,11... | collective-permute-start | bytes 417800 | tf_op jit(solution)/shard_map/ppermute | solution.py:507
  18.2 1.6 %collective-permute-done.3.refs_1_.refs_10_ = f32[272,128]{1,0:T(8,128)S(1)} collective-permute-done((f32[272,128]{1,0:T(8,128)S(1)}, f32[272,128]{1,0:T(8,128)S(1)}, u32[]{:S(2)}, u32[]{:S(2)}) %collective-permute-start.3) | collective-permute-done | bytes 139296 | tf_op jit(solution)/shard_map/ppermute | solution.py:507
  19.8 1.6 %collective-permute-start.8 = (f32[272,128]{1,0:T(8,128)S(1)}, f32[272,128]{1,0:T(8,128)S(1)}, u32[]{:S(2)}, u32[]{:S(2)}) collective-permute-start(f32[272,128]{1,0:T(8,128)S(1)} %collective-permute-done.4.refs_2_.refs_11_), channel_id=1, source_target_pairs={{0,1},{1,0},{2,3},{3,2},{4,5},{5,4},{6,7},{7,6},{8,9},{9,8},{10,11... | collective-permute-start | bytes 417800 | tf_op jit(solution)/shard_map/ppermute | solution.py:507
  21.5 0.9 %collective-permute-done.8.refs_6_.refs_15_ = f32[272,128]{1,0:T(8,128)S(1)} collective-permute-done((f32[272,128]{1,0:T(8,128)S(1)}, f32[272,128]{1,0:T(8,128)S(1)}, u32[]{:S(2)}, u32[]{:S(2)}) %collective-permute-start.8) | collective-permute-done | bytes 139296 | tf_op jit(solution)/shard_map/ppermute | solution.py:507
  22.4 0.4 collective-permute-done.7.refs_5_.refs_14_
  22.8 0.5 shard_map.47
  23.3 0.7 collective-permute-start.12
  24.0 0.7 collective-permute-start.11
  24.7 1.3 %collective-permute-start.10 = (f32[520,128]{1,0:T(8,128)S(1)}, f32[520,128]{1,0:T(8,128)S(1)}, u32[]{:S(2)}, u32[]{:S(2)}) collective-permute-start(f32[520,128]{1,0:T(8,128)S(1)} %shard_map.47), channel_id=1, source_target_pairs={{0,8},{1,9},{2,10},{3,11},{4,12},{5,13},{6,14},{7,15}} | collective-permute-start | bytes 798728 | tf_op jit(solution)/shard_map/ppermute | solution.py:507
  26.0 0.9 %broadcast_select_fusion = f32[512,256]{1,0:T(8,128)} fusion(f32[512,256]{1,0:T(8,128)S(1)} %copy-done.11, f32[512,256]{1,0:T(8,128)S(1)} %collective-permute-done.turned, pred[]{:T(512)S(6)} %eq.13), kind=kLoop, calls=%fused_computation.2 | loop fusion | flops 131072 | bytes 1572865 | tf_op jit(solution)/shard_map/jit(_where)/select_n | solution.py:553
  26.9 3.4 %collective-permute-start.14 = (f32[512,256]{1,0:T(8,128)}, f32[512,256]{1,0:T(8,128)}, u32[]{:S(2)}, u32[]{:S(2)}) collective-permute-start(f32[512,256]{1,0:T(8,128)} %broadcast_select_fusion), channel_id=1, source_target_pairs={{8,14},{9,15},{16,18},{17,19},{24,26},{25,27},{10,12},{11,13},{20,... | collective-permute-start | bytes 1572872 | tf_op jit(solution)/shard_map/ppermute | solution.py:507
  30.3 11.1 %collective-permute-done.10 = f32[520,128]{1,0:T(8,128)S(1)} collective-permute-done((f32[520,128]{1,0:T(8,128)S(1)}, f32[520,128]{1,0:T(8,128)S(1)}, u32[]{:S(2)}, u32[]{:S(2)}) %collective-permute-start.10) | collective-permute-done | bytes 266272 | tf_op jit(solution)/shard_map/ppermute | solution.py:507
  41.5 2.3 %collective-permute-start.13 = (f32[520,128]{1,0:T(8,128)S(1)}, f32[520,128]{1,0:T(8,128)S(1)}, u32[]{:S(2)}, u32[]{:S(2)}) collective-permute-start(f32[520,128]{1,0:T(8,128)S(1)} %add_select_fusion.here), channel_id=1, source_target_pairs={{0,1},{1,0},{2,3},{3,2},{4,5},{5,4},{6,7},{7,6},{8,9},{9,8},{10,11... | collective-permute-start | bytes 798728 | tf_op jit(solution)/shard_map/ppermute | solution.py:507
  43.8 1.0 %shard_map.48.refs_4_ = f32[256,512]{1,0:T(8,128)S(1)} custom-call(s32[5]{0:T(128)S(1)} %stack.23.info, f32[512,256]{1,0:T(8,128)S(1)} %collective-permute-done.turned, f32[272,128]{1,0:T(8,128)S(1)} %get-tuple-element.28.refs_0_.refs_9_, f32[272,128]{1,0:T(8,128)S(1)} %collective-permute-done.3.refs_1_.refs_10_, ...), custom_call_target="tpu_custom_call" | custom-call | flops 1048576 | bytes 1048576 | tf_op jit(solution)/shard_map/pallas_call | solution.py:482
  44.8 1.3 %collective-permute-start.18 = (f32[256,512]{1,0:T(8,128)S(1)}, f32[256,512]{1,0:T(8,128)S(1)}, u32[]{:S(2)}, u32[]{:S(2)}) collective-permute-start(f32[256,512]{1,0:T(8,128)S(1)} %shard_map.48.refs_4_), channel_id=1, source_target_pairs={{10,18},{11,19},{20,28},{21,29},{30,22},{31,23}} | collective-permute-start | bytes 1572872 | tf_op jit(solution)/shard_map/ppermute | solution.py:507
  46.1 1.3 %collective-permute-start.17 = (f32[256,512]{1,0:T(8,128)S(1)}, f32[256,512]{1,0:T(8,128)S(1)}, u32[]{:S(2)}, u32[]{:S(2)}) collective-permute-start(f32[256,512]{1,0:T(8,128)S(1)} %shard_map.48.refs_4_), channel_id=1, source_target_pairs={{10,26},{11,27},{20,12},{21,13},{30,14},{31,15}} | collective-permute-start | bytes 1572872 | tf_op jit(solution)/shard_map/ppermute | solution.py:507
  47.4 2.1 %collective-permute-start.16 = (f32[256,512]{1,0:T(8,128)S(1)}, f32[256,512]{1,0:T(8,128)}, u32[]{:S(2)}, u32[]{:S(2)}) collective-permute-start(f32[256,512]{1,0:T(8,128)S(1)} %shard_map.48.refs_4_), channel_id=1, source_target_pairs={{10,2},{11,3},{20,4},{21,5},{30,6},{31,7}} | collective-permute-start | bytes 1572872 | tf_op jit(solution)/shard_map/ppermute | solution.py:507
  49.5 4.2 %all-to-all-start = ((f32[8,136,128]{2,1,0:T(8,128)}), f32[8,136,128]{2,1,0:T(8,128)}, u32[]{:S(2)}, u32[]{:S(2)}) async-start(f32[8,136,128]{2,1,0:T(8,128)} %get-tuple-element.34), calls=%async_computation | async-start | bytes 1114112 | tf_op jit(solution)/shard_map/all_to_all | solution.py:560
  53.7 0.2 select_select_fusion.refs_2_
  54.0 13.2 %shard_map.49.refs_8_ = f32[3,256,256]{2,1,0:T(8,128)} custom-call(s32[5]{0:T(128)S(1)} %stack.23.info, f32[520,128]{1,0:T(8,128)S(1)} %add_select_fusion.here, f32[520,128]{1,0:T(8,128)S(1)} %collective-permute-done.13.there), custom_call_target="tpu_custom_call" | custom-call | flops 8589934592 | bytes 1048576 | tf_op jit(solution)/shard_map/pallas_call | solution.py:482
  67.2 1.6 %collective-permute-done.16.refs_5_ = f32[256,512]{1,0:T(8,128)} collective-permute-done((f32[256,512]{1,0:T(8,128)S(1)}, f32[256,512]{1,0:T(8,128)}, u32[]{:S(2)}, u32[]{:S(2)}) %collective-permute-start.16) | collective-permute-done | bytes 524320 | tf_op jit(solution)/shard_map/ppermute | solution.py:507
  68.8 6.0 %shard_map.50 = f32[512,256]{1,0:T(8,128)} custom-call(s32[5]{0:T(128)S(1)} %stack.23.info, f32[512,256]{1,0:T(8,128)} %refs_0_.1, f32[8,136,128]{2,1,0:T(8,128)} %all-to-all-done.refs_1_, f32[512,256]{1,0:T(8,128)S(1)} %select_select_fusion.refs_2_, f32[512,256]{1,0:T(8,128)S(1)} %collective-permute-done.15.refs_3_, f32[256,512]{1,0:T(8,128)} %copy-done.8, ...), custom_call_target="tpu_custom_call" | custom-call | flops 2147483648 | bytes 1048576 | tf_op jit(solution)/shard_map/pallas_call | solution.py:482
  (42 shorter events, 0.5 us)
Async XLA Ops:
  0.0 0.7 copy-start.9
  0.0 0.7 copy-start.10
  0.0 3.8 %copy-start.11 = (f32[512,256]{1,0:T(8,128)S(1)}, f32[512,256]{1,0:T(8,128)}, u32[]{:S(2)}) copy-start(f32[512,256]{1,0:T(8,128)} %refs_0_.1) | copy-start | bytes 1572868
  3.1 40.7 %copy-start = (f32[272,128]{1,0:T(8,128)}, f32[272,128]{1,0:T(8,128)S(1)}, u32[]{:S(2)}) copy-start(f32[272,128]{1,0:T(8,128)S(1)} %get-tuple-element.28.refs_0_.refs_9_) | copy-start | bytes 417796
  3.1 4.7 %collective-permute-start.1 = (f32[520,128]{1,0:T(8,128)S(1)}, f32[520,128]{1,0:T(8,128)S(1)}, u32[]{:S(2)}, u32[]{:S(2)}) collective-permute-start(f32[520,128]{1,0:T(8,128)S(1)} %get-tuple-element.27.diag), channel_id=1, source_target_pairs={{0,4},{1,5}} | collective-permute-start | bytes 798728 | tf_op jit(solution)/shard_map/ppermute | solution.py:507
  3.8 17.6 %collective-permute-start = (f32[512,256]{1,0:T(8,128)S(1)}, f32[512,256]{1,0:T(8,128)S(1)}, u32[]{:S(2)}, u32[]{:S(2)}) collective-permute-start(f32[512,256]{1,0:T(8,128)S(1)} %copy-done.11), channel_id=1, source_target_pairs={{2,10},{3,11},{4,20},{5,21},{6,30},{7,31}} | collective-permute-start | bytes 1572872 | tf_op jit(solution)/shard_map/ppermute | solution.py:507
  5.1 4.6 %collective-permute-start.5 = (f32[272,128]{1,0:T(8,128)S(1)}, f32[272,128]{1,0:T(8,128)S(1)}, u32[]{:S(2)}, u32[]{:S(2)}) collective-permute-start(f32[272,128]{1,0:T(8,128)S(1)} %get-tuple-element.28.refs_0_.refs_9_), channel_id=1, source_target_pairs={{0,2},{1,3},{2,0},{3,1},{4,6},{5,7},{6,4},{7,5},{8,10},{9,11},{10,... | collective-permute-start | bytes 417800 | tf_op jit(solution)/shard_map/ppermute | solution.py:507
  5.2 7.9 %collective-permute-start.4 = (f32[272,128]{1,0:T(8,128)S(1)}, f32[272,128]{1,0:T(8,128)S(1)}, u32[]{:S(2)}, u32[]{:S(2)}) collective-permute-start(f32[272,128]{1,0:T(8,128)S(1)} %get-tuple-element.28.refs_0_.refs_9_), channel_id=1, source_target_pairs={{0,4},{1,5},{2,6},{3,7},{4,0},{5,1},{6,2},{7,3},{8,12},{9,13},{10,... | collective-permute-start | bytes 417800 | tf_op jit(solution)/shard_map/ppermute | solution.py:507
  7.0 12.7 %collective-permute-start.3 = (f32[272,128]{1,0:T(8,128)S(1)}, f32[272,128]{1,0:T(8,128)S(1)}, u32[]{:S(2)}, u32[]{:S(2)}) collective-permute-start(f32[272,128]{1,0:T(8,128)S(1)} %get-tuple-element.28.refs_0_.refs_9_), channel_id=1, source_target_pairs={{0,6},{1,7},{2,4},{3,5},{4,2},{5,3},{6,0},{7,1},{8,14},{9,15},{10,... | collective-permute-start | bytes 417800 | tf_op jit(solution)/shard_map/ppermute | solution.py:507
  7.8 15.0 %collective-permute-start.2 = (f32[520,128]{1,0:T(8,128)S(1)}, f32[520,128]{1,0:T(8,128)S(1)}, u32[]{:S(2)}, u32[]{:S(2)}) collective-permute-start(f32[520,128]{1,0:T(8,128)S(1)} %broadcast_select_fusion.1), channel_id=1, source_target_pairs={{0,2},{1,3},{4,6},{5,7}} | collective-permute-start | bytes 798728 | tf_op jit(solution)/shard_map/ppermute | solution.py:507
  9.7 34.1 %copy-start.1 = (f32[272,128]{1,0:T(8,128)}, f32[272,128]{1,0:T(8,128)S(1)}, u32[]{:S(2)}) copy-start(f32[272,128]{1,0:T(8,128)S(1)} %collective-permute-done.5.refs_3_.refs_12_) | copy-start | bytes 417796
  9.7 11.8 %collective-permute-start.6 = (f32[272,128]{1,0:T(8,128)S(1)}, f32[272,128]{1,0:T(8,128)S(1)}, u32[]{:S(2)}, u32[]{:S(2)}) collective-permute-start(f32[272,128]{1,0:T(8,128)S(1)} %get-tuple-element.28.refs_0_.refs_9_), channel_id=1, source_target_pairs={{0,1},{1,0},{2,3},{3,2},{4,5},{5,4},{6,7},{7,6},{8,9},{9,8},{10,11... | collective-permute-start | bytes 417800 | tf_op jit(solution)/shard_map/ppermute | solution.py:507
  13.1 30.7 %copy-start.2 = (f32[272,128]{1,0:T(8,128)}, f32[272,128]{1,0:T(8,128)S(1)}, u32[]{:S(2)}) copy-start(f32[272,128]{1,0:T(8,128)S(1)} %collective-permute-done.4.refs_2_.refs_11_) | copy-start | bytes 417796
  13.1 8.4 %collective-permute-start.9 = (f32[272,128]{1,0:T(8,128)S(1)}, f32[272,128]{1,0:T(8,128)S(1)}, u32[]{:S(2)}, u32[]{:S(2)}) collective-permute-start(f32[272,128]{1,0:T(8,128)S(1)} %collective-permute-done.5.refs_3_.refs_12_), channel_id=1, source_target_pairs={{0,1},{1,0},{2,3},{3,2},{4,5},{5,4},{6,7},{7,6},{8,9},{9,8},{10,11... | collective-permute-start | bytes 417800 | tf_op jit(solution)/shard_map/ppermute | solution.py:507
  19.8 24.0 %copy-start.3 = (f32[272,128]{1,0:T(8,128)}, f32[272,128]{1,0:T(8,128)S(1)}, u32[]{:S(2)}) copy-start(f32[272,128]{1,0:T(8,128)S(1)} %collective-permute-done.3.refs_1_.refs_10_) | copy-start | bytes 417796
  19.8 2.6 %collective-permute-start.8 = (f32[272,128]{1,0:T(8,128)S(1)}, f32[272,128]{1,0:T(8,128)S(1)}, u32[]{:S(2)}, u32[]{:S(2)}) collective-permute-start(f32[272,128]{1,0:T(8,128)S(1)} %collective-permute-done.4.refs_2_.refs_11_), channel_id=1, source_target_pairs={{0,1},{1,0},{2,3},{3,2},{4,5},{5,4},{6,7},{7,6},{8,9},{9,8},{10,11... | collective-permute-start | bytes 417800 | tf_op jit(solution)/shard_map/ppermute | solution.py:507
  21.4 1.4 %collective-permute-start.7 = (f32[272,128]{1,0:T(8,128)S(1)}, f32[272,128]{1,0:T(8,128)S(1)}, u32[]{:S(2)}, u32[]{:S(2)}) collective-permute-start(f32[272,128]{1,0:T(8,128)S(1)} %collective-permute-done.3.refs_1_.refs_10_), channel_id=1, source_target_pairs={{0,1},{1,0},{2,3},{3,2},{4,5},{5,4},{6,7},{7,6},{8,9},{9,8},{10,11... | collective-permute-start | bytes 417800 | tf_op jit(solution)/shard_map/ppermute | solution.py:507
  21.5 22.3 %copy-start.4 = (f32[272,128]{1,0:T(8,128)}, f32[272,128]{1,0:T(8,128)S(1)}, u32[]{:S(2)}) copy-start(f32[272,128]{1,0:T(8,128)S(1)} %collective-permute-done.6.refs_4_.refs_13_) | copy-start | bytes 417796
  21.5 22.3 %copy-start.5 = (f32[272,128]{1,0:T(8,128)}, f32[272,128]{1,0:T(8,128)S(1)}, u32[]{:S(2)}) copy-start(f32[272,128]{1,0:T(8,128)S(1)} %collective-permute-done.9.refs_7_.refs_16_) | copy-start | bytes 417796
  22.4 21.4 %copy-start.6 = (f32[272,128]{1,0:T(8,128)}, f32[272,128]{1,0:T(8,128)S(1)}, u32[]{:S(2)}) copy-start(f32[272,128]{1,0:T(8,128)S(1)} %collective-permute-done.8.refs_6_.refs_15_) | copy-start | bytes 417796
  22.8 21.0 %copy-start.7 = (f32[272,128]{1,0:T(8,128)}, f32[272,128]{1,0:T(8,128)S(1)}, u32[]{:S(2)}) copy-start(f32[272,128]{1,0:T(8,128)S(1)} %collective-permute-done.7.refs_5_.refs_14_) | copy-start | bytes 417796
  23.3 6.9 %collective-permute-start.12 = (f32[520,128]{1,0:T(8,128)S(1)}, f32[520,128]{1,0:T(8,128)S(1)}, u32[]{:S(2)}, u32[]{:S(2)}) collective-permute-start(f32[520,128]{1,0:T(8,128)S(1)} %shard_map.47), channel_id=1, source_target_pairs={{0,24},{1,25},{2,26},{3,27},{4,28},{5,29},{6,30},{7,31}} | collective-permute-start | bytes 798728 | tf_op jit(solution)/shard_map/ppermute | solution.py:507
  24.0 6.2 %collective-permute-start.11 = (f32[520,128]{1,0:T(8,128)S(1)}, f32[520,128]{1,0:T(8,128)S(1)}, u32[]{:S(2)}, u32[]{:S(2)}) collective-permute-start(f32[520,128]{1,0:T(8,128)S(1)} %shard_map.47), channel_id=1, source_target_pairs={{0,16},{1,17},{2,18},{3,19},{4,20},{5,21},{6,22},{7,23}} | collective-permute-start | bytes 798728 | tf_op jit(solution)/shard_map/ppermute | solution.py:507
  24.7 16.7 %collective-permute-start.10 = (f32[520,128]{1,0:T(8,128)S(1)}, f32[520,128]{1,0:T(8,128)S(1)}, u32[]{:S(2)}, u32[]{:S(2)}) collective-permute-start(f32[520,128]{1,0:T(8,128)S(1)} %shard_map.47), channel_id=1, source_target_pairs={{0,8},{1,9},{2,10},{3,11},{4,12},{5,13},{6,14},{7,15}} | collective-permute-start | bytes 798728 | tf_op jit(solution)/shard_map/ppermute | solution.py:507
  26.9 26.8 %collective-permute-start.14 = (f32[512,256]{1,0:T(8,128)}, f32[512,256]{1,0:T(8,128)}, u32[]{:S(2)}, u32[]{:S(2)}) collective-permute-start(f32[512,256]{1,0:T(8,128)} %broadcast_select_fusion), channel_id=1, source_target_pairs={{8,14},{9,15},{16,18},{17,19},{24,26},{25,27},{10,12},{11,13},{20,... | collective-permute-start | bytes 1572872 | tf_op jit(solution)/shard_map/ppermute | solution.py:507
  41.5 12.2 %collective-permute-start.13 = (f32[520,128]{1,0:T(8,128)S(1)}, f32[520,128]{1,0:T(8,128)S(1)}, u32[]{:S(2)}, u32[]{:S(2)}) collective-permute-start(f32[520,128]{1,0:T(8,128)S(1)} %add_select_fusion.here), channel_id=1, source_target_pairs={{0,1},{1,0},{2,3},{3,2},{4,5},{5,4},{6,7},{7,6},{8,9},{9,8},{10,11... | collective-permute-start | bytes 798728 | tf_op jit(solution)/shard_map/ppermute | solution.py:507
  44.8 4.8 %copy-start.8 = (f32[256,512]{1,0:T(8,128)}, f32[256,512]{1,0:T(8,128)S(1)}, u32[]{:S(2)}) copy-start(f32[256,512]{1,0:T(8,128)S(1)} %shard_map.48.refs_4_) | copy-start | bytes 1572868
  44.8 22.4 %collective-permute-start.18 = (f32[256,512]{1,0:T(8,128)S(1)}, f32[256,512]{1,0:T(8,128)S(1)}, u32[]{:S(2)}, u32[]{:S(2)}) collective-permute-start(f32[256,512]{1,0:T(8,128)S(1)} %shard_map.48.refs_4_), channel_id=1, source_target_pairs={{10,18},{11,19},{20,28},{21,29},{30,22},{31,23}} | collective-permute-start | bytes 1572872 | tf_op jit(solution)/shard_map/ppermute | solution.py:507
  46.1 21.0 %collective-permute-start.17 = (f32[256,512]{1,0:T(8,128)S(1)}, f32[256,512]{1,0:T(8,128)S(1)}, u32[]{:S(2)}, u32[]{:S(2)}) collective-permute-start(f32[256,512]{1,0:T(8,128)S(1)} %shard_map.48.refs_4_), channel_id=1, source_target_pairs={{10,26},{11,27},{20,12},{21,13},{30,14},{31,15}} | collective-permute-start | bytes 1572872 | tf_op jit(solution)/shard_map/ppermute | solution.py:507
  47.4 21.4 %collective-permute-start.16 = (f32[256,512]{1,0:T(8,128)S(1)}, f32[256,512]{1,0:T(8,128)}, u32[]{:S(2)}, u32[]{:S(2)}) collective-permute-start(f32[256,512]{1,0:T(8,128)S(1)} %shard_map.48.refs_4_), channel_id=1, source_target_pairs={{10,2},{11,3},{20,4},{21,5},{30,6},{31,7}} | collective-permute-start | bytes 1572872 | tf_op jit(solution)/shard_map/ppermute | solution.py:507
  49.5 19.3 %all-to-all-start = ((f32[8,136,128]{2,1,0:T(8,128)}), f32[8,136,128]{2,1,0:T(8,128)}, u32[]{:S(2)}, u32[]{:S(2)}) async-start(f32[8,136,128]{2,1,0:T(8,128)} %get-tuple-element.34), calls=%async_computation | async-start | bytes 1114112 | tf_op jit(solution)/shard_map/all_to_all | solution.py:560
  53.9 14.9 %collective-permute-start.15 = (f32[512,256]{1,0:T(8,128)S(1)}, f32[512,256]{1,0:T(8,128)S(1)}, u32[]{:S(2)}, u32[]{:S(2)}) collective-permute-start(f32[512,256]{1,0:T(8,128)S(1)} %select_select_fusion.refs_2_), channel_id=1, source_target_pairs={{0,1},{1,0},{2,3},{3,2},{4,5},{5,4},{6,7},{7,6},{8,9},{9,8},{10,11... | collective-permute-start | bytes 1572872 | tf_op jit(solution)/shard_map/ppermute | solution.py:507
